TPU v7x, 32 devices: a whole 2x2x4 slice. The times are simulated.
32 devices in a mesh: fsdp: 4 (over z), ctx: 4 (over y, x), tp: 2 (over core).
Axes of the slice: x: 2, y: 2, z: 4, core: 2. Of those that a mesh axis runs over, the one named last changes fastest.
Arguments:
- tokens: bfloat16 [4096, 2048], P(('fsdp', 'ctx')), may hold values from -6 to 6
- lengths: int32 [4], replicated, may hold values from 1024 to 1024, as said below
- dealing: int32 [4], replicated, may hold values from 0 to 3, as said below
- w_query: bfloat16 [2048, 2048], P(('fsdp', 'ctx'), 'tp'), may hold values from -0.25 to 0.25
- w_key: bfloat16 [2048, 2048], P(('fsdp', 'ctx'), 'tp'), may hold values from -0.125 to 0.125
- w_value: bfloat16 [2048, 2048], P(('fsdp', 'ctx'), 'tp'), may hold values from -0.125 to 0.125
- w_out: bfloat16 [2048, 2048], P(('fsdp', 'ctx'), 'tp'), may hold values from -1 to 1
- b_query: float32 [2048], P('tp'), may hold values from -3 to 3
- b_value: float32 [2048], P('tp'), may hold values from -0.3125 to 0.3125
- b_out: float32 [2048], replicated, may hold values from -1.25 to 1.25
- gain_mid: float32 [2048], replicated, may hold values from 0.25 to 1.75
- shift_mid: float32 [2048], replicated, may hold values from -1.25 to 1.25
- w_up: bfloat16 [2048, 8192], P(('fsdp', 'ctx'), 'tp'), may hold values from -0.125 to 0.125
- b_up: float32 [8192], P('tp'), may hold values from -1.25 to 1.25
- w_down: bfloat16 [2048, 8192], P(('fsdp', 'ctx'), 'tp'), may hold values from -0.0625 to 0.0625
- b_down: float32 [2048], replicated, may hold values from -1.25 to 1.25
- gain_end: float32 [2048], replicated, may hold values from 0.25 to 1.75
- shift_end: float32 [2048], replicated, may hold values from -1.25 to 1.25
- cotangent: bfloat16 [4096, 2048], P(('fsdp', 'ctx')), may hold values from -6 to 6
Outputs:
- output: bfloat16 [4096, 2048], P(('fsdp', 'ctx'))
- grad_tokens: bfloat16 [4096, 2048], P(('fsdp', 'ctx'))
- grad_query: float32 [2048, 2048], P(('fsdp', 'ctx'), 'tp')
- grad_key: float32 [2048, 2048], P(('fsdp', 'ctx'), 'tp')
- grad_value: float32 [2048, 2048], P(('fsdp', 'ctx'), 'tp')
- grad_out: float32 [2048, 2048], P(('fsdp', 'ctx'), 'tp')
- grad_bquery: float32 [2048], P('tp')
- grad_bvalue: float32 [2048], P('tp')
- grad_bout: float32 [2048], replicated
- grad_gmid: float32 [2048], replicated
- grad_smid: float32 [2048], replicated
- grad_up: float32 [2048, 8192], P(('fsdp', 'ctx'), 'tp')
- grad_bup: float32 [8192], P('tp')
- grad_down: float32 [2048, 8192], P(('fsdp', 'ctx'), 'tp')
- grad_bdown: float32 [2048], replicated
- grad_gend: float32 [2048], replicated
- grad_send: float32 [2048], replicated
Inputs may be any that keep to these rules, and one draw needn't show every extreme that they name: `lengths`: in every draw some sequence has exactly 1024 live positions. `dealing`: A permutation: each sequence is held by exactly one group.
All inputs are finite; a program needn't handle non-finite values.
Results may differ from a plain program's by a relative error of at most 0.02.
The roundings to bfloat16 on the way count: a program that leaves them out, or rounds other values in their place, can miss the bound.
Values may be sent and summed in bfloat16 or wider, within the bound.
No kernel may reach another device: no remote copies, remote signals or barrier semaphores. Data moves between devices by JAX's collectives and lax.ppermute only.
A program may use at most 320 MiB of HBM per device.

v0:
```python
import math

import jax
import jax.numpy as jnp
from jax import lax
from jax.sharding import PartitionSpec as P

D = 2048
HEADS = 16


EPSILON = 1e-12
NEGATIVE = -1e30
WIDE = jnp.float32
LOWER = jnp.bfloat16


def layer_norm(inputs, gain_vec, shift_vec):
    row_mean = jnp.mean(inputs, axis=-1, keepdims=True)
    centred = inputs - row_mean
    spread = jnp.mean(centred * centred, axis=-1, keepdims=True)
    return centred * lax.rsqrt(spread + EPSILON) * gain_vec + shift_vec


def gelu_tanh(inputs):
    return jax.nn.gelu(inputs, approximate=True)


def pick_rows(target, row_count, carried, pieces):
    offset = target * row_count
    inside = jnp.logical_and(offset >= 0, offset + row_count <= pieces.shape[0])
    begin_row = jnp.clip(offset, 0, pieces.shape[0] - row_count)
    taken_rows = lax.dynamic_slice_in_dim(pieces, begin_row, row_count, 0)
    return jnp.where(inside, taken_rows, carried)


def fetch_attention(w_query, w_key, w_value, w_out):
    return (
        lax.all_gather(w_query, ("fsdp", "ctx"), axis=0, tiled=True),
        lax.all_gather(w_key, ("fsdp", "ctx"), axis=0, tiled=True),
        lax.all_gather(w_value, ("fsdp", "ctx"), axis=0, tiled=True),
        lax.all_gather(w_out, ("fsdp", "ctx"), axis=0, tiled=True),
    )


def fetch_up(w_up):
    return lax.all_gather(w_up, ("fsdp", "ctx"), axis=0, tiled=True)


def fetch_down(w_down):
    return lax.all_gather(w_down, ("fsdp", "ctx"), axis=0, tiled=True)


def fetch_keys(keys_own, values_own):
    return (
        lax.all_gather(keys_own, "ctx", axis=0, tiled=True),
        lax.all_gather(values_own, "ctx", axis=0, tiled=True),
    )


def head_total(partial_value):
    return lax.psum(partial_value.astype(jnp.bfloat16), "tp").astype(jnp.float32)


def block_plan(key_count):
    block_rows = min(512, key_count)
    return (block_rows, key_count // block_rows)


def masked_scores(query_heads, key_heads, key_live, first_key, block_rows, score_scale):
    key_part = lax.dynamic_slice_in_dim(key_heads, first_key, block_rows, 0)
    live_part = lax.dynamic_slice_in_dim(key_live, first_key, block_rows, 0)
    scores = (
        jnp.einsum("qhd,khd->hqk", query_heads, key_part, preferred_element_type=WIDE) * score_scale
    )
    return jnp.where(live_part[None, None, :], scores, NEGATIVE)


def softmax_totals(query_heads, key_heads, key_live, score_scale):
    block_rows, block_count = block_plan(key_heads.shape[0])

    def advance(carried, block_index):
        run_max, run_sum = carried
        scores = masked_scores(
            query_heads, key_heads, key_live, block_index * block_rows, block_rows, score_scale
        )
        new_max = jnp.maximum(run_max, jnp.max(scores, axis=-1))
        run_sum = run_sum * jnp.exp(run_max - new_max) + jnp.sum(
            jnp.exp(scores - new_max[:, :, None]), axis=-1
        )
        return ((new_max, run_sum), None)

    stat_shape = (query_heads.shape[1], query_heads.shape[0])
    start_max = jnp.full(stat_shape, NEGATIVE, WIDE)
    start_sum = jnp.zeros(stat_shape, WIDE)
    totals = lax.scan(advance, (start_max, start_sum), jnp.arange(block_count, dtype=jnp.int32))[0]
    return totals[0] + jnp.log(totals[1])


def attend_values(query_heads, key_heads, value_heads, key_live, log_total, score_scale):
    block_rows, block_count = block_plan(key_heads.shape[0])

    def advance(carried, block_index):
        first_key = block_index * block_rows
        scores = masked_scores(query_heads, key_heads, key_live, first_key, block_rows, score_scale)
        weights = jnp.exp(scores - log_total[:, :, None]).astype(LOWER)
        value_part = lax.dynamic_slice_in_dim(value_heads, first_key, block_rows, 0)
        return (
            carried + jnp.einsum("hqk,khd->qhd", weights, value_part, preferred_element_type=WIDE),
            None,
        )

    start_out = jnp.zeros(query_heads.shape, WIDE)
    return lax.scan(advance, start_out, jnp.arange(block_count, dtype=jnp.int32))[0]


def attend_back(
    query_heads, key_heads, value_heads, key_live, log_total, grad_heads, row_delta, score_scale
):
    block_rows, block_count = block_plan(key_heads.shape[0])

    def advance(grad_query, block_index):
        first_key = block_index * block_rows
        scores = masked_scores(query_heads, key_heads, key_live, first_key, block_rows, score_scale)
        softmaxed = jnp.exp(scores - log_total[:, :, None])
        key_part = lax.dynamic_slice_in_dim(key_heads, first_key, block_rows, 0)
        value_part = lax.dynamic_slice_in_dim(value_heads, first_key, block_rows, 0)
        grad_probs = jnp.einsum("qhd,khd->hqk", grad_heads, value_part, preferred_element_type=WIDE)
        grad_scores = (softmaxed * (grad_probs - row_delta[:, :, None])).astype(LOWER)
        grad_query = (
            grad_query
            + jnp.einsum("hqk,khd->qhd", grad_scores, key_part, preferred_element_type=WIDE)
            * score_scale
        )
        key_term = (
            jnp.einsum("hqk,qhd->khd", grad_scores, query_heads, preferred_element_type=WIDE)
            * score_scale
        )
        value_term = jnp.einsum(
            "hqk,qhd->khd", softmaxed.astype(LOWER), grad_heads, preferred_element_type=WIDE
        )
        return (grad_query, (key_term, value_term))

    grad_query, key_terms = lax.scan(
        advance, jnp.zeros(query_heads.shape, WIDE), jnp.arange(block_count, dtype=jnp.int32)
    )
    key_count = key_heads.shape[0]
    return (grad_query, key_terms[0].reshape(key_count, -1), key_terms[1].reshape(key_count, -1))


def local(
    tokens,
    lengths,
    dealing,
    w_query,
    w_key,
    w_value,
    w_out,
    b_query,
    b_value,
    b_out,
    gain_mid,
    shift_mid,
    w_up,
    b_up,
    w_down,
    b_down,
    gain_end,
    shift_end,
    cotangent,
):
    row_count = tokens.shape[0]
    local_width = w_query.shape[1]
    head_size = D // HEADS
    heads_here = local_width // head_size
    score_scale = 1.0 / math.sqrt(head_size)
    group_id = lax.axis_index("fsdp")
    ctx_rank = lax.axis_index("ctx")
    seq_ids = jnp.arange(dealing.shape[0], dtype=jnp.int32)
    source_seq = jnp.sum(jnp.where(seq_ids == group_id, dealing, 0))
    home_group = jnp.sum(jnp.where(dealing == group_id, seq_ids, 0))
    live_count = jnp.sum(jnp.where(seq_ids == source_seq, lengths, 0))
    inputs = pick_rows(
        source_seq,
        row_count,
        jnp.zeros_like(tokens),
        lax.all_gather(tokens, "fsdp", axis=0, tiled=True),
    )
    key_count = row_count * lax.axis_size("ctx")
    key_live = jnp.arange(key_count, dtype=jnp.int32) < live_count
    own_live = lax.dynamic_slice_in_dim(key_live, ctx_rank * row_count, row_count, 0)
    query_live = own_live[:, None]
    attn_mats = fetch_attention(w_query, w_key, w_value, w_out)
    query_full, key_full, value_full, out_full = attn_mats
    queries = (jnp.dot(inputs, query_full, preferred_element_type=WIDE) + b_query).astype(LOWER)
    keys_own = jnp.dot(inputs, key_full, preferred_element_type=WIDE).astype(LOWER)
    values_own = (jnp.dot(inputs, value_full, preferred_element_type=WIDE) + b_value).astype(LOWER)
    keys_all, values_all = fetch_keys(keys_own, values_own)
    query_heads = queries.reshape(row_count, heads_here, head_size)
    key_heads = keys_all.reshape(key_count, heads_here, head_size)
    value_heads = values_all.reshape(key_count, heads_here, head_size)
    log_total = softmax_totals(query_heads, key_heads, key_live, score_scale)
    attended = attend_values(query_heads, key_heads, value_heads, key_live, log_total, score_scale)
    attended_b = attended.reshape(row_count, local_width).astype(LOWER)
    branch = (
        head_total(jnp.einsum("th,dh->td", attended_b, out_full, preferred_element_type=WIDE))
        + b_out
    )
    middle, mid_back = jax.vjp(layer_norm, inputs.astype(WIDE) + branch, gain_mid, shift_mid)
    middle_b = middle.astype(LOWER)
    up_full = fetch_up(w_up)
    hidden = jnp.dot(middle_b, up_full, preferred_element_type=WIDE) + b_up
    active, gelu_back = jax.vjp(gelu_tanh, hidden)
    active_b = active.astype(LOWER)
    down_full = fetch_down(w_down)
    result = (
        head_total(jnp.einsum("tf,df->td", active_b, down_full, preferred_element_type=WIDE))
        + b_down
    )
    normed, end_back = jax.vjp(layer_norm, middle + result, gain_end, shift_end)
    output = jnp.where(query_live, normed, 0.0).astype(LOWER)
    grad_normed = jnp.where(query_live, cotangent.astype(WIDE), 0.0)
    grad_sum, grad_gend, grad_send = end_back(grad_normed)
    grad_result = grad_sum.astype(LOWER)
    down_back = fetch_down(w_down)
    grad_active = jnp.dot(grad_result, down_back, preferred_element_type=WIDE)
    grad_hidden = gelu_back(grad_active)[0].astype(LOWER)
    up_back = fetch_up(w_up)
    grad_middle = grad_sum + head_total(
        jnp.einsum("tf,df->td", grad_hidden, up_back, preferred_element_type=WIDE)
    )
    grad_inner, grad_gmid, grad_smid = mid_back(grad_middle)
    grad_branch = grad_inner.astype(LOWER)
    attn_back = fetch_attention(w_query, w_key, w_value, w_out)
    grad_attended = jnp.dot(grad_branch, attn_back[3], preferred_element_type=WIDE).astype(LOWER)
    grad_heads = grad_attended.reshape(row_count, heads_here, head_size)
    row_delta = jnp.einsum("qhd,qhd->hq", grad_heads.astype(WIDE), attended)
    back_keys = fetch_keys(keys_own, values_own)
    grad_qheads, key_term, value_term = attend_back(
        query_heads,
        back_keys[0].reshape(key_count, heads_here, head_size),
        back_keys[1].reshape(key_count, heads_here, head_size),
        key_live,
        log_total,
        grad_heads,
        row_delta,
        score_scale,
    )
    grad_keys, grad_values = (
        lax.psum_scatter(
            key_term.astype(jnp.bfloat16), "ctx", scatter_dimension=0, tiled=True
        ).astype(jnp.float32),
        lax.psum_scatter(
            value_term.astype(jnp.bfloat16), "ctx", scatter_dimension=0, tiled=True
        ).astype(jnp.float32),
    )
    grad_queries = grad_qheads.reshape(row_count, local_width).astype(LOWER)
    grad_keys_b = grad_keys.astype(LOWER)
    grad_values_b = grad_values.astype(LOWER)
    grad_input = jnp.einsum("th,dh->td", grad_queries, attn_back[0], preferred_element_type=WIDE)
    grad_input = grad_input + jnp.einsum(
        "th,dh->td", grad_keys_b, attn_back[1], preferred_element_type=WIDE
    )
    grad_input = grad_input + jnp.einsum(
        "th,dh->td", grad_values_b, attn_back[2], preferred_element_type=WIDE
    )
    grad_dealt = (head_total(grad_input) + grad_inner).astype(LOWER)
    grad_tokens = pick_rows(
        home_group,
        row_count,
        jnp.zeros_like(grad_dealt),
        lax.all_gather(grad_dealt, "fsdp", axis=0, tiled=True),
    )
    attn_grads = lax.psum_scatter(
        jnp.concatenate(
            [
                jnp.einsum("td,th->dh", inputs, grad_queries, preferred_element_type=WIDE),
                jnp.einsum("td,th->dh", inputs, grad_keys_b, preferred_element_type=WIDE),
                jnp.einsum("td,th->dh", inputs, grad_values_b, preferred_element_type=WIDE),
                jnp.einsum("td,th->dh", grad_branch, attended_b, preferred_element_type=WIDE),
            ],
            axis=1,
        ),
        ("fsdp", "ctx"),
        scatter_dimension=0,
        tiled=True,
    )
    ffn_grads = lax.psum_scatter(
        jnp.concatenate(
            [
                jnp.einsum("td,tf->df", middle_b, grad_hidden, preferred_element_type=WIDE),
                jnp.einsum("td,tf->df", grad_result, active_b, preferred_element_type=WIDE),
            ],
            axis=1,
        ),
        ("fsdp", "ctx"),
        scatter_dimension=0,
        tiled=True,
    )
    ffn_width = w_up.shape[1]
    small_sums = lax.psum(
        (
            jnp.sum(grad_queries.astype(WIDE), axis=0),
            jnp.sum(grad_values_b.astype(WIDE), axis=0),
            jnp.sum(grad_branch.astype(WIDE), axis=0),
            grad_gmid,
            grad_smid,
            jnp.sum(grad_hidden.astype(WIDE), axis=0),
            jnp.sum(grad_result.astype(WIDE), axis=0),
            grad_gend,
            grad_send,
        ),
        ("fsdp", "ctx"),
    )
    return (
        output,
        grad_tokens,
        attn_grads[:, :local_width],
        attn_grads[:, local_width : 2 * local_width],
        attn_grads[:, 2 * local_width : 3 * local_width],
        attn_grads[:, 3 * local_width :],
        small_sums[0],
        small_sums[1],
        small_sums[2],
        small_sums[3],
        small_sums[4],
        ffn_grads[:, :ffn_width],
        small_sums[5],
        ffn_grads[:, ffn_width:],
        small_sums[6],
        small_sums[7],
        small_sums[8],
    )


def solution(mesh):
    in_specs = (
        P(("fsdp", "ctx"), None),
        P(),
        P(),
        P(("fsdp", "ctx"), "tp"),
        P(("fsdp", "ctx"), "tp"),
        P(("fsdp", "ctx"), "tp"),
        P(("fsdp", "ctx"), "tp"),
        P("tp"),
        P("tp"),
        P(),
        P(),
        P(),
        P(("fsdp", "ctx"), "tp"),
        P("tp"),
        P(("fsdp", "ctx"), "tp"),
        P(),
        P(),
        P(),
        P(("fsdp", "ctx"), None),
    )
    out_specs = (
        P(("fsdp", "ctx"), None),
        P(("fsdp", "ctx"), None),
        P(("fsdp", "ctx"), "tp"),
        P(("fsdp", "ctx"), "tp"),
        P(("fsdp", "ctx"), "tp"),
        P(("fsdp", "ctx"), "tp"),
        P("tp"),
        P("tp"),
        P(),
        P(),
        P(),
        P(("fsdp", "ctx"), "tp"),
        P("tp"),
        P(("fsdp", "ctx"), "tp"),
        P(),
        P(),
        P(),
    )
    return jax.shard_map(local, mesh=mesh, in_specs=in_specs, out_specs=out_specs, check_vma=False)
```

profile of v0, /device:TPU:0, one launch (start us, length us, event | category | flops | bytes accessed | tf_op | source)
XLA Modules:
  0.0 3395.6 jit_solution(15699666870430159953)
XLA Ops:
  12.0 81.1 %all-gather.11.cloned.1.call-done = bf16[1024,2048]{1,0:T(8,128)(2,1)} async-done(((bf16[256,2048]{1,0:T(8,128)(2,1)}), bf16[1024,2048]{1,0:T(8,128)(2,1)}) %all-gather.11.cloned.1.call-update) | async-done | bytes 4194320 | tf_op jit(solution)/shard_map/all_gather | solution.py:187
  93.1 77.4 %all-gather.13.cloned.1.call-done = bf16[2048,1024]{1,0:T(8,128)(2,1)} async-done(((bf16[128,1024]{1,0:T(8,128)(2,1)}), bf16[2048,1024]{1,0:T(8,128)(2,1)}) %all-gather.13.cloned.1.call-update) | async-done | bytes 4194320 | tf_op jit(solution)/shard_map/all_gather | solution.py:41
  175.1 72.8 %all-gather.17.cloned.1.call-done = bf16[2048,1024]{1,0:T(8,128)(2,1)} async-done(((bf16[128,1024]{1,0:T(8,128)(2,1)}), bf16[2048,1024]{1,0:T(8,128)(2,1)}) %all-gather.17.cloned.1.call-update) | async-done | bytes 4194320 | tf_op jit(solution)/shard_map/all_gather | solution.py:40
  255.4 70.0 %all-gather.21.cloned.1.call-done = bf16[2048,1024]{1,0:T(8,128)(2,1)} async-done(((bf16[128,1024]{1,0:T(8,128)(2,1)}), bf16[2048,1024]{1,0:T(8,128)(2,1)}) %all-gather.21.cloned.1.call-update) | async-done | bytes 4194320 | tf_op jit(solution)/shard_map/all_gather | solution.py:39
  329.3 32.2 all-gather.15.cloned.1.call-done
  365.1 34.1 %all-gather.19.cloned.1.call-done = bf16[1024,1024]{1,0:T(8,128)(2,1)} async-done(((bf16[256,1024]{1,0:T(8,128)(2,1)}), bf16[1024,1024]{1,0:T(8,128)(2,1)}) %all-gather.19.cloned.1.call-update) | async-done | bytes 2097168 | tf_op jit(solution)/shard_map/all_gather | solution.py:56
  403.3 6.1 while.39
  409.4 17.2 while.40
  427.9 50.2 %all-gather.23.cloned.1.call-done = bf16[2048,1024]{1,0:T(8,128)(2,1)} async-done(((bf16[128,1024]{1,0:T(8,128)(2,1)}), bf16[2048,1024]{1,0:T(8,128)(2,1)}) %all-gather.23.cloned.1.call-update) | async-done | bytes 4194320 | tf_op jit(solution)/shard_map/all_gather | solution.py:42
  484.2 16.7 all-reduce.7.cloned.1.call-done
  505.4 191.4 %all-gather.25.cloned.1.call-done = bf16[2048,4096]{1,0:T(8,128)(2,1)} async-done(((bf16[128,4096]{1,0:T(8,128)(2,1)}), bf16[2048,4096]{1,0:T(8,128)(2,1)}) %all-gather.25.cloned.1.call-update) | async-done | bytes 16777232 | tf_op jit(solution)/shard_map/all_gather | solution.py:47
  696.9 13.3 convolution_add_fusion
  710.2 179.5 %all-gather.27.cloned.1.call-done = bf16[2048,4096]{1,0:T(8,128)(2,1)} async-done(((bf16[128,4096]{1,0:T(8,128)(2,1)}), bf16[2048,4096]{1,0:T(8,128)(2,1)}) %all-gather.27.cloned.1.call-update) | async-done | bytes 16777232 | tf_op jit(solution)/shard_map/all_gather | solution.py:51
  889.7 12.9 convolution_convert_fusion.1
  903.2 17.4 all-reduce.9.cloned.1.call-done
  930.8 12.2 convert_reduce_fusion
  943.0 11.9 convolution_convert_fusion
  955.2 20.7 all-reduce.11.cloned.1.call-done
  975.9 5.0 multiply_reduce_fusion.1
  992.5 22.5 while.41
  1030.7 25.8 reduce-scatter.5.cloned.1.call-done
  1061.4 33.6 reduce-scatter.7.cloned.1.call-done
  1095.1 5.4 fusion.42
  1100.6 19.7 all-reduce.13.cloned.1.call-done
  1122.9 5.9 fusion.60
  1133.9 15.0 pad_maximum_fusion.1
  1150.2 18.4 fusion.55
  1168.6 13.4 fusion.61
  1181.9 43.5 %pad_maximum_fusion = f32[2048,8192]{1,0:T(8,128)} fusion(f32[2048,4096]{1,0:T(8,128)} %fusion.61, f32[2048,4096]{1,0:T(8,128)} %fusion.55), kind=kLoop, calls=%fused_computation.44 | loop fusion | flops 16777216 | bytes 134217728 | tf_op jit(solution)/shard_map/concatenate | solution.py:289
  1229.5 659.7 %reduce-scatter.9.cloned.1.call-done = f32[128,4096]{0,1:T(8,128)} async-done(((f32[2048,4096]{0,1:T(8,128)}), f32[128,4096]{0,1:T(8,128)}) %reduce-scatter.9.cloned.1.call-update) | async-done | bytes 2097168 | tf_op jit(solution)/shard_map/reduce_scatter | solution.py:274
  1894.8 1359.8 %reduce-scatter.11.cloned.1.call-done = f32[128,8192]{1,0:T(8,128)} async-done(((f32[2048,8192]{1,0:T(8,128)}), f32[128,8192]{1,0:T(8,128)}) %reduce-scatter.11.cloned.1.call-update) | async-done | bytes 4194320 | tf_op jit(solution)/shard_map/reduce_scatter | solution.py:288
  3259.3 117.8 %all-reduce.15.cloned.1.call-done = (f32[1024]{0:T(1024)}, f32[1024]{0:T(1024)}, f32[2048]{0:T(1024)}, f32[2048]{0:T(1024)}, f32[2048]{0:T(1024)}, /*index=5*/f3...) async-done(((f32[1024]{0:T(1024)}, f32[1024]{0:T(1024)}, f32[2048]{0:T(1024)}, f32[2048]{0:T(1024)}, f32[2048]{0:T(1024)}, /*index=5*/f32[4096]{0:T(1024)}, ...) | async-done | bytes 73744 | tf_op jit(solution)/shard_map/psum | solution.py:301
  (242 shorter events, 158.3 us)
Async XLA Ops:
  7.2 85.9 %all-gather.11.cloned.1.call-start = ((), (), s32[]{:S(2)}) async-start(), calls=%async_computation.4 | async-start | bytes 5242880 | tf_op jit(solution)/shard_map/all_gather | solution.py:187
  7.9 162.6 %all-gather.13.cloned.1.call-start = ((), (), s32[]{:S(2)}) async-start(), calls=%async_computation.5 | async-start | bytes 4456448 | tf_op jit(solution)/shard_map/all_gather | solution.py:41
  8.7 239.3 %all-gather.17.cloned.1.call-start = ((), (), s32[]{:S(2)}) async-start(), calls=%async_computation.7 | async-start | bytes 4456448 | tf_op jit(solution)/shard_map/all_gather | solution.py:40
  9.4 315.9 %all-gather.21.cloned.1.call-start = ((), (), s32[]{:S(2)}) async-start(), calls=%async_computation.9 | async-start | bytes 4456448 | tf_op jit(solution)/shard_map/all_gather | solution.py:39
  10.0 351.6 %all-gather.15.cloned.1.call-start = ((), (), s32[]{:S(2)}) async-start(), calls=%async_computation.6 | async-start | bytes 2621440 | tf_op jit(solution)/shard_map/all_gather | solution.py:57
  175.1 78.3 %copy-start.37 = (s32[4]{0:T(128)S(1)}, s32[4]{0:T(128)}, u32[]{:S(2)}) copy-start(s32[4]{0:T(128)} %param.26) | copy-start | bytes 52
  175.1 150.3 %copy-start.36 = (f32[1024]{0:T(1024)S(1)}, f32[1024]{0:T(1024)}, u32[]{:S(2)}) copy-start(f32[1024]{0:T(1024)} %param.32) | copy-start | bytes 12292
  175.1 224.1 %all-gather.19.cloned.1.call-start = ((), (), s32[]{:S(2)}) async-start(), calls=%async_computation.8 | async-start | bytes 2621440 | tf_op jit(solution)/shard_map/all_gather | solution.py:56
  252.6 225.5 %all-gather.23.cloned.1.call-start = ((), (), s32[]{:S(2)}) async-start(), calls=%async_computation.10 | async-start | bytes 4456448 | tf_op jit(solution)/shard_map/all_gather | solution.py:42
  253.3 247.6 %all-reduce.7.cloned.1.call-start = ((), (), s32[]{:S(2)}) async-start(), calls=%async_computation.11 | async-start | bytes 2097152 | tf_op jit(solution)/shard_map/psum | solution.py:62
  482.5 18.4 copy-start.28
  482.5 214.3 %all-gather.25.cloned.1.call-start = ((), (), s32[]{:S(2)}) async-start(), calls=%async_computation.12 | async-start | bytes 17825792 | tf_op jit(solution)/shard_map/all_gather | solution.py:47
  483.3 406.4 %all-gather.27.cloned.1.call-start = ((), (), s32[]{:S(2)}) async-start(), calls=%async_computation.13 | async-start | bytes 17825792 | tf_op jit(solution)/shard_map/all_gather | solution.py:51
  483.9 213.0 %copy-start.29 = (f32[2048]{0:T(1024)S(1)}, f32[2048]{0:T(1024)}, u32[]{:S(2)}) copy-start(f32[2048]{0:T(1024)} %param.35) | copy-start | bytes 24580
  483.9 213.0 %copy-start.30 = (f32[2048]{0:T(1024)S(1)}, f32[2048]{0:T(1024)}, u32[]{:S(2)}) copy-start(f32[2048]{0:T(1024)} %param.36) | copy-start | bytes 24580
  483.9 213.0 %copy-start.35 = (f32[4096]{0:T(1024)S(1)}, f32[4096]{0:T(1024)}, u32[]{:S(2)}) copy-start(f32[4096]{0:T(1024)} %param.38) | copy-start | bytes 49156
  483.9 436.7 %all-reduce.9.cloned.1.call-start = ((), (), s32[]{:S(2)}) async-start(), calls=%async_computation.14 | async-start | bytes 2097152 | tf_op jit(solution)/shard_map/psum | solution.py:62
  710.2 210.4 %copy-start.32 = (f32[2048]{0:T(1024)S(1)}, f32[2048]{0:T(1024)}, u32[]{:S(2)}) copy-start(f32[2048]{0:T(1024)} %param.40) | copy-start | bytes 24580
  902.7 73.2 %all-reduce.11.cloned.1.call-start = ((), (), s32[]{:S(2)}) async-start(), calls=%async_computation.15 | async-start | bytes 2097152 | tf_op jit(solution)/shard_map/psum | solution.py:62
  930.8 12.2 copy-start.14
  955.0 101.5 %reduce-scatter.5.cloned.1.call-start = ((), (), s32[]{:S(2)}) async-start(), calls=%async_computation.16 | async-start | bytes 2621440 | tf_op jit(solution)/shard_map/reduce_scatter | solution.py:250
  975.9 5.0 copy-start.19
  1020.0 75.1 %reduce-scatter.7.cloned.1.call-start = ((), (), s32[]{:S(2)}) async-start(), calls=%async_computation.17 | async-start | bytes 2621440 | tf_op jit(solution)/shard_map/reduce_scatter | solution.py:253
  1024.8 95.5 %all-reduce.13.cloned.1.call-start = ((), (), s32[]{:S(2)}) async-start(), calls=%async_computation.18 | async-start | bytes 2097152 | tf_op jit(solution)/shard_map/psum | solution.py:62
  1095.1 25.2 copy-start.10
  1100.5 126.4 %all-gather.29.cloned.1.call-start = ((), (), s32[]{:S(2)}) async-start(), calls=%async_computation.19 | async-start | bytes 5242880 | tf_op jit(solution)/shard_map/all_gather | solution.py:272
  1122.8 5.9 copy-start.17
  1122.8 766.3 %reduce-scatter.9.cloned.1.call-start = ((), (), s32[]{:S(2)}) async-start(), calls=%async_computation.20 | async-start | bytes 35651584 | tf_op jit(solution)/shard_map/reduce_scatter | solution.py:274
  1149.0 19.6 copy-start.15
  1149.0 2105.6 %reduce-scatter.11.cloned.1.call-start = ((), (), s32[]{:S(2)}) async-start(), calls=%async_computation.21 | async-start | bytes 71303168 | tf_op jit(solution)/shard_map/reduce_scatter | solution.py:288
  1150.2 18.4 copy-start.13
  1225.5 2151.6 %all-reduce.15.cloned.1.call-start = ((), (), s32[]{:S(2)}) async-start(), calls=%async_computation.22 | async-start | bytes 147456 | tf_op jit(solution)/shard_map/psum | solution.py:301
  (32 other events, 64.2 us)
Sparse Core Ops, SparseCore 0:
  9.6 83.4 all-gather.10
  95.9 74.6 all-gather.12
  173.3 74.6 all-gather.16
  250.6 74.6 all-gather.20
  327.6 33.9 all-gather.14
  363.8 35.2 all-gather.18
  401.9 76.0 all-gather.22
  482.7 18.1 all-reduce.6
  504.0 192.7 all-gather.24
  699.9 189.7 all-gather.26
  902.8 17.7 all-reduce.8
  955.1 20.7 all-reduce.10
  1020.1 36.3 reduce-scatter.4
  1059.9 35.1 reduce-scatter.6
  1100.6 19.6 all-reduce.12
  1123.0 81.9 all-gather.28
  1207.1 681.9 reduce-scatter.8
  1891.4 1363.1 reduce-scatter.10
  3263.9 113.1 all-reduce.14
where the time goes:
time: 3400 us
  waiting for transfers between devices  3060 us (90%)
  matrix products  145 us (4%)
  other arithmetic  95.7 us (3%)
  local copies, waits for them, and re-layouts  68.1 us (2%)
    reduce_scatter x1, waiting for transfers between devices, local(): lax.psum_scatter(jnp.concatenate([jnp.einsum('td,tf->df', middle_b, grad_...  1360 us
    reduce_scatter x1, waiting for transfers between devices, local(): lax.psum_scatter(jnp.concatenate([jnp.einsum('td,th->dh', inputs, grad_qu...  660 us
    all_gather x1, waiting for transfers between devices, fetch_up(): return lax.all_gather(w_up, ('fsdp', 'ctx'), axis=0, tiled=True)  191 us
    all_gather x1, waiting for transfers between devices, fetch_down(): return lax.all_gather(w_down, ('fsdp', 'ctx'), axis=0, tiled=True)  179 us
    psum x1, waiting for transfers between devices, local(): lax.psum((jnp.sum(grad_queries.astype(WIDE), axis=0), jnp.sum(grad_values...  118 us
    all_gather x1, waiting for transfers between devices, local(): lax.all_gather(tokens, 'fsdp', axis=0, tiled=True)  81.1 us
    all_gather x1, waiting for transfers between devices, fetch_attention(): lax.all_gather(w_value, ('fsdp', 'ctx'), axis=0, tiled=True)  77.4 us
    psum x4, waiting for transfers between devices, head_total(): lax.psum(partial_value.astype(jnp.bfloat16), 'tp').astype(jnp.float32)  74.6 us
  transfers between devices with their start and end apart: 19, of which 18 were waited for; matrix products, arithmetic and copies ran while one was open for 6% of the time, Pallas kernels for 0%

commit v1 on v0

v1 whole, which is shorter than its diff:
```python
import math

import jax
import jax.numpy as jnp
from jax import lax
from jax.sharding import Mesh
from jax.sharding import PartitionSpec as P

HEAD = 128
EPSILON = 1e-12
NEGATIVE = -1e30
WIDE = jnp.float32
LOWER = jnp.bfloat16

TEAM = ("l", "x")
ROWS = ("h", "l", "y", "x")


def dot(left, right, dims):
    return lax.dot_general(left, right, (dims, ((), ())), preferred_element_type=WIDE)


def mm(left, right):
    return dot(left, right, ((1,), (0,)))


def mm_nt(left, right):
    return dot(left, right, ((1,), (1,)))


def mm_tn(left, right):
    return dot(left, right, ((0,), (0,)))


class Team:
    def __init__(self):
        self.sizes = {name: lax.axis_size(name) for name in ROWS + ("tp",)}
        self.at = {name: lax.axis_index(name) for name in ROWS + ("tp",)}
        ls, xs = self.sizes["l"], self.sizes["x"]
        self.offsets = [(dl, dx) for dl in range(ls) for dx in range(xs)]
        self.members = ls * xs

    def shift(self, value, offset, back=False):
        ls, xs = self.sizes["l"], self.sizes["x"]
        dl, dx = offset
        if back:
            dl, dx = -dl, -dx
        perm = [
            (l * xs + x, ((l + dl) % ls) * xs + (x + dx) % xs) for l in range(ls) for x in range(xs)
        ]
        return lax.ppermute(value, TEAM, perm)

    def ring(self, value, name, step):
        size = self.sizes[name]
        return lax.ppermute(value, name, [(i, (i + step) % size) for i in range(size)])

    def slot(self, offset, back=True):
        ls, xs = self.sizes["l"], self.sizes["x"]
        dl, dx = offset
        if back:
            dl, dx = -dl, -dx
        return lax.rem(self.at["l"] + dl + ls, ls) * xs + lax.rem(self.at["x"] + dx + xs, xs)


def swap_home(value):
    perm = [(l * 2 + y, y * 2 + l) for l in range(2) for y in range(2)]
    return lax.ppermute(value, ("l", "y"), perm)


def gather_rows(team, piece):
    pieces = [piece] + [team.shift(piece, offset) for offset in team.offsets[1:]]
    half = jnp.concatenate(pieces, axis=0)
    halves = [half] + [team.ring(half, "tp", step) for step in range(1, team.sizes["tp"])]
    return jnp.concatenate(halves, axis=0)


def row_blocks(team):
    ts = team.sizes["tp"]
    return [
        team.slot(offset) * ts + lax.rem(team.at["tp"] - step + ts, ts)
        for step in range(ts)
        for offset in team.offsets
    ]


def scatter_rows(team, product, row_count):
    ts, members = team.sizes["tp"], team.members
    half_rows = members * row_count
    total = product(0, half_rows)
    for step in range(1, ts):
        sent = product(step * half_rows, half_rows).astype(LOWER)
        total = total + team.ring(sent, "tp", -step).astype(WIDE)
    own = total[:row_count]
    for j, offset in enumerate(team.offsets):
        if j > 0:
            sent = total[j * row_count : (j + 1) * row_count].astype(LOWER)
            own = own + team.shift(sent, offset, back=True).astype(WIDE)
    return own


def put(buffer, value, starts):
    return lax.dynamic_update_slice(buffer, value, starts)


def gather_weights(team, shards):
    hs, ls, xs = (team.sizes[name] for name in ("h", "l", "x"))
    height = shards[0].shape[0]
    widths = [shard.shape[1] // team.members for shard in shards]
    width = sum(widths)

    def cut(slot):
        return jnp.concatenate(
            [
                lax.dynamic_slice_in_dim(shard, slot * each, each, 1)
                for shard, each in zip(shards, widths)
            ],
            axis=1,
        )

    zero = jnp.int32(0)
    near = jnp.zeros((team.members, height, width), LOWER)
    for j, offset in enumerate(team.offsets):
        piece = cut(team.slot(offset, back=False))
        if j > 0:
            piece = team.shift(piece, offset)
        near = put(near, piece[None], (team.slot(offset), zero, zero))
    near = near.reshape(1, ls, 1, xs * height, width)
    full = jnp.zeros((hs, ls, 2, xs * height, width), LOWER)
    for step in range(hs):
        row = lax.rem(team.at["h"] - step + hs, hs)
        block = team.ring(near, "h", step) if step else near
        full = put(full, block, (row, zero, team.at["y"], zero, zero))
        full = put(full, team.ring(block, "y", 1), (row, zero, 1 - team.at["y"], zero, zero))
    return full.reshape(-1, width)


def scatter_weights(team, grad, widths):
    hs, ls, xs = (team.sizes[name] for name in ("h", "l", "x"))
    width = grad.shape[1]
    height = grad.shape[0] // (hs * ls * 2 * xs)
    grad = grad.reshape(hs, ls, 2, xs * height, width)
    sent = lax.dynamic_slice_in_dim(grad, 1 - team.at["y"], 1, 2).astype(LOWER)
    mine = lax.dynamic_slice_in_dim(grad, team.at["y"], 1, 2)
    mine = mine + team.ring(sent, "y", 1).astype(WIDE)
    total = lax.dynamic_slice_in_dim(mine, team.at["h"], 1, 0)
    for step in range(1, hs):
        row = lax.rem(team.at["h"] + step, hs)
        sent = lax.dynamic_slice_in_dim(mine, row, 1, 0).astype(LOWER)
        total = total + team.ring(sent, "h", step).astype(WIDE)
    total = total.reshape(team.members, height, width)
    outs = [jnp.zeros((height, team.members, each), WIDE) for each in widths]
    for j, offset in enumerate(team.offsets):
        piece = lax.dynamic_slice_in_dim(total, team.slot(offset, back=False), 1, 0)[0]
        if j > 0:
            piece = team.shift(piece.astype(LOWER), offset).astype(WIDE)
        first = 0
        for i, each in enumerate(widths):
            block = piece[:, first : first + each][:, None]
            outs[i] = put(outs[i], block, (0, team.slot(offset), 0))
            first += each
    return [out.reshape(height, -1) for out in outs]


def pick(table, index):
    ids = jnp.arange(table.shape[0], dtype=jnp.int32)
    return jnp.sum(jnp.where(ids == index, table, 0))


def choose(pieces, index):
    out = pieces[0]
    for i in range(1, len(pieces)):
        out = jnp.where(index == i, pieces[i], out)
    return out


def spread_h(team, piece):
    return [piece] + [team.ring(piece, "h", step) for step in range(1, team.sizes["h"])]


def deal_in(team, home, piece):
    hs = team.sizes["h"]
    pieces = spread_h(team, piece)
    got = []
    for flip in range(2):
        target = team.at["l"] if flip == 0 else 1 - team.at["l"]
        group = pick(home, team.at["h"] * 2 + target)
        sent = choose(pieces, lax.rem(team.at["h"] - group // 2 + hs, hs))
        perm = [
            (l * 2 + y, y * 2 + (l if flip == 0 else 1 - l)) for l in range(2) for y in range(2)
        ]
        got.append(lax.ppermute(sent, ("l", "y"), perm))
    group = pick(home, team.at["h"] * 2 + team.at["y"])
    return jnp.where(lax.rem(group, 2) == team.at["y"], got[0], got[1])


def deal_out(team, dealing, piece):
    hs = team.sizes["h"]
    pieces = spread_h(team, piece)
    got = []
    for flip in range(2):
        target = team.at["y"] if flip == 0 else 1 - team.at["y"]
        seq = pick(dealing, team.at["h"] * 2 + target)
        sent = choose(pieces, lax.rem(team.at["h"] - seq // 2 + hs, hs))
        perm = [
            (l * 2 + y, (y if flip == 0 else 1 - y) * 2 + l) for l in range(2) for y in range(2)
        ]
        got.append(lax.ppermute(sent, ("l", "y"), perm))
    seq = pick(dealing, team.at["h"] * 2 + team.at["l"])
    return jnp.where(lax.rem(seq, 2) == team.at["l"], got[0], got[1])


def join_cores(team, piece):
    ts = team.sizes["tp"]
    out = jnp.zeros((ts,) + piece.shape, piece.dtype)
    for step in range(ts):
        other = team.ring(piece, "tp", step) if step else piece
        out = put(out, other[None], (lax.rem(team.at["tp"] - step + ts, ts), 0, 0))
    return out.reshape(-1, piece.shape[-1])


def layer_norm(inputs, gain_vec, shift_vec):
    row_mean = jnp.mean(inputs, axis=-1, keepdims=True)
    centred = inputs - row_mean
    spread = jnp.mean(centred * centred, axis=-1, keepdims=True)
    rate = lax.rsqrt(spread + EPSILON)
    xhat = centred * rate
    return xhat * gain_vec + shift_vec, xhat, rate


def layer_norm_back(grad, gain_vec, xhat, rate):
    scaled = grad * gain_vec
    return rate * (
        scaled
        - jnp.mean(scaled, axis=-1, keepdims=True)
        - xhat * jnp.mean(scaled * xhat, axis=-1, keepdims=True)
    )


def gelu_tanh(inputs):
    return jax.nn.gelu(inputs, approximate=True)


def local(
    tokens,
    lengths,
    dealing,
    w_query,
    w_key,
    w_value,
    w_out,
    b_query,
    b_value,
    b_out,
    gain_mid,
    shift_mid,
    w_up,
    b_up,
    w_down,
    b_down,
    gain_end,
    shift_end,
    cotangent,
):
    team = Team()
    ts, members = team.sizes["tp"], team.members
    row_count = tokens.shape[0] // ts
    key_count = row_count * ts * members
    wide = w_query.shape[1] // members
    heads_here = wide // HEAD
    score_scale = 1.0 / math.sqrt(HEAD)
    my_slot = team.at["l"] * team.sizes["x"] + team.at["x"]
    seq_ids = jnp.arange(dealing.shape[0], dtype=jnp.int32)
    home = jnp.sum(jnp.where(dealing[None, :] == seq_ids[:, None], seq_ids[None, :], 0), axis=1)
    live_count = pick(lengths, team.at["h"] * 2 + team.at["y"])
    position = jnp.concatenate(
        [block * row_count + jnp.arange(row_count, dtype=jnp.int32) for block in row_blocks(team)]
    )
    key_live = position < live_count
    query_live = key_live[:row_count, None]
    half_at = team.at["tp"] * row_count

    own = swap_home(lax.dynamic_slice_in_dim(tokens, half_at, row_count, 0))
    inputs = gather_rows(team, own)
    attn_mat = gather_weights(team, [w_query, w_key, w_value, w_out])
    up_mat = gather_weights(team, [w_up])
    down_mat = gather_weights(team, [w_down])
    bias_q = lax.dynamic_slice_in_dim(b_query, my_slot * wide, wide, 0)
    bias_v = lax.dynamic_slice_in_dim(b_value, my_slot * wide, wide, 0)
    tall = w_up.shape[1] // members
    bias_up = lax.dynamic_slice_in_dim(b_up, my_slot * tall, tall, 0)
    qkv_mat = attn_mat[:, : 3 * wide]
    out_mat = attn_mat[:, 3 * wide :]

    bias_qkv = jnp.concatenate([bias_q, jnp.zeros_like(bias_q), bias_v])
    qkv = (mm(inputs, qkv_mat) + bias_qkv).astype(LOWER)
    heads = []
    attended = []
    for i in range(heads_here):
        query, key, value = (
            qkv[:, part * wide + i * HEAD : part * wide + (i + 1) * HEAD] for part in range(3)
        )
        scores = jnp.where(key_live[None, :], mm_nt(query, key) * score_scale, NEGATIVE)
        row_max = jnp.max(scores, axis=-1, keepdims=True)
        log_sum = jnp.log(jnp.sum(jnp.exp(scores - row_max), axis=-1, keepdims=True)) + row_max
        probs = jnp.exp(scores - log_sum)
        attended.append(mm(probs.astype(LOWER), value))
        heads.append((query, key, value, log_sum))
    attended_b = jnp.concatenate(attended, axis=1).astype(LOWER)

    def out_product(first, count):
        return mm_nt(attended_b[first : first + count], out_mat)

    branch = scatter_rows(team, out_product, row_count) + b_out
    middle, mid_hat, mid_rate = layer_norm(own.astype(WIDE) + branch, gain_mid, shift_mid)
    middle_all = gather_rows(team, middle.astype(LOWER))
    hidden = mm(middle_all, up_mat) + bias_up
    active_b = gelu_tanh(hidden).astype(LOWER)

    def down_product(first, count):
        return mm_nt(active_b[first : first + count], down_mat)

    result = scatter_rows(team, down_product, row_count) + b_down
    normed, end_hat, end_rate = layer_norm(middle + result, gain_end, shift_end)
    output_own = jnp.where(query_live, normed, 0.0).astype(LOWER)
    output = join_cores(team, deal_out(team, dealing, output_own))

    cot_half = lax.dynamic_slice_in_dim(cotangent, half_at, row_count, 0)
    cot = deal_in(team, home, cot_half).astype(WIDE)
    grad_normed = jnp.where(query_live, cot, 0.0)
    grad_gend = jnp.sum(grad_normed * end_hat, axis=0)
    grad_send = jnp.sum(grad_normed, axis=0)
    grad_sum = layer_norm_back(grad_normed, gain_end, end_hat, end_rate)
    grad_result = grad_sum.astype(LOWER)
    grad_bdown = jnp.sum(grad_result.astype(WIDE), axis=0)
    result_all = gather_rows(team, grad_result)
    grad_active = mm(result_all, down_mat)
    gelu_back = jax.vjp(gelu_tanh, hidden)[1]
    grad_hidden = gelu_back(grad_active)[0].astype(LOWER)

    def up_product(first, count):
        return mm_nt(grad_hidden[first : first + count], up_mat)

    grad_middle = grad_sum + scatter_rows(team, up_product, row_count)
    grad_bup = jnp.sum(grad_hidden.astype(WIDE), axis=0)
    grad_down = scatter_weights(team, mm_tn(result_all, active_b), [tall])[0]
    grad_up = scatter_weights(team, mm_tn(middle_all, grad_hidden), [tall])[0]

    grad_gmid = jnp.sum(grad_middle * mid_hat, axis=0)
    grad_smid = jnp.sum(grad_middle, axis=0)
    grad_inner = layer_norm_back(grad_middle, gain_mid, mid_hat, mid_rate)
    grad_branch = grad_inner.astype(LOWER)
    grad_bout = jnp.sum(grad_branch.astype(WIDE), axis=0)
    branch_all = gather_rows(team, grad_branch)
    grad_attended = mm(branch_all, out_mat).astype(LOWER)
    parts = [[], [], []]
    for i in range(heads_here):
        query, key, value, log_sum = heads[i]
        grad_head = grad_attended[:, i * HEAD : (i + 1) * HEAD]
        scores = jnp.where(key_live[None, :], mm_nt(query, key) * score_scale, NEGATIVE)
        probs = jnp.exp(scores - log_sum)
        grad_probs = mm_nt(grad_head, value)
        delta = jnp.sum(probs * grad_probs, axis=-1, keepdims=True)
        grad_scores = (probs * (grad_probs - delta)).astype(LOWER)
        parts[0].append(mm(grad_scores, key) * score_scale)
        parts[1].append(mm_tn(grad_scores, query) * score_scale)
        parts[2].append(mm_tn(probs.astype(LOWER), grad_head))
    grad_qkv = jnp.concatenate(parts[0] + parts[1] + parts[2], axis=1).astype(LOWER)

    def in_product(first, count):
        return mm_nt(grad_qkv[first : first + count], qkv_mat)

    grad_own = (scatter_rows(team, in_product, row_count) + grad_inner).astype(LOWER)
    grad_tokens = join_cores(team, swap_home(grad_own))
    grad_attn = jnp.concatenate([mm_tn(inputs, grad_qkv), mm_tn(branch_all, attended_b)], axis=1)
    grad_query, grad_key, grad_value, grad_out = scatter_weights(team, grad_attn, [wide] * 4)

    qkv_sum = jnp.sum(grad_qkv.astype(WIDE), axis=0)
    zeros = jnp.zeros((members, 1), WIDE)
    by_slot = [
        put(zeros * part[None], part[None], (my_slot, 0)).reshape(-1)
        for part in (qkv_sum[:wide], qkv_sum[2 * wide :], grad_bup)
    ]
    by_row = jnp.concatenate(
        [grad_bout, grad_gmid, grad_smid, grad_bdown, grad_gend, grad_send]
    ).reshape(-1, 128)
    by_row = lax.psum(by_row, "tp").reshape(-1)
    sums = lax.psum(jnp.concatenate(by_slot + [by_row]).reshape(-1, 128), ROWS).reshape(-1)
    smalls = []
    first = 0
    for size in [b_query.shape[0], b_value.shape[0], b_up.shape[0]] + [b_out.shape[0]] * 6:
        smalls.append(sums[first : first + size])
        first += size
    return (
        output,
        grad_tokens,
        grad_query,
        grad_key,
        grad_value,
        grad_out,
        smalls[0],
        smalls[1],
        smalls[3],
        smalls[4],
        smalls[5],
        grad_up,
        smalls[2],
        grad_down,
        smalls[6],
        smalls[7],
        smalls[8],
    )


def solution(mesh):
    fsdp, ctx, tp = (mesh.shape[name] for name in ("fsdp", "ctx", "tp"))
    fine = Mesh(mesh.devices.reshape(fsdp // 2, 2, 2, ctx // 2, tp), ROWS + ("tp",))
    rows, split = P(ROWS, None), P(ROWS, "tp")
    in_specs = (
        (rows, P(), P())
        + (split,) * 4
        + (P("tp"), P("tp"), P(), P(), P(), split, P("tp"), split, P(), P(), P(), rows)
    )
    out_specs = (
        (rows, rows)
        + (split,) * 4
        + (P("tp"), P("tp"), P(), P(), P(), split, P("tp"), split, P(), P(), P())
    )
    return jax.shard_map(local, mesh=fine, in_specs=in_specs, out_specs=out_specs, check_vma=False)
```

time: 3400 us -> 1030 us (0.30)
  waiting for transfers between devices: 3060 us -> 519 us
  local copies, waits for them, and re-layouts: 68.1 us -> 226 us
  starting transfers between devices: 2.02 us -> 103 us
  matrix products: 145 us -> 82.4 us
  other arithmetic: 95.7 us -> 57.5 us
    reduce_scatter x4 -> x0, waiting for transfers between devices: 2080 us -> none  [the longest x1 1360 us: local(): lax.psum_scatter(jnp.concatenate([jnp.einsum('td,tf->df', middle_b, grad_...]
    all_gather x10 -> x0, waiting for transfers between devices: 789 us -> none  [the longest x1 191 us: fetch_up(): return lax.all_gather(w_up, ('fsdp', 'ctx'), axis=0, tiled=True)]
    ppermute x0 -> x75, waiting for transfers between devices: none -> 407 us  [the longest x27 211 us: ring(): lax.ppermute(value, name, [(i, (i + step) % size) for i in range(size)])]
    dynamic_update_slice x0 -> x53, local copies, waits for them, and re-layouts: none -> 130 us  [put(): return lax.dynamic_update_slice(buffer, value, starts)]
    ppermute x0 -> x75, starting transfers between devices: none -> 103 us  [the longest x42 72.4 us: shift(): return lax.ppermute(value, TEAM, perm)]
    psum x5 -> x1, waiting for transfers between devices: 192 us -> 112 us  [local(): lax.psum(jnp.concatenate(by_slot + [by_row]).reshape(-1, 128), ROWS)]
    dot_general x32 -> x28, matrix products: 145 us -> 82.4 us  [dot(): lax.dot_general(left, right, (dims, ((), ())), preferred_element_type=WIDE)]
    concatenate x2 -> x10, other arithmetic: 58.6 us -> 12.4 us  [the longest x1 6.22 us: local(): jnp.concatenate([mm_tn(inputs, grad_qkv), mm_tn(branch_all, attended_b)],...]
  transfers between devices with their start and end apart: 19 -> 76, of which waited for: 18 -> 32; matrix products, arithmetic and copies ran while one was open for 6% -> 30% of each run, Pallas kernels for 0% -> 0%
where the time goes in v1:
time: 1030 us; the launch traced here: 1020 us
  waiting for transfers between devices  519 us (50%)
  local copies, waits for them, and re-layouts  226 us (22%)
  starting transfers between devices  103 us (10%)
  matrix products  82.4 us (8%)
  other arithmetic  57.5 us (6%)
  between operations  31 us (3%)
    ppermute x27, waiting for transfers between devices, ring(): lax.ppermute(value, name, [(i, (i + step) % size) for i in range(size)])  211 us
    ppermute x42, waiting for transfers between devices, shift(): return lax.ppermute(value, TEAM, perm)  177 us
    dynamic_update_slice x53, local copies, waits for them, and re-layouts, put(): return lax.dynamic_update_slice(buffer, value, starts)  130 us
    psum x1, waiting for transfers between devices, local(): lax.psum(jnp.concatenate(by_slot + [by_row]).reshape(-1, 128), ROWS)  112 us
    dot_general x28, matrix products, dot(): lax.dot_general(left, right, (dims, ((), ())), preferred_element_type=WIDE)  82.4 us
    ppermute x42, starting transfers between devices, shift(): return lax.ppermute(value, TEAM, perm)  72.4 us
    unnamed x151, local copies, waits for them, and re-layouts  28.7 us
  transfers between devices with their start and end apart: 76, of which 32 were waited for; matrix products, arithmetic and copies ran while one was open for 30% of the time, Pallas kernels for 0%

profile of v1, /device:TPU:0, one launch (start us, length us, event | category | flops | bytes accessed | tf_op | source)
XLA Modules:
  0.0 1022.9 jit_solution(1025974822150286444)
XLA Ops:
  18.8 22.6 %collective-permute-start.2 = (bf16[128,2048]{1,0:T(8,128)(2,1)S(1)}, bf16[128,2048]{1,0:T(8,128)(2,1)S(1)}, u32[]{:S(2)}, u32[]{:S(2)}) collective-permute-start(bf16[128,2048]{1,0:T(8,128)(2,1)S(1)} %collective-permute-done), channel_id=1, source_target_pairs={{0,8},{2,10},{8,0},{10,2},{1,9},{3,11},{9,1},{11,3},{4,12},{6,14},... | collective-permute-start | bytes 1572872 | tf_op jit(solution)/shard_map/ppermute | solution.py:51
  46.9 26.4 %collective-permute-done.2 = bf16[128,2048]{1,0:T(8,128)(2,1)S(1)} collective-permute-done((bf16[128,2048]{1,0:T(8,128)(2,1)S(1)}, bf16[128,2048]{1,0:T(8,128)(2,1)S(1)}, u32[]{:S(2)}, u32[]{:S(2)}) %collective-permute-start.2) | collective-permute-done | bytes 524320 | tf_op jit(solution)/shard_map/ppermute | solution.py:51
  73.3 10.7 %collective-permute-done.3 = bf16[128,2048]{1,0:T(8,128)(2,1)S(1)} collective-permute-done((bf16[128,2048]{1,0:T(8,128)(2,1)S(1)}, bf16[128,2048]{1,0:T(8,128)(2,1)S(1)}, u32[]{:S(2)}, u32[]{:S(2)}) %collective-permute-start.3) | collective-permute-done | bytes 524320 | tf_op jit(solution)/shard_map/ppermute | solution.py:51
  91.9 22.5 %collective-permute-done.8 = bf16[1,2,1,256,1024]{4,3,2,1,0:T(8,128)(2,1)S(1)} collective-permute-done((bf16[1,2,1,256,1024]{4,3,2,1,0:T(8,128)(2,1)S(1)}, bf16[1,2,1,256,1024]{4,3,2,1,0:T(8,128)(2,1)S(1)}, u32[]{:S(2)}, u32[]{:S(2)}) %collective-permute-start.8) | collective-permute-done | bytes 1048608 | tf_op jit(solution)/shard_map/ppermute | solution.py:55
  115.8 20.6 %collective-permute-done.10 = bf16[1,2,1,256,1024]{4,3,2,1,0:T(8,128)(2,1)S(1)} collective-permute-done((bf16[1,2,1,256,1024]{4,3,2,1,0:T(8,128)(2,1)}, bf16[1,2,1,256,1024]{4,3,2,1,0:T(8,128)(2,1)S(1)}, u32[]{:S(2)}, u32[]{:S(2)}) %collective-permute-start.10) | collective-permute-done | bytes 1048608 | tf_op jit(solution)/shard_map/ppermute | solution.py:55
  177.7 31.4 %collective-permute-done.14 = bf16[128,2048]{1,0:T(8,128)(2,1)S(1)} collective-permute-done((bf16[128,2048]{1,0:T(8,128)(2,1)S(1)}, bf16[128,2048]{1,0:T(8,128)(2,1)S(1)}, u32[]{:S(2)}, u32[]{:S(2)}) %collective-permute-start.14) | collective-permute-done | bytes 524320 | tf_op jit(solution)/shard_map/ppermute | solution.py:51
  209.1 9.7 collective-permute-done.13
  227.5 8.9 collective-permute-done.15
  236.9 23.4 %collective-permute-done.16 = bf16[128,2048]{1,0:T(8,128)(2,1)S(1)} collective-permute-done((bf16[128,2048]{1,0:T(8,128)(2,1)S(1)}, bf16[128,2048]{1,0:T(8,128)(2,1)S(1)}, u32[]{:S(2)}, u32[]{:S(2)}) %collective-permute-start.16) | collective-permute-done | bytes 524320 | tf_op jit(solution)/shard_map/ppermute | solution.py:51
  260.8 11.6 %collective-permute-done.17 = bf16[128,2048]{1,0:T(8,128)(2,1)S(1)} collective-permute-done((bf16[128,2048]{1,0:T(8,128)(2,1)S(1)}, bf16[128,2048]{1,0:T(8,128)(2,1)S(1)}, u32[]{:S(2)}, u32[]{:S(2)}) %collective-permute-start.17) | collective-permute-done | bytes 524320 | tf_op jit(solution)/shard_map/ppermute | solution.py:51
  289.2 19.7 %collective-permute-done.24 = bf16[1,2,1,256,1024]{4,3,2,1,0:T(8,128)(2,1)} collective-permute-done((bf16[1,2,1,256,1024]{4,3,2,1,0:T(8,128)(2,1)}, bf16[1,2,1,256,1024]{4,3,2,1,0:T(8,128)(2,1)}, u32[]{:S(2)}, u32[]{:S(2)}) %collective-permute-start.24) | collective-permute-done | bytes 1048608 | tf_op jit(solution)/shard_map/ppermute | solution.py:55
  310.3 19.0 %collective-permute-done.30 = bf16[1,2,1,256,1024]{4,3,2,1,0:T(8,128)(2,1)} collective-permute-done((bf16[1,2,1,256,1024]{4,3,2,1,0:T(8,128)(2,1)}, bf16[1,2,1,256,1024]{4,3,2,1,0:T(8,128)(2,1)}, u32[]{:S(2)}, u32[]{:S(2)}) %collective-permute-start.30) | collective-permute-done | bytes 1048608 | tf_op jit(solution)/shard_map/ppermute | solution.py:55
  334.0 7.4 multiply_convert_fusion.2
  349.6 7.5 fusion.117
  382.1 12.1 %collective-permute-done.33 = bf16[128,2048]{1,0:T(8,128)(2,1)} collective-permute-done((bf16[128,2048]{1,0:T(8,128)(2,1)}, bf16[128,2048]{1,0:T(8,128)(2,1)}, u32[]{:S(2)}, u32[]{:S(2)}) %collective-permute-start.33) | collective-permute-done | bytes 524320 | tf_op jit(solution)/shard_map/ppermute | solution.py:51
  396.8 19.3 %collective-permute-done.41 = bf16[128,2048]{1,0:T(8,128)(2,1)S(1)} collective-permute-done((bf16[128,2048]{1,0:T(8,128)(2,1)S(1)}, bf16[128,2048]{1,0:T(8,128)(2,1)S(1)}, u32[]{:S(2)}, u32[]{:S(2)}) %collective-permute-start.41) | collective-permute-done | bytes 524320 | tf_op jit(solution)/shard_map/ppermute | solution.py:191
  420.8 10.5 %collective-permute-done.42 = bf16[128,2048]{1,0:T(8,128)(2,1)S(1)} collective-permute-done((bf16[128,2048]{1,0:T(8,128)(2,1)S(1)}, bf16[128,2048]{1,0:T(8,128)(2,1)S(1)}, u32[]{:S(2)}, u32[]{:S(2)}) %collective-permute-start.42) | collective-permute-done | bytes 524320 | tf_op jit(solution)/shard_map/ppermute | solution.py:51
  432.3 10.8 %collective-permute-done.44 = bf16[128,2048]{1,0:T(8,128)(2,1)S(1)} collective-permute-done((bf16[128,2048]{1,0:T(8,128)(2,1)S(1)}, bf16[128,2048]{1,0:T(8,128)(2,1)S(1)}, u32[]{:S(2)}, u32[]{:S(2)}) %collective-permute-start.44) | collective-permute-done | bytes 524320 | tf_op jit(solution)/shard_map/ppermute | solution.py:51
  497.1 19.6 %collective-permute-done.65 = bf16[2,2,1,256,1024]{4,3,2,1,0:T(8,128)(2,1)} collective-permute-done((bf16[2,2,1,256,1024]{4,3,2,1,0:T(8,128)(2,1)}, bf16[2,2,1,256,1024]{4,3,2,1,0:T(8,128)(2,1)}, u32[]{:S(2)}, u32[]{:S(2)}) %collective-permute-start.65) | collective-permute-done | bytes 2097184 | tf_op jit(solution)/shard_map/ppermute | solution.py:55
  522.6 38.4 %collective-permute-done.70 = bf16[2,2,1,256,1024]{4,3,2,1,0:T(8,128)(2,1)} collective-permute-done((bf16[2,2,1,256,1024]{4,3,2,1,0:T(8,128)(2,1)}, bf16[2,2,1,256,1024]{4,3,2,1,0:T(8,128)(2,1)}, u32[]{:S(2)}, u32[]{:S(2)}) %collective-permute-start.70) | collective-permute-done | bytes 2097184 | tf_op jit(solution)/shard_map/ppermute | solution.py:55
  575.6 26.1 %collective-permute-done.35 = bf16[128,2048]{1,0:T(8,128)(2,1)S(1)} collective-permute-done((bf16[128,2048]{1,0:T(8,128)(2,1)S(1)}, bf16[128,2048]{1,0:T(8,128)(2,1)S(1)}, u32[]{:S(2)}, u32[]{:S(2)}) %collective-permute-start.35) | collective-permute-done | bytes 524320 | tf_op jit(solution)/shard_map/ppermute | solution.py:55
  620.1 29.4 %collective-permute-done.71 = bf16[1,2,1,256,1024]{4,3,2,1,0:T(8,128)(2,1)S(1)} collective-permute-done((bf16[1,2,1,256,1024]{4,3,2,1,0:T(8,128)(2,1)}, bf16[1,2,1,256,1024]{4,3,2,1,0:T(8,128)(2,1)S(1)}, u32[]{:S(2)}, u32[]{:S(2)}) %collective-permute-start.71) | collective-permute-done | bytes 1048608 | tf_op jit(solution)/shard_map/ppermute | solution.py:55
  653.0 8.3 dynamic_update_slice.212
  663.2 10.5 %dynamic_update_slice.216 = f32[128,4,1024]{2,1,0:T(4,128)} dynamic-update-slice(f32[128,4,1024]{2,1,0:T(4,128)} %broadcast.172.clone.1, f32[128,1,1024]{2,1,0:T(1,128)S(1)} %broadcast_in_dim_squeeze.7, s32[]{:T(128)} %constant.131.clone.1, s32[]{:T(128)S(6)} %select_n.274, s32[]{:T(128)} %constant.131.clone.1) | dynamic-update-slice | bytes 1048580 | tf_op jit(solution)/shard_map/dynamic_update_slice | solution.py:102
  727.7 9.5 copy.118
  745.9 8.3 dynamic_update_slice.213
  754.3 8.4 dynamic_update_slice.214
  764.7 8.3 dynamic_update_slice.215
  777.1 10.5 %dynamic_update_slice.217 = f32[128,4,1024]{2,1,0:T(4,128)} dynamic-update-slice(f32[128,4,1024]{2,1,0:T(4,128)} %dynamic_update_slice.216, f32[128,1,1024]{2,1,0:T(1,128)S(1)} %copy.116, s32[]{:T(128)} %constant.131.clone.1, s32[]{:T(128)S(6)} %select_n.276, s32[]{:T(128)} %constant.131.clone.1) | dynamic-update-slice | bytes 1048580 | tf_op jit(solution)/shard_map/dynamic_update_slice | solution.py:102
  787.6 10.6 %dynamic_update_slice.218 = f32[128,4,1024]{2,1,0:T(4,128)} dynamic-update-slice(f32[128,4,1024]{2,1,0:T(4,128)} %dynamic_update_slice.217, f32[128,1,1024]{2,1,0:T(1,128)S(1)} %copy.117, s32[]{:T(128)} %constant.131.clone.1, s32[]{:T(128)S(6)} %select_n.278, s32[]{:T(128)} %constant.131.clone.1) | dynamic-update-slice | bytes 1048580 | tf_op jit(solution)/shard_map/dynamic_update_slice | solution.py:102
  799.5 10.5 %dynamic_update_slice.219 = f32[128,4,1024]{2,1,0:T(4,128)} dynamic-update-slice(f32[128,4,1024]{2,1,0:T(4,128)} %dynamic_update_slice.218, f32[128,1,1024]{2,1,0:T(1,128)S(1)} %reshape.287, s32[]{:T(128)} %constant.131.clone.1, s32[]{:T(128)S(6)} %select_n.280, s32[]{:T(128)} %constant.131.clone.1) | dynamic-update-slice | bytes 1048580 | tf_op jit(solution)/shard_map/dynamic_update_slice | solution.py:102
  835.2 112.1 %all-reduce.2.cloned.1.call-done = f32[144,128]{1,0:T(8,128)} async-done(((f32[144,128]{1,0:T(8,128)}), f32[144,128]{1,0:T(8,128)}) %all-reduce.2.cloned.1.call-update) | async-done | bytes 73744 | tf_op jit(solution)/shard_map/psum | solution.py:387
  (502 shorter events, 387.0 us)
Async XLA Ops:
  7.2 940.1 %all-reduce.2.cloned.1.call-start = ((), (), s32[]{:S(2)}) async-start(), calls=%async_computation | async-start | bytes 147456 | tf_op jit(solution)/shard_map/psum | solution.py:387
  18.8 54.6 %collective-permute-start.2 = (bf16[128,2048]{1,0:T(8,128)(2,1)S(1)}, bf16[128,2048]{1,0:T(8,128)(2,1)S(1)}, u32[]{:S(2)}, u32[]{:S(2)}) collective-permute-start(bf16[128,2048]{1,0:T(8,128)(2,1)S(1)} %collective-permute-done), channel_id=1, source_target_pairs={{0,8},{2,10},{8,0},{10,2},{1,9},{3,11},{9,1},{11,3},{4,12},{6,14},... | collective-permute-start | bytes 1572872 | tf_op jit(solution)/shard_map/ppermute | solution.py:51
  44.2 46.7 %collective-permute-start.9 = (bf16[1,2,1,256,1024]{4,3,2,1,0:T(8,128)(2,1)S(1)}, bf16[1,2,1,256,1024]{4,3,2,1,0:T(8,128)(2,1)}, u32[]{:S(2)}, u32[]{:S(2)}) collective-permute-start(bf16[1,2,1,256,1024]{4,3,2,1,0:T(8,128)(2,1)S(1)} %bitcast.215), channel_id=1, source_target_pairs={{0,16},{16,0},{1,17},{17,1},{2,18},{18,2},{3,19},{19,3},{4,20},{20... | collective-permute-start | bytes 3145736 | tf_op jit(solution)/shard_map/ppermute | solution.py:55
  85.5 51.1 %collective-permute-start.4 = (bf16[512,2048]{1,0:T(8,128)(2,1)}, bf16[512,2048]{1,0:T(8,128)(2,1)}, u32[]{:S(2)}, u32[]{:S(2)}) collective-permute-start(bf16[512,2048]{1,0:T(8,128)(2,1)} %pad_maximum_fusion.1), channel_id=1, source_target_pairs={{0,1},{1,0},{2,3},{3,2},{4,5},{5,4},{6,7},{7,6},{8,9},{9,8},{10,11... | collective-permute-start | bytes 6291464 | tf_op jit(solution)/shard_map/ppermute | solution.py:55
  170.7 48.1 %collective-permute-start.13 = (bf16[128,2048]{1,0:T(8,128)(2,1)S(1)}, bf16[128,2048]{1,0:T(8,128)(2,1)S(1)}, u32[]{:S(2)}, u32[]{:S(2)}) collective-permute-start(bf16[128,2048]{1,0:T(8,128)(2,1)S(1)} %get-tuple-element.74), channel_id=1, source_target_pairs={{0,8},{2,10},{8,0},{10,2},{1,9},{3,11},{9,1},{11,3},{4,12},{6,14},... | collective-permute-start | bytes 1572872 | tf_op jit(solution)/shard_map/ppermute | solution.py:51
  171.4 47.4 %collective-permute-start.12 = (bf16[128,2048]{1,0:T(8,128)(2,1)S(1)}, bf16[128,2048]{1,0:T(8,128)(2,1)S(1)}, u32[]{:S(2)}, u32[]{:S(2)}) collective-permute-start(bf16[128,2048]{1,0:T(8,128)(2,1)S(1)} %get-tuple-element.72), channel_id=1, source_target_pairs={{0,2},{2,0},{8,10},{10,8},{1,3},{3,1},{9,11},{11,9},{4,6},{6,4},{1... | collective-permute-start | bytes 1572872 | tf_op jit(solution)/shard_map/ppermute | solution.py:51
  174.4 50.9 %collective-permute-start.27 = (bf16[128,1024]{1,0:T(8,128)(2,1)S(1)}, bf16[128,1024]{1,0:T(8,128)(2,1)S(1)}, u32[]{:S(2)}, u32[]{:S(2)}) collective-permute-start(bf16[128,1024]{1,0:T(8,128)(2,1)S(1)} %copy-done.38), channel_id=1, source_target_pairs={{0,10},{2,8},{8,2},{10,0},{1,11},{3,9},{9,3},{11,1},{4,14},{6,12},... | collective-permute-start | bytes 786440 | tf_op jit(solution)/shard_map/ppermute | solution.py:51
  176.9 97.0 %collective-permute-start.23 = (bf16[1,2,1,256,1024]{4,3,2,1,0:T(8,128)(2,1)}, bf16[1,2,1,256,1024]{4,3,2,1,0:T(8,128)(2,1)}, u32[]{:S(2)}, u32[]{:S(2)}) collective-permute-start(bf16[1,2,1,256,1024]{4,3,2,1,0:T(8,128)(2,1)} %bitcast.10), channel_id=1, source_target_pairs={{0,16},{16,0},{1,17},{17,1},{2,18},{18,2},{3,19},{19,3},{4,20},{20... | collective-permute-start | bytes 3145736 | tf_op jit(solution)/shard_map/ppermute | solution.py:55
  225.3 48.9 %collective-permute-start.29 = (bf16[1,2,1,256,1024]{4,3,2,1,0:T(8,128)(2,1)S(1)}, bf16[1,2,1,256,1024]{4,3,2,1,0:T(8,128)(2,1)}, u32[]{:S(2)}, u32[]{:S(2)}) collective-permute-start(bf16[1,2,1,256,1024]{4,3,2,1,0:T(8,128)(2,1)S(1)} %bitcast.218), channel_id=1, source_target_pairs={{0,16},{16,0},{1,17},{17,1},{2,18},{18,2},{3,19},{19,3},{4,20},{20... | collective-permute-start | bytes 3145736 | tf_op jit(solution)/shard_map/ppermute | solution.py:55
  273.9 56.9 %collective-permute-start.18 = (bf16[512,2048]{1,0:T(8,128)(2,1)}, bf16[512,2048]{1,0:T(8,128)(2,1)}, u32[]{:S(2)}, u32[]{:S(2)}) collective-permute-start(bf16[512,2048]{1,0:T(8,128)(2,1)} %pad_maximum_fusion.2), channel_id=1, source_target_pairs={{0,1},{1,0},{2,3},{3,2},{4,5},{5,4},{6,7},{7,6},{8,9},{9,8},{10,11... | collective-permute-start | bytes 6291464 | tf_op jit(solution)/shard_map/ppermute | solution.py:55
  274.3 55.0 %collective-permute-start.30 = (bf16[1,2,1,256,1024]{4,3,2,1,0:T(8,128)(2,1)}, bf16[1,2,1,256,1024]{4,3,2,1,0:T(8,128)(2,1)}, u32[]{:S(2)}, u32[]{:S(2)}) collective-permute-start(bf16[1,2,1,256,1024]{4,3,2,1,0:T(8,128)(2,1)} %collective-permute-done.29), channel_id=1, source_target_pairs={{0,4},{4,0},{1,5},{5,1},{2,6},{6,2},{3,7},{7,3},{8,12},{12,8},{9,1... | collective-permute-start | bytes 3145736 | tf_op jit(solution)/shard_map/ppermute | solution.py:55
  467.9 48.8 %collective-permute-start.65 = (bf16[2,2,1,256,1024]{4,3,2,1,0:T(8,128)(2,1)}, bf16[2,2,1,256,1024]{4,3,2,1,0:T(8,128)(2,1)}, u32[]{:S(2)}, u32[]{:S(2)}) collective-permute-start(bf16[2,2,1,256,1024]{4,3,2,1,0:T(8,128)(2,1)} %dynamic-slice_convert_fusion.1), channel_id=1, source_target_pairs={{0,4},{4,0},{1,5},{5,1},{2,6},{6,2},{3,7},{7,3},{8,12},{12,8},{9,1... | collective-permute-start | bytes 6291464 | tf_op jit(solution)/shard_map/ppermute | solution.py:55
  477.6 83.5 %collective-permute-start.70 = (bf16[2,2,1,256,1024]{4,3,2,1,0:T(8,128)(2,1)}, bf16[2,2,1,256,1024]{4,3,2,1,0:T(8,128)(2,1)}, u32[]{:S(2)}, u32[]{:S(2)}) collective-permute-start(bf16[2,2,1,256,1024]{4,3,2,1,0:T(8,128)(2,1)} %dynamic-slice_convert_fusion), channel_id=1, source_target_pairs={{0,4},{4,0},{1,5},{5,1},{2,6},{6,2},{3,7},{7,3},{8,12},{12,8},{9,1... | collective-permute-start | bytes 6291464 | tf_op jit(solution)/shard_map/ppermute | solution.py:55
  493.5 71.5 %collective-permute-start.49 = (bf16[128,2048]{1,0:T(8,128)(2,1)S(1)}, bf16[128,2048]{1,0:T(8,128)(2,1)S(1)}, u32[]{:S(2)}, u32[]{:S(2)}) collective-permute-start(bf16[128,2048]{1,0:T(8,128)(2,1)S(1)} %get-tuple-element.67), channel_id=1, source_target_pairs={{0,10},{2,8},{8,2},{10,0},{1,11},{3,9},{9,3},{11,1},{4,14},{6,12},... | collective-permute-start | bytes 1572872 | tf_op jit(solution)/shard_map/ppermute | solution.py:51
  494.0 71.1 %collective-permute-start.48 = (bf16[128,2048]{1,0:T(8,128)(2,1)S(1)}, bf16[128,2048]{1,0:T(8,128)(2,1)S(1)}, u32[]{:S(2)}, u32[]{:S(2)}) collective-permute-start(bf16[128,2048]{1,0:T(8,128)(2,1)S(1)} %get-tuple-element.68), channel_id=1, source_target_pairs={{0,8},{2,10},{8,0},{10,2},{1,9},{3,11},{9,1},{11,3},{4,12},{6,14},... | collective-permute-start | bytes 1572872 | tf_op jit(solution)/shard_map/ppermute | solution.py:51
  495.7 69.3 %collective-permute-start.47 = (bf16[128,2048]{1,0:T(8,128)(2,1)S(1)}, bf16[128,2048]{1,0:T(8,128)(2,1)S(1)}, u32[]{:S(2)}, u32[]{:S(2)}) collective-permute-start(bf16[128,2048]{1,0:T(8,128)(2,1)S(1)} %get-tuple-element.66), channel_id=1, source_target_pairs={{0,2},{2,0},{8,10},{10,8},{1,3},{3,1},{9,11},{11,9},{4,6},{6,4},{1... | collective-permute-start | bytes 1572872 | tf_op jit(solution)/shard_map/ppermute | solution.py:51
  521.5 92.1 %collective-permute-start.66 = (bf16[1,2,1,256,1024]{4,3,2,1,0:T(8,128)(2,1)}, bf16[1,2,1,256,1024]{4,3,2,1,0:T(8,128)(2,1)}, u32[]{:S(2)}, u32[]{:S(2)}) collective-permute-start(bf16[1,2,1,256,1024]{4,3,2,1,0:T(8,128)(2,1)} %dynamic-slice_convert_fusion.4), channel_id=1, source_target_pairs={{0,16},{16,0},{1,17},{17,1},{2,18},{18,2},{3,19},{19,3},{4,20},{20... | collective-permute-start | bytes 3145736 | tf_op jit(solution)/shard_map/ppermute | solution.py:55
  601.8 47.7 %collective-permute-start.71 = (bf16[1,2,1,256,1024]{4,3,2,1,0:T(8,128)(2,1)}, bf16[1,2,1,256,1024]{4,3,2,1,0:T(8,128)(2,1)S(1)}, u32[]{:S(2)}, u32[]{:S(2)}) collective-permute-start(bf16[1,2,1,256,1024]{4,3,2,1,0:T(8,128)(2,1)} %dynamic-slice_convert_fusion.3), channel_id=1, source_target_pairs={{0,16},{16,0},{1,17},{17,1},{2,18},{18,2},{3,19},{19,3},{4,20},{20... | collective-permute-start | bytes 3145736 | tf_op jit(solution)/shard_map/ppermute | solution.py:55
  606.2 82.6 %collective-permute-start.36 = (bf16[128,2048]{1,0:T(8,128)(2,1)}, bf16[128,2048]{1,0:T(8,128)(2,1)}, u32[]{:S(2)}, u32[]{:S(2)}) collective-permute-start(bf16[128,2048]{1,0:T(8,128)(2,1)} %get-tuple-element.79), channel_id=1, source_target_pairs={{0,0},{4,8},{8,4},{12,12},{1,1},{5,9},{9,5},{13,13},{2,2},{6,10},{... | collective-permute-start | bytes 1572872 | tf_op jit(solution)/shard_map/ppermute | solution.py:207
  611.6 78.7 %collective-permute-start.37 = (bf16[128,2048]{1,0:T(8,128)(2,1)}, bf16[128,2048]{1,0:T(8,128)(2,1)}, u32[]{:S(2)}, u32[]{:S(2)}) collective-permute-start(bf16[128,2048]{1,0:T(8,128)(2,1)} %get-tuple-element.78), channel_id=1, source_target_pairs={{0,8},{4,0},{8,12},{12,4},{1,9},{5,1},{9,13},{13,5},{2,10},{6,2},{... | collective-permute-start | bytes 1572872 | tf_op jit(solution)/shard_map/ppermute | solution.py:207
  613.5 80.1 %collective-permute-start.53 = (bf16[512,2048]{1,0:T(8,128)(2,1)}, bf16[512,2048]{1,0:T(8,128)(2,1)}, u32[]{:S(2)}, u32[]{:S(2)}) collective-permute-start(bf16[512,2048]{1,0:T(8,128)(2,1)} %pad_maximum_fusion.4), channel_id=1, source_target_pairs={{0,1},{1,0},{2,3},{3,2},{4,5},{5,4},{6,7},{7,6},{8,9},{9,8},{10,11... | collective-permute-start | bytes 6291464 | tf_op jit(solution)/shard_map/ppermute | solution.py:55
  616.1 57.6 %collective-permute-start.67 = (bf16[128,1024]{1,0:T(8,128)(2,1)}, bf16[128,1024]{1,0:T(8,128)(2,1)}, u32[]{:S(2)}, u32[]{:S(2)}) collective-permute-start(bf16[128,1024]{1,0:T(8,128)(2,1)} %get-tuple-element.59), channel_id=1, source_target_pairs={{0,2},{2,0},{8,10},{10,8},{1,3},{3,1},{9,11},{11,9},{4,6},{6,4},{1... | collective-permute-start | bytes 786440 | tf_op jit(solution)/shard_map/ppermute | solution.py:51
  676.1 86.6 %collective-permute-start.69 = (bf16[128,1024]{1,0:T(8,128)(2,1)}, bf16[128,1024]{1,0:T(8,128)(2,1)}, u32[]{:S(2)}, u32[]{:S(2)}) collective-permute-start(bf16[128,1024]{1,0:T(8,128)(2,1)} %get-tuple-element.57), channel_id=1, source_target_pairs={{0,10},{2,8},{8,2},{10,0},{1,11},{3,9},{9,3},{11,1},{4,14},{6,12},... | collective-permute-start | bytes 786440 | tf_op jit(solution)/shard_map/ppermute | solution.py:51
  687.0 54.2 %collective-permute-start.73 = (bf16[128,1024]{1,0:T(8,128)(2,1)}, bf16[128,1024]{1,0:T(8,128)(2,1)}, u32[]{:S(2)}, u32[]{:S(2)}) collective-permute-start(bf16[128,1024]{1,0:T(8,128)(2,1)} %get-tuple-element.55), channel_id=1, source_target_pairs={{0,8},{2,10},{8,0},{10,2},{1,9},{3,11},{9,1},{11,3},{4,12},{6,14},... | collective-permute-start | bytes 786440 | tf_op jit(solution)/shard_map/ppermute | solution.py:51
  688.8 109.4 %collective-permute-start.74 = (bf16[128,1024]{1,0:T(8,128)(2,1)}, bf16[128,1024]{1,0:T(8,128)(2,1)}, u32[]{:S(2)}, u32[]{:S(2)}) collective-permute-start(bf16[128,1024]{1,0:T(8,128)(2,1)} %get-tuple-element.54), channel_id=1, source_target_pairs={{0,10},{2,8},{8,2},{10,0},{1,11},{3,9},{9,3},{11,1},{4,14},{6,12},... | collective-permute-start | bytes 786440 | tf_op jit(solution)/shard_map/ppermute | solution.py:51
  693.6 120.9 %collective-permute-start.38 = (bf16[128,2048]{1,0:T(8,128)(2,1)}, bf16[128,2048]{1,0:T(8,128)(2,1)}, u32[]{:S(2)}, u32[]{:S(2)}) collective-permute-start(bf16[128,2048]{1,0:T(8,128)(2,1)} %get-tuple-element.47), channel_id=1, source_target_pairs={{0,1},{1,0},{2,3},{3,2},{4,5},{5,4},{6,7},{7,6},{8,9},{9,8},{10,11... | collective-permute-start | bytes 1572872 | tf_op jit(solution)/shard_map/ppermute | solution.py:55
  718.3 99.2 %collective-permute-start.54 = (bf16[512,2048]{1,0:T(8,128)(2,1)}, bf16[512,2048]{1,0:T(8,128)(2,1)}, u32[]{:S(2)}, u32[]{:S(2)}) collective-permute-start(bf16[512,2048]{1,0:T(8,128)(2,1)} %convolution_convert_fusion.3), channel_id=1, source_target_pairs={{0,1},{1,0},{2,3},{3,2},{4,5},{5,4},{6,7},{7,6},{8,9},{9,8},{10,11... | collective-permute-start | bytes 6291464 | tf_op jit(solution)/shard_map/ppermute | solution.py:55
  741.2 87.5 %collective-permute-start.60 = (bf16[2,2,1,256,1024]{4,3,2,1,0:T(8,128)(2,1)}, bf16[2,2,1,256,1024]{4,3,2,1,0:T(8,128)(2,1)}, u32[]{:S(2)}, u32[]{:S(2)}) collective-permute-start(bf16[2,2,1,256,1024]{4,3,2,1,0:T(8,128)(2,1)} %dynamic-slice_convert_fusion.2), channel_id=1, source_target_pairs={{0,4},{4,0},{1,5},{5,1},{2,6},{6,2},{3,7},{7,3},{8,12},{12,8},{9,1... | collective-permute-start | bytes 6291464 | tf_op jit(solution)/shard_map/ppermute | solution.py:55
  825.2 126.2 %collective-permute-start.57 = (bf16[128,2048]{1,0:T(8,128)(2,1)}, bf16[128,2048]{1,0:T(8,128)(2,1)}, u32[]{:S(2)}, u32[]{:S(2)}) collective-permute-start(bf16[128,2048]{1,0:T(8,128)(2,1)} %get-tuple-element.64), channel_id=1, source_target_pairs={{0,10},{2,8},{8,2},{10,0},{1,11},{3,9},{9,3},{11,1},{4,14},{6,12},... | collective-permute-start | bytes 1572872 | tf_op jit(solution)/shard_map/ppermute | solution.py:51
  826.7 124.8 %collective-permute-start.56 = (bf16[128,2048]{1,0:T(8,128)(2,1)}, bf16[128,2048]{1,0:T(8,128)(2,1)}, u32[]{:S(2)}, u32[]{:S(2)}) collective-permute-start(bf16[128,2048]{1,0:T(8,128)(2,1)} %get-tuple-element.65), channel_id=1, source_target_pairs={{0,8},{2,10},{8,0},{10,2},{1,9},{3,11},{9,1},{11,3},{4,12},{6,14},... | collective-permute-start | bytes 1572872 | tf_op jit(solution)/shard_map/ppermute | solution.py:51
  827.0 124.5 %collective-permute-start.55 = (bf16[128,2048]{1,0:T(8,128)(2,1)}, bf16[128,2048]{1,0:T(8,128)(2,1)}, u32[]{:S(2)}, u32[]{:S(2)}) collective-permute-start(bf16[128,2048]{1,0:T(8,128)(2,1)} %get-tuple-element.63), channel_id=1, source_target_pairs={{0,2},{2,0},{8,10},{10,8},{1,3},{3,1},{9,11},{11,9},{4,6},{6,4},{1... | collective-permute-start | bytes 1572872 | tf_op jit(solution)/shard_map/ppermute | solution.py:51
  834.4 125.5 %collective-permute-start.61 = (bf16[1,2,1,256,1024]{4,3,2,1,0:T(8,128)(2,1)S(1)}, bf16[1,2,1,256,1024]{4,3,2,1,0:T(8,128)(2,1)S(1)}, u32[]{:S(2)}, u32[]{:S(2)}) collective-permute-start(bf16[1,2,1,256,1024]{4,3,2,1,0:T(8,128)(2,1)S(1)} %dynamic-slice_convert_fusion.5), channel_id=1, source_target_pairs={{0,16},{16,0},{1,17},{17,1},{2,18},{18,2},{3,19},{19,3},{4,20},{20... | collective-permute-start | bytes 3145736 | tf_op jit(solution)/shard_map/ppermute | solution.py:55
  (105 other events, 2288.5 us)
Sparse Core Ops, SparseCore 0:
  817.6 129.5 all-reduce.1

commit v2 on v1

v2 whole, which is shorter than its diff:
```python
import functools
import math

import jax
import jax.numpy as jnp
from jax import lax
from jax.experimental import pallas as pl
from jax.experimental.pallas import tpu as pltpu
from jax.sharding import Mesh
from jax.sharding import PartitionSpec as P

HEAD = 128
EPSILON = 1e-12
NEGATIVE = -1e30
WIDE = jnp.float32
LOWER = jnp.bfloat16

TEAM = ("l", "x")
ROWS = ("h", "l", "y", "x")


def dot(left, right, dims):
    return lax.dot_general(left, right, (dims, ((), ())), preferred_element_type=WIDE)


def mm(left, right):
    return dot(left, right, ((1,), (0,)))


def mm_nt(left, right):
    return dot(left, right, ((1,), (1,)))


def mm_tn(left, right):
    return dot(left, right, ((0,), (0,)))


class Team:
    def __init__(self):
        self.sizes = {name: lax.axis_size(name) for name in ROWS + ("tp",)}
        self.at = {name: lax.axis_index(name) for name in ROWS + ("tp",)}
        ls, xs = self.sizes["l"], self.sizes["x"]
        self.offsets = [(dl, dx) for dl in range(ls) for dx in range(xs)]
        self.members = ls * xs

    def shift(self, value, offset, back=False):
        with jax.named_scope("team%d%d" % offset):
            return self.shift_(value, offset, back)

    def shift_(self, value, offset, back):
        ls, xs = self.sizes["l"], self.sizes["x"]
        dl, dx = offset
        if back:
            dl, dx = -dl, -dx
        perm = [
            (l * xs + x, ((l + dl) % ls) * xs + (x + dx) % xs) for l in range(ls) for x in range(xs)
        ]
        return lax.ppermute(value, TEAM, perm)

    def ring(self, value, name, step):
        size = self.sizes[name]
        with jax.named_scope("ring_" + name):
            return lax.ppermute(value, name, [(i, (i + step) % size) for i in range(size)])

    def slot(self, offset, back=True):
        ls, xs = self.sizes["l"], self.sizes["x"]
        dl, dx = offset
        if back:
            dl, dx = -dl, -dx
        return lax.rem(self.at["l"] + dl + ls, ls) * xs + lax.rem(self.at["x"] + dx + xs, xs)


def fence(*values):
    return lax.optimization_barrier(values)


def swap_home(value):
    perm = [(l * 2 + y, y * 2 + l) for l in range(2) for y in range(2)]
    return lax.ppermute(value, ("l", "y"), perm)


def team_pieces(team, piece):
    return [piece] + [team.shift(piece, offset) for offset in team.offsets[1:]]


def cores(team, value):
    return [team.ring(value, "tp", step) for step in range(1, team.sizes["tp"])]


def row_blocks(team):
    ts = team.sizes["tp"]
    return [
        team.slot(offset) * ts + lax.rem(team.at["tp"] - step + ts, ts)
        for step in range(ts)
        for offset in team.offsets
    ]


def core_send(team, product, half_rows):
    got = []
    for step in range(1, team.sizes["tp"]):
        sent = product(step * half_rows, half_rows).astype(LOWER)
        got.append(team.ring(sent, "tp", -step))
    return got


def core_total(team, product, half_rows, got):
    total = product(0, half_rows)
    for value in got:
        total = total + value.astype(WIDE)
    row_count = half_rows // team.members
    sent = [
        total[j * row_count : (j + 1) * row_count].astype(LOWER) for j in range(1, team.members)
    ]
    return total[:row_count], sent


def team_send(team, sent):
    return [
        team.shift(value, offset, back=True) for value, offset in zip(sent, team.offsets[1:])
    ]


def team_total(own, got):
    for value in got:
        own = own + value.astype(WIDE)
    return own


def put(buffer, value, starts):
    return lax.dynamic_update_slice(buffer, value, starts)


def share_columns(team, shards):
    widths = [shard.shape[1] // team.members for shard in shards]
    pieces = []
    for j, offset in enumerate(team.offsets):
        slot = team.slot(offset, back=False)
        cuts = [
            lax.dynamic_slice_in_dim(shard, slot * each, each, 1)
            for shard, each in zip(shards, widths)
        ]
        piece = jnp.concatenate(cuts, axis=1)
        pieces.append(team.shift(piece, offset) if j > 0 else piece)
    return pieces


def near_rows(team, pieces, first, width):
    near = jnp.zeros((team.members, pieces[0].shape[0], width), LOWER)
    for piece, offset in zip(pieces, team.offsets):
        near = put(near, piece[None, :, first : first + width], (team.slot(offset), 0, 0))
    return near.reshape(-1, width)


def across(team, value):
    return [team.ring(value, "h", -step) for step in range(1, team.sizes["h"])]


def beside(team, values):
    return [team.ring(value, "y", 1) for value in values]


def halves(value):
    middle = value.shape[0] // 2
    return value[:middle], value[middle:]


def pairs(firsts, seconds):
    return [part for pair in zip(firsts, seconds) for part in pair]


class Grads:
    def __init__(self, team, product, rows, name):
        self.team, self.product, self.name = team, product, name
        self.far = rows // 2
        self.near = self.far // team.sizes["h"]

    def send_far(self):
        return self.product(self.far + self.near, self.far - self.near).astype(LOWER)

    def send_near(self):
        return self.product(self.far, self.near).astype(LOWER)

    def cross(self, got):
        mine = self.product(self.near, self.far - self.near) + got.astype(WIDE)
        mine = mine.astype(LOWER)
        return [
            mine[step * self.near : (step + 1) * self.near]
            for step in range(self.team.sizes["h"] - 1)
        ]

    def go(self, sent):
        return [self.team.ring(value, "h", step) for step, value in enumerate(sent, 1)]

    def total(self, got, crossed):
        mine = self.product(0, self.near) + got.astype(WIDE)
        for value in crossed:
            mine = mine + value.astype(WIDE)
        return mine


def home_pieces(team, total):
    height = total.shape[0] // team.members
    total = total.reshape(team.members, height, -1)
    pieces = []
    for j, offset in enumerate(team.offsets):
        piece = lax.dynamic_index_in_dim(total, team.slot(offset, back=False), 0, False)
        pieces.append(team.shift(piece.astype(LOWER), offset) if j > 0 else piece)
    return pieces


def home_join(team, pieces, widths):
    slots = [team.slot(offset) for offset in team.offsets]
    outs = []
    first = 0
    for each in widths:
        blocks = []
        for slot in range(team.members):
            block = pieces[0][:, first : first + each]
            for piece, at in zip(pieces[1:], slots[1:]):
                other = piece[:, first : first + each].astype(WIDE)
                block = jnp.where(at == slot, other, block)
            blocks.append(block)
        outs.append(jnp.concatenate(blocks, axis=1))
        first += each
    return outs


def to_team_order(team, value):
    hs = team.sizes["h"]
    count = value.shape[0]
    value = value.reshape(count, hs, 2, 2, -1).transpose(0, 3, 1, 2, 4)
    value = jnp.roll(value, (-team.at["y"], -team.at["h"]), (1, 2))
    return value.reshape(count, -1)


def from_team_order(team, value):
    hs = team.sizes["h"]
    count = value.shape[0]
    value = value.reshape(count, 2, hs, 2, -1)
    value = jnp.roll(value, (team.at["y"], team.at["h"]), (1, 2))
    return value.transpose(0, 2, 3, 1, 4).reshape(count, -1)


def pick(table, index):
    ids = jnp.arange(table.shape[0], dtype=jnp.int32)
    return jnp.sum(jnp.where(ids == index, table, 0))


def choose(pieces, index):
    out = pieces[0]
    for i in range(1, len(pieces)):
        out = jnp.where(index == i, pieces[i], out)
    return out


def spread_h(team, piece):
    return [piece] + [team.ring(piece, "h", step) for step in range(1, team.sizes["h"])]


def deal(team, table, pieces, inward):
    hs = team.sizes["h"]
    place = team.at["l"] if inward else team.at["y"]
    got = []
    for flip in range(2):
        source = pick(table, team.at["h"] * 2 + (place if flip == 0 else 1 - place))
        sent = choose(pieces, lax.rem(team.at["h"] - source // 2 + hs, hs))
        perm = []
        for l in range(2):
            for y in range(2):
                if inward:
                    perm.append((l * 2 + y, y * 2 + (l if flip == 0 else 1 - l)))
                else:
                    perm.append((l * 2 + y, (y if flip == 0 else 1 - y) * 2 + l))
        with jax.named_scope("flip"):
            got.append(lax.ppermute(sent, ("l", "y"), perm))
    return got


def pick_dealt(team, table, got, inward):
    place = team.at["y"] if inward else team.at["l"]
    source = pick(table, team.at["h"] * 2 + place)
    return jnp.where(lax.rem(source, 2) == place, got[0], got[1])


def join_cores(team, piece):
    ts = team.sizes["tp"]
    out = jnp.zeros((ts,) + piece.shape, piece.dtype)
    for step in range(ts):
        other = team.ring(piece, "tp", step) if step else piece
        out = put(out, other[None], (lax.rem(team.at["tp"] - step + ts, ts), 0, 0))
    return out.reshape(-1, piece.shape[-1])


def layer_norm(inputs, gain_vec, shift_vec):
    row_mean = jnp.mean(inputs, axis=-1, keepdims=True)
    centred = inputs - row_mean
    spread = jnp.mean(centred * centred, axis=-1, keepdims=True)
    rate = lax.rsqrt(spread + EPSILON)
    xhat = centred * rate
    return xhat * gain_vec + shift_vec, xhat, rate


def layer_norm_back(grad, gain_vec, xhat, rate):
    scaled = grad * gain_vec
    return rate * (
        scaled
        - jnp.mean(scaled, axis=-1, keepdims=True)
        - xhat * jnp.mean(scaled * xhat, axis=-1, keepdims=True)
    )


def gelu_tanh(inputs):
    return jax.nn.gelu(inputs, approximate=True)


def masked_scores(key_ref, query, limits_ref, scale):
    count = limits_ref.shape[0]
    height = key_ref.shape[0] // count
    blocks = []
    for j in range(count):
        block = mm_nt(key_ref[j * height : (j + 1) * height, :], query) * scale
        row = lax.broadcasted_iota(jnp.int32, block.shape, 0)
        blocks.append(jnp.where(row < limits_ref[j], block, NEGATIVE))
    return blocks


def attend_kernel(scale, limits_ref, query_ref, key_ref, value_ref, out_ref, log_ref):
    blocks = masked_scores(key_ref, query_ref[...], limits_ref, scale)
    row_max = functools.reduce(jnp.maximum, blocks)
    row_max = jnp.max(row_max, axis=0, keepdims=True)
    blocks = [jnp.exp(block - row_max) for block in blocks]
    total = jnp.sum(functools.reduce(jnp.add, blocks), axis=0, keepdims=True)
    inverse = 1.0 / total
    height = key_ref.shape[0] // len(blocks)
    out = None
    for j, block in enumerate(blocks):
        value = value_ref[j * height : (j + 1) * height, :]
        term = mm_tn(value, (block * inverse).astype(LOWER))
        out = term if out is None else out + term
    out_ref[...] = out.T.astype(LOWER)
    log_ref[0] = row_max + jnp.log(total)


def attend_back_kernel(
    scale, wide, limits_ref, query_ref, key_ref, value_ref, grad_ref, log_ref, out_ref, key_sum, value_sum
):
    head, step = pl.program_id(0), pl.program_id(1)
    query, grad = query_ref[...], grad_ref[...]
    blocks = masked_scores(key_ref, query, limits_ref, scale)
    count = len(blocks)
    height = key_ref.shape[0] // count
    part = [slice(j * height, (j + 1) * height) for j in range(count)]
    log_sum = log_ref[0]
    probs = [jnp.exp(block - log_sum) for block in blocks]
    grad_probs = [mm_nt(value_ref[rows, :], grad) for rows in part]
    delta = functools.reduce(jnp.add, [p * g for p, g in zip(probs, grad_probs)])
    delta = jnp.sum(delta, axis=0, keepdims=True)

    @pl.when(step == 0)
    def _():
        key_sum[...] = jnp.zeros_like(key_sum)
        value_sum[...] = jnp.zeros_like(value_sum)

    grad_query = None
    for j, rows in enumerate(part):
        scores = (probs[j] * (grad_probs[j] - delta)).astype(LOWER)
        term = mm_tn(key_ref[rows, :], scores)
        grad_query = term if grad_query is None else grad_query + term
        key_sum[rows, :] += mm(scores, query)
        value_sum[rows, :] += mm(probs[j].astype(LOWER), grad)
    count = query.shape[0]
    first = pl.multiple_of(step * count, count)
    column = pl.multiple_of(head * HEAD, HEAD)
    out_ref[pl.ds(first, count), pl.ds(column, HEAD)] = (grad_query.T * scale).astype(LOWER)

    @pl.when(step == pl.num_programs(1) - 1)
    def _():
        out_ref[:, pl.ds(wide + column, HEAD)] = (key_sum[...] * scale).astype(LOWER)
        out_ref[:, pl.ds(2 * wide + column, HEAD)] = value_sum[...].astype(LOWER)


LIGHT = pl.CostEstimate(flops=1000000, bytes_accessed=100000, transcendentals=0)
KERNEL = pltpu.CompilerParams(vmem_limit_bytes=24 * 1024 * 1024)


def query_block(rows):
    return min(256, rows)


def attend(qkv, limits, scale):
    rows, wide = qkv.shape[0], qkv.shape[1] // 3
    heads, block = wide // HEAD, query_block(rows)
    return pl.pallas_call(
        functools.partial(attend_kernel, scale),
        grid=(heads, rows // block),
        in_specs=[
            pl.BlockSpec(memory_space=pltpu.SMEM),
            pl.BlockSpec((block, HEAD), lambda h, i: (i, h)),
            pl.BlockSpec((rows, HEAD), lambda h, i: (0, heads + h)),
            pl.BlockSpec((rows, HEAD), lambda h, i: (0, 2 * heads + h)),
        ],
        out_specs=[
            pl.BlockSpec((block, HEAD), lambda h, i: (i, h)),
            pl.BlockSpec((1, 1, block), lambda h, i: (h, 0, i)),
        ],
        out_shape=[
            jax.ShapeDtypeStruct((rows, wide), LOWER),
            jax.ShapeDtypeStruct((heads, 1, rows), WIDE),
        ],
        cost_estimate=LIGHT,
        compiler_params=KERNEL,
    )(limits, qkv, qkv, qkv)


def attend_back(qkv, grad, log_sum, limits, scale):
    rows, wide = grad.shape
    heads, block = wide // HEAD, query_block(rows)
    return pl.pallas_call(
        functools.partial(attend_back_kernel, scale, wide),
        grid=(heads, rows // block),
        in_specs=[
            pl.BlockSpec(memory_space=pltpu.SMEM),
            pl.BlockSpec((block, HEAD), lambda h, i: (i, h)),
            pl.BlockSpec((rows, HEAD), lambda h, i: (0, heads + h)),
            pl.BlockSpec((rows, HEAD), lambda h, i: (0, 2 * heads + h)),
            pl.BlockSpec((block, HEAD), lambda h, i: (i, h)),
            pl.BlockSpec((1, 1, block), lambda h, i: (h, 0, i)),
        ],
        out_specs=pl.BlockSpec((rows, 3 * wide), lambda h, i: (0, 0)),
        out_shape=jax.ShapeDtypeStruct((rows, 3 * wide), LOWER),
        scratch_shapes=[pltpu.VMEM((rows, HEAD), WIDE), pltpu.VMEM((rows, HEAD), WIDE)],
        cost_estimate=LIGHT,
        compiler_params=KERNEL,
    )(limits, qkv, qkv, qkv, grad, log_sum)


def local(
    tokens,
    lengths,
    dealing,
    w_query,
    w_key,
    w_value,
    w_out,
    b_query,
    b_value,
    b_out,
    gain_mid,
    shift_mid,
    w_up,
    b_up,
    w_down,
    b_down,
    gain_end,
    shift_end,
    cotangent,
):
    team = Team()
    ts, members = team.sizes["tp"], team.members
    row_count = tokens.shape[0] // ts
    wide = w_query.shape[1] // members
    tall = w_up.shape[1] // members
    width = tokens.shape[1]
    score_scale = 1.0 / math.sqrt(HEAD)
    my_slot = team.at["l"] * team.sizes["x"] + team.at["x"]
    seq_ids = jnp.arange(dealing.shape[0], dtype=jnp.int32)
    home = jnp.sum(jnp.where(dealing[None, :] == seq_ids[:, None], seq_ids[None, :], 0), axis=1)
    live_count = pick(lengths, team.at["h"] * 2 + team.at["y"])
    limits = live_count - jnp.stack(row_blocks(team)).astype(jnp.int32) * row_count
    query_live = (jnp.arange(row_count, dtype=jnp.int32) < limits[0])[:, None]
    half_at = team.at["tp"] * row_count

    half_rows = members * row_count
    vectors = jnp.stack([b_out, gain_mid, shift_mid, b_down, gain_end, shift_end])
    b_out, gain_mid, shift_mid, b_down, gain_end, shift_end = to_team_order(team, vectors)
    bias_q = lax.dynamic_slice_in_dim(b_query, my_slot * wide, wide, 0)
    bias_v = lax.dynamic_slice_in_dim(b_value, my_slot * wide, wide, 0)
    bias_up = lax.dynamic_slice_in_dim(b_up, my_slot * tall, tall, 0)
    bias_qkv = jnp.concatenate([bias_q, jnp.zeros_like(bias_q), bias_v])
    steps = team.sizes["h"] - 1

    with jax.named_scope("a0"):
        own = swap_home(lax.dynamic_slice_in_dim(tokens, half_at, row_count, 0))
        share = share_columns(team, [w_query, w_key, w_value, w_out])
        own, w_up, w_down, *share = fence(own, w_up, w_down, *share)
    with jax.named_scope("a1"):
        own = to_team_order(team, own)
        near_qkv = near_rows(team, share, 0, 3 * wide)
        near_out = near_rows(team, share, 3 * wide, wide)
        pieces = team_pieces(team, own)
        cross_qkv = across(team, near_qkv)
        side_qkv, side_out = beside(team, [near_qkv, near_out])
        near_out, w_up, w_down, side_qkv, side_out, *rest = fence(
            near_out, w_up, w_down, side_qkv, side_out, *pieces, *cross_qkv
        )
        pieces, cross_qkv = rest[:members], rest[members:]
    with jax.named_scope("a2"):
        half = jnp.concatenate(pieces, axis=0)
        other = cores(team, half)
        far_qkv = beside(team, cross_qkv)
        cross_out = across(team, near_out)
        share = share_columns(team, [w_up, w_down])
        rest = fence(half, *other, *share, *far_qkv, *cross_out)
        inputs = jnp.concatenate(rest[:ts], axis=0)
        share, rest = rest[ts : ts + members], rest[ts + members :]
        far_qkv, cross_out = rest[:steps], rest[steps:]
    with jax.named_scope("c1"):
        near_up = near_rows(team, share, 0, tall)
        near_down = near_rows(team, share, tall, tall)
        up_a, up_b = halves(near_up)
        cross_up_a = across(team, up_a)
        far_out = beside(team, cross_out)
        (side_up,) = beside(team, [near_up])
        qkv_mat = jnp.concatenate([near_qkv, *cross_qkv, side_qkv, *far_qkv], axis=0)
        qkv = (mm(inputs, qkv_mat) + bias_qkv).astype(LOWER)
        attended, log_sum = attend(qkv, limits, score_scale)
        out_mat = jnp.concatenate([near_out, *cross_out, side_out, *far_out], axis=0)

        def out_product(first, count):
            return mm_nt(attended[first : first + count], out_mat)

        got = core_send(team, out_product, half_rows)
        total, sent = core_total(team, out_product, half_rows, got)
        up_b, near_down, side_up, *rest = fence(up_b, near_down, side_up, *cross_up_a, *sent)
        cross_up_a, sent = rest[:steps], rest[steps:]
    with jax.named_scope("s3"):
        got = team_send(team, sent)
        cross_up_b = across(team, up_b)
        far_up_a = beside(team, cross_up_a)
        near_down, *rest = fence(near_down, *got, *cross_up_b, *far_up_a)
        got, rest = rest[: members - 1], rest[members - 1 :]
        cross_up_b, far_up_a = rest[:steps], rest[steps:]
    with jax.named_scope("s4"):
        branch = team_total(total, got) + b_out
        middle, mid_hat, mid_rate = layer_norm(own.astype(WIDE) + branch, gain_mid, shift_mid)
        pieces = team_pieces(team, middle.astype(LOWER))
        down_a, down_b = halves(near_down)
        cross_down_a = across(team, down_a)
        far_up_b = beside(team, cross_up_b)
        near_down, down_b, *rest = fence(near_down, down_b, *pieces, *cross_down_a, *far_up_b)
        pieces, rest = rest[:members], rest[members:]
        cross_down_a, far_up_b = rest[:steps], rest[steps:]
    with jax.named_scope("c2"):
        half = jnp.concatenate(pieces, axis=0)
        other = cores(team, half)
        cross_down_b = across(team, down_b)
        (side_down,) = beside(team, [near_down])
        far_down_a = beside(team, cross_down_a)
        middle_all = jnp.concatenate([half] + other, axis=0)
        up_mat = jnp.concatenate(
            [near_up]
            + pairs(cross_up_a, cross_up_b)
            + [side_up]
            + pairs(far_up_a, far_up_b),
            axis=0,
        )
        hidden = mm(middle_all, up_mat) + bias_up
        active = gelu_tanh(hidden).astype(LOWER)
        active, hidden, side_down, cotangent, *rest = fence(
            active, hidden, side_down, cotangent, *cross_down_b, *far_down_a
        )
        cross_down_b, far_down_a = rest[:steps], rest[steps:]
    with jax.named_scope("s5"):
        cot_pieces = spread_h(team, lax.dynamic_slice_in_dim(cotangent, half_at, row_count, 0))
        far_down_b = beside(team, cross_down_b)
        down_mat = jnp.concatenate(
            [near_down]
            + pairs(cross_down_a, cross_down_b)
            + [side_down]
            + pairs(far_down_a, far_down_b),
            axis=0,
        )

        def down_product(first, count):
            return mm_nt(active[first : first + count], down_mat)

        got = core_send(team, down_product, half_rows)
        total, sent = core_total(team, down_product, half_rows, got)
        rest = fence(*sent, *cot_pieces)
        sent, cot_pieces = rest[: members - 1], rest[members - 1 :]
    with jax.named_scope("s6"):
        got = team_send(team, sent)
        cot_two = deal(team, home, cot_pieces, True)
        rest = fence(*got, *cot_two)
        got, cot_two = rest[: members - 1], rest[members - 1 :]
    with jax.named_scope("s7"):
        result = team_total(total, got) + b_down
        normed, end_hat, end_rate = layer_norm(middle + result, gain_end, shift_end)
        output_own = jnp.where(query_live, normed, 0.0).astype(LOWER)
        cot = to_team_order(team, pick_dealt(team, home, cot_two, True)).astype(WIDE)
        grad_normed = jnp.where(query_live, cot, 0.0)
        grad_sum = layer_norm_back(grad_normed, gain_end, end_hat, end_rate)
        grad_result = grad_sum.astype(LOWER)
        pieces = team_pieces(team, grad_result)
        out_pieces = spread_h(team, from_team_order(team, output_own))
        rest = fence(*pieces, *out_pieces)
        pieces, out_pieces = rest[:members], rest[members:]
        grad_gend = jnp.sum(grad_normed * end_hat, axis=0)
        grad_send = jnp.sum(grad_normed, axis=0)
        grad_bdown = jnp.sum(grad_result.astype(WIDE), axis=0)
    with jax.named_scope("c3"):
        half = jnp.concatenate(pieces, axis=0)
        other = cores(team, half)
        result_all = jnp.concatenate([half] + other, axis=0)
        flow_down = Grads(
            team, lambda f, n: mm_tn(result_all[:, f : f + n], active), width, "down"
        )
        (far_down,) = beside(team, [flow_down.send_far()])
        grad_active = mm(result_all, down_mat)
        gelu_back = jax.vjp(gelu_tanh, hidden)[1]
        grad_hidden = gelu_back(grad_active)[0].astype(LOWER)

        def up_product(first, count):
            return mm_nt(grad_hidden[first : first + count], up_mat)

        got = core_send(team, up_product, half_rows)
        total, sent = core_total(team, up_product, half_rows, got)
        cross_down = flow_down.cross(far_down)
        flow_up = Grads(
            team, lambda f, n: mm_tn(middle_all[:, f : f + n], grad_hidden), width, "up"
        )
        rest = fence(*sent, *cross_down)
        sent, cross_down = rest[: members - 1], rest[members - 1 :]
    with jax.named_scope("s8"):
        got = team_send(team, sent)
        down_halves = [halves(value) for value in cross_down]
        got_down_a = flow_down.go([a for a, b in down_halves])
        (far_up,) = beside(team, [flow_up.send_far()])
        far_up, *rest = fence(far_up, *got, *got_down_a, *[b for a, b in down_halves])
        got, rest = rest[: members - 1], rest[members - 1 :]
        got_down_a, down_b = rest[:steps], rest[steps:]
    with jax.named_scope("s9"):
        grad_middle = team_total(total, got) + grad_sum
        grad_inner = layer_norm_back(grad_middle, gain_mid, mid_hat, mid_rate)
        grad_branch = grad_inner.astype(LOWER)
        pieces = team_pieces(team, grad_branch)
        got_down_b = flow_down.go(down_b)
        (near_down,) = beside(team, [flow_down.send_near()])
        cross_up = flow_up.cross(far_up)
        near_down, *rest = fence(near_down, *pieces, *got_down_b, *cross_up)
        pieces, rest = rest[:members], rest[members:]
        got_down_b, cross_up = rest[:steps], rest[steps:]
        grad_gmid = jnp.sum(grad_middle * mid_hat, axis=0)
        grad_smid = jnp.sum(grad_middle, axis=0)
        grad_bout = jnp.sum(grad_branch.astype(WIDE), axis=0)
    with jax.named_scope("c4"):
        half = jnp.concatenate(pieces, axis=0)
        other = cores(team, half)
        up_halves = [halves(value) for value in cross_up]
        got_up_a = flow_up.go([a for a, b in up_halves])
        (near_up,) = beside(team, [flow_up.send_near()])
        branch_all = jnp.concatenate([half] + other, axis=0)
        flow_out = Grads(
            team, lambda f, n: mm_tn(branch_all[:, f : f + n], attended), width, "out"
        )
        (far_out,) = beside(team, [flow_out.send_far()])
        grad_attended = mm(branch_all, out_mat).astype(LOWER)
        grad_qkv = attend_back(qkv, grad_attended, log_sum, limits, score_scale)

        def in_product(first, count):
            return mm_nt(grad_qkv[first : first + count], qkv_mat)

        got = core_send(team, in_product, half_rows)
        total, sent = core_total(team, in_product, half_rows, got)
        flow_qkv = Grads(
            team, lambda f, n: mm_tn(inputs[:, f : f + n], grad_qkv), width, "qkv"
        )
        cross_out = flow_out.cross(far_out)
        near_up, *rest = fence(
            near_up, *sent, *got_up_a, *[b for a, b in up_halves], *cross_out
        )
        sent, rest = rest[: members - 1], rest[members - 1 :]
        got_up_a, up_b, cross_out = rest[:steps], rest[steps : 2 * steps], rest[2 * steps :]
        total_down = flow_down.total(
            near_down,
            [jnp.concatenate(both, axis=0) for both in zip(got_down_a, got_down_b)],
        )

    qkv_sum = jnp.sum(grad_qkv.astype(WIDE), axis=0)
    grad_bup = jnp.sum(grad_hidden.astype(WIDE), axis=0)
    zeros = jnp.zeros((members, 1), WIDE)
    by_slot = [
        put(zeros * part[None], part[None], (my_slot, 0)).reshape(-1)
        for part in (qkv_sum[:wide], qkv_sum[2 * wide :], grad_bup)
    ]
    by_row = jnp.stack([grad_bout, grad_gmid, grad_smid, grad_bdown, grad_gend, grad_send])
    by_row = from_team_order(team, by_row).reshape(-1)
    sums = jnp.concatenate([by_row] + by_slot).reshape(-1, 128)
    by_row_rows = by_row.shape[0] // 128

    def add_ring(value, name):
        return value + sum(team.ring(value, name, step) for step in range(1, team.sizes[name]))

    with jax.named_scope("s10"):
        got = team_send(team, sent)
        got_up_b = flow_up.go(up_b)
        (far_qkv,) = beside(team, [flow_qkv.send_far()])
        cross_qkv = flow_qkv.cross(far_qkv)
        both = add_ring(sums[:by_row_rows], "tp")
        sums = jnp.concatenate([both, sums[by_row_rows:]], axis=0)
        sums, total_down, near_up, *rest = fence(
            sums, total_down, near_up, *got, *got_up_b, *cross_qkv, *cross_out
        )
        got, rest = rest[: members - 1], rest[members - 1 :]
        got_up_b, cross_qkv, cross_out = rest[:steps], rest[steps : 2 * steps], rest[2 * steps :]
    with jax.named_scope("s11"):
        got_qkv = flow_qkv.go(cross_qkv)
        got_out = flow_out.go(cross_out)
        grad_own = (team_total(total, got) + grad_inner).astype(LOWER)
        swapped = swap_home(from_team_order(team, grad_own))
        sums = add_ring(sums, "y")
        near_qkv, near_out = beside(team, [flow_qkv.send_near(), flow_out.send_near()])
        home_down = home_pieces(team, total_down)
        total_up = flow_up.total(
            near_up, [jnp.concatenate(both, axis=0) for both in zip(got_up_a, got_up_b)]
        )
        rest = fence(sums, swapped, near_qkv, near_out, total_up, *home_down)
        sums, swapped, near_qkv, near_out, total_up = rest[:5]
        home_down = rest[5:]
        (grad_down,) = home_join(team, home_down, [tall])
    with jax.named_scope("s12"):
        home_up = home_pieces(team, total_up)
        out_two = deal(team, dealing, out_pieces, False)
        grad_tokens = join_cores(team, swapped)
        sums = add_ring(sums, "h")
        total_qkv = flow_qkv.total(near_qkv, got_qkv)
        total_out = flow_out.total(near_out, got_out)
        rest = fence(sums, grad_tokens, total_qkv, total_out, *home_up, *out_two)
        sums, grad_tokens, total_qkv, total_out = rest[:4]
        home_up, out_two = rest[4 : 4 + members], rest[4 + members :]
        (grad_up,) = home_join(team, home_up, [tall])
    with jax.named_scope("s13"):
        home_att = home_pieces(team, jnp.concatenate([total_qkv, total_out], axis=1))
        output = join_cores(team, pick_dealt(team, dealing, out_two, False))
        sums = add_ring(add_ring(sums, "l"), "x").reshape(-1)
        grad_query, grad_key, grad_value, grad_out = home_join(team, home_att, [wide] * 4)
    smalls = []
    first = 0
    for size in [width] * 6 + [b_query.shape[0], b_value.shape[0], b_up.shape[0]]:
        smalls.append(sums[first : first + size])
        first += size
    return (
        output,
        grad_tokens,
        grad_query,
        grad_key,
        grad_value,
        grad_out,
        smalls[6],
        smalls[7],
        smalls[0],
        smalls[1],
        smalls[2],
        grad_up,
        smalls[8],
        grad_down,
        smalls[3],
        smalls[4],
        smalls[5],
    )


def solution(mesh):
    fsdp, ctx, tp = (mesh.shape[name] for name in ("fsdp", "ctx", "tp"))
    fine = Mesh(mesh.devices.reshape(fsdp // 2, 2, 2, ctx // 2, tp), ROWS + ("tp",))
    rows, split = P(ROWS, None), P(ROWS, "tp")
    in_specs = (
        (rows, P(), P())
        + (split,) * 4
        + (P("tp"), P("tp"), P(), P(), P(), split, P("tp"), split, P(), P(), P(), rows)
    )
    out_specs = (
        (rows, rows)
        + (split,) * 4
        + (P("tp"), P("tp"), P(), P(), P(), split, P("tp"), split, P(), P(), P())
    )
    return jax.shard_map(local, mesh=fine, in_specs=in_specs, out_specs=out_specs, check_vma=False)
```

time: 1030 us -> 810 us (0.79)
  local copies, waits for them, and re-layouts: 226 us -> 72 us
  waiting for transfers between devices: 519 us -> 450 us
  Pallas kernels: 0 us -> 20.7 us
  between operations: 31 us -> 17.6 us
  matrix products: 82.4 us -> 94.1 us
    dynamic_update_slice x53 -> x21, local copies, waits for them, and re-layouts: 130 us -> 9.92 us  [put(): return lax.dynamic_update_slice(buffer, value, starts)]
    psum x1 -> x0, waiting for transfers between devices: 112 us -> none  [local(): lax.psum(jnp.concatenate(by_slot + [by_row]).reshape(-1, 128), ROWS)]
    ppermute x46 -> x43, waiting for transfers between devices: 196 us -> 284 us  [the longest x39 264 us: shift_(): return lax.ppermute(value, TEAM, perm)]
    ppermute x27 -> x47, waiting for transfers between devices: 211 us -> 166 us  [ring(): lax.ppermute(value, name, [(i, (i + step) % size) for i in range(size)])]
    ppermute x46 -> x43, starting transfers between devices: 80.5 us -> 58.7 us  [the longest x39 49.6 us: shift_(): return lax.ppermute(value, TEAM, perm)]
    pallas_call x0 -> x2, Pallas kernels: none -> 20.7 us  [the longest x1 10.8 us: attend_back(): pl.pallas_call(functools.partial(attend_back_kernel, scale, wide), grid=(...]
    ppermute x27 -> x47, starting transfers between devices: 16.3 us -> 34.7 us  [ring(): lax.ppermute(value, name, [(i, (i + step) % size) for i in range(size)])]
    broadcast_in_dim x25 -> x3, local copies, waits for them, and re-layouts: 16 us -> 2.21 us  [the longest x1 1.24 us: join_cores(): out = put(out, other[None], (lax.rem(team.at['tp'] - step + ts, ts), 0, 0))]
  transfers between devices with their start and end apart: 76 -> 92, of which waited for: 32 -> 49; matrix products, arithmetic and copies ran while one was open for 30% -> 20% of each run, Pallas kernels for 0% -> 3%
where the time goes in v2:
time: 810 us; the launch traced here: 801 us
  waiting for transfers between devices  450 us (56%)
  starting transfers between devices  94.7 us (12%)
  matrix products  94.1 us (12%)
  local copies, waits for them, and re-layouts  72 us (9%)
  other arithmetic  51.3 us (6%)
  Pallas kernels  20.7 us (3%)
  between operations  17.6 us (2%)
    ppermute x39, waiting for transfers between devices, shift_(): return lax.ppermute(value, TEAM, perm)  264 us
    ppermute x47, waiting for transfers between devices, ring(): lax.ppermute(value, name, [(i, (i + step) % size) for i in range(size)])  166 us
    dot_general x28, matrix products, dot(): lax.dot_general(left, right, (dims, ((), ())), preferred_element_type=WIDE)  94.1 us
    ppermute x39, starting transfers between devices, shift_(): return lax.ppermute(value, TEAM, perm)  49.6 us
    ppermute x47, starting transfers between devices, ring(): lax.ppermute(value, name, [(i, (i + step) % size) for i in range(size)])  34.7 us
    unnamed x206, local copies, waits for them, and re-layouts  21.7 us
    ppermute x4, waiting for transfers between devices, deal(): got.append(lax.ppermute(sent, ('l', 'y'), perm))  20.5 us
  transfers between devices with their start and end apart: 92, of which 49 were waited for; matrix products, arithmetic and copies ran while one was open for 20% of the time, Pallas kernels for 3%

profile of v2, /device:TPU:0, one launch (start us, length us, event | category | flops | bytes accessed | tf_op | source)
XLA Modules:
  0.0 800.8 jit_solution(4558554382976965836)
XLA Ops:
  14.3 12.4 %collective-permute-done.2 = bf16[128,1024]{1,0:T(8,128)(2,1)S(1)} collective-permute-done((bf16[128,1024]{1,0:T(8,128)(2,1)S(1)}, bf16[128,1024]{1,0:T(8,128)(2,1)S(1)}, u32[]{:S(2)}, u32[]{:S(2)}) %collective-permute-start.2) | collective-permute-done | bytes 262176 | tf_op jit(solution)/shard_map/a0/team10/ppermute | solution.py:58
  45.1 14.9 %collective-permute-done.5 = bf16[512,256]{1,0:T(8,128)(2,1)S(1)} collective-permute-done((bf16[512,256]{1,0:T(8,128)(2,1)S(1)}, bf16[512,256]{1,0:T(8,128)(2,1)S(1)}, u32[]{:S(2)}, u32[]{:S(2)}) %collective-permute-start.5) | collective-permute-done | bytes 262176 | tf_op jit(solution)/shard_map/a1/ring_y/ppermute | solution.py:63
  67.9 16.5 %collective-permute-done.8 = bf16[128,2048]{1,0:T(8,128)(2,1)S(1)} collective-permute-done((bf16[128,2048]{1,0:T(8,128)(2,1)S(1)}, bf16[128,2048]{1,0:T(8,128)(2,1)S(1)}, u32[]{:S(2)}, u32[]{:S(2)}) %collective-permute-start.8) | collective-permute-done | bytes 524320 | tf_op jit(solution)/shard_map/a1/team11/ppermute | solution.py:58
  96.8 8.9 %collective-permute-done.15 = bf16[512,256]{1,0:T(8,128)(2,1)} collective-permute-done((bf16[512,256]{1,0:T(8,128)(2,1)S(1)}, bf16[512,256]{1,0:T(8,128)(2,1)}, u32[]{:S(2)}, u32[]{:S(2)}) %collective-permute-start.15) | collective-permute-done | bytes 262176 | tf_op jit(solution)/shard_map/a2/ring_h/ppermute | solution.py:63
  113.1 11.2 %collective-permute-done.13 = bf16[128,2048]{1,0:T(8,128)(2,1)S(1)} collective-permute-done((bf16[128,2048]{1,0:T(8,128)(2,1)}, bf16[128,2048]{1,0:T(8,128)(2,1)S(1)}, u32[]{:S(2)}, u32[]{:S(2)}) %collective-permute-start.13) | collective-permute-done | bytes 524320 | tf_op jit(solution)/shard_map/a2/team11/ppermute | solution.py:58
  135.7 10.0 %c1.1 = (bf16[1024,256]{1,0:T(8,128)(2,1)S(1)}, f32[2,1,1024]{2,1,0:T(1,128)S(1)}) custom-call(s32[8]{0:T(128)S(1)} %multiply_subtract_fusion.limits_ref, bf16[1024,768]{1,0:T(8,128)(2,1)S(1)} %add_convert_fusion.query_ref.key_ref.value_ref, bf16[1024,768]{1,0:T(8,128)(2,1)S(1)} %add_convert_fusion.query_ref.key_ref.value_ref, ...), custom_call_target="tpu_custom_call" | custom-call | flops 1000000 | bytes 100000 | tf_op jit(solution)/shard_map/c1/pallas_call | solution.py:394
  157.7 22.5 %collective-permute-done.19 = bf16[256,1024]{1,0:T(8,128)(2,1)S(1)} collective-permute-done((bf16[256,1024]{1,0:T(8,128)(2,1)S(1)}, bf16[256,1024]{1,0:T(8,128)(2,1)S(1)}, u32[]{:S(2)}, u32[]{:S(2)}) %collective-permute-start.19) | collective-permute-done | bytes 524320 | tf_op jit(solution)/shard_map/c1/ring_h/ppermute | solution.py:63
  185.6 8.6 %collective-permute-done.20 = bf16[128,2048]{1,0:T(8,128)(2,1)S(1)} collective-permute-done((bf16[128,2048]{1,0:T(8,128)(2,1)S(1)}, bf16[128,2048]{1,0:T(8,128)(2,1)S(1)}, u32[]{:S(2)}, u32[]{:S(2)}) %collective-permute-start.20) | collective-permute-done | bytes 524320 | tf_op jit(solution)/shard_map/s3/team01/ppermute | solution.py:58
  194.2 13.7 %collective-permute-done.21 = bf16[128,2048]{1,0:T(8,128)(2,1)S(1)} collective-permute-done((bf16[128,2048]{1,0:T(8,128)(2,1)S(1)}, bf16[128,2048]{1,0:T(8,128)(2,1)S(1)}, u32[]{:S(2)}, u32[]{:S(2)}) %collective-permute-start.21) | collective-permute-done | bytes 524320 | tf_op jit(solution)/shard_map/s3/team10/ppermute | solution.py:58
  207.9 10.0 %collective-permute-done.22 = bf16[128,2048]{1,0:T(8,128)(2,1)S(1)} collective-permute-done((bf16[128,2048]{1,0:T(8,128)(2,1)S(1)}, bf16[128,2048]{1,0:T(8,128)(2,1)S(1)}, u32[]{:S(2)}, u32[]{:S(2)}) %collective-permute-start.22) | collective-permute-done | bytes 524320 | tf_op jit(solution)/shard_map/s3/team11/ppermute | solution.py:58
  231.7 14.9 %collective-permute-done.26 = bf16[128,2048]{1,0:T(8,128)(2,1)S(1)} collective-permute-done((bf16[128,2048]{1,0:T(8,128)(2,1)S(1)}, bf16[128,2048]{1,0:T(8,128)(2,1)S(1)}, u32[]{:S(2)}, u32[]{:S(2)}) %collective-permute-start.26) | collective-permute-done | bytes 524320 | tf_op jit(solution)/shard_map/s4/team10/ppermute | solution.py:58
  246.6 8.8 %collective-permute-done.27 = bf16[128,2048]{1,0:T(8,128)(2,1)S(1)} collective-permute-done((bf16[128,2048]{1,0:T(8,128)(2,1)S(1)}, bf16[128,2048]{1,0:T(8,128)(2,1)S(1)}, u32[]{:S(2)}, u32[]{:S(2)}) %collective-permute-start.27) | collective-permute-done | bytes 524320 | tf_op jit(solution)/shard_map/s4/team11/ppermute | solution.py:58
  277.0 13.3 %collective-permute-done.32 = bf16[256,1024]{1,0:T(8,128)(2,1)S(1)} collective-permute-done((bf16[256,1024]{1,0:T(8,128)(2,1)S(1)}, bf16[256,1024]{1,0:T(8,128)(2,1)S(1)}, u32[]{:S(2)}, u32[]{:S(2)}) %collective-permute-start.32) | collective-permute-done | bytes 524320 | tf_op jit(solution)/shard_map/c2/ring_h/ppermute | solution.py:63
  290.3 9.3 %collective-permute-done.33 = bf16[256,1024]{1,0:T(8,128)(2,1)S(1)} collective-permute-done((bf16[256,1024]{1,0:T(8,128)(2,1)S(1)}, bf16[256,1024]{1,0:T(8,128)(2,1)S(1)}, u32[]{:S(2)}, u32[]{:S(2)}) %collective-permute-start.33) | collective-permute-done | bytes 524320 | tf_op jit(solution)/shard_map/c2/ring_y/ppermute | solution.py:63
  301.2 11.9 %collective-permute-done.34 = bf16[256,1024]{1,0:T(8,128)(2,1)S(1)} collective-permute-done((bf16[256,1024]{1,0:T(8,128)(2,1)S(1)}, bf16[256,1024]{1,0:T(8,128)(2,1)S(1)}, u32[]{:S(2)}, u32[]{:S(2)}) %collective-permute-start.34) | collective-permute-done | bytes 524320 | tf_op jit(solution)/shard_map/s5/ring_y/ppermute | solution.py:63
  334.2 16.3 %collective-permute-done.36 = bf16[128,2048]{1,0:T(8,128)(2,1)S(1)} collective-permute-done((bf16[128,2048]{1,0:T(8,128)(2,1)S(1)}, bf16[128,2048]{1,0:T(8,128)(2,1)S(1)}, u32[]{:S(2)}, u32[]{:S(2)}) %collective-permute-start.36) | collective-permute-done | bytes 524320 | tf_op jit(solution)/shard_map/s5/ring_h/ppermute | solution.py:63
  367.1 11.2 %collective-permute-done.39 = bf16[128,2048]{1,0:T(8,128)(2,1)} collective-permute-done((bf16[128,2048]{1,0:T(8,128)(2,1)}, bf16[128,2048]{1,0:T(8,128)(2,1)}, u32[]{:S(2)}, u32[]{:S(2)}) %collective-permute-start.39) | collective-permute-done | bytes 524320 | tf_op jit(solution)/shard_map/s6/team11/ppermute | solution.py:58
  379.1 20.5 %collective-permute-done.41 = bf16[128,2048]{1,0:T(8,128)(2,1)} collective-permute-done((bf16[128,2048]{1,0:T(8,128)(2,1)}, bf16[128,2048]{1,0:T(8,128)(2,1)}, u32[]{:S(2)}, u32[]{:S(2)}) %collective-permute-start.41) | collective-permute-done | bytes 524320 | tf_op jit(solution)/shard_map/s6/flip/ppermute | solution.py:276
  429.8 13.9 %collective-permute-done.43 = bf16[128,2048]{1,0:T(8,128)(2,1)} collective-permute-done((bf16[128,2048]{1,0:T(8,128)(2,1)S(1)}, bf16[128,2048]{1,0:T(8,128)(2,1)}, u32[]{:S(2)}, u32[]{:S(2)}) %collective-permute-start.43) | collective-permute-done | bytes 524320 | tf_op jit(solution)/shard_map/s7/team10/ppermute | solution.py:58
  443.7 9.8 %collective-permute-done.44 = bf16[128,2048]{1,0:T(8,128)(2,1)} collective-permute-done((bf16[128,2048]{1,0:T(8,128)(2,1)S(1)}, bf16[128,2048]{1,0:T(8,128)(2,1)}, u32[]{:S(2)}, u32[]{:S(2)}) %collective-permute-start.44) | collective-permute-done | bytes 524320 | tf_op jit(solution)/shard_map/s7/team11/ppermute | solution.py:58
  489.2 10.7 %collective-permute-done.49 = bf16[512,1024]{1,0:T(8,128)(2,1)} collective-permute-done((bf16[512,1024]{1,0:T(8,128)(2,1)}, bf16[512,1024]{1,0:T(8,128)(2,1)}, u32[]{:S(2)}, u32[]{:S(2)}) %collective-permute-start.49) | collective-permute-done | bytes 1048608 | tf_op jit(solution)/shard_map/c3/ring_y/ppermute | solution.py:63
  522.0 11.2 %collective-permute-done.51 = bf16[128,2048]{1,0:T(8,128)(2,1)S(1)} collective-permute-done((bf16[128,2048]{1,0:T(8,128)(2,1)S(1)}, bf16[128,2048]{1,0:T(8,128)(2,1)S(1)}, u32[]{:S(2)}, u32[]{:S(2)}) %collective-permute-start.51) | collective-permute-done | bytes 524320 | tf_op jit(solution)/shard_map/s8/team10/ppermute | solution.py:58
  533.2 9.9 %collective-permute-done.52 = bf16[128,2048]{1,0:T(8,128)(2,1)S(1)} collective-permute-done((bf16[128,2048]{1,0:T(8,128)(2,1)S(1)}, bf16[128,2048]{1,0:T(8,128)(2,1)S(1)}, u32[]{:S(2)}, u32[]{:S(2)}) %collective-permute-start.52) | collective-permute-done | bytes 524320 | tf_op jit(solution)/shard_map/s8/team11/ppermute | solution.py:58
  557.0 15.0 %collective-permute-done.57 = bf16[128,2048]{1,0:T(8,128)(2,1)S(1)} collective-permute-done((bf16[128,2048]{1,0:T(8,128)(2,1)S(1)}, bf16[128,2048]{1,0:T(8,128)(2,1)S(1)}, u32[]{:S(2)}, u32[]{:S(2)}) %collective-permute-start.57) | collective-permute-done | bytes 524320 | tf_op jit(solution)/shard_map/s9/team10/ppermute | solution.py:58
  572.0 8.8 %collective-permute-done.58 = bf16[128,2048]{1,0:T(8,128)(2,1)} collective-permute-done((bf16[128,2048]{1,0:T(8,128)(2,1)S(1)}, bf16[128,2048]{1,0:T(8,128)(2,1)}, u32[]{:S(2)}, u32[]{:S(2)}) %collective-permute-start.58) | collective-permute-done | bytes 524320 | tf_op jit(solution)/shard_map/s9/team11/ppermute | solution.py:58
  599.3 10.8 %c4.1 = bf16[1024,768]{1,0:T(8,128)(2,1)S(1)} custom-call(s32[8]{0:T(128)S(1)} %multiply_subtract_fusion.limits_ref, bf16[1024,768]{1,0:T(8,128)(2,1)S(1)} %add_convert_fusion.query_ref.key_ref.value_ref, bf16[1024,768]{1,0:T(8,128)(2,1)S(1)} %add_convert_fusion.query_ref.key_ref.value_ref, ...), custom_call_target="tpu_custom_call" | custom-call | flops 1000000 | bytes 100000 | tf_op jit(solution)/shard_map/c4/pallas_call | solution.py:419
  648.8 12.3 %collective-permute-done.66 = bf16[128,2048]{1,0:T(8,128)(2,1)S(1)} collective-permute-done((bf16[128,2048]{1,0:T(8,128)(2,1)S(1)}, bf16[128,2048]{1,0:T(8,128)(2,1)S(1)}, u32[]{:S(2)}, u32[]{:S(2)}) %collective-permute-start.66) | collective-permute-done | bytes 524320 | tf_op jit(solution)/shard_map/s10/team10/ppermute | solution.py:58
  661.1 10.6 %collective-permute-done.67 = bf16[128,2048]{1,0:T(8,128)(2,1)S(1)} collective-permute-done((bf16[128,2048]{1,0:T(8,128)(2,1)S(1)}, bf16[128,2048]{1,0:T(8,128)(2,1)S(1)}, u32[]{:S(2)}, u32[]{:S(2)}) %collective-permute-start.67) | collective-permute-done | bytes 524320 | tf_op jit(solution)/shard_map/s10/team11/ppermute | solution.py:58
  692.4 13.4 %collective-permute-done.75 = bf16[128,1024]{1,0:T(8,128)(2,1)S(1)} collective-permute-done((bf16[128,1024]{1,0:T(8,128)(2,1)S(1)}, bf16[128,1024]{1,0:T(8,128)(2,1)S(1)}, u32[]{:S(2)}, u32[]{:S(2)}) %collective-permute-start.75) | collective-permute-done | bytes 262176 | tf_op jit(solution)/shard_map/s11/team10/ppermute | solution.py:58
  705.8 8.1 %collective-permute-done.76 = bf16[128,1024]{1,0:T(8,128)(2,1)S(1)} collective-permute-done((bf16[128,1024]{1,0:T(8,128)(2,1)S(1)}, bf16[128,1024]{1,0:T(8,128)(2,1)S(1)}, u32[]{:S(2)}, u32[]{:S(2)}) %collective-permute-start.76) | collective-permute-done | bytes 262176 | tf_op jit(solution)/shard_map/s11/team11/ppermute | solution.py:58
  714.6 34.5 %collective-permute-done.80 = bf16[512,256]{1,0:T(8,128)(2,1)S(1)} collective-permute-done((bf16[512,256]{1,0:T(8,128)(2,1)S(1)}, bf16[512,256]{1,0:T(8,128)(2,1)S(1)}, u32[]{:S(2)}, u32[]{:S(2)}) %collective-permute-start.80) | collective-permute-done | bytes 262176 | tf_op jit(solution)/shard_map/s11/ring_h/ppermute | solution.py:63
  778.1 9.3 %collective-permute-done.90 = f32[144,128]{1,0:T(8,128)S(1)} collective-permute-done((f32[144,128]{1,0:T(8,128)S(1)}, f32[144,128]{1,0:T(8,128)S(1)}, u32[]{:S(2)}, u32[]{:S(2)}) %collective-permute-start.90) | collective-permute-done | bytes 73760 | tf_op jit(solution)/shard_map/s13/ring_l/ppermute | solution.py:63
  (569 shorter events, 370.2 us)
Async XLA Ops:
  35.8 48.6 %collective-permute-start.4 = (bf16[512,768]{1,0:T(8,128)(2,1)}, bf16[512,768]{1,0:T(8,128)(2,1)}, u32[]{:S(2)}, u32[]{:S(2)}) collective-permute-start(bf16[512,768]{1,0:T(8,128)(2,1)} %bitcast.20), channel_id=1, source_target_pairs={{0,4},{4,0},{1,5},{5,1},{2,6},{6,2},{3,7},{7,3},{8,12},{12,8},{9,1... | collective-permute-start | bytes 2359304 | tf_op jit(solution)/shard_map/a1/ring_y/ppermute | solution.py:63
  35.8 48.6 %collective-permute-start.9 = (bf16[512,768]{1,0:T(8,128)(2,1)}, bf16[512,768]{1,0:T(8,128)(2,1)}, u32[]{:S(2)}, u32[]{:S(2)}) collective-permute-start(bf16[512,768]{1,0:T(8,128)(2,1)} %bitcast.20), channel_id=1, source_target_pairs={{0,16},{16,0},{1,17},{17,1},{2,18},{18,2},{3,19},{19,3},{4,20},{20... | collective-permute-start | bytes 2359304 | tf_op jit(solution)/shard_map/a1/ring_h/ppermute | solution.py:63
  87.7 36.6 %collective-permute-start.10 = (bf16[512,2048]{1,0:T(8,128)(2,1)}, bf16[512,2048]{1,0:T(8,128)(2,1)}, u32[]{:S(2)}, u32[]{:S(2)}) collective-permute-start(bf16[512,2048]{1,0:T(8,128)(2,1)} %constant_dynamic-update-slice_fusion), channel_id=1, source_target_pairs={{0,1},{1,0},{2,3},{3,2},{4,5},{5,4},{6,7},{7,6},{8,9},{9,8},{10,11... | collective-permute-start | bytes 6291464 | tf_op jit(solution)/shard_map/a2/ring_tp/ppermute | solution.py:63
  181.8 36.0 %collective-permute-start.22 = (bf16[128,2048]{1,0:T(8,128)(2,1)S(1)}, bf16[128,2048]{1,0:T(8,128)(2,1)S(1)}, u32[]{:S(2)}, u32[]{:S(2)}) collective-permute-start(bf16[128,2048]{1,0:T(8,128)(2,1)S(1)} %get-tuple-element.170), channel_id=1, source_target_pairs={{0,10},{2,8},{8,2},{10,0},{1,11},{3,9},{9,3},{11,1},{4,14},{6,12},... | collective-permute-start | bytes 1572872 | tf_op jit(solution)/shard_map/s3/team11/ppermute | solution.py:58
  183.8 34.0 %collective-permute-start.23 = (bf16[256,1024]{1,0:T(8,128)(2,1)S(1)}, bf16[256,1024]{1,0:T(8,128)(2,1)S(1)}, u32[]{:S(2)}, u32[]{:S(2)}) collective-permute-start(bf16[256,1024]{1,0:T(8,128)(2,1)S(1)} %bitcast.202), channel_id=1, source_target_pairs={{0,16},{16,0},{1,17},{17,1},{2,18},{18,2},{3,19},{19,3},{4,20},{20... | collective-permute-start | bytes 1572872 | tf_op jit(solution)/shard_map/s3/ring_h/ppermute | solution.py:63
  184.6 33.2 %collective-permute-start.24 = (bf16[256,1024]{1,0:T(8,128)(2,1)S(1)}, bf16[256,1024]{1,0:T(8,128)(2,1)S(1)}, u32[]{:S(2)}, u32[]{:S(2)}) collective-permute-start(bf16[256,1024]{1,0:T(8,128)(2,1)S(1)} %collective-permute-done.19), channel_id=1, source_target_pairs={{0,4},{4,0},{1,5},{5,1},{2,6},{6,2},{3,7},{7,3},{8,12},{12,8},{9,1... | collective-permute-start | bytes 1572872 | tf_op jit(solution)/shard_map/s3/ring_y/ppermute | solution.py:63
  220.6 34.7 %collective-permute-start.27 = (bf16[128,2048]{1,0:T(8,128)(2,1)S(1)}, bf16[128,2048]{1,0:T(8,128)(2,1)S(1)}, u32[]{:S(2)}, u32[]{:S(2)}) collective-permute-start(bf16[128,2048]{1,0:T(8,128)(2,1)S(1)} %fusion.58), channel_id=1, source_target_pairs={{0,10},{2,8},{8,2},{10,0},{1,11},{3,9},{9,3},{11,1},{4,14},{6,12},... | collective-permute-start | bytes 1572872 | tf_op jit(solution)/shard_map/s4/team11/ppermute | solution.py:58
  223.4 32.0 %collective-permute-start.28 = (bf16[256,1024]{1,0:T(8,128)(2,1)S(1)}, bf16[256,1024]{1,0:T(8,128)(2,1)S(1)}, u32[]{:S(2)}, u32[]{:S(2)}) collective-permute-start(bf16[256,1024]{1,0:T(8,128)(2,1)S(1)} %get-tuple-element.347), channel_id=1, source_target_pairs={{0,16},{16,0},{1,17},{17,1},{2,18},{18,2},{3,19},{19,3},{4,20},{20... | collective-permute-start | bytes 1572872 | tf_op jit(solution)/shard_map/s4/ring_h/ppermute | solution.py:63
  224.5 30.8 %collective-permute-start.29 = (bf16[256,1024]{1,0:T(8,128)(2,1)S(1)}, bf16[256,1024]{1,0:T(8,128)(2,1)S(1)}, u32[]{:S(2)}, u32[]{:S(2)}) collective-permute-start(bf16[256,1024]{1,0:T(8,128)(2,1)S(1)} %collective-permute-done.23), channel_id=1, source_target_pairs={{0,4},{4,0},{1,5},{5,1},{2,6},{6,2},{3,7},{7,3},{8,12},{12,8},{9,1... | collective-permute-start | bytes 1572872 | tf_op jit(solution)/shard_map/s4/ring_y/ppermute | solution.py:63
  262.7 36.9 %collective-permute-start.31 = (bf16[512,1024]{1,0:T(8,128)(2,1)S(1)}, bf16[512,1024]{1,0:T(8,128)(2,1)S(1)}, u32[]{:S(2)}, u32[]{:S(2)}) collective-permute-start(bf16[512,1024]{1,0:T(8,128)(2,1)S(1)} %bitcast.183), channel_id=1, source_target_pairs={{0,4},{4,0},{1,5},{5,1},{2,6},{6,2},{3,7},{7,3},{8,12},{12,8},{9,1... | collective-permute-start | bytes 3145736 | tf_op jit(solution)/shard_map/c2/ring_y/ppermute | solution.py:63
  264.8 34.7 %collective-permute-start.33 = (bf16[256,1024]{1,0:T(8,128)(2,1)S(1)}, bf16[256,1024]{1,0:T(8,128)(2,1)S(1)}, u32[]{:S(2)}, u32[]{:S(2)}) collective-permute-start(bf16[256,1024]{1,0:T(8,128)(2,1)S(1)} %copy-done.48), channel_id=1, source_target_pairs={{0,4},{4,0},{1,5},{5,1},{2,6},{6,2},{3,7},{7,3},{8,12},{12,8},{9,1... | collective-permute-start | bytes 1572872 | tf_op jit(solution)/shard_map/c2/ring_y/ppermute | solution.py:63
  356.7 42.9 %collective-permute-start.41 = (bf16[128,2048]{1,0:T(8,128)(2,1)}, bf16[128,2048]{1,0:T(8,128)(2,1)}, u32[]{:S(2)}, u32[]{:S(2)}) collective-permute-start(bf16[128,2048]{1,0:T(8,128)(2,1)} %get-tuple-element.345), channel_id=1, source_target_pairs={{0,4},{4,12},{8,0},{12,8},{1,5},{5,13},{9,1},{13,9},{2,6},{6,14},{... | collective-permute-start | bytes 1572872 | tf_op jit(solution)/shard_map/s6/flip/ppermute | solution.py:276
  417.5 36.0 %collective-permute-start.44 = (bf16[128,2048]{1,0:T(8,128)(2,1)S(1)}, bf16[128,2048]{1,0:T(8,128)(2,1)}, u32[]{:S(2)}, u32[]{:S(2)}) collective-permute-start(bf16[128,2048]{1,0:T(8,128)(2,1)S(1)} %get-tuple-element.203), channel_id=1, source_target_pairs={{0,10},{2,8},{8,2},{10,0},{1,11},{3,9},{9,3},{11,1},{4,14},{6,12},... | collective-permute-start | bytes 1572872 | tf_op jit(solution)/shard_map/s7/team11/ppermute | solution.py:58
  471.2 31.2 %collective-permute-start.47 = (bf16[512,2048]{1,0:T(8,128)(2,1)}, bf16[512,2048]{1,0:T(8,128)(2,1)}, u32[]{:S(2)}, u32[]{:S(2)}) collective-permute-start(bf16[512,2048]{1,0:T(8,128)(2,1)} %convolution_convert_fusion), channel_id=1, source_target_pairs={{0,1},{1,0},{2,3},{3,2},{4,5},{5,4},{6,7},{7,6},{8,9},{9,8},{10,11... | collective-permute-start | bytes 6291464 | tf_op jit(solution)/shard_map/c3/ring_tp/ppermute | solution.py:63
  487.1 34.6 %collective-permute-start.48 = (bf16[512,1024]{1,0:T(8,128)(2,1)S(1)}, bf16[512,1024]{1,0:T(8,128)(2,1)S(1)}, u32[]{:S(2)}, u32[]{:S(2)}) collective-permute-start(bf16[512,1024]{1,0:T(8,128)(2,1)S(1)} %convolution_convert_fusion.7), channel_id=1, source_target_pairs={{0,4},{4,0},{1,5},{5,1},{2,6},{6,2},{3,7},{7,3},{8,12},{12,8},{9,1... | collective-permute-start | bytes 3145736 | tf_op jit(solution)/shard_map/s8/ring_y/ppermute | solution.py:63
  507.8 35.3 %collective-permute-start.52 = (bf16[128,2048]{1,0:T(8,128)(2,1)S(1)}, bf16[128,2048]{1,0:T(8,128)(2,1)S(1)}, u32[]{:S(2)}, u32[]{:S(2)}) collective-permute-start(bf16[128,2048]{1,0:T(8,128)(2,1)S(1)} %get-tuple-element.210), channel_id=1, source_target_pairs={{0,10},{2,8},{8,2},{10,0},{1,11},{3,9},{9,3},{11,1},{4,14},{6,12},... | collective-permute-start | bytes 1572872 | tf_op jit(solution)/shard_map/s8/team11/ppermute | solution.py:58
  510.9 32.1 %collective-permute-start.53 = (bf16[256,1024]{1,0:T(8,128)(2,1)S(1)}, bf16[256,1024]{1,0:T(8,128)(2,1)S(1)}, u32[]{:S(2)}, u32[]{:S(2)}) collective-permute-start(bf16[256,1024]{1,0:T(8,128)(2,1)S(1)} %get-tuple-element.344), channel_id=1, source_target_pairs={{0,16},{16,0},{1,17},{17,1},{2,18},{18,2},{3,19},{19,3},{4,20},{20... | collective-permute-start | bytes 1572872 | tf_op jit(solution)/shard_map/s8/ring_h/ppermute | solution.py:63
  521.7 32.5 %collective-permute-start.55 = (bf16[512,1024]{1,0:T(8,128)(2,1)}, bf16[512,1024]{1,0:T(8,128)(2,1)}, u32[]{:S(2)}, u32[]{:S(2)}) collective-permute-start(bf16[512,1024]{1,0:T(8,128)(2,1)} %convolution_convert_fusion.5), channel_id=1, source_target_pairs={{0,4},{4,0},{1,5},{5,1},{2,6},{6,2},{3,7},{7,3},{8,12},{12,8},{9,1... | collective-permute-start | bytes 3145736 | tf_op jit(solution)/shard_map/s9/ring_y/ppermute | solution.py:63
  546.1 34.6 %collective-permute-start.58 = (bf16[128,2048]{1,0:T(8,128)(2,1)S(1)}, bf16[128,2048]{1,0:T(8,128)(2,1)}, u32[]{:S(2)}, u32[]{:S(2)}) collective-permute-start(bf16[128,2048]{1,0:T(8,128)(2,1)S(1)} %get-tuple-element.217), channel_id=1, source_target_pairs={{0,10},{2,8},{8,2},{10,0},{1,11},{3,9},{9,3},{11,1},{4,14},{6,12},... | collective-permute-start | bytes 1572872 | tf_op jit(solution)/shard_map/s9/team11/ppermute | solution.py:58
  548.8 31.9 %collective-permute-start.59 = (bf16[256,1024]{1,0:T(8,128)(2,1)}, bf16[256,1024]{1,0:T(8,128)(2,1)}, u32[]{:S(2)}, u32[]{:S(2)}) collective-permute-start(bf16[256,1024]{1,0:T(8,128)(2,1)} %get-tuple-element.215), channel_id=1, source_target_pairs={{0,16},{16,0},{1,17},{17,1},{2,18},{18,2},{3,19},{19,3},{4,20},{20... | collective-permute-start | bytes 1572872 | tf_op jit(solution)/shard_map/s9/ring_h/ppermute | solution.py:63
  584.2 49.4 %collective-permute-start.61 = (bf16[512,1024]{1,0:T(8,128)(2,1)}, bf16[512,1024]{1,0:T(8,128)(2,1)}, u32[]{:S(2)}, u32[]{:S(2)}) collective-permute-start(bf16[512,1024]{1,0:T(8,128)(2,1)} %convolution_convert_fusion.4), channel_id=1, source_target_pairs={{0,4},{4,0},{1,5},{5,1},{2,6},{6,2},{3,7},{7,3},{8,12},{12,8},{9,1... | collective-permute-start | bytes 3145736 | tf_op jit(solution)/shard_map/c4/ring_y/ppermute | solution.py:63
  589.5 44.2 %collective-permute-start.63 = (bf16[256,1024]{1,0:T(8,128)(2,1)}, bf16[256,1024]{1,0:T(8,128)(2,1)}, u32[]{:S(2)}, u32[]{:S(2)}) collective-permute-start(bf16[256,1024]{1,0:T(8,128)(2,1)} %get-tuple-element.342), channel_id=1, source_target_pairs={{0,16},{16,0},{1,17},{17,1},{2,18},{18,2},{3,19},{19,3},{4,20},{20... | collective-permute-start | bytes 1572872 | tf_op jit(solution)/shard_map/c4/ring_h/ppermute | solution.py:63
  636.3 35.4 %collective-permute-start.67 = (bf16[128,2048]{1,0:T(8,128)(2,1)S(1)}, bf16[128,2048]{1,0:T(8,128)(2,1)S(1)}, u32[]{:S(2)}, u32[]{:S(2)}) collective-permute-start(bf16[128,2048]{1,0:T(8,128)(2,1)S(1)} %get-tuple-element.229), channel_id=1, source_target_pairs={{0,10},{2,8},{8,2},{10,0},{1,11},{3,9},{9,3},{11,1},{4,14},{6,12},... | collective-permute-start | bytes 1572872 | tf_op jit(solution)/shard_map/s10/team11/ppermute | solution.py:58
  637.2 34.4 %collective-permute-start.68 = (bf16[256,1024]{1,0:T(8,128)(2,1)S(1)}, bf16[256,1024]{1,0:T(8,128)(2,1)S(1)}, u32[]{:S(2)}, u32[]{:S(2)}) collective-permute-start(bf16[256,1024]{1,0:T(8,128)(2,1)S(1)} %copy-done.53), channel_id=1, source_target_pairs={{0,16},{16,0},{1,17},{17,1},{2,18},{18,2},{3,19},{19,3},{4,20},{20... | collective-permute-start | bytes 1572872 | tf_op jit(solution)/shard_map/s10/ring_h/ppermute | solution.py:63
  642.9 43.9 %collective-permute-start.72 = (bf16[512,768]{1,0:T(8,128)(2,1)}, bf16[512,768]{1,0:T(8,128)(2,1)}, u32[]{:S(2)}, u32[]{:S(2)}) collective-permute-start(bf16[512,768]{1,0:T(8,128)(2,1)} %convolution_convert_fusion.8), channel_id=1, source_target_pairs={{0,4},{4,0},{1,5},{5,1},{2,6},{6,2},{3,7},{7,3},{8,12},{12,8},{9,1... | collective-permute-start | bytes 2359304 | tf_op jit(solution)/shard_map/s11/ring_y/ppermute | solution.py:63
  674.5 39.5 %collective-permute-start.71 = (bf16[128,2048]{0,1:T(8,128)(2,1)S(1)}, bf16[128,2048]{0,1:T(8,128)(2,1)S(1)}, u32[]{:S(2)}, u32[]{:S(2)}) collective-permute-start(bf16[128,2048]{0,1:T(8,128)(2,1)S(1)} %bitcast.201), channel_id=1, source_target_pairs={{0,0},{4,8},{8,4},{12,12},{1,1},{5,9},{9,5},{13,13},{2,2},{6,10},{... | collective-permute-start | bytes 1572872 | tf_op jit(solution)/shard_map/s11/ppermute | solution.py:79
  681.5 32.4 %collective-permute-start.76 = (bf16[128,1024]{1,0:T(8,128)(2,1)S(1)}, bf16[128,1024]{1,0:T(8,128)(2,1)S(1)}, u32[]{:S(2)}, u32[]{:S(2)}) collective-permute-start(bf16[128,1024]{1,0:T(8,128)(2,1)S(1)} %get-tuple-element.300), channel_id=1, source_target_pairs={{0,10},{2,8},{8,2},{10,0},{1,11},{3,9},{9,3},{11,1},{4,14},{6,12},... | collective-permute-start | bytes 786440 | tf_op jit(solution)/shard_map/s11/team11/ppermute | solution.py:58
  686.8 74.1 %collective-permute-start.84 = (bf16[128,2048]{0,1:T(8,128)(2,1)}, bf16[128,2048]{0,1:T(8,128)(2,1)}, u32[]{:S(2)}, u32[]{:S(2)}) collective-permute-start(bf16[128,2048]{0,1:T(8,128)(2,1)} %get-tuple-element.340), channel_id=1, source_target_pairs={{0,0},{4,8},{8,4},{12,12},{1,1},{5,9},{9,5},{13,13},{2,2},{6,10},{... | collective-permute-start | bytes 1572872 | tf_op jit(solution)/shard_map/s12/flip/ppermute | solution.py:276
  692.2 68.7 %collective-permute-start.85 = (bf16[128,2048]{0,1:T(8,128)(2,1)}, bf16[128,2048]{0,1:T(8,128)(2,1)}, u32[]{:S(2)}, u32[]{:S(2)}) collective-permute-start(bf16[128,2048]{0,1:T(8,128)(2,1)} %get-tuple-element.339), channel_id=1, source_target_pairs={{0,8},{4,0},{8,12},{12,4},{1,9},{5,1},{9,13},{13,5},{2,10},{6,2},{... | collective-permute-start | bytes 1572872 | tf_op jit(solution)/shard_map/s12/flip/ppermute | solution.py:276
  705.8 49.8 %collective-permute-start.79 = (bf16[512,768]{1,0:T(8,128)(2,1)S(1)}, bf16[512,768]{1,0:T(8,128)(2,1)S(1)}, u32[]{:S(2)}, u32[]{:S(2)}) collective-permute-start(bf16[512,768]{1,0:T(8,128)(2,1)S(1)} %copy-done.72), channel_id=1, source_target_pairs={{0,16},{16,0},{1,17},{17,1},{2,18},{18,2},{3,19},{19,3},{4,20},{20... | collective-permute-start | bytes 2359304 | tf_op jit(solution)/shard_map/s11/ring_h/ppermute | solution.py:63
  714.0 35.2 %collective-permute-start.80 = (bf16[512,256]{1,0:T(8,128)(2,1)S(1)}, bf16[512,256]{1,0:T(8,128)(2,1)S(1)}, u32[]{:S(2)}, u32[]{:S(2)}) collective-permute-start(bf16[512,256]{1,0:T(8,128)(2,1)S(1)} %copy-done.77), channel_id=1, source_target_pairs={{0,16},{16,0},{1,17},{17,1},{2,18},{18,2},{3,19},{19,3},{4,20},{20... | collective-permute-start | bytes 786440 | tf_op jit(solution)/shard_map/s11/ring_h/ppermute | solution.py:63
  714.0 43.1 %collective-permute-start.78 = (bf16[128,2048]{0,1:T(8,128)(2,1)S(1)}, bf16[128,2048]{0,1:T(8,128)(2,1)S(1)}, u32[]{:S(2)}, u32[]{:S(2)}) collective-permute-start(bf16[128,2048]{0,1:T(8,128)(2,1)S(1)} %collective-permute-done.71), channel_id=1, source_target_pairs={{0,1},{1,0},{2,3},{3,2},{4,5},{5,4},{6,7},{7,6},{8,9},{9,8},{10,11... | collective-permute-start | bytes 1572872 | tf_op jit(solution)/shard_map/s12/ring_tp/ppermute | solution.py:63
  (140 other events, 2117.5 us)

commit v3 on v2

--- a/solution.py
+++ b/solution.py
@@ -80,7 +80,14 @@
 
 
 def team_pieces(team, piece):
-    return [piece] + [team.shift(piece, offset) for offset in team.offsets[1:]]
+    far = team.shift(piece, (1, 0))
+    across_x = [(0, dx) for dx in range(1, team.sizes["x"])]
+    return (
+        [piece]
+        + [team.shift(piece, offset) for offset in across_x]
+        + [far]
+        + [team.shift(far, offset) for offset in across_x]
+    )
 
 
 def cores(team, value):
@@ -96,29 +103,25 @@
     ]
 
 
-def core_send(team, product, half_rows):
-    got = []
-    for step in range(1, team.sizes["tp"]):
-        sent = product(step * half_rows, half_rows).astype(LOWER)
-        got.append(team.ring(sent, "tp", -step))
-    return got
-
-
-def core_total(team, product, half_rows, got):
-    total = product(0, half_rows)
-    for value in got:
-        total = total + value.astype(WIDE)
-    row_count = half_rows // team.members
-    sent = [
-        total[j * row_count : (j + 1) * row_count].astype(LOWER) for j in range(1, team.members)
-    ]
-    return total[:row_count], sent
+def core_send(team, rows, pieces, half_rows, *others):
+    sent = [spread(rows, step, pieces, half_rows) for step in range(1, team.sizes["tp"])]
+    sent = fence(*sent, *others)[: len(sent)]
+    return [team.ring(value, "tp", -step) for step, value in enumerate(sent, 1)]
+
+
+def core_total(team, rows, pieces, half_rows, got):
+    total, *sent = spread(rows, 0, pieces, half_rows, got, team.members)
+    return total, sent
 
 
 def team_send(team, sent):
-    return [
-        team.shift(value, offset, back=True) for value, offset in zip(sent, team.offsets[1:])
-    ]
+    xs = team.sizes["x"]
+    across_x = [(0, dx) for dx in range(1, xs)]
+    far = sent[xs - 1].astype(WIDE)
+    for value, offset in zip(sent[xs:], across_x):
+        far = far + team.shift(value, offset, back=True).astype(WIDE)
+    got = [team.shift(value, offset, back=True) for value, offset in zip(sent, across_x)]
+    return got + [team.shift(far.astype(LOWER), (1, 0), back=True)]
 
 
 def team_total(own, got):
@@ -145,11 +148,46 @@
     return pieces
 
 
-def near_rows(team, pieces, first, width):
-    near = jnp.zeros((team.members, pieces[0].shape[0], width), LOWER)
-    for piece, offset in zip(pieces, team.offsets):
-        near = put(near, piece[None, :, first : first + width], (team.slot(offset), 0, 0))
-    return near.reshape(-1, width)
+def place_rows_kernel(widths, slots_ref, *refs):
+    pieces, outs = refs[: len(refs) - len(widths)], refs[len(refs) - len(widths) :]
+    for j, piece in enumerate(pieces):
+        height = piece.shape[0]
+        row = pl.multiple_of(slots_ref[j] * height, height)
+        first = 0
+        for out, width in zip(outs, widths):
+            out[pl.ds(row, height), :] = piece[:, first : first + width]
+            first += width
+
+
+def place_columns_kernel(widths, slots_ref, *refs):
+    pieces, outs = refs[: len(refs) - len(widths)], refs[len(refs) - len(widths) :]
+    for j, piece in enumerate(pieces):
+        first = 0
+        for out, width in zip(outs, widths):
+            column = pl.multiple_of(slots_ref[j] * width, width)
+            block = piece[:, first : first + width].astype(out.dtype)
+            out[:, pl.ds(column, width)] = block
+            first += width
+
+
+def place(team, kernel, pieces, widths, shapes):
+    slots = jnp.stack([team.slot(offset) for offset in team.offsets]).astype(jnp.int32)
+    whole = [pl.BlockSpec(piece.shape, lambda n: (0, 0)) for piece in pieces]
+    return pl.pallas_call(
+        functools.partial(kernel, widths),
+        grid=(1,),
+        in_specs=[pl.BlockSpec(memory_space=pltpu.SMEM)] + whole,
+        out_specs=[pl.BlockSpec(shape.shape, lambda n: (0, 0)) for shape in shapes],
+        out_shape=shapes,
+        cost_estimate=LIGHT,
+        compiler_params=KERNEL,
+    )(slots, *pieces)
+
+
+def near_rows(team, pieces, widths):
+    rows = pieces[0].shape[0] * team.members
+    shapes = [jax.ShapeDtypeStruct((rows, width), LOWER) for width in widths]
+    return place(team, place_rows_kernel, pieces, widths, shapes)
 
 
 def across(team, value):
@@ -170,20 +208,22 @@
 
 
 class Grads:
-    def __init__(self, team, product, rows, name):
-        self.team, self.product, self.name = team, product, name
-        self.far = rows // 2
+    def __init__(self, team, lefts, rights):
+        self.team, self.lefts, self.rights = team, lefts, rights
+        self.far = lefts[0].shape[1] // 2
         self.near = self.far // team.sizes["h"]
 
+    def rows(self, first, count, adds=(), dtype=LOWER):
+        return outer(self.lefts, self.rights, first, count, adds, dtype)
+
     def send_far(self):
-        return self.product(self.far + self.near, self.far - self.near).astype(LOWER)
+        return self.rows(self.far + self.near, self.far - self.near)
 
     def send_near(self):
-        return self.product(self.far, self.near).astype(LOWER)
+        return self.rows(self.far, self.near)
 
     def cross(self, got):
-        mine = self.product(self.near, self.far - self.near) + got.astype(WIDE)
-        mine = mine.astype(LOWER)
+        mine = self.rows(self.near, self.far - self.near, [got])
         return [
             mine[step * self.near : (step + 1) * self.near]
             for step in range(self.team.sizes["h"] - 1)
@@ -193,10 +233,7 @@
         return [self.team.ring(value, "h", step) for step, value in enumerate(sent, 1)]
 
     def total(self, got, crossed):
-        mine = self.product(0, self.near) + got.astype(WIDE)
-        for value in crossed:
-            mine = mine + value.astype(WIDE)
-        return mine
+        return self.rows(0, self.near, [got, *crossed])
 
 
 def home_pieces(team, total):
@@ -205,41 +242,55 @@
     pieces = []
     for j, offset in enumerate(team.offsets):
         piece = lax.dynamic_index_in_dim(total, team.slot(offset, back=False), 0, False)
-        pieces.append(team.shift(piece.astype(LOWER), offset) if j > 0 else piece)
+        pieces.append(team.shift(piece, offset) if j > 0 else piece)
     return pieces
 
 
 def home_join(team, pieces, widths):
-    slots = [team.slot(offset) for offset in team.offsets]
-    outs = []
-    first = 0
-    for each in widths:
-        blocks = []
-        for slot in range(team.members):
-            block = pieces[0][:, first : first + each]
-            for piece, at in zip(pieces[1:], slots[1:]):
-                other = piece[:, first : first + each].astype(WIDE)
-                block = jnp.where(at == slot, other, block)
-            blocks.append(block)
-        outs.append(jnp.concatenate(blocks, axis=1))
-        first += each
-    return outs
+    height = pieces[0].shape[0]
+    shapes = [jax.ShapeDtypeStruct((height, width * team.members), WIDE) for width in widths]
+    return place(team, place_columns_kernel, pieces, widths, shapes)
+
+
+def permute_kernel(count, table_ref, value_ref, out_ref):
+    block = value_ref.shape[1] // count
+    for i in range(count):
+        column = pl.multiple_of(table_ref[i] * block, block)
+        out_ref[:, i * block : (i + 1) * block] = value_ref[:, pl.ds(column, block)]
+
+
+def permute_columns(value, table):
+    whole = pl.BlockSpec(value.shape, lambda n: (0, 0))
+    return pl.pallas_call(
+        functools.partial(permute_kernel, len(table)),
+        grid=(1,),
+        in_specs=[pl.BlockSpec(memory_space=pltpu.SMEM), whole],
+        out_specs=whole,
+        out_shape=jax.ShapeDtypeStruct(value.shape, value.dtype),
+        cost_estimate=LIGHT,
+    )(jnp.stack(table).astype(jnp.int32), value)
 
 
 def to_team_order(team, value):
     hs = team.sizes["h"]
-    count = value.shape[0]
-    value = value.reshape(count, hs, 2, 2, -1).transpose(0, 3, 1, 2, 4)
-    value = jnp.roll(value, (-team.at["y"], -team.at["h"]), (1, 2))
-    return value.reshape(count, -1)
+    table = []
+    for dy in range(2):
+        for dh in range(hs):
+            for l in range(2):
+                h, y = lax.rem(team.at["h"] + dh, hs), lax.rem(team.at["y"] + dy, 2)
+                table.append((h * 2 + l) * 2 + y)
+    return permute_columns(value, table)
 
 
 def from_team_order(team, value):
     hs = team.sizes["h"]
-    count = value.shape[0]
-    value = value.reshape(count, 2, hs, 2, -1)
-    value = jnp.roll(value, (team.at["y"], team.at["h"]), (1, 2))
-    return value.transpose(0, 2, 3, 1, 4).reshape(count, -1)
+    table = []
+    for h in range(hs):
+        for l in range(2):
+            for y in range(2):
+                dh, dy = lax.rem(h - team.at["h"] + hs, hs), lax.rem(y - team.at["y"] + 2, 2)
+                table.append((dy * hs + dh) * 2 + l)
+    return permute_columns(value, table)
 
 
 def pick(table, index):
@@ -258,29 +309,55 @@
     return [piece] + [team.ring(piece, "h", step) for step in range(1, team.sizes["h"])]
 
 
-def deal(team, table, pieces, inward):
-    hs = team.sizes["h"]
-    place = team.at["l"] if inward else team.at["y"]
+def deal_flips(team, piece):
     got = []
     for flip in range(2):
-        source = pick(table, team.at["h"] * 2 + (place if flip == 0 else 1 - place))
-        sent = choose(pieces, lax.rem(team.at["h"] - source // 2 + hs, hs))
         perm = []
         for l in range(2):
             for y in range(2):
-                if inward:
-                    perm.append((l * 2 + y, y * 2 + (l if flip == 0 else 1 - l)))
-                else:
-                    perm.append((l * 2 + y, (y if flip == 0 else 1 - y) * 2 + l))
+                perm.append((l * 2 + y, y * 2 + (l if flip == 0 else 1 - l)))
+        with jax.named_scope("flip"):
+            got.append(lax.ppermute(piece, ("l", "y"), perm))
+    return got
+
+
+def deal_across(team, home, two):
+    hs = team.sizes["h"]
+
+    def needed(h):
+        group = pick(home, h * 2 + team.at["y"])
+        return jnp.where(lax.rem(group, 2) == team.at["y"], two[0], two[1])
+
+    return [needed(team.at["h"])] + [
+        team.ring(needed(lax.rem(team.at["h"] + step, hs)), "h", step) for step in range(1, hs)
+    ]
+
+
+def dealt_in(team, home, pieces):
+    hs = team.sizes["h"]
+    group = pick(home, team.at["h"] * 2 + team.at["y"])
+    return choose(pieces, lax.rem(team.at["h"] - group // 2 + hs, hs))
+
+
+def deal(team, dealing, pieces):
+    hs = team.sizes["h"]
+    got = []
+    for flip in range(2):
+        target = team.at["y"] if flip == 0 else 1 - team.at["y"]
+        seq = pick(dealing, team.at["h"] * 2 + target)
+        sent = choose(pieces, lax.rem(team.at["h"] - seq // 2 + hs, hs))
+        perm = []
+        for l in range(2):
+            for y in range(2):
+                perm.append((l * 2 + y, (y if flip == 0 else 1 - y) * 2 + l))
         with jax.named_scope("flip"):
             got.append(lax.ppermute(sent, ("l", "y"), perm))
     return got
 
 
-def pick_dealt(team, table, got, inward):
-    place = team.at["y"] if inward else team.at["l"]
-    source = pick(table, team.at["h"] * 2 + place)
-    return jnp.where(lax.rem(source, 2) == place, got[0], got[1])
+def dealt_out(team, dealing, got):
+    seq = pick(dealing, team.at["h"] * 2 + team.at["l"])
+    return jnp.where(lax.rem(seq, 2) == team.at["l"], got[0], got[1])
 
 
 def join_cores(team, piece):
@@ -381,7 +458,154 @@
 
 
 LIGHT = pl.CostEstimate(flops=1000000, bytes_accessed=100000, transcendentals=0)
-KERNEL = pltpu.CompilerParams(vmem_limit_bytes=24 * 1024 * 1024)
+KERNEL = pltpu.CompilerParams(vmem_limit_bytes=32 * 1024 * 1024)
+
+
+def gelu_slope(value):
+    inner = math.sqrt(2.0 / math.pi)
+    square = value * value
+    tanh = jnp.tanh(inner * value * (1.0 + 0.044715 * square))
+    return 0.5 * (1.0 + tanh) + 0.5 * value * (1.0 - tanh * tanh) * inner * (
+        1.0 + 3.0 * 0.044715 * square
+    )
+
+
+def project_kernel(mode, part_count, piece_count, steps, *refs):
+    parts, pieces = refs[:part_count], refs[part_count : part_count + piece_count]
+    rest = refs[part_count + piece_count :]
+    index = pl.program_id(0)
+
+    def run(rows):
+        total = None
+        first = 0
+        for piece in pieces:
+            depth = piece.shape[0]
+            term = mm(rows[:, first : first + depth], piece[...])
+            total = term if total is None else total + term
+            first += depth
+        if mode == "bias":
+            rest[1][...] = (total + rest[0][...]).astype(LOWER)
+        elif mode == "gelu":
+            total = total + rest[0][...]
+            rest[1][...] = total
+            rest[2][...] = gelu_tanh(total).astype(LOWER)
+        elif mode == "slope":
+            rest[1][...] = (total * gelu_slope(rest[0][...])).astype(LOWER)
+        else:
+            rest[0][...] = total.astype(LOWER)
+
+    for place in range(part_count):
+
+        @pl.when(index // steps == place)
+        def _():
+            run(parts[place][...])
+
+
+def project(mode, parts, pieces, width, extra=None):
+    half_rows, depth = parts[0].shape
+    block = min(256, half_rows)
+    steps = half_rows // block
+    rows = half_rows * len(parts)
+
+    def part_at(place):
+        return lambda i: (jnp.clip(i - place * steps, 0, steps - 1), 0)
+
+    in_specs = [pl.BlockSpec((block, depth), part_at(place)) for place in range(len(parts))]
+    for array, column in pieces:
+        in_specs.append(
+            pl.BlockSpec((array.shape[0], width), functools.partial(lambda c, i: (0, c), column))
+        )
+    arrays = list(parts) + [array for array, _ in pieces]
+    tile = pl.BlockSpec((block, width), lambda i: (i, 0))
+    if mode in ("bias", "gelu"):
+        in_specs.append(pl.BlockSpec((1, width), lambda i: (0, 0)))
+        arrays.append(extra[None])
+    elif mode == "slope":
+        in_specs.append(tile)
+        arrays.append(extra)
+    shapes = [jax.ShapeDtypeStruct((rows, width), LOWER)]
+    if mode == "gelu":
+        shapes = [jax.ShapeDtypeStruct((rows, width), WIDE)] + shapes
+    return pl.pallas_call(
+        functools.partial(project_kernel, mode, len(parts), len(pieces), steps),
+        grid=(len(parts) * steps,),
+        in_specs=in_specs,
+        out_specs=[tile] * len(shapes),
+        out_shape=shapes,
+        cost_estimate=LIGHT,
+        compiler_params=KERNEL,
+    )(*arrays)
+
+
+def spread_kernel(piece_count, got_count, members, rows_ref, *refs):
+    pieces, gots = refs[:piece_count], refs[piece_count : piece_count + got_count]
+    outs = refs[piece_count + got_count :]
+    rows = rows_ref[...]
+    height = rows.shape[0] // members
+    first = 0
+    for piece in pieces:
+        columns = slice(first, first + piece.shape[0])
+        total = mm_nt(rows, piece[...])
+        for got in gots:
+            total = total + got[:, columns].astype(WIDE)
+        for j, out in enumerate(outs):
+            out[:, columns] = total[j * height : (j + 1) * height].astype(out.dtype)
+        first += piece.shape[0]
+
+
+def spread(rows, place, pieces, half_rows, got=(), members=0):
+    if isinstance(rows, (list, tuple)):
+        rows, place = rows[place], 0
+    depth = rows.shape[1]
+    width = sum(array.shape[0] for array, _ in pieces)
+    in_specs = [pl.BlockSpec((half_rows, depth), lambda n: (place, 0))]
+    for array, column in pieces:
+        in_specs.append(
+            pl.BlockSpec((array.shape[0], depth), functools.partial(lambda c, n: (0, c), column))
+        )
+    in_specs += [pl.BlockSpec((half_rows, width), lambda n: (0, 0))] * len(got)
+    split = max(members, 1)
+    height = half_rows // split
+    dtypes = [WIDE] + [LOWER] * (members - 1) if members else [LOWER]
+    out = pl.pallas_call(
+        functools.partial(spread_kernel, len(pieces), len(got), split),
+        grid=(1,),
+        in_specs=in_specs,
+        out_specs=[pl.BlockSpec((height, width), lambda n: (0, 0))] * split,
+        out_shape=[jax.ShapeDtypeStruct((height, width), dtype) for dtype in dtypes],
+        cost_estimate=LIGHT,
+        compiler_params=KERNEL,
+    )(rows, *[array for array, _ in pieces], *got)
+    return out if members else out[0]
+
+
+def outer_kernel(part_count, add_count, *refs):
+    lefts, rights = refs[:part_count], refs[part_count : 2 * part_count]
+    adds, out = refs[2 * part_count : 2 * part_count + add_count], refs[-1]
+    total = None
+    for left, right in zip(lefts, rights):
+        term = mm_tn(left[...], right[...])
+        total = term if total is None else total + term
+    for add in adds:
+        total = total + add[...].astype(WIDE)
+    out[...] = total.astype(out.dtype)
+
+
+def outer(lefts, rights, first, count, adds=(), dtype=LOWER):
+    height, width = rights[0].shape
+    block = math.gcd(256, count)
+    in_specs = [pl.BlockSpec((height, block), lambda i: (0, first // block + i)) for _ in lefts]
+    in_specs += [pl.BlockSpec((height, width), lambda i: (0, 0)) for _ in rights]
+    tile = pl.BlockSpec((block, width), lambda i: (i, 0))
+    return pl.pallas_call(
+        functools.partial(outer_kernel, len(lefts), len(adds)),
+        grid=(count // block,),
+        in_specs=in_specs + [tile] * len(adds),
+        out_specs=tile,
+        out_shape=jax.ShapeDtypeStruct((count, width), dtype),
+        cost_estimate=LIGHT,
+        compiler_params=KERNEL,
+    )(*lefts, *rights, *adds)
 
 
 def query_block(rows):
@@ -479,6 +703,11 @@
     bias_up = lax.dynamic_slice_in_dim(b_up, my_slot * tall, tall, 0)
     bias_qkv = jnp.concatenate([bias_q, jnp.zeros_like(bias_q), bias_v])
     steps = team.sizes["h"] - 1
+    team_count = team.sizes["x"]
+
+
+    def first_column(arrays):
+        return [(array, 0) for array in arrays]
 
     with jax.named_scope("a0"):
         own = swap_home(lax.dynamic_slice_in_dim(tokens, half_at, row_count, 0))
@@ -486,110 +715,109 @@
         own, w_up, w_down, *share = fence(own, w_up, w_down, *share)
     with jax.named_scope("a1"):
         own = to_team_order(team, own)
-        near_qkv = near_rows(team, share, 0, 3 * wide)
-        near_out = near_rows(team, share, 3 * wide, wide)
+        (near_att,) = near_rows(team, share, [4 * wide])
         pieces = team_pieces(team, own)
-        cross_qkv = across(team, near_qkv)
-        side_qkv, side_out = beside(team, [near_qkv, near_out])
-        near_out, w_up, w_down, side_qkv, side_out, *rest = fence(
-            near_out, w_up, w_down, side_qkv, side_out, *pieces, *cross_qkv
+        cross_qkv = across(team, near_att[:, : 3 * wide])
+        (side_att,) = beside(team, [near_att])
+        near_att, w_up, w_down, cotangent, side_att, *rest = fence(
+            near_att, w_up, w_down, cotangent, side_att, *pieces, *cross_qkv
         )
         pieces, cross_qkv = rest[:members], rest[members:]
     with jax.named_scope("a2"):
         half = jnp.concatenate(pieces, axis=0)
         other = cores(team, half)
         far_qkv = beside(team, cross_qkv)
-        cross_out = across(team, near_out)
+        cross_out = across(team, near_att[:, 3 * wide :])
         share = share_columns(team, [w_up, w_down])
-        rest = fence(half, *other, *share, *far_qkv, *cross_out)
-        inputs = jnp.concatenate(rest[:ts], axis=0)
+        cotangent, *rest = fence(cotangent, half, *other, *share, *far_qkv, *cross_out)
+        in_parts = rest[:ts]
         share, rest = rest[ts : ts + members], rest[ts + members :]
         far_qkv, cross_out = rest[:steps], rest[steps:]
+    qkv_mat = first_column([near_att, *cross_qkv, side_att, *far_qkv])
     with jax.named_scope("c1"):
-        near_up = near_rows(team, share, 0, tall)
-        near_down = near_rows(team, share, tall, tall)
+        near_up, near_down = near_rows(team, share, [tall, tall])
         up_a, up_b = halves(near_up)
         cross_up_a = across(team, up_a)
         far_out = beside(team, cross_out)
-        (side_up,) = beside(team, [near_up])
-        qkv_mat = jnp.concatenate([near_qkv, *cross_qkv, side_qkv, *far_qkv], axis=0)
-        qkv = (mm(inputs, qkv_mat) + bias_qkv).astype(LOWER)
+        cot_two = deal_flips(team, lax.dynamic_slice_in_dim(cotangent, half_at, row_count, 0))
+        (qkv,) = project("bias", in_parts, qkv_mat, 3 * wide, bias_qkv)
         attended, log_sum = attend(qkv, limits, score_scale)
-        out_mat = jnp.concatenate([near_out, *cross_out, side_out, *far_out], axis=0)
-
-        def out_product(first, count):
-            return mm_nt(attended[first : first + count], out_mat)
-
-        got = core_send(team, out_product, half_rows)
-        total, sent = core_total(team, out_product, half_rows, got)
-        up_b, near_down, side_up, *rest = fence(up_b, near_down, side_up, *cross_up_a, *sent)
-        cross_up_a, sent = rest[:steps], rest[steps:]
+        out_mat = [(near_att, 3), *first_column(cross_out), (side_att, 3), *first_column(far_out)]
+        got = core_send(team, attended, out_mat, half_rows, *cross_up_a, *cot_two)
+        total, sent = core_total(team, attended, out_mat, half_rows, got)
+        up_b, near_up, near_down, *rest = fence(
+            up_b, near_up, near_down, *cross_up_a, *sent, *cot_two
+        )
+        cross_up_a, rest = rest[:steps], rest[steps:]
+        sent, cot_two = rest[: members - 1], rest[members - 1 :]
     with jax.named_scope("s3"):
         got = team_send(team, sent)
         cross_up_b = across(team, up_b)
-        far_up_a = beside(team, cross_up_a)
-        near_down, *rest = fence(near_down, *got, *cross_up_b, *far_up_a)
-        got, rest = rest[: members - 1], rest[members - 1 :]
-        cross_up_b, far_up_a = rest[:steps], rest[steps:]
+        side = beside(team, [jnp.concatenate([near_up, *cross_up_a], axis=0)])
+        near_down, *rest = fence(near_down, *got, *cross_up_b, *side)
+        got, rest = rest[:team_count], rest[team_count:]
+        cross_up_b, side_a = rest[:steps], rest[steps]
     with jax.named_scope("s4"):
         branch = team_total(total, got) + b_out
         middle, mid_hat, mid_rate = layer_norm(own.astype(WIDE) + branch, gain_mid, shift_mid)
         pieces = team_pieces(team, middle.astype(LOWER))
         down_a, down_b = halves(near_down)
         cross_down_a = across(team, down_a)
-        far_up_b = beside(team, cross_up_b)
-        near_down, down_b, *rest = fence(near_down, down_b, *pieces, *cross_down_a, *far_up_b)
+        side = beside(team, [jnp.concatenate([near_down, *cross_up_b], axis=0)])
+        near_down, down_b, *rest = fence(near_down, down_b, *pieces, *cross_down_a, *side)
         pieces, rest = rest[:members], rest[members:]
-        cross_down_a, far_up_b = rest[:steps], rest[steps:]
+        cross_down_a, side_b = rest[:steps], rest[steps]
+    near_count = near_down.shape[0]
+    side_up, side_down = side_a[:near_count], side_b[:near_count]
+    far_up_a, far_up_b = (
+        [
+            side[near_count + k * near_count // 2 : near_count + (k + 1) * near_count // 2]
+            for k in range(steps)
+        ]
+        for side in (side_a, side_b)
+    )
+    up_mat = first_column(
+        [near_up]
+        + pairs(cross_up_a, cross_up_b)
+        + [side_up]
+        + pairs(far_up_a, far_up_b)
+    )
     with jax.named_scope("c2"):
         half = jnp.concatenate(pieces, axis=0)
         other = cores(team, half)
         cross_down_b = across(team, down_b)
-        (side_down,) = beside(team, [near_down])
         far_down_a = beside(team, cross_down_a)
-        middle_all = jnp.concatenate([half] + other, axis=0)
-        up_mat = jnp.concatenate(
-            [near_up]
-            + pairs(cross_up_a, cross_up_b)
-            + [side_up]
-            + pairs(far_up_a, far_up_b),
-            axis=0,
-        )
-        hidden = mm(middle_all, up_mat) + bias_up
-        active = gelu_tanh(hidden).astype(LOWER)
-        active, hidden, side_down, cotangent, *rest = fence(
-            active, hidden, side_down, cotangent, *cross_down_b, *far_down_a
-        )
-        cross_down_b, far_down_a = rest[:steps], rest[steps:]
+        mid_parts = [half] + other
+        hidden, active = [], []
+        for part in mid_parts:
+            hidden_part, active_part = project("gelu", [part], up_mat, tall, bias_up)
+            hidden.append(hidden_part)
+            active.append(active_part)
+        rest = fence(*active, *cross_down_b, *far_down_a, *cot_two)
+        active, rest = rest[:ts], rest[ts:]
+        cross_down_b, rest = rest[:steps], rest[steps:]
+        far_down_a, cot_two = rest[:steps], rest[steps:]
     with jax.named_scope("s5"):
-        cot_pieces = spread_h(team, lax.dynamic_slice_in_dim(cotangent, half_at, row_count, 0))
         far_down_b = beside(team, cross_down_b)
-        down_mat = jnp.concatenate(
+        cot_pieces = deal_across(team, home, cot_two)
+        down_mat = first_column(
             [near_down]
             + pairs(cross_down_a, cross_down_b)
             + [side_down]
-            + pairs(far_down_a, far_down_b),
-            axis=0,
-        )
-
-        def down_product(first, count):
-            return mm_nt(active[first : first + count], down_mat)
-
-        got = core_send(team, down_product, half_rows)
-        total, sent = core_total(team, down_product, half_rows, got)
+            + pairs(far_down_a, far_down_b)
+        )
+        got = core_send(team, active, down_mat, half_rows, *cot_pieces)
+        total, sent = core_total(team, active, down_mat, half_rows, got)
         rest = fence(*sent, *cot_pieces)
         sent, cot_pieces = rest[: members - 1], rest[members - 1 :]
     with jax.named_scope("s6"):
-        got = team_send(team, sent)
-        cot_two = deal(team, home, cot_pieces, True)
-        rest = fence(*got, *cot_two)
-        got, cot_two = rest[: members - 1], rest[members - 1 :]
+        cot = to_team_order(team, dealt_in(team, home, cot_pieces))
+        cot, *got = fence(cot, *team_send(team, sent))
     with jax.named_scope("s7"):
         result = team_total(total, got) + b_down
         normed, end_hat, end_rate = layer_norm(middle + result, gain_end, shift_end)
         output_own = jnp.where(query_live, normed, 0.0).astype(LOWER)
-        cot = to_team_order(team, pick_dealt(team, home, cot_two, True)).astype(WIDE)
-        grad_normed = jnp.where(query_live, cot, 0.0)
+        grad_normed = jnp.where(query_live, cot.astype(WIDE), 0.0)
         grad_sum = layer_norm_back(grad_normed, gain_end, end_hat, end_rate)
         grad_result = grad_sum.astype(LOWER)
         pieces = team_pieces(team, grad_result)
@@ -602,33 +830,27 @@
     with jax.named_scope("c3"):
         half = jnp.concatenate(pieces, axis=0)
         other = cores(team, half)
-        result_all = jnp.concatenate([half] + other, axis=0)
-        flow_down = Grads(
-            team, lambda f, n: mm_tn(result_all[:, f : f + n], active), width, "down"
-        )
+        result_parts = [half] + other
+        flow_down = Grads(team, result_parts, active)
         (far_down,) = beside(team, [flow_down.send_far()])
-        grad_active = mm(result_all, down_mat)
-        gelu_back = jax.vjp(gelu_tanh, hidden)[1]
-        grad_hidden = gelu_back(grad_active)[0].astype(LOWER)
-
-        def up_product(first, count):
-            return mm_nt(grad_hidden[first : first + count], up_mat)
-
-        got = core_send(team, up_product, half_rows)
-        total, sent = core_total(team, up_product, half_rows, got)
+        out_two = deal(team, dealing, out_pieces)
+        grad_hidden = []
+        for part, hidden_part in zip(result_parts, hidden):
+            grad_hidden += project("slope", [part], down_mat, tall, hidden_part)
+        got = core_send(team, grad_hidden, up_mat, half_rows, far_down, *grad_hidden, *out_two)
+        total, sent = core_total(team, grad_hidden, up_mat, half_rows, got)
         cross_down = flow_down.cross(far_down)
-        flow_up = Grads(
-            team, lambda f, n: mm_tn(middle_all[:, f : f + n], grad_hidden), width, "up"
-        )
-        rest = fence(*sent, *cross_down)
-        sent, cross_down = rest[: members - 1], rest[members - 1 :]
+        flow_up = Grads(team, mid_parts, grad_hidden)
+        rest = fence(*sent, *cross_down, *out_two)
+        sent, rest = rest[: members - 1], rest[members - 1 :]
+        cross_down, out_two = rest[:steps], rest[steps:]
     with jax.named_scope("s8"):
         got = team_send(team, sent)
         down_halves = [halves(value) for value in cross_down]
         got_down_a = flow_down.go([a for a, b in down_halves])
         (far_up,) = beside(team, [flow_up.send_far()])
         far_up, *rest = fence(far_up, *got, *got_down_a, *[b for a, b in down_halves])
-        got, rest = rest[: members - 1], rest[members - 1 :]
+        got, rest = rest[:team_count], rest[team_count:]
         got_down_a, down_b = rest[:steps], rest[steps:]
     with jax.named_scope("s9"):
         grad_middle = team_total(total, got) + grad_sum
@@ -650,35 +872,24 @@
         up_halves = [halves(value) for value in cross_up]
         got_up_a = flow_up.go([a for a, b in up_halves])
         (near_up,) = beside(team, [flow_up.send_near()])
-        branch_all = jnp.concatenate([half] + other, axis=0)
-        flow_out = Grads(
-            team, lambda f, n: mm_tn(branch_all[:, f : f + n], attended), width, "out"
-        )
+        branch_parts = [half] + other
+        attended_parts = [attended[k * half_rows : (k + 1) * half_rows] for k in range(ts)]
+        flow_out = Grads(team, branch_parts, attended_parts)
         (far_out,) = beside(team, [flow_out.send_far()])
-        grad_attended = mm(branch_all, out_mat).astype(LOWER)
+        (grad_attended,) = project("plain", branch_parts, out_mat, wide)
         grad_qkv = attend_back(qkv, grad_attended, log_sum, limits, score_scale)
-
-        def in_product(first, count):
-            return mm_nt(grad_qkv[first : first + count], qkv_mat)
-
-        got = core_send(team, in_product, half_rows)
-        total, sent = core_total(team, in_product, half_rows, got)
-        flow_qkv = Grads(
-            team, lambda f, n: mm_tn(inputs[:, f : f + n], grad_qkv), width, "qkv"
-        )
-        cross_out = flow_out.cross(far_out)
-        near_up, *rest = fence(
-            near_up, *sent, *got_up_a, *[b for a, b in up_halves], *cross_out
+        got = core_send(team, grad_qkv, qkv_mat, half_rows, near_up, *got_up_a)
+        total, sent = core_total(team, grad_qkv, qkv_mat, half_rows, got)
+        grad_parts = [grad_qkv[k * half_rows : (k + 1) * half_rows] for k in range(ts)]
+        flow_qkv = Grads(team, in_parts, grad_parts)
+        near_up, far_out, near_down, *rest = fence(
+            near_up, far_out, near_down, *sent, *got_up_a, *[b for a, b in up_halves]
         )
         sent, rest = rest[: members - 1], rest[members - 1 :]
-        got_up_a, up_b, cross_out = rest[:steps], rest[steps : 2 * steps], rest[2 * steps :]
-        total_down = flow_down.total(
-            near_down,
-            [jnp.concatenate(both, axis=0) for both in zip(got_down_a, got_down_b)],
-        )
+        got_up_a, up_b = rest[:steps], rest[steps:]
 
     qkv_sum = jnp.sum(grad_qkv.astype(WIDE), axis=0)
-    grad_bup = jnp.sum(grad_hidden.astype(WIDE), axis=0)
+    grad_bup = sum(jnp.sum(part.astype(WIDE), axis=0) for part in grad_hidden)
     zeros = jnp.zeros((members, 1), WIDE)
     by_slot = [
         put(zeros * part[None], part[None], (my_slot, 0)).reshape(-1)
@@ -694,46 +905,63 @@
 
     with jax.named_scope("s10"):
         got = team_send(team, sent)
+        total_down = flow_down.total(
+            near_down,
+            [jnp.concatenate(both, axis=0) for both in zip(got_down_a, got_down_b)],
+        )
         got_up_b = flow_up.go(up_b)
         (far_qkv,) = beside(team, [flow_qkv.send_far()])
-        cross_qkv = flow_qkv.cross(far_qkv)
+        cross_qkv, cross_out = flow_qkv.cross(far_qkv), flow_out.cross(far_out)
         both = add_ring(sums[:by_row_rows], "tp")
         sums = jnp.concatenate([both, sums[by_row_rows:]], axis=0)
+        cross_att = [
+            jnp.concatenate(blocks, axis=1) for blocks in zip(cross_qkv, cross_out)
+        ]
         sums, total_down, near_up, *rest = fence(
-            sums, total_down, near_up, *got, *got_up_b, *cross_qkv, *cross_out
-        )
-        got, rest = rest[: members - 1], rest[members - 1 :]
-        got_up_b, cross_qkv, cross_out = rest[:steps], rest[steps : 2 * steps], rest[2 * steps :]
+            sums, total_down, near_up, *got, *got_up_b, *cross_att
+        )
+        got, rest = rest[:team_count], rest[team_count:]
+        got_up_b, cross_att = rest[:steps], rest[steps:]
     with jax.named_scope("s11"):
-        got_qkv = flow_qkv.go(cross_qkv)
-        got_out = flow_out.go(cross_out)
+        att_halves = [halves(value) for value in cross_att]
+        got_att_a = flow_qkv.go([a for a, b in att_halves])
         grad_own = (team_total(total, got) + grad_inner).astype(LOWER)
         swapped = swap_home(from_team_order(team, grad_own))
-        sums = add_ring(sums, "y")
-        near_qkv, near_out = beside(team, [flow_qkv.send_near(), flow_out.send_near()])
         home_down = home_pieces(team, total_down)
         total_up = flow_up.total(
             near_up, [jnp.concatenate(both, axis=0) for both in zip(got_up_a, got_up_b)]
         )
-        rest = fence(sums, swapped, near_qkv, near_out, total_up, *home_down)
-        sums, swapped, near_qkv, near_out, total_up = rest[:5]
-        home_down = rest[5:]
+        near_att = jnp.concatenate([flow_qkv.send_near(), flow_out.send_near()], axis=1)
+        (near_att,) = beside(team, [near_att])
+        sums, swapped, near_att, total_up, *rest = fence(
+            sums, swapped, near_att, total_up, *out_two,
+            *home_down, *got_att_a, *[b for a, b in att_halves]
+        )
+        out_two, rest = rest[:2], rest[2:]
+        home_down, rest = rest[:members], rest[members:]
+        got_att_a, att_b = rest[:steps], rest[steps:]
         (grad_down,) = home_join(team, home_down, [tall])
     with jax.named_scope("s12"):
+        got_att_b = flow_qkv.go(att_b)
         home_up = home_pieces(team, total_up)
-        out_two = deal(team, dealing, out_pieces, False)
+        sums = add_ring(sums, "y")
         grad_tokens = join_cores(team, swapped)
-        sums = add_ring(sums, "h")
-        total_qkv = flow_qkv.total(near_qkv, got_qkv)
-        total_out = flow_out.total(near_out, got_out)
-        rest = fence(sums, grad_tokens, total_qkv, total_out, *home_up, *out_two)
-        sums, grad_tokens, total_qkv, total_out = rest[:4]
-        home_up, out_two = rest[4 : 4 + members], rest[4 + members :]
+        output = join_cores(team, dealt_out(team, dealing, out_two))
+        got_att = [jnp.concatenate(both, axis=0) for both in zip(got_att_a, got_att_b)]
+        total_qkv = flow_qkv.total(
+            near_att[:, : 3 * wide], [value[:, : 3 * wide] for value in got_att]
+        )
+        total_out = flow_out.total(
+            near_att[:, 3 * wide :], [value[:, 3 * wide :] for value in got_att]
+        )
+        total_att = jnp.concatenate([total_qkv, total_out], axis=1)
+        sums, grad_tokens, output, total_att, *home_up = fence(
+            sums, grad_tokens, output, total_att, *home_up
+        )
         (grad_up,) = home_join(team, home_up, [tall])
     with jax.named_scope("s13"):
-        home_att = home_pieces(team, jnp.concatenate([total_qkv, total_out], axis=1))
-        output = join_cores(team, pick_dealt(team, dealing, out_two, False))
-        sums = add_ring(add_ring(sums, "l"), "x").reshape(-1)
+        home_att = home_pieces(team, total_att)
+        sums = add_ring(add_ring(add_ring(sums, "h"), "l"), "x").reshape(-1)
         grad_query, grad_key, grad_value, grad_out = home_join(team, home_att, [wide] * 4)
     smalls = []
     first = 0

time: 810 us -> 708 us (0.87)
  Pallas kernels: 20.7 us -> 131 us
  matrix products: 94.1 us -> 0 us
  waiting for transfers between devices: 450 us -> 370 us
  other arithmetic: 51.3 us -> 31.9 us
  starting transfers between devices: 94.7 us -> 82.4 us
    pallas_call x0 -> x41, Pallas kernels: none -> 111 us  [the longest x16 38.3 us: outer(): pl.pallas_call(functools.partial(outer_kernel, len(lefts), len(adds)), gr...]
    dot_general x28 -> x0, matrix products: 94.1 us -> none  [dot(): lax.dot_general(left, right, (dims, ((), ())), preferred_element_type=WIDE)]
    ppermute x47 -> x43, waiting for transfers between devices: 166 us -> 129 us  [ring(): lax.ppermute(value, name, [(i, (i + step) % size) for i in range(size)])]
    ppermute x39, waiting for transfers between devices: 264 us -> 229 us  [shift_(): return lax.ppermute(value, TEAM, perm)]
    unnamed x206 -> x254, local copies, waits for them, and re-layouts: 21.7 us -> 41.2 us
    ppermute x39, starting transfers between devices: 49.6 us -> 35.2 us  [shift_(): return lax.ppermute(value, TEAM, perm)]
    concatenate x20 -> x7, other arithmetic: 19.4 us -> 6.19 us  [the longest x2 2.46 us: local(): jnp.concatenate(both, axis=0)]
    ppermute x4 -> x2, waiting for transfers between devices: 20.5 us -> 7.5 us  [deal(): got.append(lax.ppermute(sent, ('l', 'y'), perm))]
  transfers between devices with their start and end apart: 92 -> 88, of which waited for: 49 -> 50; matrix products, arithmetic and copies ran while one was open for 20% -> 7% of each run, Pallas kernels for 3% -> 16%
where the time goes in v3:
time: 708 us; the launch traced here: 703 us
  waiting for transfers between devices  370 us (52%)
  Pallas kernels  131 us (19%)
  starting transfers between devices  82.4 us (12%)
  local copies, waits for them, and re-layouts  71.9 us (10%)
  other arithmetic  31.9 us (5%)
  between operations  14.7 us (2%)
    ppermute x39, waiting for transfers between devices, shift_(): return lax.ppermute(value, TEAM, perm)  229 us
    ppermute x43, waiting for transfers between devices, ring(): lax.ppermute(value, name, [(i, (i + step) % size) for i in range(size)])  129 us
    unnamed x254, local copies, waits for them, and re-layouts  41.2 us
    pallas_call x16, Pallas kernels, outer(): pl.pallas_call(functools.partial(outer_kernel, len(lefts), len(adds)), gr...  38.3 us
    ppermute x39, starting transfers between devices, shift_(): return lax.ppermute(value, TEAM, perm)  35.2 us
    ppermute x43, starting transfers between devices, ring(): lax.ppermute(value, name, [(i, (i + step) % size) for i in range(size)])  31.7 us
    pallas_call x6, Pallas kernels, project(): pl.pallas_call(functools.partial(project_kernel, mode, len(parts), len(pi...  29.4 us
    pallas_call x8, Pallas kernels, spread(): pl.pallas_call(functools.partial(spread_kernel, len(pieces), len(got), sp...  24.7 us
  transfers between devices with their start and end apart: 88, of which 50 were waited for; matrix products, arithmetic and copies ran while one was open for 7% of the time, Pallas kernels for 16%

profile of v3, /device:TPU:0, one launch (start us, length us, event | category | flops | bytes accessed | tf_op | source)
XLA Modules:
  0.0 702.6 jit_solution(3561024558293231171)
XLA Ops:
  13.2 13.4 %collective-permute-done.2.refs_2_ = bf16[128,1024]{1,0:T(8,128)(2,1)S(1)} collective-permute-done((bf16[128,1024]{1,0:T(8,128)(2,1)S(1)}, bf16[128,1024]{1,0:T(8,128)(2,1)S(1)}, u32[]{:S(2)}, u32[]{:S(2)}) %collective-permute-start.2) | collective-permute-done | bytes 262176 | tf_op jit(solution)/shard_map/a0/team10/ppermute | solution.py:58
  40.0 18.8 %collective-permute-done.6 = bf16[128,2048]{1,0:T(8,128)(2,1)S(1)} collective-permute-done((bf16[128,2048]{1,0:T(8,128)(2,1)}, bf16[128,2048]{1,0:T(8,128)(2,1)S(1)}, u32[]{:S(2)}, u32[]{:S(2)}) %collective-permute-start.6) | collective-permute-done | bytes 524320 | tf_op jit(solution)/shard_map/a1/team10/ppermute | solution.py:58
  59.4 13.2 %collective-permute-done.8.refs_3_.refs_1_ = bf16[512,768]{1,0:T(8,128)(2,1)S(1)} collective-permute-done((bf16[512,768]{1,0:T(8,128)(2,1)S(1)}, bf16[512,768]{1,0:T(8,128)(2,1)S(1)}, u32[]{:S(2)}, u32[]{:S(2)}) %collective-permute-start.8) | collective-permute-done | bytes 786464 | tf_op jit(solution)/shard_map/a1/ring_h/ppermute | solution.py:63
  85.3 11.5 %collective-permute-done.14.refs_1_.refs_3_ = bf16[512,256]{1,0:T(8,128)(2,1)} collective-permute-done((bf16[512,256]{1,0:T(8,128)(2,1)S(1)}, bf16[512,256]{1,0:T(8,128)(2,1)}, u32[]{:S(2)}, u32[]{:S(2)}) %collective-permute-start.14) | collective-permute-done | bytes 262176 | tf_op jit(solution)/shard_map/a2/ring_h/ppermute | solution.py:63
  96.9 6.6 collective-permute-done.11.refs_2_
  103.6 11.2 %collective-permute-done.12.refs_3_ = bf16[128,2048]{1,0:T(8,128)(2,1)S(1)} collective-permute-done((bf16[128,2048]{1,0:T(8,128)(2,1)S(1)}, bf16[128,2048]{1,0:T(8,128)(2,1)S(1)}, u32[]{:S(2)}, u32[]{:S(2)}) %collective-permute-start.12) | collective-permute-done | bytes 524320 | tf_op jit(solution)/shard_map/a2/team11/ppermute | solution.py:58
  134.7 5.9 c1.5.query_ref.key_ref.value_ref
  140.5 9.8 %c1.6 = (bf16[1024,256]{1,0:T(8,128)(2,1)S(1)}, f32[2,1,1024]{2,1,0:T(1,128)S(1)}) custom-call(s32[8]{0:T(128)S(1)} %multiply_subtract_fusion.limits_ref, bf16[1024,768]{1,0:T(8,128)(2,1)S(1)} %c1.5.query_ref.key_ref.value_ref, bf16[1024,768]{1,0:T(8,128)(2,1)S(1)} %c1.5.query_ref.key_ref.value_ref, bf16[1024,768]{1,0:T(8,128)(2,1)S(1)} %c1.5.query_ref.key_ref.value_ref), custom_call_target="tpu_custom_call" | custom-call | flops 1000000 | bytes 100000 | tf_op jit(solution)/shard_map/c1/pallas_call | solution.py:618
  170.6 9.9 %collective-permute-done.21 = bf16[128,2048]{1,0:T(8,128)(2,1)S(1)} collective-permute-done((bf16[128,2048]{1,0:T(8,128)(2,1)S(1)}, bf16[128,2048]{1,0:T(8,128)(2,1)S(1)}, u32[]{:S(2)}, u32[]{:S(2)}) %collective-permute-start.21) | collective-permute-done | bytes 524320 | tf_op jit(solution)/shard_map/s3/team01/ppermute | solution.py:58
  185.1 6.0 collective-permute-done.20
  193.7 11.2 %collective-permute-done.22 = bf16[128,2048]{1,0:T(8,128)(2,1)} collective-permute-done((bf16[128,2048]{1,0:T(8,128)(2,1)}, bf16[128,2048]{1,0:T(8,128)(2,1)}, u32[]{:S(2)}, u32[]{:S(2)}) %collective-permute-start.22) | collective-permute-done | bytes 524320 | tf_op jit(solution)/shard_map/s3/team10/ppermute | solution.py:58
  212.8 18.9 %collective-permute-done.26 = bf16[128,2048]{1,0:T(8,128)(2,1)S(1)} collective-permute-done((bf16[128,2048]{1,0:T(8,128)(2,1)S(1)}, bf16[128,2048]{1,0:T(8,128)(2,1)S(1)}, u32[]{:S(2)}, u32[]{:S(2)}) %collective-permute-start.26) | collective-permute-done | bytes 524320 | tf_op jit(solution)/shard_map/s4/team10/ppermute | solution.py:58
  236.3 8.1 %collective-permute-done.27 = bf16[128,2048]{1,0:T(8,128)(2,1)S(1)} collective-permute-done((bf16[128,2048]{1,0:T(8,128)(2,1)S(1)}, bf16[128,2048]{1,0:T(8,128)(2,1)S(1)}, u32[]{:S(2)}, u32[]{:S(2)}) %collective-permute-start.27) | collective-permute-done | bytes 524320 | tf_op jit(solution)/shard_map/s4/team01/ppermute | solution.py:58
  276.5 11.8 %collective-permute-done.33.refs_5_.refs_6_ = bf16[256,1024]{1,0:T(8,128)(2,1)S(1)} collective-permute-done((bf16[256,1024]{1,0:T(8,128)(2,1)}, bf16[256,1024]{1,0:T(8,128)(2,1)S(1)}, u32[]{:S(2)}, u32[]{:S(2)}) %collective-permute-start.33) | collective-permute-done | bytes 524320 | tf_op jit(solution)/shard_map/s5/ring_y/ppermute | solution.py:63
  292.3 9.5 %collective-permute-done.34 = bf16[128,2048]{1,0:T(8,128)(2,1)S(1)} collective-permute-done((bf16[128,2048]{1,0:T(8,128)(2,1)S(1)}, bf16[128,2048]{1,0:T(8,128)(2,1)S(1)}, u32[]{:S(2)}, u32[]{:S(2)}) %collective-permute-start.34) | collective-permute-done | bytes 524320 | tf_op jit(solution)/shard_map/s5/ring_h/ppermute | solution.py:63
  313.4 12.7 %collective-permute-done.37 = bf16[128,2048]{1,0:T(8,128)(2,1)S(1)} collective-permute-done((bf16[128,2048]{1,0:T(8,128)(2,1)S(1)}, bf16[128,2048]{1,0:T(8,128)(2,1)S(1)}, u32[]{:S(2)}, u32[]{:S(2)}) %collective-permute-start.37) | collective-permute-done | bytes 524320 | tf_op jit(solution)/shard_map/s6/team01/ppermute | solution.py:58
  350.4 14.4 %collective-permute-done.40 = bf16[128,2048]{1,0:T(8,128)(2,1)} collective-permute-done((bf16[128,2048]{1,0:T(8,128)(2,1)}, bf16[128,2048]{1,0:T(8,128)(2,1)}, u32[]{:S(2)}, u32[]{:S(2)}) %collective-permute-start.40) | collective-permute-done | bytes 524320 | tf_op jit(solution)/shard_map/s7/team10/ppermute | solution.py:58
  364.8 7.1 %collective-permute-done.42 = bf16[128,2048]{1,0:T(8,128)(2,1)} collective-permute-done((bf16[128,2048]{1,0:T(8,128)(2,1)}, bf16[128,2048]{1,0:T(8,128)(2,1)}, u32[]{:S(2)}, u32[]{:S(2)}) %collective-permute-start.42) | collective-permute-done | bytes 524320 | tf_op jit(solution)/shard_map/s7/ring_h/ppermute | solution.py:63
  407.7 5.7 c3.6.rows_ref.refs_2_
  413.5 5.5 c3.7.rows_ref.refs_3_
  421.4 7.5 %collective-permute-done.46 = bf16[128,2048]{1,0:T(8,128)(2,1)S(1)} collective-permute-done((bf16[128,2048]{1,0:T(8,128)(2,1)S(1)}, bf16[128,2048]{1,0:T(8,128)(2,1)S(1)}, u32[]{:S(2)}, u32[]{:S(2)}) %collective-permute-start.46) | collective-permute-done | bytes 524320 | tf_op jit(solution)/shard_map/c3/flip/ppermute | solution.py:354
  442.1 9.0 %collective-permute-done.50 = bf16[128,2048]{1,0:T(8,128)(2,1)S(1)} collective-permute-done((bf16[128,2048]{1,0:T(8,128)(2,1)S(1)}, bf16[128,2048]{1,0:T(8,128)(2,1)S(1)}, u32[]{:S(2)}, u32[]{:S(2)}) %collective-permute-start.50) | collective-permute-done | bytes 524320 | tf_op jit(solution)/shard_map/s8/team01/ppermute | solution.py:58
  455.3 9.9 %collective-permute-done.48.refs_4_ = bf16[512,1024]{1,0:T(8,128)(2,1)S(1)} collective-permute-done((bf16[512,1024]{1,0:T(8,128)(2,1)S(1)}, bf16[512,1024]{1,0:T(8,128)(2,1)S(1)}, u32[]{:S(2)}, u32[]{:S(2)}) %collective-permute-start.48) | collective-permute-done | bytes 1048608 | tf_op jit(solution)/shard_map/s8/ring_y/ppermute | solution.py:63
  467.1 7.6 %collective-permute-done.51 = bf16[128,2048]{1,0:T(8,128)(2,1)S(1)} collective-permute-done((bf16[128,2048]{1,0:T(8,128)(2,1)S(1)}, bf16[128,2048]{1,0:T(8,128)(2,1)S(1)}, u32[]{:S(2)}, u32[]{:S(2)}) %collective-permute-start.51) | collective-permute-done | bytes 524320 | tf_op jit(solution)/shard_map/s8/team10/ppermute | solution.py:58
  479.4 19.3 %collective-permute-done.56 = bf16[128,2048]{1,0:T(8,128)(2,1)S(1)} collective-permute-done((bf16[128,2048]{1,0:T(8,128)(2,1)S(1)}, bf16[128,2048]{1,0:T(8,128)(2,1)S(1)}, u32[]{:S(2)}, u32[]{:S(2)}) %collective-permute-start.56) | collective-permute-done | bytes 524320 | tf_op jit(solution)/shard_map/s9/team10/ppermute | solution.py:58
  502.1 9.5 %collective-permute-done.57 = bf16[128,2048]{1,0:T(8,128)(2,1)S(1)} collective-permute-done((bf16[128,2048]{1,0:T(8,128)(2,1)S(1)}, bf16[128,2048]{1,0:T(8,128)(2,1)S(1)}, u32[]{:S(2)}, u32[]{:S(2)}) %collective-permute-start.57) | collective-permute-done | bytes 524320 | tf_op jit(solution)/shard_map/s9/team01/ppermute | solution.py:58
  521.6 10.8 %c4.7.rows_ref = bf16[1024,768]{1,0:T(8,128)(2,1)S(1)} custom-call(s32[8]{0:T(128)S(1)} %multiply_subtract_fusion.limits_ref, bf16[1024,768]{1,0:T(8,128)(2,1)S(1)} %c1.5.query_ref.key_ref.value_ref, bf16[1024,768]{1,0:T(8,128)(2,1)S(1)} %c1.5.query_ref.key_ref.value_ref, bf16[1024,768]{1,0:T(8,128)(2,1)S(1)} %c1.5.query_ref.key_ref.value_ref, ...), custom_call_target="tpu_custom_call" | custom-call | flops 1000000 | bytes 100000 | tf_op jit(solution)/shard_map/c4/pallas_call | solution.py:643
  569.4 6.2 collective-permute-done.65
  595.0 5.6 collective-permute-done.66
  624.9 14.5 %collective-permute-done.72.refs_2_ = bf16[128,1024]{1,0:T(8,128)(2,1)} collective-permute-done((bf16[128,1024]{1,0:T(8,128)(2,1)}, bf16[128,1024]{1,0:T(8,128)(2,1)}, u32[]{:S(2)}, u32[]{:S(2)}) %collective-permute-start.72) | collective-permute-done | bytes 262176 | tf_op jit(solution)/shard_map/s11/team10/ppermute | solution.py:58
  652.6 19.8 %collective-permute-done.78 = bf16[256,1024]{1,0:T(8,128)(2,1)S(1)} collective-permute-done((bf16[256,1024]{1,0:T(8,128)(2,1)S(1)}, bf16[256,1024]{1,0:T(8,128)(2,1)S(1)}, u32[]{:S(2)}, u32[]{:S(2)}) %collective-permute-start.78) | collective-permute-done | bytes 524320 | tf_op jit(solution)/shard_map/s12/ring_h/ppermute | solution.py:63
  676.3 5.6 collective-permute-done.85
  (559 shorter events, 351.4 us)
Async XLA Ops:
  1.9 30.1 %collective-permute-start = (bf16[128,2048]{1,0:T(8,128)(2,1)S(1)}, bf16[128,2048]{1,0:T(8,128)(2,1)S(1)}, u32[]{:S(2)}, u32[]{:S(2)}) collective-permute-start(bf16[128,2048]{1,0:T(8,128)(2,1)S(1)} %constant_dynamic-slice_fusion.25), channel_id=1, source_target_pairs={{0,0},{4,8},{8,4},{12,12},{1,1},{5,9},{9,5},{13,13},{2,2},{6,10},{... | collective-permute-start | bytes 1572872 | tf_op jit(solution)/shard_map/a0/ppermute | solution.py:79
  32.7 39.9 %collective-permute-start.4 = (bf16[512,1024]{1,0:T(8,128)(2,1)S(1)}, bf16[512,1024]{1,0:T(8,128)(2,1)S(1)}, u32[]{:S(2)}, u32[]{:S(2)}) collective-permute-start(bf16[512,1024]{1,0:T(8,128)(2,1)S(1)} %a1.3.refs_2_.refs_0_), channel_id=1, source_target_pairs={{0,4},{4,0},{1,5},{5,1},{2,6},{6,2},{3,7},{7,3},{8,12},{12,8},{9,1... | collective-permute-start | bytes 3145736 | tf_op jit(solution)/shard_map/a1/ring_y/ppermute | solution.py:63
  36.8 35.7 %collective-permute-start.8 = (bf16[512,768]{1,0:T(8,128)(2,1)S(1)}, bf16[512,768]{1,0:T(8,128)(2,1)S(1)}, u32[]{:S(2)}, u32[]{:S(2)}) collective-permute-start(bf16[512,768]{1,0:T(8,128)(2,1)S(1)} %slice.193), channel_id=1, source_target_pairs={{0,16},{16,0},{1,17},{17,1},{2,18},{18,2},{3,19},{19,3},{4,20},{20... | collective-permute-start | bytes 2359304 | tf_op jit(solution)/shard_map/a1/ring_h/ppermute | solution.py:63
  77.3 38.4 %collective-permute-start.9 = (bf16[512,2048]{1,0:T(8,128)(2,1)}, bf16[512,2048]{1,0:T(8,128)(2,1)}, u32[]{:S(2)}, u32[]{:S(2)}) collective-permute-start(bf16[512,2048]{1,0:T(8,128)(2,1)} %constant_dynamic-update-slice_fusion.refs_0_), channel_id=1, source_target_pairs={{0,1},{1,0},{2,3},{3,2},{4,5},{5,4},{6,7},{7,6},{8,9},{9,8},{10,11... | collective-permute-start | bytes 6291464 | tf_op jit(solution)/shard_map/a2/ring_tp/ppermute | solution.py:63
  80.5 34.3 %collective-permute-start.13 = (bf16[512,768]{1,0:T(8,128)(2,1)S(1)}, bf16[512,768]{1,0:T(8,128)(2,1)S(1)}, u32[]{:S(2)}, u32[]{:S(2)}) collective-permute-start(bf16[512,768]{1,0:T(8,128)(2,1)S(1)} %collective-permute-done.8.refs_3_.refs_1_), channel_id=1, source_target_pairs={{0,4},{4,0},{1,5},{5,1},{2,6},{6,2},{3,7},{7,3},{8,12},{12,8},{9,1... | collective-permute-start | bytes 2359304 | tf_op jit(solution)/shard_map/a2/ring_y/ppermute | solution.py:63
  119.4 33.6 %collective-permute-start.16 = (bf16[256,1024]{1,0:T(8,128)(2,1)}, bf16[256,1024]{1,0:T(8,128)(2,1)S(1)}, u32[]{:S(2)}, u32[]{:S(2)}) collective-permute-start(bf16[256,1024]{1,0:T(8,128)(2,1)} %get-tuple-element.377), channel_id=1, source_target_pairs={{0,16},{16,0},{1,17},{17,1},{2,18},{18,2},{3,19},{19,3},{4,20},{20... | collective-permute-start | bytes 1572872 | tf_op jit(solution)/shard_map/c1/ring_h/ppermute | solution.py:63
  120.5 32.6 %collective-permute-start.17 = (bf16[128,2048]{1,0:T(8,128)(2,1)}, bf16[128,2048]{1,0:T(8,128)(2,1)}, u32[]{:S(2)}, u32[]{:S(2)}) collective-permute-start(bf16[128,2048]{1,0:T(8,128)(2,1)} %constant_dynamic-slice_fusion), channel_id=1, source_target_pairs={{0,0},{4,8},{8,4},{12,12},{1,1},{5,9},{9,5},{13,13},{2,2},{6,10},{... | collective-permute-start | bytes 1572872 | tf_op jit(solution)/shard_map/c1/flip/ppermute | solution.py:320
  125.8 32.0 %collective-permute-start.18 = (bf16[128,2048]{1,0:T(8,128)(2,1)}, bf16[128,2048]{1,0:T(8,128)(2,1)}, u32[]{:S(2)}, u32[]{:S(2)}) collective-permute-start(bf16[128,2048]{1,0:T(8,128)(2,1)} %constant_dynamic-slice_fusion), channel_id=1, source_target_pairs={{0,4},{4,12},{8,0},{12,8},{1,5},{5,13},{9,1},{13,9},{2,6},{6,14},{... | collective-permute-start | bytes 1572872 | tf_op jit(solution)/shard_map/c1/flip/ppermute | solution.py:320
  165.8 39.1 %collective-permute-start.24 = (bf16[768,1024]{1,0:T(8,128)(2,1)}, bf16[768,1024]{1,0:T(8,128)(2,1)}, u32[]{:S(2)}, u32[]{:S(2)}) collective-permute-start(bf16[768,1024]{1,0:T(8,128)(2,1)} %pad_maximum_fusion), channel_id=1, source_target_pairs={{0,4},{4,0},{1,5},{5,1},{2,6},{6,2},{3,7},{7,3},{8,12},{12,8},{9,1... | collective-permute-start | bytes 4718600 | tf_op jit(solution)/shard_map/s3/ring_y/ppermute | solution.py:63
  167.8 25.8 %collective-permute-start.23 = (bf16[256,1024]{1,0:T(8,128)(2,1)}, bf16[256,1024]{1,0:T(8,128)(2,1)S(1)}, u32[]{:S(2)}, u32[]{:S(2)}) collective-permute-start(bf16[256,1024]{1,0:T(8,128)(2,1)} %get-tuple-element.208), channel_id=1, source_target_pairs={{0,16},{16,0},{1,17},{17,1},{2,18},{18,2},{3,19},{19,3},{4,20},{20... | collective-permute-start | bytes 1572872 | tf_op jit(solution)/shard_map/s3/ring_h/ppermute | solution.py:63
  207.2 37.3 %collective-permute-start.29 = (bf16[768,1024]{1,0:T(8,128)(2,1)S(1)}, bf16[768,1024]{1,0:T(8,128)(2,1)S(1)}, u32[]{:S(2)}, u32[]{:S(2)}) collective-permute-start(bf16[768,1024]{1,0:T(8,128)(2,1)S(1)} %pad_maximum_fusion.1), channel_id=1, source_target_pairs={{0,4},{4,0},{1,5},{5,1},{2,6},{6,2},{3,7},{7,3},{8,12},{12,8},{9,1... | collective-permute-start | bytes 4718600 | tf_op jit(solution)/shard_map/s4/ring_y/ppermute | solution.py:63
  210.7 25.6 %collective-permute-start.28 = (bf16[256,1024]{1,0:T(8,128)(2,1)S(1)}, bf16[256,1024]{1,0:T(8,128)(2,1)}, u32[]{:S(2)}, u32[]{:S(2)}) collective-permute-start(bf16[256,1024]{1,0:T(8,128)(2,1)S(1)} %get-tuple-element.375), channel_id=1, source_target_pairs={{0,16},{16,0},{1,17},{17,1},{2,18},{18,2},{3,19},{19,3},{4,20},{20... | collective-permute-start | bytes 1572872 | tf_op jit(solution)/shard_map/s4/ring_h/ppermute | solution.py:63
  247.8 26.4 %collective-permute-start.31 = (bf16[256,1024]{1,0:T(8,128)(2,1)}, bf16[256,1024]{1,0:T(8,128)(2,1)}, u32[]{:S(2)}, u32[]{:S(2)}) collective-permute-start(bf16[256,1024]{1,0:T(8,128)(2,1)} %get-tuple-element.223), channel_id=1, source_target_pairs={{0,16},{16,0},{1,17},{17,1},{2,18},{18,2},{3,19},{19,3},{4,20},{20... | collective-permute-start | bytes 1572872 | tf_op jit(solution)/shard_map/c2/ring_h/ppermute | solution.py:63
  248.0 26.2 %collective-permute-start.32 = (bf16[256,1024]{1,0:T(8,128)(2,1)}, bf16[256,1024]{1,0:T(8,128)(2,1)}, u32[]{:S(2)}, u32[]{:S(2)}) collective-permute-start(bf16[256,1024]{1,0:T(8,128)(2,1)} %collective-permute-done.28.refs_1_.refs_2_), channel_id=1, source_target_pairs={{0,4},{4,0},{1,5},{5,1},{2,6},{6,2},{3,7},{7,3},{8,12},{12,8},{9,1... | collective-permute-start | bytes 1572872 | tf_op jit(solution)/shard_map/c2/ring_y/ppermute | solution.py:63
  276.4 25.3 %collective-permute-start.34 = (bf16[128,2048]{1,0:T(8,128)(2,1)S(1)}, bf16[128,2048]{1,0:T(8,128)(2,1)S(1)}, u32[]{:S(2)}, u32[]{:S(2)}) collective-permute-start(bf16[128,2048]{1,0:T(8,128)(2,1)S(1)} %get-tuple-element.373), channel_id=1, source_target_pairs={{0,16},{16,0},{1,17},{17,1},{2,18},{18,2},{3,19},{19,3},{4,20},{20... | collective-permute-start | bytes 1572872 | tf_op jit(solution)/shard_map/s5/ring_h/ppermute | solution.py:63
  311.6 25.0 %collective-permute-start.36 = (bf16[128,2048]{1,0:T(8,128)(2,1)}, bf16[128,2048]{1,0:T(8,128)(2,1)}, u32[]{:S(2)}, u32[]{:S(2)}) collective-permute-start(bf16[128,2048]{1,0:T(8,128)(2,1)} %get-tuple-element.241), channel_id=1, source_target_pairs={{0,2},{2,0},{8,10},{10,8},{1,3},{3,1},{9,11},{11,9},{4,6},{6,4},{1... | collective-permute-start | bytes 1572872 | tf_op jit(solution)/shard_map/s6/team01/ppermute | solution.py:58
  392.3 36.7 %collective-permute-start.44 = (bf16[512,1024]{1,0:T(8,128)(2,1)}, bf16[512,1024]{1,0:T(8,128)(2,1)}, u32[]{:S(2)}, u32[]{:S(2)}) collective-permute-start(bf16[512,1024]{1,0:T(8,128)(2,1)} %c3.9), channel_id=1, source_target_pairs={{0,4},{4,0},{1,5},{5,1},{2,6},{6,2},{3,7},{7,3},{8,12},{12,8},{9,1... | collective-permute-start | bytes 3145736 | tf_op jit(solution)/shard_map/c3/ring_y/ppermute | solution.py:63
  402.0 26.9 %collective-permute-start.46 = (bf16[128,2048]{1,0:T(8,128)(2,1)S(1)}, bf16[128,2048]{1,0:T(8,128)(2,1)S(1)}, u32[]{:S(2)}, u32[]{:S(2)}) collective-permute-start(bf16[128,2048]{1,0:T(8,128)(2,1)S(1)} %get-tuple-element.371), channel_id=1, source_target_pairs={{0,8},{4,0},{8,12},{12,4},{1,9},{5,1},{9,13},{13,5},{2,10},{6,2},{... | collective-permute-start | bytes 1572872 | tf_op jit(solution)/shard_map/c3/flip/ppermute | solution.py:354
  439.1 26.1 %collective-permute-start.48 = (bf16[512,1024]{1,0:T(8,128)(2,1)S(1)}, bf16[512,1024]{1,0:T(8,128)(2,1)S(1)}, u32[]{:S(2)}, u32[]{:S(2)}) collective-permute-start(bf16[512,1024]{1,0:T(8,128)(2,1)S(1)} %s8_.1), channel_id=1, source_target_pairs={{0,4},{4,0},{1,5},{5,1},{2,6},{6,2},{3,7},{7,3},{8,12},{12,8},{9,1... | collective-permute-start | bytes 3145736 | tf_op jit(solution)/shard_map/s8/ring_y/ppermute | solution.py:63
  440.2 25.0 %collective-permute-start.49 = (bf16[128,2048]{1,0:T(8,128)(2,1)S(1)}, bf16[128,2048]{1,0:T(8,128)(2,1)S(1)}, u32[]{:S(2)}, u32[]{:S(2)}) collective-permute-start(bf16[128,2048]{1,0:T(8,128)(2,1)S(1)} %get-tuple-element.260), channel_id=1, source_target_pairs={{0,2},{2,0},{8,10},{10,8},{1,3},{3,1},{9,11},{11,9},{4,6},{6,4},{1... | collective-permute-start | bytes 1572872 | tf_op jit(solution)/shard_map/s8/team01/ppermute | solution.py:58
  442.0 25.1 %collective-permute-start.52 = (bf16[256,1024]{1,0:T(8,128)(2,1)S(1)}, bf16[256,1024]{1,0:T(8,128)(2,1)S(1)}, u32[]{:S(2)}, u32[]{:S(2)}) collective-permute-start(bf16[256,1024]{1,0:T(8,128)(2,1)S(1)} %get-tuple-element.370), channel_id=1, source_target_pairs={{0,16},{16,0},{1,17},{17,1},{2,18},{18,2},{3,19},{19,3},{4,20},{20... | collective-permute-start | bytes 1572872 | tf_op jit(solution)/shard_map/s8/ring_h/ppermute | solution.py:63
  454.0 47.2 %collective-permute-start.54 = (bf16[512,1024]{1,0:T(8,128)(2,1)S(1)}, bf16[512,1024]{1,0:T(8,128)(2,1)S(1)}, u32[]{:S(2)}, u32[]{:S(2)}) collective-permute-start(bf16[512,1024]{1,0:T(8,128)(2,1)S(1)} %s9.2), channel_id=1, source_target_pairs={{0,4},{4,0},{1,5},{5,1},{2,6},{6,2},{3,7},{7,3},{8,12},{12,8},{9,1... | collective-permute-start | bytes 3145736 | tf_op jit(solution)/shard_map/s9/ring_y/ppermute | solution.py:63
  515.0 25.9 %collective-permute-start.60 = (bf16[512,1024]{1,0:T(8,128)(2,1)S(1)}, bf16[512,1024]{1,0:T(8,128)(2,1)S(1)}, u32[]{:S(2)}, u32[]{:S(2)}) collective-permute-start(bf16[512,1024]{1,0:T(8,128)(2,1)S(1)} %c4.8), channel_id=1, source_target_pairs={{0,4},{4,0},{1,5},{5,1},{2,6},{6,2},{3,7},{7,3},{8,12},{12,8},{9,1... | collective-permute-start | bytes 3145736 | tf_op jit(solution)/shard_map/c4/ring_y/ppermute | solution.py:63
  567.6 27.4 %collective-permute-start.64 = (bf16[128,2048]{1,0:T(8,128)(2,1)}, bf16[128,2048]{1,0:T(8,128)(2,1)}, u32[]{:S(2)}, u32[]{:S(2)}) collective-permute-start(bf16[128,2048]{1,0:T(8,128)(2,1)} %get-tuple-element.283), channel_id=1, source_target_pairs={{0,2},{2,0},{8,10},{10,8},{1,3},{3,1},{9,11},{11,9},{4,6},{6,4},{1... | collective-permute-start | bytes 1572872 | tf_op jit(solution)/shard_map/s10/team01/ppermute | solution.py:58
  569.4 25.6 %collective-permute-start.67 = (bf16[256,1024]{1,0:T(8,128)(2,1)}, bf16[256,1024]{1,0:T(8,128)(2,1)}, u32[]{:S(2)}, u32[]{:S(2)}) collective-permute-start(bf16[256,1024]{1,0:T(8,128)(2,1)} %get-tuple-element.286), channel_id=1, source_target_pairs={{0,16},{16,0},{1,17},{17,1},{2,18},{18,2},{3,19},{19,3},{4,20},{20... | collective-permute-start | bytes 1572872 | tf_op jit(solution)/shard_map/s10/ring_h/ppermute | solution.py:63
  582.4 32.6 %collective-permute-start.70 = (bf16[512,1024]{1,0:T(8,128)(2,1)}, bf16[512,1024]{1,0:T(8,128)(2,1)}, u32[]{:S(2)}, u32[]{:S(2)}) collective-permute-start(bf16[512,1024]{1,0:T(8,128)(2,1)} %pad_maximum_fusion.4), channel_id=1, source_target_pairs={{0,4},{4,0},{1,5},{5,1},{2,6},{6,2},{3,7},{7,3},{8,12},{12,8},{9,1... | collective-permute-start | bytes 3145736 | tf_op jit(solution)/shard_map/s11/ring_y/ppermute | solution.py:63
  604.8 37.2 %collective-permute-start.69 = (bf16[128,2048]{1,0:T(8,128)(2,1)}, bf16[128,2048]{1,0:T(8,128)(2,1)}, u32[]{:S(2)}, u32[]{:S(2)}) collective-permute-start(bf16[128,2048]{1,0:T(8,128)(2,1)} %s11.5), channel_id=1, source_target_pairs={{0,0},{4,8},{8,4},{12,12},{1,1},{5,9},{9,5},{13,13},{2,2},{6,10},{... | collective-permute-start | bytes 1572872 | tf_op jit(solution)/shard_map/s11/ppermute | solution.py:79
  612.4 29.6 %collective-permute-start.74 = (bf16[256,1024]{1,0:T(8,128)(2,1)}, bf16[256,1024]{1,0:T(8,128)(2,1)}, u32[]{:S(2)}, u32[]{:S(2)}) collective-permute-start(bf16[256,1024]{1,0:T(8,128)(2,1)} %get-tuple-element.362), channel_id=1, source_target_pairs={{0,16},{16,0},{1,17},{17,1},{2,18},{18,2},{3,19},{19,3},{4,20},{20... | collective-permute-start | bytes 1572872 | tf_op jit(solution)/shard_map/s11/ring_h/ppermute | solution.py:63
  615.0 26.9 %collective-permute-start.73 = (bf16[128,1024]{1,0:T(8,128)(2,1)}, bf16[128,1024]{1,0:T(8,128)(2,1)}, u32[]{:S(2)}, u32[]{:S(2)}) collective-permute-start(bf16[128,1024]{1,0:T(8,128)(2,1)} %get-tuple-element.363), channel_id=1, source_target_pairs={{0,10},{2,8},{8,2},{10,0},{1,11},{3,9},{9,3},{11,1},{4,14},{6,12},... | collective-permute-start | bytes 786440 | tf_op jit(solution)/shard_map/s11/team11/ppermute | solution.py:58
  646.2 26.1 %collective-permute-start.78 = (bf16[256,1024]{1,0:T(8,128)(2,1)S(1)}, bf16[256,1024]{1,0:T(8,128)(2,1)S(1)}, u32[]{:S(2)}, u32[]{:S(2)}) collective-permute-start(bf16[256,1024]{1,0:T(8,128)(2,1)S(1)} %copy-done.105), channel_id=1, source_target_pairs={{0,16},{16,0},{1,17},{17,1},{2,18},{18,2},{3,19},{19,3},{4,20},{20... | collective-permute-start | bytes 1572872 | tf_op jit(solution)/shard_map/s12/ring_h/ppermute | solution.py:63
  648.3 27.8 %collective-permute-start.79 = (bf16[128,1024]{1,0:T(8,128)(2,1)S(1)}, bf16[128,1024]{1,0:T(8,128)(2,1)S(1)}, u32[]{:S(2)}, u32[]{:S(2)}) collective-permute-start(bf16[128,1024]{1,0:T(8,128)(2,1)S(1)} %get-tuple-element.359), channel_id=1, source_target_pairs={{0,2},{2,0},{8,10},{10,8},{1,3},{3,1},{9,11},{11,9},{4,6},{6,4},{1... | collective-permute-start | bytes 786440 | tf_op jit(solution)/shard_map/s12/team01/ppermute | solution.py:58
  649.7 26.5 %collective-permute-start.80 = (bf16[128,1024]{1,0:T(8,128)(2,1)S(1)}, bf16[128,1024]{1,0:T(8,128)(2,1)S(1)}, u32[]{:S(2)}, u32[]{:S(2)}) collective-permute-start(bf16[128,1024]{1,0:T(8,128)(2,1)S(1)} %get-tuple-element.358), channel_id=1, source_target_pairs={{0,8},{2,10},{8,0},{10,2},{1,9},{3,11},{9,1},{11,3},{4,12},{6,14},... | collective-permute-start | bytes 786440 | tf_op jit(solution)/shard_map/s12/team10/ppermute | solution.py:58
  (175 other events, 1965.7 us)

commit v4 on v3

--- a/solution.py
+++ b/solution.py
@@ -184,6 +184,26 @@
     )(slots, *pieces)
 
 
+def stack_rows_kernel(*refs):
+    height = refs[0].shape[0]
+    for j, piece in enumerate(refs[:-1]):
+        refs[-1][j * height : (j + 1) * height, :] = piece[...]
+
+
+def stack_rows(pieces):
+    height, width = pieces[0].shape
+    rows = height * len(pieces)
+    return pl.pallas_call(
+        stack_rows_kernel,
+        grid=(1,),
+        in_specs=[pl.BlockSpec((height, width), lambda n: (0, 0)) for _ in pieces],
+        out_specs=pl.BlockSpec((rows, width), lambda n: (0, 0)),
+        out_shape=jax.ShapeDtypeStruct((rows, width), pieces[0].dtype),
+        cost_estimate=LIGHT,
+        compiler_params=KERNEL,
+    )(*pieces)
+
+
 def near_rows(team, pieces, widths):
     rows = pieces[0].shape[0] * team.members
     shapes = [jax.ShapeDtypeStruct((rows, width), LOWER) for width in widths]
@@ -205,6 +225,10 @@
 
 def pairs(firsts, seconds):
     return [part for pair in zip(firsts, seconds) for part in pair]
+
+
+def add_ring(team, value, name):
+    return value + sum(team.ring(value, name, step) for step in range(1, team.sizes[name]))
 
 
 class Grads:
@@ -213,27 +237,42 @@
         self.far = lefts[0].shape[1] // 2
         self.near = self.far // team.sizes["h"]
 
-    def rows(self, first, count, adds=(), dtype=LOWER):
-        return outer(self.lefts, self.rights, first, count, adds, dtype)
+        self.half = self.near // 2
+        self.steps = range(1, team.sizes["h"])
+
+    def rows(self, first, count, adds=(), offset=0, column=0):
+        return outer(self.lefts, self.rights, first, count, adds, offset, column)
 
     def send_far(self):
         return self.rows(self.far + self.near, self.far - self.near)
 
+    def send_half(self, part):
+        start = self.far + part * self.half
+        return [self.rows(start + step * self.near, self.half) for step in self.steps]
+
     def send_near(self):
         return self.rows(self.far, self.near)
 
     def cross(self, got):
-        mine = self.rows(self.near, self.far - self.near, [got])
+        offsets = [(step - 1) * self.near for step in self.steps]
+        return [self.rows(self.near + first, self.near, [got], first) for first in offsets]
+
+    def cross_half(self, part, got):
+        offsets = [(step - 1) * self.near + part * self.half for step in self.steps]
+        return [self.rows(self.near + first, self.half, [got], first) for first in offsets]
+
+    def cross_halves(self, part, gots):
+        start = part * self.half
         return [
-            mine[step * self.near : (step + 1) * self.near]
-            for step in range(self.team.sizes["h"] - 1)
+            self.rows(start + step * self.near, self.half, [got])
+            for step, got in zip(self.steps, gots)
         ]
 
     def go(self, sent):
-        return [self.team.ring(value, "h", step) for step, value in enumerate(sent, 1)]
-
-    def total(self, got, crossed):
-        return self.rows(0, self.near, [got, *crossed])
+        return [self.team.ring(value, "h", step) for step, value in zip(self.steps, sent)]
+
+    def total(self, got, crossed, column=0):
+        return self.rows(0, self.near, [got, *crossed], column=column)
 
 
 def home_pieces(team, total):
@@ -309,16 +348,13 @@
     return [piece] + [team.ring(piece, "h", step) for step in range(1, team.sizes["h"])]
 
 
-def deal_flips(team, piece):
-    got = []
-    for flip in range(2):
-        perm = []
-        for l in range(2):
-            for y in range(2):
-                perm.append((l * 2 + y, y * 2 + (l if flip == 0 else 1 - l)))
-        with jax.named_scope("flip"):
-            got.append(lax.ppermute(piece, ("l", "y"), perm))
-    return got
+def deal_flip(team, piece, flip):
+    perm = []
+    for l in range(2):
+        for y in range(2):
+            perm.append((l * 2 + y, y * 2 + (l if flip == 0 else 1 - l)))
+    with jax.named_scope("flip"):
+        return lax.ppermute(piece, ("l", "y"), perm)
 
 
 def deal_across(team, home, two):
@@ -458,7 +494,7 @@
 
 
 LIGHT = pl.CostEstimate(flops=1000000, bytes_accessed=100000, transcendentals=0)
-KERNEL = pltpu.CompilerParams(vmem_limit_bytes=32 * 1024 * 1024)
+KERNEL = pltpu.CompilerParams(vmem_limit_bytes=24 * 1024 * 1024)
 
 
 def gelu_slope(value):
@@ -591,18 +627,20 @@
     out[...] = total.astype(out.dtype)
 
 
-def outer(lefts, rights, first, count, adds=(), dtype=LOWER):
+def outer(lefts, rights, first, count, adds, offset, column):
     height, width = rights[0].shape
     block = math.gcd(256, count)
     in_specs = [pl.BlockSpec((height, block), lambda i: (0, first // block + i)) for _ in lefts]
     in_specs += [pl.BlockSpec((height, width), lambda i: (0, 0)) for _ in rights]
     tile = pl.BlockSpec((block, width), lambda i: (i, 0))
+    add_tile = pl.BlockSpec((block, width), lambda i: (offset // block + i, 0))
+    first_tile = pl.BlockSpec((block, width), lambda i: (offset // block + i, column))
     return pl.pallas_call(
         functools.partial(outer_kernel, len(lefts), len(adds)),
         grid=(count // block,),
-        in_specs=in_specs + [tile] * len(adds),
+        in_specs=in_specs + [first_tile] * len(adds[:1]) + [add_tile] * len(adds[1:]),
         out_specs=tile,
-        out_shape=jax.ShapeDtypeStruct((count, width), dtype),
+        out_shape=jax.ShapeDtypeStruct((count, width), LOWER),
         cost_estimate=LIGHT,
         compiler_params=KERNEL,
     )(*lefts, *rights, *adds)
@@ -712,7 +750,9 @@
     with jax.named_scope("a0"):
         own = swap_home(lax.dynamic_slice_in_dim(tokens, half_at, row_count, 0))
         share = share_columns(team, [w_query, w_key, w_value, w_out])
-        own, w_up, w_down, *share = fence(own, w_up, w_down, *share)
+        own, w_up, w_down, bias_qkv, bias_up, *share = fence(
+            own, w_up, w_down, bias_qkv, bias_up, *share
+        )
     with jax.named_scope("a1"):
         own = to_team_order(team, own)
         (near_att,) = near_rows(team, share, [4 * wide])
@@ -724,35 +764,40 @@
         )
         pieces, cross_qkv = rest[:members], rest[members:]
     with jax.named_scope("a2"):
-        half = jnp.concatenate(pieces, axis=0)
+        half = stack_rows(pieces)
         other = cores(team, half)
         far_qkv = beside(team, cross_qkv)
         cross_out = across(team, near_att[:, 3 * wide :])
-        share = share_columns(team, [w_up, w_down])
-        cotangent, *rest = fence(cotangent, half, *other, *share, *far_qkv, *cross_out)
+        share = share_columns(team, [w_up])
+        cotangent, w_down, *rest = fence(
+            cotangent, w_down, half, *other, *share, *far_qkv, *cross_out
+        )
         in_parts = rest[:ts]
         share, rest = rest[ts : ts + members], rest[ts + members :]
         far_qkv, cross_out = rest[:steps], rest[steps:]
     qkv_mat = first_column([near_att, *cross_qkv, side_att, *far_qkv])
     with jax.named_scope("c1"):
-        near_up, near_down = near_rows(team, share, [tall, tall])
+        (near_up,) = near_rows(team, share, [tall])
         up_a, up_b = halves(near_up)
         cross_up_a = across(team, up_a)
         far_out = beside(team, cross_out)
-        cot_two = deal_flips(team, lax.dynamic_slice_in_dim(cotangent, half_at, row_count, 0))
+        cot_half = lax.dynamic_slice_in_dim(cotangent, half_at, row_count, 0)
+        cot_one = deal_flip(team, cot_half, 0)
+        share = share_columns(team, [w_down])
         (qkv,) = project("bias", in_parts, qkv_mat, 3 * wide, bias_qkv)
         attended, log_sum = attend(qkv, limits, score_scale)
         out_mat = [(near_att, 3), *first_column(cross_out), (side_att, 3), *first_column(far_out)]
-        got = core_send(team, attended, out_mat, half_rows, *cross_up_a, *cot_two)
+        got = core_send(team, attended, out_mat, half_rows, cot_one, *cross_up_a, *share)
         total, sent = core_total(team, attended, out_mat, half_rows, got)
-        up_b, near_up, near_down, *rest = fence(
-            up_b, near_up, near_down, *cross_up_a, *sent, *cot_two
+        up_b, near_up, cot_half, cot_one, *rest = fence(
+            up_b, near_up, cot_half, cot_one, *cross_up_a, *share, *sent
         )
         cross_up_a, rest = rest[:steps], rest[steps:]
-        sent, cot_two = rest[: members - 1], rest[members - 1 :]
+        share, sent = rest[:members], rest[members:]
     with jax.named_scope("s3"):
         got = team_send(team, sent)
         cross_up_b = across(team, up_b)
+        (near_down,) = near_rows(team, share, [tall])
         side = beside(team, [jnp.concatenate([near_up, *cross_up_a], axis=0)])
         near_down, *rest = fence(near_down, *got, *cross_up_b, *side)
         got, rest = rest[:team_count], rest[team_count:]
@@ -767,13 +812,10 @@
         near_down, down_b, *rest = fence(near_down, down_b, *pieces, *cross_down_a, *side)
         pieces, rest = rest[:members], rest[members:]
         cross_down_a, side_b = rest[:steps], rest[steps]
-    near_count = near_down.shape[0]
-    side_up, side_down = side_a[:near_count], side_b[:near_count]
+    whole, part = near_down.shape[0], down_a.shape[0]
+    side_up, side_down = side_a[:whole], side_b[:whole]
     far_up_a, far_up_b = (
-        [
-            side[near_count + k * near_count // 2 : near_count + (k + 1) * near_count // 2]
-            for k in range(steps)
-        ]
+        [side[whole + k * part : whole + (k + 1) * part] for k in range(steps)]
         for side in (side_a, side_b)
     )
     up_mat = first_column(
@@ -783,7 +825,7 @@
         + pairs(far_up_a, far_up_b)
     )
     with jax.named_scope("c2"):
-        half = jnp.concatenate(pieces, axis=0)
+        half = stack_rows(pieces)
         other = cores(team, half)
         cross_down_b = across(team, down_b)
         far_down_a = beside(team, cross_down_a)
@@ -793,6 +835,7 @@
             hidden_part, active_part = project("gelu", [part], up_mat, tall, bias_up)
             hidden.append(hidden_part)
             active.append(active_part)
+        cot_two = [cot_one, deal_flip(team, cot_half, 1)]
         rest = fence(*active, *cross_down_b, *far_down_a, *cot_two)
         active, rest = rest[:ts], rest[ts:]
         cross_down_b, rest = rest[:steps], rest[steps:]
@@ -828,80 +871,79 @@
         grad_send = jnp.sum(grad_normed, axis=0)
         grad_bdown = jnp.sum(grad_result.astype(WIDE), axis=0)
     with jax.named_scope("c3"):
-        half = jnp.concatenate(pieces, axis=0)
+        half = stack_rows(pieces)
         other = cores(team, half)
         result_parts = [half] + other
         flow_down = Grads(team, result_parts, active)
-        (far_down,) = beside(team, [flow_down.send_far()])
-        out_two = deal(team, dealing, out_pieces)
+        far_down_a = beside(team, flow_down.send_half(0))
         grad_hidden = []
         for part, hidden_part in zip(result_parts, hidden):
             grad_hidden += project("slope", [part], down_mat, tall, hidden_part)
-        got = core_send(team, grad_hidden, up_mat, half_rows, far_down, *grad_hidden, *out_two)
+        got = core_send(team, grad_hidden, up_mat, half_rows, *far_down_a, *grad_hidden)
         total, sent = core_total(team, grad_hidden, up_mat, half_rows, got)
-        cross_down = flow_down.cross(far_down)
+        cross_down = flow_down.cross_halves(0, far_down_a)
         flow_up = Grads(team, mid_parts, grad_hidden)
-        rest = fence(*sent, *cross_down, *out_two)
-        sent, rest = rest[: members - 1], rest[members - 1 :]
-        cross_down, out_two = rest[:steps], rest[steps:]
+        rest = fence(*sent, *cross_down)
+        sent, cross_down = rest[: members - 1], rest[members - 1 :]
     with jax.named_scope("s8"):
         got = team_send(team, sent)
-        down_halves = [halves(value) for value in cross_down]
-        got_down_a = flow_down.go([a for a, b in down_halves])
-        (far_up,) = beside(team, [flow_up.send_far()])
-        far_up, *rest = fence(far_up, *got, *got_down_a, *[b for a, b in down_halves])
+        got_down_a = flow_down.go(cross_down)
+        far_down_b = beside(team, flow_down.send_half(1))
+        far_up, *far_down_b = fence(flow_up.send_far(), *far_down_b)
+        (far_up,) = beside(team, [far_up])
+        cross_down = flow_down.cross_halves(1, far_down_b)
+        far_up, *rest = fence(far_up, *got, *got_down_a, *cross_down)
         got, rest = rest[:team_count], rest[team_count:]
-        got_down_a, down_b = rest[:steps], rest[steps:]
+        got_down_a, cross_down = rest[:steps], rest[steps:]
     with jax.named_scope("s9"):
         grad_middle = team_total(total, got) + grad_sum
         grad_inner = layer_norm_back(grad_middle, gain_mid, mid_hat, mid_rate)
         grad_branch = grad_inner.astype(LOWER)
         pieces = team_pieces(team, grad_branch)
-        got_down_b = flow_down.go(down_b)
+        got_down_b = flow_down.go(cross_down)
         (near_down,) = beside(team, [flow_down.send_near()])
-        cross_up = flow_up.cross(far_up)
-        near_down, *rest = fence(near_down, *pieces, *got_down_b, *cross_up)
-        pieces, rest = rest[:members], rest[members:]
-        got_down_b, cross_up = rest[:steps], rest[steps:]
         grad_gmid = jnp.sum(grad_middle * mid_hat, axis=0)
         grad_smid = jnp.sum(grad_middle, axis=0)
         grad_bout = jnp.sum(grad_branch.astype(WIDE), axis=0)
+        by_row = jnp.stack([grad_bout, grad_gmid, grad_smid, grad_bdown, grad_gend, grad_send])
+        by_row = add_ring(team, from_team_order(team, by_row), "tp")
+        cross_up_a, cross_up_b = flow_up.cross_half(0, far_up), flow_up.cross_half(1, far_up)
+        by_row, near_down, *rest = fence(by_row, near_down, *pieces, *got_down_b, *cross_up_a, *cross_up_b)
+        pieces, rest = rest[:members], rest[members:]
+        got_down_b, rest = rest[:steps], rest[steps:]
+        cross_up_a, cross_up_b = rest[:steps], rest[steps:]
     with jax.named_scope("c4"):
-        half = jnp.concatenate(pieces, axis=0)
+        half = stack_rows(pieces)
         other = cores(team, half)
-        up_halves = [halves(value) for value in cross_up]
-        got_up_a = flow_up.go([a for a, b in up_halves])
-        (near_up,) = beside(team, [flow_up.send_near()])
+        got_up_a, got_up_b = flow_up.go(cross_up_a), flow_up.go(cross_up_b)
+        out_two = deal(team, dealing, out_pieces)
         branch_parts = [half] + other
         attended_parts = [attended[k * half_rows : (k + 1) * half_rows] for k in range(ts)]
         flow_out = Grads(team, branch_parts, attended_parts)
         (far_out,) = beside(team, [flow_out.send_far()])
         (grad_attended,) = project("plain", branch_parts, out_mat, wide)
         grad_qkv = attend_back(qkv, grad_attended, log_sum, limits, score_scale)
-        got = core_send(team, grad_qkv, qkv_mat, half_rows, near_up, *got_up_a)
+        got = core_send(team, grad_qkv, qkv_mat, half_rows, far_out, *got_up_a, *out_two)
         total, sent = core_total(team, grad_qkv, qkv_mat, half_rows, got)
         grad_parts = [grad_qkv[k * half_rows : (k + 1) * half_rows] for k in range(ts)]
         flow_qkv = Grads(team, in_parts, grad_parts)
-        near_up, far_out, near_down, *rest = fence(
-            near_up, far_out, near_down, *sent, *got_up_a, *[b for a, b in up_halves]
-        )
+        qkv_sum = jnp.sum(grad_qkv.astype(WIDE), axis=0)
+        grad_bup = sum(jnp.sum(part.astype(WIDE), axis=0) for part in grad_hidden)
+        zeros = jnp.zeros((members, 1), WIDE)
+        by_slot = [
+            put(zeros * part[None], part[None], (my_slot, 0)).reshape(-1)
+            for part in (qkv_sum[:wide], qkv_sum[2 * wide :], grad_bup)
+        ]
+        sums = jnp.concatenate([by_row.reshape(-1)] + by_slot).reshape(-1, 128)
+        sums = add_ring(team, sums, "l")
+        (far_qkv,) = beside(team, [flow_qkv.send_far()])
+        cross_out, cross_qkv = flow_out.cross(far_out), flow_qkv.cross(far_qkv)
+        sums, near_down, *rest = fence(
+            sums, near_down, *cross_out, *cross_qkv, *sent, *got_up_a, *got_up_b, *out_two
+        )
+        cross_out, cross_qkv, rest = rest[:steps], rest[steps : 2 * steps], rest[2 * steps :]
         sent, rest = rest[: members - 1], rest[members - 1 :]
-        got_up_a, up_b = rest[:steps], rest[steps:]
-
-    qkv_sum = jnp.sum(grad_qkv.astype(WIDE), axis=0)
-    grad_bup = sum(jnp.sum(part.astype(WIDE), axis=0) for part in grad_hidden)
-    zeros = jnp.zeros((members, 1), WIDE)
-    by_slot = [
-        put(zeros * part[None], part[None], (my_slot, 0)).reshape(-1)
-        for part in (qkv_sum[:wide], qkv_sum[2 * wide :], grad_bup)
-    ]
-    by_row = jnp.stack([grad_bout, grad_gmid, grad_smid, grad_bdown, grad_gend, grad_send])
-    by_row = from_team_order(team, by_row).reshape(-1)
-    sums = jnp.concatenate([by_row] + by_slot).reshape(-1, 128)
-    by_row_rows = by_row.shape[0] // 128
-
-    def add_ring(value, name):
-        return value + sum(team.ring(value, name, step) for step in range(1, team.sizes[name]))
+        got_up_a, got_up_b, out_two = rest[:steps], rest[steps : 2 * steps], rest[2 * steps :]
 
     with jax.named_scope("s10"):
         got = team_send(team, sent)
@@ -909,60 +951,41 @@
             near_down,
             [jnp.concatenate(both, axis=0) for both in zip(got_down_a, got_down_b)],
         )
-        got_up_b = flow_up.go(up_b)
-        (far_qkv,) = beside(team, [flow_qkv.send_far()])
-        cross_qkv, cross_out = flow_qkv.cross(far_qkv), flow_out.cross(far_out)
-        both = add_ring(sums[:by_row_rows], "tp")
-        sums = jnp.concatenate([both, sums[by_row_rows:]], axis=0)
-        cross_att = [
-            jnp.concatenate(blocks, axis=1) for blocks in zip(cross_qkv, cross_out)
-        ]
+        got_qkv = flow_qkv.go(cross_qkv)
+        (near_up,) = beside(team, [flow_up.send_near()])
+        sums = add_ring(team, sums, "x")
         sums, total_down, near_up, *rest = fence(
-            sums, total_down, near_up, *got, *got_up_b, *cross_att
-        )
+            sums, total_down, near_up, *out_two, *got, *got_qkv, *cross_out
+        )
+        out_two, rest = rest[:2], rest[2:]
         got, rest = rest[:team_count], rest[team_count:]
-        got_up_b, cross_att = rest[:steps], rest[steps:]
+        got_qkv, cross_out = rest[:steps], rest[steps:]
     with jax.named_scope("s11"):
-        att_halves = [halves(value) for value in cross_att]
-        got_att_a = flow_qkv.go([a for a, b in att_halves])
+        got_out = flow_out.go(cross_out)
+        home_down = home_pieces(team, total_down)
         grad_own = (team_total(total, got) + grad_inner).astype(LOWER)
         swapped = swap_home(from_team_order(team, grad_own))
-        home_down = home_pieces(team, total_down)
+        near_att = jnp.concatenate([flow_qkv.send_near(), flow_out.send_near()], axis=1)
+        (near_att,) = beside(team, [near_att])
         total_up = flow_up.total(
             near_up, [jnp.concatenate(both, axis=0) for both in zip(got_up_a, got_up_b)]
         )
-        near_att = jnp.concatenate([flow_qkv.send_near(), flow_out.send_near()], axis=1)
-        (near_att,) = beside(team, [near_att])
-        sums, swapped, near_att, total_up, *rest = fence(
-            sums, swapped, near_att, total_up, *out_two,
-            *home_down, *got_att_a, *[b for a, b in att_halves]
-        )
-        out_two, rest = rest[:2], rest[2:]
-        home_down, rest = rest[:members], rest[members:]
-        got_att_a, att_b = rest[:steps], rest[steps:]
+        total_out = flow_out.total(near_att, got_out, 3)
+        sums = add_ring(team, sums, "y")
+        total_qkv = flow_qkv.total(near_att, got_qkv, 0)
+        sums, swapped, total_up, total_out, total_qkv, *rest = fence(
+            sums, swapped, total_up, total_out, total_qkv, *home_down, *out_two
+        )
+        home_down, out_two = rest[:members], rest[members:]
         (grad_down,) = home_join(team, home_down, [tall])
     with jax.named_scope("s12"):
-        got_att_b = flow_qkv.go(att_b)
-        home_up = home_pieces(team, total_up)
-        sums = add_ring(sums, "y")
         grad_tokens = join_cores(team, swapped)
+        home_all = home_pieces(team, jnp.concatenate([total_up, total_qkv, total_out], axis=1))
         output = join_cores(team, dealt_out(team, dealing, out_two))
-        got_att = [jnp.concatenate(both, axis=0) for both in zip(got_att_a, got_att_b)]
-        total_qkv = flow_qkv.total(
-            near_att[:, : 3 * wide], [value[:, : 3 * wide] for value in got_att]
-        )
-        total_out = flow_out.total(
-            near_att[:, 3 * wide :], [value[:, 3 * wide :] for value in got_att]
-        )
-        total_att = jnp.concatenate([total_qkv, total_out], axis=1)
-        sums, grad_tokens, output, total_att, *home_up = fence(
-            sums, grad_tokens, output, total_att, *home_up
-        )
-        (grad_up,) = home_join(team, home_up, [tall])
-    with jax.named_scope("s13"):
-        home_att = home_pieces(team, total_att)
-        sums = add_ring(add_ring(add_ring(sums, "h"), "l"), "x").reshape(-1)
-        grad_query, grad_key, grad_value, grad_out = home_join(team, home_att, [wide] * 4)
+        sums = add_ring(team, sums, "h").reshape(-1)
+        grad_up, grad_query, grad_key, grad_value, grad_out = home_join(
+            team, home_all, [tall] + [wide] * 4
+        )
     smalls = []
     first = 0
     for size in [width] * 6 + [b_query.shape[0], b_value.shape[0], b_up.shape[0]]:

time: 708 us -> 654 us (0.924)
  waiting for transfers between devices: 370 us -> 303 us
  starting transfers between devices: 82.4 us -> 105 us
  local copies, waits for them, and re-layouts: 71.9 us -> 55.2 us
    ppermute x39, waiting for transfers between devices: 229 us -> 191 us  [shift_(): return lax.ppermute(value, TEAM, perm)]
    ppermute x43 -> x44, waiting for transfers between devices: 129 us -> 108 us  [ring(): lax.ppermute(value, name, [(i, (i + step) % size) for i in range(size)])]
    ppermute x39, starting transfers between devices: 35.2 us -> 52.5 us  [shift_(): return lax.ppermute(value, TEAM, perm)]
    unnamed x254 -> x271, local copies, waits for them, and re-layouts: 41.2 us -> 28.2 us
    ppermute x2, waiting for transfers between devices: 7.5 us -> 0.01 us  [deal(): got.append(lax.ppermute(sent, ('l', 'y'), perm))]
    ppermute x43 -> x44, starting transfers between devices: 31.7 us -> 36.6 us  [ring(): lax.ppermute(value, name, [(i, (i + step) % size) for i in range(size)])]
    pallas_call x16 -> x19, Pallas kernels: 38.3 us -> 39.1 us  [outer(): pl.pallas_call(functools.partial(outer_kernel, len(lefts), len(adds)), gr...]
  transfers between devices with their start and end apart: 88 -> 89, of which waited for: 50 -> 46; matrix products, arithmetic and copies ran while one was open for 7% -> 7% of each run, Pallas kernels for 16% -> 19%
where the time goes in v4:
time: 654 us; the launch traced here: 644 us
  waiting for transfers between devices  303 us (46%)
  Pallas kernels  138 us (21%)
  starting transfers between devices  105 us (16%)
  local copies, waits for them, and re-layouts  55.2 us (8%)
  other arithmetic  28.6 us (4%)
  between operations  15 us (2%)
    ppermute x39, waiting for transfers between devices, shift_(): return lax.ppermute(value, TEAM, perm)  191 us
    ppermute x44, waiting for transfers between devices, ring(): lax.ppermute(value, name, [(i, (i + step) % size) for i in range(size)])  108 us
    ppermute x39, starting transfers between devices, shift_(): return lax.ppermute(value, TEAM, perm)  52.5 us
    pallas_call x19, Pallas kernels, outer(): pl.pallas_call(functools.partial(outer_kernel, len(lefts), len(adds)), gr...  39.1 us
    ppermute x44, starting transfers between devices, ring(): lax.ppermute(value, name, [(i, (i + step) % size) for i in range(size)])  36.6 us
    pallas_call x6, Pallas kernels, project(): pl.pallas_call(functools.partial(project_kernel, mode, len(parts), len(pi...  29.2 us
    unnamed x271, local copies, waits for them, and re-layouts  28.2 us
    pallas_call x8, Pallas kernels, spread(): pl.pallas_call(functools.partial(spread_kernel, len(pieces), len(got), sp...  27.1 us
  transfers between devices with their start and end apart: 89, of which 46 were waited for; matrix products, arithmetic and copies ran while one was open for 7% of the time, Pallas kernels for 19%

profile of v4, /device:TPU:0, one launch (start us, length us, event | category | flops | bytes accessed | tf_op | source)
XLA Modules:
  0.0 644.0 jit_solution(18073537108385630252)
XLA Ops:
  18.1 13.0 %collective-permute-done.2.refs_2_ = bf16[128,1024]{1,0:T(8,128)(2,1)S(1)} collective-permute-done((bf16[128,1024]{1,0:T(8,128)(2,1)S(1)}, bf16[128,1024]{1,0:T(8,128)(2,1)S(1)}, u32[]{:S(2)}, u32[]{:S(2)}) %collective-permute-start.2) | collective-permute-done | bytes 262176 | tf_op jit(solution)/shard_map/a0/team10/ppermute | solution.py:58
  40.1 18.7 %collective-permute-done.6.refs_2_ = bf16[128,2048]{1,0:T(8,128)(2,1)S(1)} collective-permute-done((bf16[128,2048]{1,0:T(8,128)(2,1)}, bf16[128,2048]{1,0:T(8,128)(2,1)S(1)}, u32[]{:S(2)}, u32[]{:S(2)}) %collective-permute-start.6) | collective-permute-done | bytes 524320 | tf_op jit(solution)/shard_map/a1/team10/ppermute | solution.py:58
  59.3 13.4 %collective-permute-done.8.refs_3_.refs_1_ = bf16[512,768]{1,0:T(8,128)(2,1)} collective-permute-done((bf16[512,768]{1,0:T(8,128)(2,1)S(1)}, bf16[512,768]{1,0:T(8,128)(2,1)}, u32[]{:S(2)}, u32[]{:S(2)}) %collective-permute-start.8) | collective-permute-done | bytes 786464 | tf_op jit(solution)/shard_map/a1/ring_h/ppermute | solution.py:63
  86.7 10.2 %collective-permute-done.12.refs_3_ = bf16[128,1024]{1,0:T(8,128)(2,1)S(1)} collective-permute-done((bf16[128,1024]{1,0:T(8,128)(2,1)S(1)}, bf16[128,1024]{1,0:T(8,128)(2,1)S(1)}, u32[]{:S(2)}, u32[]{:S(2)}) %collective-permute-start.12) | collective-permute-done | bytes 262176 | tf_op jit(solution)/shard_map/a2/team11/ppermute | solution.py:58
  105.3 5.3 collective-permute-start.16
  120.0 5.7 c1.5.query_ref.key_ref.value_ref
  125.8 9.8 %c1.6 = (bf16[1024,256]{1,0:T(8,128)(2,1)S(1)}, f32[2,1,1024]{2,1,0:T(1,128)S(1)}) custom-call(s32[8]{0:T(128)S(1)} %multiply_subtract_fusion.limits_ref, bf16[1024,768]{1,0:T(8,128)(2,1)S(1)} %c1.5.query_ref.key_ref.value_ref, bf16[1024,768]{1,0:T(8,128)(2,1)S(1)} %c1.5.query_ref.key_ref.value_ref, bf16[1024,768]{1,0:T(8,128)(2,1)S(1)} %c1.5.query_ref.key_ref.value_ref), custom_call_target="tpu_custom_call" | custom-call | flops 1000000 | bytes 100000 | tf_op jit(solution)/shard_map/c1/pallas_call | solution.py:656
  154.9 11.1 %collective-permute-done.23 = bf16[128,2048]{1,0:T(8,128)(2,1)S(1)} collective-permute-done((bf16[128,2048]{1,0:T(8,128)(2,1)S(1)}, bf16[128,2048]{1,0:T(8,128)(2,1)S(1)}, u32[]{:S(2)}, u32[]{:S(2)}) %collective-permute-start.23) | collective-permute-done | bytes 524320 | tf_op jit(solution)/shard_map/s3/team01/ppermute | solution.py:58
  171.0 5.9 collective-permute-done.22
  179.5 10.7 %collective-permute-done.24 = bf16[128,2048]{1,0:T(8,128)(2,1)} collective-permute-done((bf16[128,2048]{1,0:T(8,128)(2,1)S(1)}, bf16[128,2048]{1,0:T(8,128)(2,1)}, u32[]{:S(2)}, u32[]{:S(2)}) %collective-permute-start.24) | collective-permute-done | bytes 524320 | tf_op jit(solution)/shard_map/s3/team10/ppermute | solution.py:58
  198.7 17.6 %collective-permute-done.28.refs_2_ = bf16[128,2048]{1,0:T(8,128)(2,1)S(1)} collective-permute-done((bf16[128,2048]{1,0:T(8,128)(2,1)S(1)}, bf16[128,2048]{1,0:T(8,128)(2,1)S(1)}, u32[]{:S(2)}, u32[]{:S(2)}) %collective-permute-start.28) | collective-permute-done | bytes 524320 | tf_op jit(solution)/shard_map/s4/team10/ppermute | solution.py:58
  221.6 7.5 %collective-permute-done.29.refs_3_ = bf16[128,2048]{1,0:T(8,128)(2,1)S(1)} collective-permute-done((bf16[128,2048]{1,0:T(8,128)(2,1)S(1)}, bf16[128,2048]{1,0:T(8,128)(2,1)S(1)}, u32[]{:S(2)}, u32[]{:S(2)}) %collective-permute-start.29) | collective-permute-done | bytes 524320 | tf_op jit(solution)/shard_map/s4/team01/ppermute | solution.py:58
  259.7 11.3 %collective-permute-done.36.refs_5_.refs_6_ = bf16[256,1024]{1,0:T(8,128)(2,1)S(1)} collective-permute-done((bf16[256,1024]{1,0:T(8,128)(2,1)}, bf16[256,1024]{1,0:T(8,128)(2,1)S(1)}, u32[]{:S(2)}, u32[]{:S(2)}) %collective-permute-start.36) | collective-permute-done | bytes 524320 | tf_op jit(solution)/shard_map/s5/ring_y/ppermute | solution.py:63
  275.0 9.6 %collective-permute-done.37 = bf16[128,2048]{1,0:T(8,128)(2,1)S(1)} collective-permute-done((bf16[128,2048]{1,0:T(8,128)(2,1)S(1)}, bf16[128,2048]{1,0:T(8,128)(2,1)S(1)}, u32[]{:S(2)}, u32[]{:S(2)}) %collective-permute-start.37) | collective-permute-done | bytes 524320 | tf_op jit(solution)/shard_map/s5/ring_h/ppermute | solution.py:63
  295.4 12.7 %collective-permute-done.40 = bf16[128,2048]{1,0:T(8,128)(2,1)S(1)} collective-permute-done((bf16[128,2048]{1,0:T(8,128)(2,1)S(1)}, bf16[128,2048]{1,0:T(8,128)(2,1)S(1)}, u32[]{:S(2)}, u32[]{:S(2)}) %collective-permute-start.40) | collective-permute-done | bytes 524320 | tf_op jit(solution)/shard_map/s6/team01/ppermute | solution.py:58
  313.6 5.1 collective-permute-done.39
  331.5 12.6 %collective-permute-done.43.refs_2_ = bf16[128,2048]{1,0:T(8,128)(2,1)S(1)} collective-permute-done((bf16[128,2048]{1,0:T(8,128)(2,1)S(1)}, bf16[128,2048]{1,0:T(8,128)(2,1)S(1)}, u32[]{:S(2)}, u32[]{:S(2)}) %collective-permute-start.43) | collective-permute-done | bytes 524320 | tf_op jit(solution)/shard_map/s7/team10/ppermute | solution.py:58
  345.5 7.3 %collective-permute-done.45 = bf16[128,2048]{1,0:T(8,128)(2,1)S(1)} collective-permute-done((bf16[128,2048]{1,0:T(8,128)(2,1)}, bf16[128,2048]{1,0:T(8,128)(2,1)S(1)}, u32[]{:S(2)}, u32[]{:S(2)}) %collective-permute-start.45) | collective-permute-done | bytes 524320 | tf_op jit(solution)/shard_map/s7/ring_h/ppermute | solution.py:63
  363.5 4.9 c3.8.rows_ref.refs_2_
  368.4 5.1 c3.9.rows_ref.refs_3_
  394.2 5.6 collective-permute-done.52
  404.8 13.8 %collective-permute-done.50.refs_4_ = bf16[512,1024]{1,0:T(8,128)(2,1)S(1)} collective-permute-done((bf16[512,1024]{1,0:T(8,128)(2,1)S(1)}, bf16[512,1024]{1,0:T(8,128)(2,1)S(1)}, u32[]{:S(2)}, u32[]{:S(2)}) %collective-permute-start.50) | collective-permute-done | bytes 1048608 | tf_op jit(solution)/shard_map/s8/ring_y/ppermute | solution.py:63
  418.6 4.9 collective-permute-done.53
  428.9 18.7 %collective-permute-done.58.refs_2_ = bf16[128,2048]{1,0:T(8,128)(2,1)} collective-permute-done((bf16[128,2048]{1,0:T(8,128)(2,1)}, bf16[128,2048]{1,0:T(8,128)(2,1)}, u32[]{:S(2)}, u32[]{:S(2)}) %collective-permute-start.58) | collective-permute-done | bytes 524320 | tf_op jit(solution)/shard_map/s9/team10/ppermute | solution.py:58
  483.3 10.8 %c4.11.rows_ref = bf16[1024,768]{1,0:T(8,128)(2,1)S(1)} custom-call(s32[8]{0:T(128)S(1)} %multiply_subtract_fusion.limits_ref, bf16[1024,768]{1,0:T(8,128)(2,1)S(1)} %copy-done.10, bf16[1024,768]{1,0:T(8,128)(2,1)S(1)} %copy-done.10, bf16[1024,768]{1,0:T(8,128)(2,1)S(1)} %copy-done.10, bf16[1024,256]{1,0:T(8,128)(2,1)S(1)} %c4.10.grad_ref, ...), custom_call_target="tpu_custom_call" | custom-call | flops 1000000 | bytes 100000 | tf_op jit(solution)/shard_map/c4/pallas_call | solution.py:681
  494.1 4.9 c4.16
  522.0 6.7 %collective-permute-done.64.refs_4_ = bf16[512,768]{1,0:T(8,128)(2,1)} collective-permute-done((bf16[512,768]{1,0:T(8,128)(2,1)}, bf16[512,768]{1,0:T(8,128)(2,1)}, u32[]{:S(2)}, u32[]{:S(2)}) %collective-permute-start.64) | collective-permute-done | bytes 786464 | tf_op jit(solution)/shard_map/c4/ring_y/ppermute | solution.py:63
  542.4 7.5 %collective-permute-done.73 = bf16[128,2048]{1,0:T(8,128)(2,1)S(1)} collective-permute-done((bf16[128,2048]{1,0:T(8,128)(2,1)S(1)}, bf16[128,2048]{1,0:T(8,128)(2,1)S(1)}, u32[]{:S(2)}, u32[]{:S(2)}) %collective-permute-start.73) | collective-permute-done | bytes 524320 | tf_op jit(solution)/shard_map/s10/team01/ppermute | solution.py:58
  568.9 7.6 %collective-permute-done.75.refs_5_ = bf16[512,768]{1,0:T(8,128)(2,1)S(1)} collective-permute-done((bf16[512,768]{1,0:T(8,128)(2,1)S(1)}, bf16[512,768]{1,0:T(8,128)(2,1)S(1)}, u32[]{:S(2)}, u32[]{:S(2)}) %collective-permute-start.75) | collective-permute-done | bytes 786464 | tf_op jit(solution)/shard_map/s10/ring_h/ppermute | solution.py:63
  580.7 5.4 collective-permute-start.77
  590.8 9.5 %collective-permute-start.81 = (bf16[128,1024]{1,0:T(8,128)(2,1)}, bf16[128,1024]{1,0:T(8,128)(2,1)}, u32[]{:S(2)}, u32[]{:S(2)}) collective-permute-start(bf16[128,1024]{1,0:T(8,128)(2,1)} %get-tuple-element.364), channel_id=1, source_target_pairs={{0,8},{2,10},{8,0},{10,2},{1,9},{3,11},{9,1},{11,3},{4,12},{6,14},... | collective-permute-start | bytes 786440 | tf_op jit(solution)/shard_map/s11/team10/ppermute | solution.py:58
  630.8 9.9 %collective-permute-done.87.refs_3_ = bf16[128,2048]{1,0:T(8,128)(2,1)S(1)} collective-permute-done((bf16[128,2048]{1,0:T(8,128)(2,1)S(1)}, bf16[128,2048]{1,0:T(8,128)(2,1)S(1)}, u32[]{:S(2)}, u32[]{:S(2)}) %collective-permute-start.87) | collective-permute-done | bytes 524320 | tf_op jit(solution)/shard_map/s12/team11/ppermute | solution.py:58
  (566 shorter events, 326.3 us)
Async XLA Ops:
  31.7 41.0 %collective-permute-start.4 = (bf16[512,1024]{1,0:T(8,128)(2,1)S(1)}, bf16[512,1024]{1,0:T(8,128)(2,1)S(1)}, u32[]{:S(2)}, u32[]{:S(2)}) collective-permute-start(bf16[512,1024]{1,0:T(8,128)(2,1)S(1)} %a1.3.refs_2_.refs_0_), channel_id=1, source_target_pairs={{0,4},{4,0},{1,5},{5,1},{2,6},{6,2},{3,7},{7,3},{8,12},{12,8},{9,1... | collective-permute-start | bytes 3145736 | tf_op jit(solution)/shard_map/a1/ring_y/ppermute | solution.py:63
  36.9 35.8 %collective-permute-start.8 = (bf16[512,768]{1,0:T(8,128)(2,1)S(1)}, bf16[512,768]{1,0:T(8,128)(2,1)}, u32[]{:S(2)}, u32[]{:S(2)}) collective-permute-start(bf16[512,768]{1,0:T(8,128)(2,1)S(1)} %slice.140), channel_id=1, source_target_pairs={{0,16},{16,0},{1,17},{17,1},{2,18},{18,2},{3,19},{19,3},{4,20},{20... | collective-permute-start | bytes 2359304 | tf_op jit(solution)/shard_map/a1/ring_h/ppermute | solution.py:63
  74.9 25.5 %collective-permute-start.9 = (bf16[512,2048]{1,0:T(8,128)(2,1)S(1)}, bf16[512,2048]{1,0:T(8,128)(2,1)}, u32[]{:S(2)}, u32[]{:S(2)}) collective-permute-start(bf16[512,2048]{1,0:T(8,128)(2,1)S(1)} %a2.1.refs_0_), channel_id=1, source_target_pairs={{0,1},{1,0},{2,3},{3,2},{4,5},{5,4},{6,7},{7,6},{8,9},{9,8},{10,11... | collective-permute-start | bytes 6291464 | tf_op jit(solution)/shard_map/a2/ring_tp/ppermute | solution.py:63
  104.5 36.2 %collective-permute-start.17 = (bf16[256,1024]{1,0:T(8,128)(2,1)}, bf16[256,1024]{1,0:T(8,128)(2,1)}, u32[]{:S(2)}, u32[]{:S(2)}) collective-permute-start(bf16[256,1024]{1,0:T(8,128)(2,1)} %get-tuple-element.377), channel_id=1, source_target_pairs={{0,16},{16,0},{1,17},{17,1},{2,18},{18,2},{3,19},{19,3},{4,20},{20... | collective-permute-start | bytes 1572872 | tf_op jit(solution)/shard_map/c1/ring_h/ppermute | solution.py:63
  105.3 35.4 %collective-permute-start.16 = (bf16[128,2048]{1,0:T(8,128)(2,1)}, bf16[128,2048]{1,0:T(8,128)(2,1)}, u32[]{:S(2)}, u32[]{:S(2)}) collective-permute-start(bf16[128,2048]{1,0:T(8,128)(2,1)} %constant_dynamic-slice_fusion.4), channel_id=1, source_target_pairs={{0,0},{4,8},{8,4},{12,12},{1,1},{5,9},{9,5},{13,13},{2,2},{6,10},{... | collective-permute-start | bytes 1572872 | tf_op jit(solution)/shard_map/c1/flip/ppermute | solution.py:357
  113.4 26.6 %collective-permute-start.19 = (bf16[128,1024]{1,0:T(8,128)(2,1)}, bf16[128,1024]{1,0:T(8,128)(2,1)}, u32[]{:S(2)}, u32[]{:S(2)}) collective-permute-start(bf16[128,1024]{1,0:T(8,128)(2,1)} %get-tuple-element.374), channel_id=1, source_target_pairs={{0,8},{2,10},{8,0},{10,2},{1,9},{3,11},{9,1},{11,3},{4,12},{6,14},... | collective-permute-start | bytes 786440 | tf_op jit(solution)/shard_map/c1/team10/ppermute | solution.py:58
  113.4 27.3 %collective-permute-start.20 = (bf16[128,1024]{1,0:T(8,128)(2,1)}, bf16[128,1024]{1,0:T(8,128)(2,1)}, u32[]{:S(2)}, u32[]{:S(2)}) collective-permute-start(bf16[128,1024]{1,0:T(8,128)(2,1)} %get-tuple-element.373), channel_id=1, source_target_pairs={{0,10},{2,8},{8,2},{10,0},{1,11},{3,9},{9,3},{11,1},{4,14},{6,12},... | collective-permute-start | bytes 786440 | tf_op jit(solution)/shard_map/c1/team11/ppermute | solution.py:58
  149.8 40.4 %collective-permute-start.26 = (bf16[768,1024]{1,0:T(8,128)(2,1)}, bf16[768,1024]{1,0:T(8,128)(2,1)}, u32[]{:S(2)}, u32[]{:S(2)}) collective-permute-start(bf16[768,1024]{1,0:T(8,128)(2,1)} %pad_maximum_fusion.1), channel_id=1, source_target_pairs={{0,4},{4,0},{1,5},{5,1},{2,6},{6,2},{3,7},{7,3},{8,12},{12,8},{9,1... | collective-permute-start | bytes 4718600 | tf_op jit(solution)/shard_map/s3/ring_y/ppermute | solution.py:63
  153.4 26.1 %collective-permute-start.25 = (bf16[256,1024]{1,0:T(8,128)(2,1)}, bf16[256,1024]{1,0:T(8,128)(2,1)S(1)}, u32[]{:S(2)}, u32[]{:S(2)}) collective-permute-start(bf16[256,1024]{1,0:T(8,128)(2,1)} %get-tuple-element.214), channel_id=1, source_target_pairs={{0,16},{16,0},{1,17},{17,1},{2,18},{18,2},{3,19},{19,3},{4,20},{20... | collective-permute-start | bytes 1572872 | tf_op jit(solution)/shard_map/s3/ring_h/ppermute | solution.py:63
  190.3 38.9 %collective-permute-start.31 = (bf16[768,1024]{1,0:T(8,128)(2,1)S(1)}, bf16[768,1024]{1,0:T(8,128)(2,1)S(1)}, u32[]{:S(2)}, u32[]{:S(2)}) collective-permute-start(bf16[768,1024]{1,0:T(8,128)(2,1)S(1)} %pad_maximum_fusion.2), channel_id=1, source_target_pairs={{0,4},{4,0},{1,5},{5,1},{2,6},{6,2},{3,7},{7,3},{8,12},{12,8},{9,1... | collective-permute-start | bytes 4718600 | tf_op jit(solution)/shard_map/s4/ring_y/ppermute | solution.py:63
  196.1 25.6 %collective-permute-start.30 = (bf16[256,1024]{1,0:T(8,128)(2,1)S(1)}, bf16[256,1024]{1,0:T(8,128)(2,1)}, u32[]{:S(2)}, u32[]{:S(2)}) collective-permute-start(bf16[256,1024]{1,0:T(8,128)(2,1)S(1)} %get-tuple-element.371), channel_id=1, source_target_pairs={{0,16},{16,0},{1,17},{17,1},{2,18},{18,2},{3,19},{19,3},{4,20},{20... | collective-permute-start | bytes 1572872 | tf_op jit(solution)/shard_map/s4/ring_h/ppermute | solution.py:63
  231.2 26.5 %collective-permute-start.33 = (bf16[256,1024]{1,0:T(8,128)(2,1)}, bf16[256,1024]{1,0:T(8,128)(2,1)}, u32[]{:S(2)}, u32[]{:S(2)}) collective-permute-start(bf16[256,1024]{1,0:T(8,128)(2,1)} %get-tuple-element.230), channel_id=1, source_target_pairs={{0,16},{16,0},{1,17},{17,1},{2,18},{18,2},{3,19},{19,3},{4,20},{20... | collective-permute-start | bytes 1572872 | tf_op jit(solution)/shard_map/c2/ring_h/ppermute | solution.py:63
  231.2 26.5 %collective-permute-start.34 = (bf16[256,1024]{1,0:T(8,128)(2,1)}, bf16[256,1024]{1,0:T(8,128)(2,1)}, u32[]{:S(2)}, u32[]{:S(2)}) collective-permute-start(bf16[256,1024]{1,0:T(8,128)(2,1)} %collective-permute-done.30.refs_1_.refs_2_), channel_id=1, source_target_pairs={{0,4},{4,0},{1,5},{5,1},{2,6},{6,2},{3,7},{7,3},{8,12},{12,8},{9,1... | collective-permute-start | bytes 1572872 | tf_op jit(solution)/shard_map/c2/ring_y/ppermute | solution.py:63
  259.3 25.3 %collective-permute-start.37 = (bf16[128,2048]{1,0:T(8,128)(2,1)S(1)}, bf16[128,2048]{1,0:T(8,128)(2,1)S(1)}, u32[]{:S(2)}, u32[]{:S(2)}) collective-permute-start(bf16[128,2048]{1,0:T(8,128)(2,1)S(1)} %get-tuple-element.369), channel_id=1, source_target_pairs={{0,16},{16,0},{1,17},{17,1},{2,18},{18,2},{3,19},{19,3},{4,20},{20... | collective-permute-start | bytes 1572872 | tf_op jit(solution)/shard_map/s5/ring_h/ppermute | solution.py:63
  326.7 26.1 %collective-permute-start.42 = (bf16[128,2048]{1,0:T(8,128)(2,1)S(1)}, bf16[128,2048]{1,0:T(8,128)(2,1)S(1)}, u32[]{:S(2)}, u32[]{:S(2)}) collective-permute-start(bf16[128,2048]{1,0:T(8,128)(2,1)S(1)} %get-tuple-element.254.refs_0_), channel_id=1, source_target_pairs={{0,2},{2,0},{8,10},{10,8},{1,3},{3,1},{9,11},{11,9},{4,6},{6,4},{1... | collective-permute-start | bytes 1572872 | tf_op jit(solution)/shard_map/s7/team01/ppermute | solution.py:58
  392.5 26.1 %collective-permute-start.50 = (bf16[512,1024]{1,0:T(8,128)(2,1)S(1)}, bf16[512,1024]{1,0:T(8,128)(2,1)S(1)}, u32[]{:S(2)}, u32[]{:S(2)}) collective-permute-start(bf16[512,1024]{1,0:T(8,128)(2,1)S(1)} %s8_.3), channel_id=1, source_target_pairs={{0,4},{4,0},{1,5},{5,1},{2,6},{6,2},{3,7},{7,3},{8,12},{12,8},{9,1... | collective-permute-start | bytes 3145736 | tf_op jit(solution)/shard_map/s8/ring_y/ppermute | solution.py:63
  393.0 25.6 %collective-permute-start.51 = (bf16[128,2048]{1,0:T(8,128)(2,1)S(1)}, bf16[128,2048]{1,0:T(8,128)(2,1)S(1)}, u32[]{:S(2)}, u32[]{:S(2)}) collective-permute-start(bf16[128,2048]{1,0:T(8,128)(2,1)S(1)} %get-tuple-element.266), channel_id=1, source_target_pairs={{0,2},{2,0},{8,10},{10,8},{1,3},{3,1},{9,11},{11,9},{4,6},{6,4},{1... | collective-permute-start | bytes 1572872 | tf_op jit(solution)/shard_map/s8/team01/ppermute | solution.py:58
  402.7 55.6 %collective-permute-start.56 = (bf16[512,1024]{1,0:T(8,128)(2,1)}, bf16[512,1024]{1,0:T(8,128)(2,1)}, u32[]{:S(2)}, u32[]{:S(2)}) collective-permute-start(bf16[512,1024]{1,0:T(8,128)(2,1)} %s9.5), channel_id=1, source_target_pairs={{0,4},{4,0},{1,5},{5,1},{2,6},{6,2},{3,7},{7,3},{8,12},{12,8},{9,1... | collective-permute-start | bytes 3145736 | tf_op jit(solution)/shard_map/s9/ring_y/ppermute | solution.py:63
  426.1 32.2 %collective-permute-start.57 = (bf16[128,2048]{1,0:T(8,128)(2,1)}, bf16[128,2048]{1,0:T(8,128)(2,1)}, u32[]{:S(2)}, u32[]{:S(2)}) collective-permute-start(bf16[128,2048]{1,0:T(8,128)(2,1)} %get-tuple-element.276.refs_0_), channel_id=1, source_target_pairs={{0,2},{2,0},{8,10},{10,8},{1,3},{3,1},{9,11},{11,9},{4,6},{6,4},{1... | collective-permute-start | bytes 1572872 | tf_op jit(solution)/shard_map/s9/team01/ppermute | solution.py:58
  426.8 31.5 %collective-permute-start.60 = (bf16[256,1024]{1,0:T(8,128)(2,1)}, bf16[256,1024]{1,0:T(8,128)(2,1)}, u32[]{:S(2)}, u32[]{:S(2)}) collective-permute-start(bf16[256,1024]{1,0:T(8,128)(2,1)} %s8_.5), channel_id=1, source_target_pairs={{0,16},{16,0},{1,17},{17,1},{2,18},{18,2},{3,19},{19,3},{4,20},{20... | collective-permute-start | bytes 1572872 | tf_op jit(solution)/shard_map/s9/ring_h/ppermute | solution.py:63
  470.6 28.4 %collective-permute-start.66 = (bf16[128,2048]{1,0:T(8,128)(2,1)S(1)}, bf16[128,2048]{1,0:T(8,128)(2,1)S(1)}, u32[]{:S(2)}, u32[]{:S(2)}) collective-permute-start(bf16[128,2048]{1,0:T(8,128)(2,1)S(1)} %get-tuple-element.368), channel_id=1, source_target_pairs={{0,0},{4,8},{8,4},{12,12},{1,1},{5,9},{9,5},{13,13},{2,2},{6,10},{... | collective-permute-start | bytes 1572872 | tf_op jit(solution)/shard_map/c4/flip/ppermute | solution.py:390
  471.3 27.7 %collective-permute-start.67 = (bf16[128,2048]{1,0:T(8,128)(2,1)S(1)}, bf16[128,2048]{1,0:T(8,128)(2,1)S(1)}, u32[]{:S(2)}, u32[]{:S(2)}) collective-permute-start(bf16[128,2048]{1,0:T(8,128)(2,1)S(1)} %get-tuple-element.367), channel_id=1, source_target_pairs={{0,8},{4,0},{8,12},{12,4},{1,9},{5,1},{9,13},{13,5},{2,10},{6,2},{... | collective-permute-start | bytes 1572872 | tf_op jit(solution)/shard_map/c4/flip/ppermute | solution.py:390
  474.2 25.7 %collective-permute-start.65 = (bf16[256,1024]{1,0:T(8,128)(2,1)S(1)}, bf16[256,1024]{1,0:T(8,128)(2,1)S(1)}, u32[]{:S(2)}, u32[]{:S(2)}) collective-permute-start(bf16[256,1024]{1,0:T(8,128)(2,1)S(1)} %copy-done.97), channel_id=1, source_target_pairs={{0,16},{16,0},{1,17},{17,1},{2,18},{18,2},{3,19},{19,3},{4,20},{20... | collective-permute-start | bytes 1572872 | tf_op jit(solution)/shard_map/c4/ring_h/ppermute | solution.py:63
  501.4 29.7 %collective-permute-start.68 = (bf16[512,2048]{1,0:T(8,128)(2,1)}, bf16[512,2048]{1,0:T(8,128)(2,1)}, u32[]{:S(2)}, u32[]{:S(2)}) collective-permute-start(bf16[512,2048]{1,0:T(8,128)(2,1)} %c4.16), channel_id=1, source_target_pairs={{0,1},{1,0},{2,3},{3,2},{4,5},{5,4},{6,7},{7,6},{8,9},{9,8},{10,11... | collective-permute-start | bytes 6291464 | tf_op jit(solution)/shard_map/c4/ring_tp/ppermute | solution.py:63
  503.2 31.9 %collective-permute-start.69 = (bf16[256,1024]{1,0:T(8,128)(2,1)}, bf16[256,1024]{1,0:T(8,128)(2,1)}, u32[]{:S(2)}, u32[]{:S(2)}) collective-permute-start(bf16[256,1024]{1,0:T(8,128)(2,1)} %copy-done.95), channel_id=1, source_target_pairs={{0,16},{16,0},{1,17},{17,1},{2,18},{18,2},{3,19},{19,3},{4,20},{20... | collective-permute-start | bytes 1572872 | tf_op jit(solution)/shard_map/c4/ring_h/ppermute | solution.py:63
  539.2 28.7 %collective-permute-start.71 = (bf16[512,1024]{1,0:T(8,128)(2,1)S(1)}, bf16[512,1024]{1,0:T(8,128)(2,1)S(1)}, u32[]{:S(2)}, u32[]{:S(2)}) collective-permute-start(bf16[512,1024]{1,0:T(8,128)(2,1)S(1)} %s10.3), channel_id=1, source_target_pairs={{0,4},{4,0},{1,5},{5,1},{2,6},{6,2},{3,7},{7,3},{8,12},{12,8},{9,1... | collective-permute-start | bytes 3145736 | tf_op jit(solution)/shard_map/s10/ring_y/ppermute | solution.py:63
  540.3 36.2 %collective-permute-start.75 = (bf16[512,768]{1,0:T(8,128)(2,1)S(1)}, bf16[512,768]{1,0:T(8,128)(2,1)S(1)}, u32[]{:S(2)}, u32[]{:S(2)}) collective-permute-start(bf16[512,768]{1,0:T(8,128)(2,1)S(1)} %c4.15), channel_id=1, source_target_pairs={{0,16},{16,0},{1,17},{17,1},{2,18},{18,2},{3,19},{19,3},{4,20},{20... | collective-permute-start | bytes 2359304 | tf_op jit(solution)/shard_map/s10/ring_h/ppermute | solution.py:63
  542.0 26.9 %collective-permute-start.72 = (bf16[128,2048]{1,0:T(8,128)(2,1)S(1)}, bf16[128,2048]{1,0:T(8,128)(2,1)S(1)}, u32[]{:S(2)}, u32[]{:S(2)}) collective-permute-start(bf16[128,2048]{1,0:T(8,128)(2,1)S(1)} %get-tuple-element.296), channel_id=1, source_target_pairs={{0,2},{2,0},{8,10},{10,8},{1,3},{3,1},{9,11},{11,9},{4,6},{6,4},{1... | collective-permute-start | bytes 1572872 | tf_op jit(solution)/shard_map/s10/team01/ppermute | solution.py:58
  550.1 27.6 %collective-permute-start.74 = (bf16[128,2048]{1,0:T(8,128)(2,1)S(1)}, bf16[128,2048]{1,0:T(8,128)(2,1)S(1)}, u32[]{:S(2)}, u32[]{:S(2)}) collective-permute-start(bf16[128,2048]{1,0:T(8,128)(2,1)S(1)} %add_convert_fusion.1), channel_id=1, source_target_pairs={{0,8},{2,10},{8,0},{10,2},{1,9},{3,11},{9,1},{11,3},{4,12},{6,14},... | collective-permute-start | bytes 1572872 | tf_op jit(solution)/shard_map/s10/team10/ppermute | solution.py:58
  561.3 29.5 %collective-permute-start.78 = (bf16[512,1024]{1,0:T(8,128)(2,1)}, bf16[512,1024]{1,0:T(8,128)(2,1)}, u32[]{:S(2)}, u32[]{:S(2)}) collective-permute-start(bf16[512,1024]{1,0:T(8,128)(2,1)} %pad_maximum_fusion.5), channel_id=1, source_target_pairs={{0,4},{4,0},{1,5},{5,1},{2,6},{6,2},{3,7},{7,3},{8,12},{12,8},{9,1... | collective-permute-start | bytes 3145736 | tf_op jit(solution)/shard_map/s11/ring_y/ppermute | solution.py:63
  580.7 33.4 %collective-permute-start.77 = (bf16[128,2048]{1,0:T(8,128)(2,1)}, bf16[128,2048]{1,0:T(8,128)(2,1)}, u32[]{:S(2)}, u32[]{:S(2)}) collective-permute-start(bf16[128,2048]{1,0:T(8,128)(2,1)} %s11.7), channel_id=1, source_target_pairs={{0,0},{4,8},{8,4},{12,12},{1,1},{5,9},{9,5},{13,13},{2,2},{6,10},{... | collective-permute-start | bytes 1572872 | tf_op jit(solution)/shard_map/s11/ppermute | solution.py:79
  586.0 26.1 %collective-permute-start.79 = (bf16[512,256]{1,0:T(8,128)(2,1)}, bf16[512,256]{1,0:T(8,128)(2,1)}, u32[]{:S(2)}, u32[]{:S(2)}) collective-permute-start(bf16[512,256]{1,0:T(8,128)(2,1)} %c4.13), channel_id=1, source_target_pairs={{0,16},{16,0},{1,17},{17,1},{2,18},{18,2},{3,19},{19,3},{4,20},{20... | collective-permute-start | bytes 786440 | tf_op jit(solution)/shard_map/s11/ring_h/ppermute | solution.py:63
  (191 other events, 2054.3 us)

commit v5 on v4

--- a/solution.py
+++ b/solution.py
@@ -33,6 +33,12 @@
 
 def mm_tn(left, right):
     return dot(left, right, ((0,), (0,)))
+
+
+def modulo(value, size):
+    if isinstance(size, int) and size & (size - 1) == 0:
+        return jnp.bitwise_and(value, size - 1)
+    return lax.rem(value, size)
 
 
 class Team:
@@ -63,11 +69,36 @@
             return lax.ppermute(value, name, [(i, (i + step) % size) for i in range(size)])
 
     def slot(self, offset, back=True):
+        return self.slots[back][self.offsets.index(offset)]
+
+    def plan(self, dealing, home):
+        hs, h, l, y = self.sizes["h"], self.at["h"], self.at["l"], self.at["y"]
+        own = pick(home, h * 2 + y)
+        needs = [
+            modulo(pick(home, modulo(h + step, hs) * 2 + y), 2) == y for step in range(hs)
+        ]
+        sources = [pick(dealing, h * 2 + target) for target in (y, 1 - y)]
+        steps = [modulo(h - lax.shift_right_logical(source, 1) + hs, hs) for source in sources]
+        here = pick(dealing, h * 2 + l)
+        return (
+            [self.slot_(offset, back) for back in (False, True) for offset in self.offsets]
+            + [l == y, modulo(h - lax.shift_right_logical(own, 1) + hs, hs), modulo(here, 2) == l]
+            + steps
+            + needs
+        )
+
+    def set_plan(self, plan):
+        self.slots = {False: plan[: self.members], True: plan[self.members : 2 * self.members]}
+        rest = plan[2 * self.members :]
+        self.same, self.in_step, self.out_first = rest[:3]
+        self.out_steps, self.needs = rest[3:5], rest[5:]
+
+    def slot_(self, offset, back):
         ls, xs = self.sizes["l"], self.sizes["x"]
         dl, dx = offset
         if back:
             dl, dx = -dl, -dx
-        return lax.rem(self.at["l"] + dl + ls, ls) * xs + lax.rem(self.at["x"] + dx + xs, xs)
+        return modulo(self.at["l"] + dl + ls, ls) * xs + modulo(self.at["x"] + dx + xs, xs)
 
 
 def fence(*values):
@@ -75,8 +106,11 @@
 
 
 def swap_home(value):
-    perm = [(l * 2 + y, y * 2 + l) for l in range(2) for y in range(2)]
-    return lax.ppermute(value, ("l", "y"), perm)
+    return lax.ppermute(value, ("l", "y"), [(1, 2), (2, 1)])
+
+
+def swapped_home(team, value, moved):
+    return jnp.where(team.same, value, moved)
 
 
 def team_pieces(team, piece):
@@ -97,7 +131,7 @@
 def row_blocks(team):
     ts = team.sizes["tp"]
     return [
-        team.slot(offset) * ts + lax.rem(team.at["tp"] - step + ts, ts)
+        team.slot(offset) * ts + modulo(team.at["tp"] - step + ts, ts)
         for step in range(ts)
         for offset in team.offsets
     ]
@@ -112,6 +146,12 @@
 def core_total(team, rows, pieces, half_rows, got):
     total, *sent = spread(rows, 0, pieces, half_rows, got, team.members)
     return total, sent
+
+
+def team_send_direct(team, sent):
+    return [
+        team.shift(value, offset, back=True) for value, offset in zip(sent, team.offsets[1:])
+    ]
 
 
 def team_send(team, sent):
@@ -174,7 +214,7 @@
     slots = jnp.stack([team.slot(offset) for offset in team.offsets]).astype(jnp.int32)
     whole = [pl.BlockSpec(piece.shape, lambda n: (0, 0)) for piece in pieces]
     return pl.pallas_call(
-        functools.partial(kernel, widths),
+        kernel if widths is None else functools.partial(kernel, widths),
         grid=(1,),
         in_specs=[pl.BlockSpec(memory_space=pltpu.SMEM)] + whole,
         out_specs=[pl.BlockSpec(shape.shape, lambda n: (0, 0)) for shape in shapes],
@@ -204,10 +244,25 @@
     )(*pieces)
 
 
-def near_rows(team, pieces, widths):
-    rows = pieces[0].shape[0] * team.members
-    shapes = [jax.ShapeDtypeStruct((rows, width), LOWER) for width in widths]
-    return place(team, place_rows_kernel, pieces, widths, shapes)
+def place_halves_kernel(slots_ref, *refs):
+    pieces, outs = refs[:-2], refs[-2:]
+    split = len(pieces) // 2
+    for j, piece in enumerate(pieces):
+        height = piece.shape[0]
+        for part, out in enumerate(outs):
+
+            @pl.when(lax.div(slots_ref[j], split) == part)
+            def _():
+                row = pl.multiple_of(lax.rem(slots_ref[j], split) * height, height)
+                out[pl.ds(row, height), :] = piece[...]
+
+
+def near_rows(team, pieces, parts=1):
+    height, width = pieces[0].shape
+    shape = jax.ShapeDtypeStruct((height * team.members // parts, width), LOWER)
+    if parts == 1:
+        return place(team, place_rows_kernel, pieces, [width], [shape])
+    return place(team, place_halves_kernel, pieces, None, [shape] * 2)
 
 
 def across(team, value):
@@ -316,7 +371,7 @@
     for dy in range(2):
         for dh in range(hs):
             for l in range(2):
-                h, y = lax.rem(team.at["h"] + dh, hs), lax.rem(team.at["y"] + dy, 2)
+                h, y = modulo(team.at["h"] + dh, hs), modulo(team.at["y"] + dy, 2)
                 table.append((h * 2 + l) * 2 + y)
     return permute_columns(value, table)
 
@@ -327,7 +382,7 @@
     for h in range(hs):
         for l in range(2):
             for y in range(2):
-                dh, dy = lax.rem(h - team.at["h"] + hs, hs), lax.rem(y - team.at["y"] + 2, 2)
+                dh, dy = modulo(h - team.at["h"] + hs, hs), modulo(y - team.at["y"] + 2, 2)
                 table.append((dy * hs + dh) * 2 + l)
     return permute_columns(value, table)
 
@@ -349,51 +404,31 @@
 
 
 def deal_flip(team, piece, flip):
-    perm = []
-    for l in range(2):
-        for y in range(2):
-            perm.append((l * 2 + y, y * 2 + (l if flip == 0 else 1 - l)))
+    if flip == 0:
+        return swap_home(piece)
+    perm = [(l * 2 + y, y * 2 + 1 - l) for l in range(2) for y in range(2)]
     with jax.named_scope("flip"):
         return lax.ppermute(piece, ("l", "y"), perm)
 
 
-def deal_across(team, home, two):
-    hs = team.sizes["h"]
-
-    def needed(h):
-        group = pick(home, h * 2 + team.at["y"])
-        return jnp.where(lax.rem(group, 2) == team.at["y"], two[0], two[1])
-
-    return [needed(team.at["h"])] + [
-        team.ring(needed(lax.rem(team.at["h"] + step, hs)), "h", step) for step in range(1, hs)
-    ]
-
-
-def dealt_in(team, home, pieces):
-    hs = team.sizes["h"]
-    group = pick(home, team.at["h"] * 2 + team.at["y"])
-    return choose(pieces, lax.rem(team.at["h"] - group // 2 + hs, hs))
-
-
-def deal(team, dealing, pieces):
-    hs = team.sizes["h"]
-    got = []
-    for flip in range(2):
-        target = team.at["y"] if flip == 0 else 1 - team.at["y"]
-        seq = pick(dealing, team.at["h"] * 2 + target)
-        sent = choose(pieces, lax.rem(team.at["h"] - seq // 2 + hs, hs))
-        perm = []
-        for l in range(2):
-            for y in range(2):
-                perm.append((l * 2 + y, (y if flip == 0 else 1 - y) * 2 + l))
-        with jax.named_scope("flip"):
-            got.append(lax.ppermute(sent, ("l", "y"), perm))
-    return got
-
-
-def dealt_out(team, dealing, got):
-    seq = pick(dealing, team.at["h"] * 2 + team.at["l"])
-    return jnp.where(lax.rem(seq, 2) == team.at["l"], got[0], got[1])
+def deal_across(team, two):
+    first = swapped_home(team, two[0], two[1])
+    chosen = [jnp.where(need, first, two[2]) for need in team.needs]
+    return chosen[:1] + [team.ring(value, "h", step) for step, value in enumerate(chosen) if step]
+
+
+def dealt_in(team, pieces):
+    return choose(pieces, team.in_step)
+
+
+def deal(team, pieces):
+    first, second = (choose(pieces, step) for step in team.out_steps)
+    perm = [(l * 2 + y, (1 - y) * 2 + l) for l in range(2) for y in range(2)]
+    return [first, swap_home(first), lax.ppermute(second, ("l", "y"), perm)]
+
+
+def dealt_out(team, got):
+    return jnp.where(team.out_first, swapped_home(team, got[0], got[1]), got[2])
 
 
 def join_cores(team, piece):
@@ -401,7 +436,7 @@
     out = jnp.zeros((ts,) + piece.shape, piece.dtype)
     for step in range(ts):
         other = team.ring(piece, "tp", step) if step else piece
-        out = put(out, other[None], (lax.rem(team.at["tp"] - step + ts, ts), 0, 0))
+        out = put(out, other[None], (modulo(team.at["tp"] - step + ts, ts), 0, 0))
     return out.reshape(-1, piece.shape[-1])
 
 
@@ -628,10 +663,15 @@
 
 
 def outer(lefts, rights, first, count, adds, offset, column):
-    height, width = rights[0].shape
+    height = lefts[0].shape[0]
+    rights = [right if isinstance(right, tuple) else (right, 0) for right in rights]
+    width = rights[0][0].shape[1]
     block = math.gcd(256, count)
     in_specs = [pl.BlockSpec((height, block), lambda i: (0, first // block + i)) for _ in lefts]
-    in_specs += [pl.BlockSpec((height, width), lambda i: (0, 0)) for _ in rights]
+    for _, row in rights:
+        in_specs.append(
+            pl.BlockSpec((height, width), functools.partial(lambda r, i: (r, 0), row))
+        )
     tile = pl.BlockSpec((block, width), lambda i: (i, 0))
     add_tile = pl.BlockSpec((block, width), lambda i: (offset // block + i, 0))
     first_tile = pl.BlockSpec((block, width), lambda i: (offset // block + i, column))
@@ -643,7 +683,7 @@
         out_shape=jax.ShapeDtypeStruct((count, width), LOWER),
         cost_estimate=LIGHT,
         compiler_params=KERNEL,
-    )(*lefts, *rights, *adds)
+    )(*lefts, *[right for right, _ in rights], *adds)
 
 
 def query_block(rows):
@@ -728,6 +768,8 @@
     my_slot = team.at["l"] * team.sizes["x"] + team.at["x"]
     seq_ids = jnp.arange(dealing.shape[0], dtype=jnp.int32)
     home = jnp.sum(jnp.where(dealing[None, :] == seq_ids[:, None], seq_ids[None, :], 0), axis=1)
+    plan = team.plan(dealing, home)
+    team.set_plan(plan)
     live_count = pick(lengths, team.at["h"] * 2 + team.at["y"])
     limits = live_count - jnp.stack(row_blocks(team)).astype(jnp.int32) * row_count
     query_live = (jnp.arange(row_count, dtype=jnp.int32) < limits[0])[:, None]
@@ -748,14 +790,17 @@
         return [(array, 0) for array in arrays]
 
     with jax.named_scope("a0"):
-        own = swap_home(lax.dynamic_slice_in_dim(tokens, half_at, row_count, 0))
+        mine = lax.dynamic_slice_in_dim(tokens, half_at, row_count, 0)
+        own = swap_home(mine)
         share = share_columns(team, [w_query, w_key, w_value, w_out])
-        own, w_up, w_down, bias_qkv, bias_up, *share = fence(
-            own, w_up, w_down, bias_qkv, bias_up, *share
-        )
+        own, w_up, w_down, bias_qkv, bias_up, limits, query_live, *rest = fence(
+            own, w_up, w_down, bias_qkv, bias_up, limits, query_live, *share, *plan
+        )
+        share, plan = rest[:members], rest[members:]
+        team.set_plan(plan)
     with jax.named_scope("a1"):
-        own = to_team_order(team, own)
-        (near_att,) = near_rows(team, share, [4 * wide])
+        own = to_team_order(team, swapped_home(team, mine, own))
+        (near_att,) = near_rows(team, share)
         pieces = team_pieces(team, own)
         cross_qkv = across(team, near_att[:, : 3 * wide])
         (side_att,) = beside(team, [near_att])
@@ -777,76 +822,82 @@
         far_qkv, cross_out = rest[:steps], rest[steps:]
     qkv_mat = first_column([near_att, *cross_qkv, side_att, *far_qkv])
     with jax.named_scope("c1"):
-        (near_up,) = near_rows(team, share, [tall])
-        up_a, up_b = halves(near_up)
+        up_a, up_b = near_rows(team, share, 2)
         cross_up_a = across(team, up_a)
         far_out = beside(team, cross_out)
         cot_half = lax.dynamic_slice_in_dim(cotangent, half_at, row_count, 0)
-        cot_one = deal_flip(team, cot_half, 0)
         share = share_columns(team, [w_down])
         (qkv,) = project("bias", in_parts, qkv_mat, 3 * wide, bias_qkv)
         attended, log_sum = attend(qkv, limits, score_scale)
         out_mat = [(near_att, 3), *first_column(cross_out), (side_att, 3), *first_column(far_out)]
-        got = core_send(team, attended, out_mat, half_rows, cot_one, *cross_up_a, *share)
+        got = core_send(team, attended, out_mat, half_rows, *cross_up_a, *share)
         total, sent = core_total(team, attended, out_mat, half_rows, got)
-        up_b, near_up, cot_half, cot_one, *rest = fence(
-            up_b, near_up, cot_half, cot_one, *cross_up_a, *share, *sent
+        up_a, up_b, cot_half, *rest = fence(
+            up_a, up_b, cot_half, *cross_up_a, *share, *sent
         )
         cross_up_a, rest = rest[:steps], rest[steps:]
         share, sent = rest[:members], rest[members:]
     with jax.named_scope("s3"):
         got = team_send(team, sent)
         cross_up_b = across(team, up_b)
-        (near_down,) = near_rows(team, share, [tall])
-        side = beside(team, [jnp.concatenate([near_up, *cross_up_a], axis=0)])
-        near_down, *rest = fence(near_down, *got, *cross_up_b, *side)
+        down_a, down_b = near_rows(team, share, 2)
+        side = beside(team, [jnp.concatenate([up_a, *cross_up_a], axis=0)])
+        cot_one = deal_flip(team, cot_half, 0)
+        cot_half, cot_one, up_b, down_a, down_b, *rest = fence(
+            cot_half, cot_one, up_b, down_a, down_b, *got, *cross_up_b, *side
+        )
         got, rest = rest[:team_count], rest[team_count:]
         cross_up_b, side_a = rest[:steps], rest[steps]
     with jax.named_scope("s4"):
         branch = team_total(total, got) + b_out
         middle, mid_hat, mid_rate = layer_norm(own.astype(WIDE) + branch, gain_mid, shift_mid)
         pieces = team_pieces(team, middle.astype(LOWER))
-        down_a, down_b = halves(near_down)
         cross_down_a = across(team, down_a)
-        side = beside(team, [jnp.concatenate([near_down, *cross_up_b], axis=0)])
-        near_down, down_b, *rest = fence(near_down, down_b, *pieces, *cross_down_a, *side)
+        side = beside(team, [jnp.concatenate([up_b, *cross_up_b], axis=0)])
+        cot_two = [cot_half, cot_one, deal_flip(team, cot_half, 1)]
+        down_a, down_b, *rest = fence(
+            down_a, down_b, *cot_two, *pieces, *cross_down_a, *side
+        )
+        cot_two, rest = rest[:3], rest[3:]
         pieces, rest = rest[:members], rest[members:]
         cross_down_a, side_b = rest[:steps], rest[steps]
-    whole, part = near_down.shape[0], down_a.shape[0]
-    side_up, side_down = side_a[:whole], side_b[:whole]
-    far_up_a, far_up_b = (
-        [side[whole + k * part : whole + (k + 1) * part] for k in range(steps)]
-        for side in (side_a, side_b)
-    )
+    part_rows = down_a.shape[0]
+
+    def split_side(side):
+        blocks = [side[k * part_rows : (k + 1) * part_rows] for k in range(steps + 1)]
+        return blocks[0], blocks[1:]
+
+    side_up_a, far_up_a = split_side(side_a)
+    side_up_b, far_up_b = split_side(side_b)
     up_mat = first_column(
-        [near_up]
+        [up_a, up_b]
         + pairs(cross_up_a, cross_up_b)
-        + [side_up]
+        + [side_up_a, side_up_b]
         + pairs(far_up_a, far_up_b)
     )
     with jax.named_scope("c2"):
         half = stack_rows(pieces)
         other = cores(team, half)
         cross_down_b = across(team, down_b)
-        far_down_a = beside(team, cross_down_a)
+        side = beside(team, [jnp.concatenate([down_a, *cross_down_a], axis=0)])
         mid_parts = [half] + other
         hidden, active = [], []
         for part in mid_parts:
             hidden_part, active_part = project("gelu", [part], up_mat, tall, bias_up)
             hidden.append(hidden_part)
             active.append(active_part)
-        cot_two = [cot_one, deal_flip(team, cot_half, 1)]
-        rest = fence(*active, *cross_down_b, *far_down_a, *cot_two)
+        down_b, *rest = fence(down_b, *active, *cross_down_b, *side, *cot_two)
         active, rest = rest[:ts], rest[ts:]
-        cross_down_b, rest = rest[:steps], rest[steps:]
-        far_down_a, cot_two = rest[:steps], rest[steps:]
+        cross_down_b, side, cot_two = rest[:steps], rest[steps], rest[steps + 1 :]
+        side_down_a, far_down_a = split_side(side)
     with jax.named_scope("s5"):
-        far_down_b = beside(team, cross_down_b)
-        cot_pieces = deal_across(team, home, cot_two)
+        (side,) = beside(team, [jnp.concatenate([down_b, *cross_down_b], axis=0)])
+        side_down_b, far_down_b = split_side(side)
+        cot_pieces = deal_across(team, cot_two)
         down_mat = first_column(
-            [near_down]
+            [down_a, down_b]
             + pairs(cross_down_a, cross_down_b)
-            + [side_down]
+            + [side_down_a, side_down_b]
             + pairs(far_down_a, far_down_b)
         )
         got = core_send(team, active, down_mat, half_rows, *cot_pieces)
@@ -854,8 +905,8 @@
         rest = fence(*sent, *cot_pieces)
         sent, cot_pieces = rest[: members - 1], rest[members - 1 :]
     with jax.named_scope("s6"):
-        cot = to_team_order(team, dealt_in(team, home, cot_pieces))
-        cot, *got = fence(cot, *team_send(team, sent))
+        cot = to_team_order(team, dealt_in(team, cot_pieces))
+        cot, *got = fence(cot, *team_send_direct(team, sent))
     with jax.named_scope("s7"):
         result = team_total(total, got) + b_down
         normed, end_hat, end_rate = layer_norm(middle + result, gain_end, shift_end)
@@ -916,16 +967,16 @@
         half = stack_rows(pieces)
         other = cores(team, half)
         got_up_a, got_up_b = flow_up.go(cross_up_a), flow_up.go(cross_up_b)
-        out_two = deal(team, dealing, out_pieces)
+        out_two = deal(team, out_pieces)
         branch_parts = [half] + other
-        attended_parts = [attended[k * half_rows : (k + 1) * half_rows] for k in range(ts)]
+        attended_parts = [(attended, k) for k in range(ts)]
         flow_out = Grads(team, branch_parts, attended_parts)
         (far_out,) = beside(team, [flow_out.send_far()])
         (grad_attended,) = project("plain", branch_parts, out_mat, wide)
         grad_qkv = attend_back(qkv, grad_attended, log_sum, limits, score_scale)
         got = core_send(team, grad_qkv, qkv_mat, half_rows, far_out, *got_up_a, *out_two)
         total, sent = core_total(team, grad_qkv, qkv_mat, half_rows, got)
-        grad_parts = [grad_qkv[k * half_rows : (k + 1) * half_rows] for k in range(ts)]
+        grad_parts = [(grad_qkv, k) for k in range(ts)]
         flow_qkv = Grads(team, in_parts, grad_parts)
         qkv_sum = jnp.sum(grad_qkv.astype(WIDE), axis=0)
         grad_bup = sum(jnp.sum(part.astype(WIDE), axis=0) for part in grad_hidden)
@@ -935,43 +986,42 @@
             for part in (qkv_sum[:wide], qkv_sum[2 * wide :], grad_bup)
         ]
         sums = jnp.concatenate([by_row.reshape(-1)] + by_slot).reshape(-1, 128)
-        sums = add_ring(team, sums, "l")
+        sums = add_ring(team, sums, "x")
         (far_qkv,) = beside(team, [flow_qkv.send_far()])
-        cross_out, cross_qkv = flow_out.cross(far_out), flow_qkv.cross(far_qkv)
-        sums, near_down, *rest = fence(
-            sums, near_down, *cross_out, *cross_qkv, *sent, *got_up_a, *got_up_b, *out_two
-        )
-        cross_out, cross_qkv, rest = rest[:steps], rest[steps : 2 * steps], rest[2 * steps :]
+        cross_out = flow_out.cross(far_out)
+        sums, near_down, far_qkv, *rest = fence(
+            sums, near_down, far_qkv, *cross_out, *sent, *got_up_a, *got_up_b, *out_two
+        )
+        cross_out, rest = rest[:steps], rest[steps:]
         sent, rest = rest[: members - 1], rest[members - 1 :]
         got_up_a, got_up_b, out_two = rest[:steps], rest[steps : 2 * steps], rest[2 * steps :]
-
     with jax.named_scope("s10"):
         got = team_send(team, sent)
         total_down = flow_down.total(
             near_down,
             [jnp.concatenate(both, axis=0) for both in zip(got_down_a, got_down_b)],
         )
-        got_qkv = flow_qkv.go(cross_qkv)
+        got_qkv = flow_qkv.go(flow_qkv.cross(far_qkv))
         (near_up,) = beside(team, [flow_up.send_near()])
-        sums = add_ring(team, sums, "x")
+        sums = add_ring(team, sums, "l")
         sums, total_down, near_up, *rest = fence(
             sums, total_down, near_up, *out_two, *got, *got_qkv, *cross_out
         )
-        out_two, rest = rest[:2], rest[2:]
+        out_two, rest = rest[:3], rest[3:]
         got, rest = rest[:team_count], rest[team_count:]
         got_qkv, cross_out = rest[:steps], rest[steps:]
     with jax.named_scope("s11"):
         got_out = flow_out.go(cross_out)
         home_down = home_pieces(team, total_down)
         grad_own = (team_total(total, got) + grad_inner).astype(LOWER)
-        swapped = swap_home(from_team_order(team, grad_own))
+        grad_own = from_team_order(team, grad_own)
+        swapped = swap_home(grad_own)
         near_att = jnp.concatenate([flow_qkv.send_near(), flow_out.send_near()], axis=1)
         (near_att,) = beside(team, [near_att])
         total_up = flow_up.total(
             near_up, [jnp.concatenate(both, axis=0) for both in zip(got_up_a, got_up_b)]
         )
         total_out = flow_out.total(near_att, got_out, 3)
-        sums = add_ring(team, sums, "y")
         total_qkv = flow_qkv.total(near_att, got_qkv, 0)
         sums, swapped, total_up, total_out, total_qkv, *rest = fence(
             sums, swapped, total_up, total_out, total_qkv, *home_down, *out_two
@@ -979,10 +1029,10 @@
         home_down, out_two = rest[:members], rest[members:]
         (grad_down,) = home_join(team, home_down, [tall])
     with jax.named_scope("s12"):
-        grad_tokens = join_cores(team, swapped)
+        grad_tokens = join_cores(team, swapped_home(team, grad_own, swapped))
         home_all = home_pieces(team, jnp.concatenate([total_up, total_qkv, total_out], axis=1))
-        output = join_cores(team, dealt_out(team, dealing, out_two))
-        sums = add_ring(team, sums, "h").reshape(-1)
+        output = join_cores(team, dealt_out(team, out_two))
+        sums = add_ring(team, add_ring(team, sums, "h"), "y").reshape(-1)
         grad_up, grad_query, grad_key, grad_value, grad_out = home_join(
             team, home_all, [tall] + [wide] * 4
         )

time: 654 us -> 639 us (0.977)
  local copies, waits for them, and re-layouts: 55.2 us -> 41.1 us
  Pallas kernels: 138 us -> 126 us
  starting transfers between devices: 105 us -> 114 us
  between operations: 15 us -> 7.12 us
    ppermute x44, waiting for transfers between devices: 108 us -> 143 us  [ring(): lax.ppermute(value, name, [(i, (i + step) % size) for i in range(size)])]
    ppermute x39, waiting for transfers between devices: 191 us -> 156 us  [shift_(): return lax.ppermute(value, TEAM, perm)]
    ppermute x39, starting transfers between devices: 52.5 us -> 71.3 us  [shift_(): return lax.ppermute(value, TEAM, perm)]
    unnamed x271 -> x289, local copies, waits for them, and re-layouts: 28.2 us -> 21 us
  transfers between devices with their start and end apart: 89 -> 89, of which waited for: 46 -> 44; matrix products, arithmetic and copies ran while one was open for 7% -> 7% of each run, Pallas kernels for 19% -> 18%
where the time goes in v5:
time: 639 us; the launch traced here: 629 us
  waiting for transfers between devices  308 us (48%)
  Pallas kernels  126 us (20%)
  starting transfers between devices  114 us (18%)
  local copies, waits for them, and re-layouts  41.1 us (6%)
  other arithmetic  31.9 us (5%)
  between operations  7.12 us (1%)
    ppermute x39, waiting for transfers between devices, shift_(): return lax.ppermute(value, TEAM, perm)  156 us
    ppermute x44, waiting for transfers between devices, ring(): lax.ppermute(value, name, [(i, (i + step) % size) for i in range(size)])  143 us
    ppermute x39, starting transfers between devices, shift_(): return lax.ppermute(value, TEAM, perm)  71.3 us
    pallas_call x19, Pallas kernels, outer(): pl.pallas_call(functools.partial(outer_kernel, len(lefts), len(adds)), gr...  33.6 us
    ppermute x44, starting transfers between devices, ring(): lax.ppermute(value, name, [(i, (i + step) % size) for i in range(size)])  33.5 us
    pallas_call x6, Pallas kernels, project(): pl.pallas_call(functools.partial(project_kernel, mode, len(parts), len(pi...  25.8 us
    pallas_call x8, Pallas kernels, spread(): pl.pallas_call(functools.partial(spread_kernel, len(pieces), len(got), sp...  23.9 us
    unnamed x289, local copies, waits for them, and re-layouts  21 us
  transfers between devices with their start and end apart: 89, of which 44 were waited for; matrix products, arithmetic and copies ran while one was open for 7% of the time, Pallas kernels for 18%

profile of v5, /device:TPU:0, one launch (start us, length us, event | category | flops | bytes accessed | tf_op | source)
XLA Modules:
  0.0 628.8 jit_solution(8436716371838497113)
XLA Ops:
  26.0 13.5 %collective-permute-start.6 = (bf16[128,2048]{1,0:T(8,128)(2,1)}, bf16[128,2048]{1,0:T(8,128)(2,1)S(1)}, u32[]{:S(2)}, u32[]{:S(2)}) collective-permute-start(bf16[128,2048]{1,0:T(8,128)(2,1)} %a1.2.refs_0_), channel_id=1, source_target_pairs={{0,8},{2,10},{8,0},{10,2},{1,9},{3,11},{9,1},{11,3},{4,12},{6,14},... | collective-permute-start | bytes 1572872 | tf_op jit(solution)/shard_map/a1/team10/ppermute | solution.py:64
  43.5 17.3 %collective-permute-done.6.refs_2_ = bf16[128,2048]{1,0:T(8,128)(2,1)S(1)} collective-permute-done((bf16[128,2048]{1,0:T(8,128)(2,1)}, bf16[128,2048]{1,0:T(8,128)(2,1)S(1)}, u32[]{:S(2)}, u32[]{:S(2)}) %collective-permute-start.6) | collective-permute-done | bytes 524320 | tf_op jit(solution)/shard_map/a1/team10/ppermute | solution.py:64
  61.3 14.8 %collective-permute-done.8.refs_3_.refs_1_ = bf16[512,768]{1,0:T(8,128)(2,1)} collective-permute-done((bf16[512,768]{1,0:T(8,128)(2,1)S(1)}, bf16[512,768]{1,0:T(8,128)(2,1)}, u32[]{:S(2)}, u32[]{:S(2)}) %collective-permute-start.8) | collective-permute-done | bytes 786464 | tf_op jit(solution)/shard_map/a1/ring_h/ppermute | solution.py:69
  84.2 4.8 collective-permute-done.10.refs_1_
  90.3 10.0 %collective-permute-done.12.refs_3_ = bf16[128,1024]{1,0:T(8,128)(2,1)S(1)} collective-permute-done((bf16[128,1024]{1,0:T(8,128)(2,1)S(1)}, bf16[128,1024]{1,0:T(8,128)(2,1)S(1)}, u32[]{:S(2)}, u32[]{:S(2)}) %collective-permute-start.12) | collective-permute-done | bytes 262176 | tf_op jit(solution)/shard_map/a2/team11/ppermute | solution.py:64
  110.6 6.0 c1.5.query_ref.key_ref.value_ref
  116.6 9.8 %c1.6 = (bf16[1024,256]{1,0:T(8,128)(2,1)S(1)}, f32[2,1,1024]{2,1,0:T(1,128)S(1)}) custom-call(s32[8]{0:T(128)S(1)} %multiply_subtract_fusion.limits_ref, bf16[1024,768]{1,0:T(8,128)(2,1)S(1)} %c1.5.query_ref.key_ref.value_ref, bf16[1024,768]{1,0:T(8,128)(2,1)S(1)} %c1.5.query_ref.key_ref.value_ref, bf16[1024,768]{1,0:T(8,128)(2,1)S(1)} %c1.5.query_ref.key_ref.value_ref), custom_call_target="tpu_custom_call" | custom-call | flops 1000000 | bytes 100000 | tf_op jit(solution)/shard_map/c1/pallas_call | solution.py:696
  141.8 8.8 %collective-permute-done.23 = bf16[128,2048]{1,0:T(8,128)(2,1)S(1)} collective-permute-done((bf16[128,2048]{1,0:T(8,128)(2,1)S(1)}, bf16[128,2048]{1,0:T(8,128)(2,1)S(1)}, u32[]{:S(2)}, u32[]{:S(2)}) %collective-permute-start.23) | collective-permute-done | bytes 524320 | tf_op jit(solution)/shard_map/s3/team01/ppermute | solution.py:64
  156.0 5.5 collective-permute-done.22
  161.5 11.7 %collective-permute-done.26 = bf16[512,1024]{1,0:T(8,128)(2,1)} collective-permute-done((bf16[512,1024]{1,0:T(8,128)(2,1)}, bf16[512,1024]{1,0:T(8,128)(2,1)}, u32[]{:S(2)}, u32[]{:S(2)}) %collective-permute-start.26) | collective-permute-done | bytes 1048608 | tf_op jit(solution)/shard_map/s3/ring_y/ppermute | solution.py:69
  173.3 4.6 collective-permute-done.24
  186.8 20.5 %collective-permute-done.29.refs_2_ = bf16[128,2048]{1,0:T(8,128)(2,1)S(1)} collective-permute-done((bf16[128,2048]{1,0:T(8,128)(2,1)S(1)}, bf16[128,2048]{1,0:T(8,128)(2,1)S(1)}, u32[]{:S(2)}, u32[]{:S(2)}) %collective-permute-start.29) | collective-permute-done | bytes 524320 | tf_op jit(solution)/shard_map/s4/team10/ppermute | solution.py:64
  208.4 9.2 %collective-permute-done.27 = bf16[128,2048]{1,0:T(8,128)(2,1)S(1)} collective-permute-done((bf16[128,2048]{1,0:T(8,128)(2,1)}, bf16[128,2048]{1,0:T(8,128)(2,1)S(1)}, u32[]{:S(2)}, u32[]{:S(2)}) %collective-permute-start.27) | collective-permute-done | bytes 524320 | tf_op jit(solution)/shard_map/s4/flip/ppermute | solution.py:411
  222.4 4.6 c2.4
  228.4 4.4 c2.5
  232.9 13.4 %collective-permute-done.34.refs_3_.refs_4_ = bf16[256,1024]{1,0:T(8,128)(2,1)S(1)} collective-permute-done((bf16[256,1024]{1,0:T(8,128)(2,1)S(1)}, bf16[256,1024]{1,0:T(8,128)(2,1)S(1)}, u32[]{:S(2)}, u32[]{:S(2)}) %collective-permute-start.34) | collective-permute-done | bytes 524320 | tf_op jit(solution)/shard_map/c2/ring_h/ppermute | solution.py:69
  249.1 22.2 %collective-permute-done.36 = bf16[512,1024]{1,0:T(8,128)(2,1)S(1)} collective-permute-done((bf16[512,1024]{1,0:T(8,128)(2,1)S(1)}, bf16[512,1024]{1,0:T(8,128)(2,1)S(1)}, u32[]{:S(2)}, u32[]{:S(2)}) %collective-permute-start.36) | collective-permute-done | bytes 1048608 | tf_op jit(solution)/shard_map/s5/ring_y/ppermute | solution.py:69
  290.3 7.0 %collective-permute-done.39 = bf16[128,2048]{1,0:T(8,128)(2,1)} collective-permute-done((bf16[128,2048]{1,0:T(8,128)(2,1)}, bf16[128,2048]{1,0:T(8,128)(2,1)}, u32[]{:S(2)}, u32[]{:S(2)}) %collective-permute-start.39) | collective-permute-done | bytes 524320 | tf_op jit(solution)/shard_map/s6/team01/ppermute | solution.py:64
  299.2 10.5 %collective-permute-done.41 = bf16[128,2048]{1,0:T(8,128)(2,1)} collective-permute-done((bf16[128,2048]{1,0:T(8,128)(2,1)}, bf16[128,2048]{1,0:T(8,128)(2,1)}, u32[]{:S(2)}, u32[]{:S(2)}) %collective-permute-start.41) | collective-permute-done | bytes 524320 | tf_op jit(solution)/shard_map/s6/team11/ppermute | solution.py:64
  320.9 13.1 %collective-permute-done.43.refs_2_ = bf16[128,2048]{1,0:T(8,128)(2,1)S(1)} collective-permute-done((bf16[128,2048]{1,0:T(8,128)(2,1)S(1)}, bf16[128,2048]{1,0:T(8,128)(2,1)S(1)}, u32[]{:S(2)}, u32[]{:S(2)}) %collective-permute-start.43) | collective-permute-done | bytes 524320 | tf_op jit(solution)/shard_map/s7/team10/ppermute | solution.py:64
  336.6 6.7 %collective-permute-done.45 = bf16[128,2048]{1,0:T(8,128)(2,1)S(1)} collective-permute-done((bf16[128,2048]{1,0:T(8,128)(2,1)}, bf16[128,2048]{1,0:T(8,128)(2,1)S(1)}, u32[]{:S(2)}, u32[]{:S(2)}) %collective-permute-start.45) | collective-permute-done | bytes 524320 | tf_op jit(solution)/shard_map/s7/ring_h/ppermute | solution.py:69
  384.7 4.9 collective-permute-done.52
  395.2 13.2 %collective-permute-done.50.refs_4_ = bf16[512,1024]{1,0:T(8,128)(2,1)S(1)} collective-permute-done((bf16[512,1024]{1,0:T(8,128)(2,1)S(1)}, bf16[512,1024]{1,0:T(8,128)(2,1)S(1)}, u32[]{:S(2)}, u32[]{:S(2)}) %collective-permute-start.50) | collective-permute-done | bytes 1048608 | tf_op jit(solution)/shard_map/s8/ring_y/ppermute | solution.py:69
  420.5 16.7 %collective-permute-done.58.refs_2_ = bf16[128,2048]{1,0:T(8,128)(2,1)} collective-permute-done((bf16[128,2048]{1,0:T(8,128)(2,1)}, bf16[128,2048]{1,0:T(8,128)(2,1)}, u32[]{:S(2)}, u32[]{:S(2)}) %collective-permute-start.58) | collective-permute-done | bytes 524320 | tf_op jit(solution)/shard_map/s9/team10/ppermute | solution.py:64
  467.2 10.8 %c4.10.refs_2_.refs_3_.rows_ref = bf16[1024,768]{1,0:T(8,128)(2,1)S(1)} custom-call(s32[8]{0:T(128)S(1)} %multiply_subtract_fusion.limits_ref, bf16[1024,768]{1,0:T(8,128)(2,1)S(1)} %copy-done.10, bf16[1024,768]{1,0:T(8,128)(2,1)S(1)} %copy-done.10, bf16[1024,768]{1,0:T(8,128)(2,1)S(1)} %copy-done.10, bf16[1024,256]{1,0:T(8,128)(2,1)S(1)} %c4.9.grad_ref, ...), custom_call_target="tpu_custom_call" | custom-call | flops 1000000 | bytes 100000 | tf_op jit(solution)/shard_map/c4/pallas_call | solution.py:721
  478.0 4.6 c4.14
  507.0 7.3 %collective-permute-done.69 = bf16[256,1024]{1,0:T(8,128)(2,1)} collective-permute-done((bf16[256,1024]{1,0:T(8,128)(2,1)}, bf16[256,1024]{1,0:T(8,128)(2,1)}, u32[]{:S(2)}, u32[]{:S(2)}) %collective-permute-start.69) | collective-permute-done | bytes 524320 | tf_op jit(solution)/shard_map/c4/ring_h/ppermute | solution.py:69
  522.2 7.0 %collective-permute-done.73 = bf16[128,2048]{1,0:T(8,128)(2,1)S(1)} collective-permute-done((bf16[128,2048]{1,0:T(8,128)(2,1)S(1)}, bf16[128,2048]{1,0:T(8,128)(2,1)S(1)}, u32[]{:S(2)}, u32[]{:S(2)}) %collective-permute-start.73) | collective-permute-done | bytes 524320 | tf_op jit(solution)/shard_map/s10/team01/ppermute | solution.py:64
  536.7 21.3 %collective-permute-done.70 = f32[144,128]{1,0:T(8,128)S(1)} collective-permute-done((f32[144,128]{1,0:T(8,128)S(1)}, f32[144,128]{1,0:T(8,128)S(1)}, u32[]{:S(2)}, u32[]{:S(2)}) %collective-permute-start.70) | collective-permute-done | bytes 73760 | tf_op jit(solution)/shard_map/s10/ring_l/ppermute | solution.py:69
  579.5 8.5 %collective-permute-start.81 = (bf16[128,1024]{1,0:T(8,128)(2,1)}, bf16[128,1024]{1,0:T(8,128)(2,1)}, u32[]{:S(2)}, u32[]{:S(2)}) collective-permute-start(bf16[128,1024]{1,0:T(8,128)(2,1)} %get-tuple-element.432), channel_id=1, source_target_pairs={{0,10},{2,8},{8,2},{10,0},{1,11},{3,9},{9,3},{11,1},{4,14},{6,12},... | collective-permute-start | bytes 786440 | tf_op jit(solution)/shard_map/s11/team11/ppermute | solution.py:64
  602.4 4.9 collective-permute-start.84
  619.9 5.6 collective-permute-done.86.refs_3_
  (582 shorter events, 298.4 us)
Async XLA Ops:
  26.0 34.8 %collective-permute-start.6 = (bf16[128,2048]{1,0:T(8,128)(2,1)}, bf16[128,2048]{1,0:T(8,128)(2,1)S(1)}, u32[]{:S(2)}, u32[]{:S(2)}) collective-permute-start(bf16[128,2048]{1,0:T(8,128)(2,1)} %a1.2.refs_0_), channel_id=1, source_target_pairs={{0,8},{2,10},{8,0},{10,2},{1,9},{3,11},{9,1},{11,3},{4,12},{6,14},... | collective-permute-start | bytes 1572872 | tf_op jit(solution)/shard_map/a1/team10/ppermute | solution.py:64
  40.2 35.9 %collective-permute-start.4 = (bf16[512,1024]{1,0:T(8,128)(2,1)S(1)}, bf16[512,1024]{1,0:T(8,128)(2,1)S(1)}, u32[]{:S(2)}, u32[]{:S(2)}) collective-permute-start(bf16[512,1024]{1,0:T(8,128)(2,1)S(1)} %a1.3.refs_2_.refs_0_), channel_id=1, source_target_pairs={{0,4},{4,0},{1,5},{5,1},{2,6},{6,2},{3,7},{7,3},{8,12},{12,8},{9,1... | collective-permute-start | bytes 3145736 | tf_op jit(solution)/shard_map/a1/ring_y/ppermute | solution.py:69
  40.3 35.8 %collective-permute-start.8 = (bf16[512,768]{1,0:T(8,128)(2,1)S(1)}, bf16[512,768]{1,0:T(8,128)(2,1)}, u32[]{:S(2)}, u32[]{:S(2)}) collective-permute-start(bf16[512,768]{1,0:T(8,128)(2,1)S(1)} %slice.124), channel_id=1, source_target_pairs={{0,16},{16,0},{1,17},{17,1},{2,18},{18,2},{3,19},{19,3},{4,20},{20... | collective-permute-start | bytes 2359304 | tf_op jit(solution)/shard_map/a1/ring_h/ppermute | solution.py:69
  77.3 26.0 %collective-permute-start.9 = (bf16[512,2048]{1,0:T(8,128)(2,1)S(1)}, bf16[512,2048]{1,0:T(8,128)(2,1)}, u32[]{:S(2)}, u32[]{:S(2)}) collective-permute-start(bf16[512,2048]{1,0:T(8,128)(2,1)S(1)} %a2.1.refs_0_), channel_id=1, source_target_pairs={{0,1},{1,0},{2,3},{3,2},{4,5},{5,4},{6,7},{7,6},{8,9},{9,8},{10,11... | collective-permute-start | bytes 6291464 | tf_op jit(solution)/shard_map/a2/ring_tp/ppermute | solution.py:69
  77.3 25.9 %collective-permute-start.13 = (bf16[512,768]{1,0:T(8,128)(2,1)}, bf16[512,768]{1,0:T(8,128)(2,1)}, u32[]{:S(2)}, u32[]{:S(2)}) collective-permute-start(bf16[512,768]{1,0:T(8,128)(2,1)} %collective-permute-done.8.refs_3_.refs_1_), channel_id=1, source_target_pairs={{0,4},{4,0},{1,5},{5,1},{2,6},{6,2},{3,7},{7,3},{8,12},{12,8},{9,1... | collective-permute-start | bytes 2359304 | tf_op jit(solution)/shard_map/a2/ring_y/ppermute | solution.py:69
  139.0 34.3 %collective-permute-start.26 = (bf16[512,1024]{1,0:T(8,128)(2,1)}, bf16[512,1024]{1,0:T(8,128)(2,1)}, u32[]{:S(2)}, u32[]{:S(2)}) collective-permute-start(bf16[512,1024]{1,0:T(8,128)(2,1)} %pad_maximum_fusion.1), channel_id=1, source_target_pairs={{0,4},{4,0},{1,5},{5,1},{2,6},{6,2},{3,7},{7,3},{8,12},{12,8},{9,1... | collective-permute-start | bytes 3145736 | tf_op jit(solution)/shard_map/s3/ring_y/ppermute | solution.py:69
  151.6 26.3 %collective-permute-start.24 = (bf16[128,2048]{1,0:T(8,128)(2,1)}, bf16[128,2048]{1,0:T(8,128)(2,1)}, u32[]{:S(2)}, u32[]{:S(2)}) collective-permute-start(bf16[128,2048]{1,0:T(8,128)(2,1)} %add_convert_fusion.3), channel_id=1, source_target_pairs={{0,8},{2,10},{8,0},{10,2},{1,9},{3,11},{9,1},{11,3},{4,12},{6,14},... | collective-permute-start | bytes 1572872 | tf_op jit(solution)/shard_map/s3/team10/ppermute | solution.py:64
  179.0 38.6 %collective-permute-start.32 = (bf16[512,1024]{1,0:T(8,128)(2,1)S(1)}, bf16[512,1024]{1,0:T(8,128)(2,1)S(1)}, u32[]{:S(2)}, u32[]{:S(2)}) collective-permute-start(bf16[512,1024]{1,0:T(8,128)(2,1)S(1)} %pad_maximum_fusion.2), channel_id=1, source_target_pairs={{0,4},{4,0},{1,5},{5,1},{2,6},{6,2},{3,7},{7,3},{8,12},{12,8},{9,1... | collective-permute-start | bytes 3145736 | tf_op jit(solution)/shard_map/s4/ring_y/ppermute | solution.py:69
  181.2 26.1 %collective-permute-start.29 = (bf16[128,2048]{1,0:T(8,128)(2,1)S(1)}, bf16[128,2048]{1,0:T(8,128)(2,1)S(1)}, u32[]{:S(2)}, u32[]{:S(2)}) collective-permute-start(bf16[128,2048]{1,0:T(8,128)(2,1)S(1)} %fusion.3.refs_0_), channel_id=1, source_target_pairs={{0,8},{2,10},{8,0},{10,2},{1,9},{3,11},{9,1},{11,3},{4,12},{6,14},... | collective-permute-start | bytes 1572872 | tf_op jit(solution)/shard_map/s4/team10/ppermute | solution.py:64
  182.8 25.5 %collective-permute-start.28 = (bf16[128,2048]{1,0:T(8,128)(2,1)S(1)}, bf16[128,2048]{1,0:T(8,128)(2,1)S(1)}, u32[]{:S(2)}, u32[]{:S(2)}) collective-permute-start(bf16[128,2048]{1,0:T(8,128)(2,1)S(1)} %fusion.3.refs_0_), channel_id=1, source_target_pairs={{0,2},{2,0},{8,10},{10,8},{1,3},{3,1},{9,11},{11,9},{4,6},{6,4},{1... | collective-permute-start | bytes 1572872 | tf_op jit(solution)/shard_map/s4/team01/ppermute | solution.py:64
  183.2 34.5 %collective-permute-start.27 = (bf16[128,2048]{1,0:T(8,128)(2,1)}, bf16[128,2048]{1,0:T(8,128)(2,1)S(1)}, u32[]{:S(2)}, u32[]{:S(2)}) collective-permute-start(bf16[128,2048]{1,0:T(8,128)(2,1)} %constant_dynamic-slice_fusion), channel_id=1, source_target_pairs={{0,4},{4,12},{8,0},{12,8},{1,5},{5,13},{9,1},{13,9},{2,6},{6,14},{... | collective-permute-start | bytes 1572872 | tf_op jit(solution)/shard_map/s4/flip/ppermute | solution.py:411
  184.4 33.3 %collective-permute-start.31 = (bf16[256,1024]{1,0:T(8,128)(2,1)S(1)}, bf16[256,1024]{1,0:T(8,128)(2,1)S(1)}, u32[]{:S(2)}, u32[]{:S(2)}) collective-permute-start(bf16[256,1024]{1,0:T(8,128)(2,1)S(1)} %get-tuple-element.284.refs_0_.refs_1_), channel_id=1, source_target_pairs={{0,16},{16,0},{1,17},{17,1},{2,18},{18,2},{3,19},{19,3},{4,20},{20... | collective-permute-start | bytes 1572872 | tf_op jit(solution)/shard_map/s4/ring_h/ppermute | solution.py:69
  219.7 26.6 %collective-permute-start.35 = (bf16[512,1024]{1,0:T(8,128)(2,1)S(1)}, bf16[512,1024]{1,0:T(8,128)(2,1)S(1)}, u32[]{:S(2)}, u32[]{:S(2)}) collective-permute-start(bf16[512,1024]{1,0:T(8,128)(2,1)S(1)} %pad_maximum_fusion.3), channel_id=1, source_target_pairs={{0,4},{4,0},{1,5},{5,1},{2,6},{6,2},{3,7},{7,3},{8,12},{12,8},{9,1... | collective-permute-start | bytes 3145736 | tf_op jit(solution)/shard_map/c2/ring_y/ppermute | solution.py:69
  219.8 26.5 %collective-permute-start.34 = (bf16[256,1024]{1,0:T(8,128)(2,1)S(1)}, bf16[256,1024]{1,0:T(8,128)(2,1)S(1)}, u32[]{:S(2)}, u32[]{:S(2)}) collective-permute-start(bf16[256,1024]{1,0:T(8,128)(2,1)S(1)} %get-tuple-element.290.refs_1_.refs_2_), channel_id=1, source_target_pairs={{0,16},{16,0},{1,17},{17,1},{2,18},{18,2},{3,19},{19,3},{4,20},{20... | collective-permute-start | bytes 1572872 | tf_op jit(solution)/shard_map/c2/ring_h/ppermute | solution.py:69
  246.4 25.0 %collective-permute-start.36 = (bf16[512,1024]{1,0:T(8,128)(2,1)S(1)}, bf16[512,1024]{1,0:T(8,128)(2,1)S(1)}, u32[]{:S(2)}, u32[]{:S(2)}) collective-permute-start(bf16[512,1024]{1,0:T(8,128)(2,1)S(1)} %pad_maximum_fusion.4), channel_id=1, source_target_pairs={{0,4},{4,0},{1,5},{5,1},{2,6},{6,2},{3,7},{7,3},{8,12},{12,8},{9,1... | collective-permute-start | bytes 3145736 | tf_op jit(solution)/shard_map/s5/ring_y/ppermute | solution.py:69
  249.0 25.3 %collective-permute-start.37 = (bf16[128,2048]{1,0:T(8,128)(2,1)S(1)}, bf16[128,2048]{1,0:T(8,128)(2,1)S(1)}, u32[]{:S(2)}, u32[]{:S(2)}) collective-permute-start(bf16[128,2048]{1,0:T(8,128)(2,1)S(1)} %get-tuple-element.429), channel_id=1, source_target_pairs={{0,16},{16,0},{1,17},{17,1},{2,18},{18,2},{3,19},{19,3},{4,20},{20... | collective-permute-start | bytes 1572872 | tf_op jit(solution)/shard_map/s5/ring_h/ppermute | solution.py:69
  284.1 25.6 %collective-permute-start.41 = (bf16[128,2048]{1,0:T(8,128)(2,1)}, bf16[128,2048]{1,0:T(8,128)(2,1)}, u32[]{:S(2)}, u32[]{:S(2)}) collective-permute-start(bf16[128,2048]{1,0:T(8,128)(2,1)} %get-tuple-element.309), channel_id=1, source_target_pairs={{0,10},{2,8},{8,2},{10,0},{1,11},{3,9},{9,3},{11,1},{4,14},{6,12},... | collective-permute-start | bytes 1572872 | tf_op jit(solution)/shard_map/s6/team11/ppermute | solution.py:64
  315.3 27.9 %collective-permute-start.42 = (bf16[128,2048]{1,0:T(8,128)(2,1)S(1)}, bf16[128,2048]{1,0:T(8,128)(2,1)}, u32[]{:S(2)}, u32[]{:S(2)}) collective-permute-start(bf16[128,2048]{1,0:T(8,128)(2,1)S(1)} %get-tuple-element.315.refs_0_), channel_id=1, source_target_pairs={{0,2},{2,0},{8,10},{10,8},{1,3},{3,1},{9,11},{11,9},{4,6},{6,4},{1... | collective-permute-start | bytes 1572872 | tf_op jit(solution)/shard_map/s7/team01/ppermute | solution.py:64
  382.4 26.1 %collective-permute-start.50 = (bf16[512,1024]{1,0:T(8,128)(2,1)S(1)}, bf16[512,1024]{1,0:T(8,128)(2,1)S(1)}, u32[]{:S(2)}, u32[]{:S(2)}) collective-permute-start(bf16[512,1024]{1,0:T(8,128)(2,1)S(1)} %s8_.3), channel_id=1, source_target_pairs={{0,4},{4,0},{1,5},{5,1},{2,6},{6,2},{3,7},{7,3},{8,12},{12,8},{9,1... | collective-permute-start | bytes 3145736 | tf_op jit(solution)/shard_map/s8/ring_y/ppermute | solution.py:69
  392.3 56.7 %collective-permute-start.56 = (bf16[512,1024]{1,0:T(8,128)(2,1)}, bf16[512,1024]{1,0:T(8,128)(2,1)}, u32[]{:S(2)}, u32[]{:S(2)}) collective-permute-start(bf16[512,1024]{1,0:T(8,128)(2,1)} %s9.5), channel_id=1, source_target_pairs={{0,4},{4,0},{1,5},{5,1},{2,6},{6,2},{3,7},{7,3},{8,12},{12,8},{9,1... | collective-permute-start | bytes 3145736 | tf_op jit(solution)/shard_map/s9/ring_y/ppermute | solution.py:69
  416.0 33.1 %collective-permute-start.57 = (bf16[128,2048]{1,0:T(8,128)(2,1)}, bf16[128,2048]{1,0:T(8,128)(2,1)}, u32[]{:S(2)}, u32[]{:S(2)}) collective-permute-start(bf16[128,2048]{1,0:T(8,128)(2,1)} %get-tuple-element.337.refs_0_), channel_id=1, source_target_pairs={{0,2},{2,0},{8,10},{10,8},{1,3},{3,1},{9,11},{11,9},{4,6},{6,4},{1... | collective-permute-start | bytes 1572872 | tf_op jit(solution)/shard_map/s9/team01/ppermute | solution.py:64
  417.7 31.3 %collective-permute-start.60 = (bf16[256,1024]{1,0:T(8,128)(2,1)}, bf16[256,1024]{1,0:T(8,128)(2,1)}, u32[]{:S(2)}, u32[]{:S(2)}) collective-permute-start(bf16[256,1024]{1,0:T(8,128)(2,1)} %s8_.5), channel_id=1, source_target_pairs={{0,16},{16,0},{1,17},{17,1},{2,18},{18,2},{3,19},{19,3},{4,20},{20... | collective-permute-start | bytes 1572872 | tf_op jit(solution)/shard_map/s9/ring_h/ppermute | solution.py:69
  455.6 26.9 %collective-permute-start.66 = (bf16[128,2048]{1,0:T(8,128)(2,1)S(1)}, bf16[128,2048]{1,0:T(8,128)(2,1)S(1)}, u32[]{:S(2)}, u32[]{:S(2)}) collective-permute-start(bf16[128,2048]{1,0:T(8,128)(2,1)S(1)} %get-tuple-element.378), channel_id=1, source_target_pairs={{4,8},{8,4},{5,9},{9,5},{6,10},{10,6},{7,11},{11,7},{20,24},{24,20... | collective-permute-start | bytes 1572872 | tf_op jit(solution)/shard_map/c4/ppermute | solution.py:109
  456.5 26.0 %collective-permute-start.67 = (bf16[128,2048]{1,0:T(8,128)(2,1)S(1)}, bf16[128,2048]{1,0:T(8,128)(2,1)S(1)}, u32[]{:S(2)}, u32[]{:S(2)}) collective-permute-start(bf16[128,2048]{1,0:T(8,128)(2,1)S(1)} %get-tuple-element.436), channel_id=1, source_target_pairs={{0,8},{4,0},{8,12},{12,4},{1,9},{5,1},{9,13},{13,5},{2,10},{6,2},{... | collective-permute-start | bytes 1572872 | tf_op jit(solution)/shard_map/c4/ppermute | solution.py:427
  459.6 25.3 %collective-permute-start.65 = (bf16[256,1024]{1,0:T(8,128)(2,1)S(1)}, bf16[256,1024]{1,0:T(8,128)(2,1)S(1)}, u32[]{:S(2)}, u32[]{:S(2)}) collective-permute-start(bf16[256,1024]{1,0:T(8,128)(2,1)S(1)} %copy-done.101), channel_id=1, source_target_pairs={{0,16},{16,0},{1,17},{17,1},{2,18},{18,2},{3,19},{19,3},{4,20},{20... | collective-permute-start | bytes 1572872 | tf_op jit(solution)/shard_map/c4/ring_h/ppermute | solution.py:69
  488.1 26.2 %collective-permute-start.69 = (bf16[256,1024]{1,0:T(8,128)(2,1)}, bf16[256,1024]{1,0:T(8,128)(2,1)}, u32[]{:S(2)}, u32[]{:S(2)}) collective-permute-start(bf16[256,1024]{1,0:T(8,128)(2,1)} %s9.7), channel_id=1, source_target_pairs={{0,16},{16,0},{1,17},{17,1},{2,18},{18,2},{3,19},{19,3},{4,20},{20... | collective-permute-start | bytes 1572872 | tf_op jit(solution)/shard_map/c4/ring_h/ppermute | solution.py:69
  516.9 46.2 %collective-permute-start.71 = (bf16[512,1024]{1,0:T(8,128)(2,1)S(1)}, bf16[512,1024]{1,0:T(8,128)(2,1)S(1)}, u32[]{:S(2)}, u32[]{:S(2)}) collective-permute-start(bf16[512,1024]{1,0:T(8,128)(2,1)S(1)} %s10.4), channel_id=1, source_target_pairs={{0,4},{4,0},{1,5},{5,1},{2,6},{6,2},{3,7},{7,3},{8,12},{12,8},{9,1... | collective-permute-start | bytes 3145736 | tf_op jit(solution)/shard_map/s10/ring_y/ppermute | solution.py:69
  519.6 44.5 %collective-permute-start.75 = (bf16[512,768]{1,0:T(8,128)(2,1)S(1)}, bf16[512,768]{1,0:T(8,128)(2,1)S(1)}, u32[]{:S(2)}, u32[]{:S(2)}) collective-permute-start(bf16[512,768]{1,0:T(8,128)(2,1)S(1)} %s10.5), channel_id=1, source_target_pairs={{0,16},{16,0},{1,17},{17,1},{2,18},{18,2},{3,19},{19,3},{4,20},{20... | collective-permute-start | bytes 2359304 | tf_op jit(solution)/shard_map/s10/ring_h/ppermute | solution.py:69
  520.4 43.6 %collective-permute-start.72 = (bf16[128,2048]{1,0:T(8,128)(2,1)S(1)}, bf16[128,2048]{1,0:T(8,128)(2,1)S(1)}, u32[]{:S(2)}, u32[]{:S(2)}) collective-permute-start(bf16[128,2048]{1,0:T(8,128)(2,1)S(1)} %get-tuple-element.360), channel_id=1, source_target_pairs={{0,2},{2,0},{8,10},{10,8},{1,3},{3,1},{9,11},{11,9},{4,6},{6,4},{1... | collective-permute-start | bytes 1572872 | tf_op jit(solution)/shard_map/s10/team01/ppermute | solution.py:64
  529.3 35.7 %collective-permute-start.74 = (bf16[128,2048]{1,0:T(8,128)(2,1)S(1)}, bf16[128,2048]{1,0:T(8,128)(2,1)S(1)}, u32[]{:S(2)}, u32[]{:S(2)}) collective-permute-start(bf16[128,2048]{1,0:T(8,128)(2,1)S(1)} %add_convert_fusion.1), channel_id=1, source_target_pairs={{0,8},{2,10},{8,0},{10,2},{1,9},{3,11},{9,1},{11,3},{4,12},{6,14},... | collective-permute-start | bytes 1572872 | tf_op jit(solution)/shard_map/s10/team10/ppermute | solution.py:64
  567.9 29.9 %collective-permute-start.76 = (bf16[128,2048]{1,0:T(8,128)(2,1)}, bf16[128,2048]{1,0:T(8,128)(2,1)}, u32[]{:S(2)}, u32[]{:S(2)}) collective-permute-start(bf16[128,2048]{1,0:T(8,128)(2,1)} %s11.7), channel_id=1, source_target_pairs={{4,8},{8,4},{5,9},{9,5},{6,10},{10,6},{7,11},{11,7},{20,24},{24,20... | collective-permute-start | bytes 1572872 | tf_op jit(solution)/shard_map/s11/ppermute | solution.py:109
  571.7 26.1 %collective-permute-start.79 = (bf16[128,1024]{1,0:T(8,128)(2,1)}, bf16[128,1024]{1,0:T(8,128)(2,1)}, u32[]{:S(2)}, u32[]{:S(2)}) collective-permute-start(bf16[128,1024]{1,0:T(8,128)(2,1)} %get-tuple-element.434), channel_id=1, source_target_pairs={{0,2},{2,0},{8,10},{10,8},{1,3},{3,1},{9,11},{11,9},{4,6},{6,4},{1... | collective-permute-start | bytes 786440 | tf_op jit(solution)/shard_map/s11/team01/ppermute | solution.py:64
  (200 other events, 3081.1 us)

commit v6 on v5

--- a/solution.py
+++ b/solution.py
@@ -423,8 +423,12 @@
 
 def deal(team, pieces):
     first, second = (choose(pieces, step) for step in team.out_steps)
+    return first, swap_home(first), second
+
+
+def deal_second(value):
     perm = [(l * 2 + y, (1 - y) * 2 + l) for l in range(2) for y in range(2)]
-    return [first, swap_home(first), lax.ppermute(second, ("l", "y"), perm)]
+    return lax.ppermute(value, ("l", "y"), perm)
 
 
 def dealt_out(team, got):
@@ -687,7 +691,7 @@
 
 
 def query_block(rows):
-    return min(256, rows)
+    return min(512, rows)
 
 
 def attend(qkv, limits, scale):
@@ -958,8 +962,10 @@
         grad_bout = jnp.sum(grad_branch.astype(WIDE), axis=0)
         by_row = jnp.stack([grad_bout, grad_gmid, grad_smid, grad_bdown, grad_gend, grad_send])
         by_row = add_ring(team, from_team_order(team, by_row), "tp")
+        out_first, out_swapped, out_second = deal(team, out_pieces)
         cross_up_a, cross_up_b = flow_up.cross_half(0, far_up), flow_up.cross_half(1, far_up)
-        by_row, near_down, *rest = fence(by_row, near_down, *pieces, *got_down_b, *cross_up_a, *cross_up_b)
+        by_row, near_down, out_first, out_swapped, out_second, *rest = fence(
+            by_row, near_down, out_first, out_swapped, out_second, *pieces, *got_down_b, *cross_up_a, *cross_up_b)
         pieces, rest = rest[:members], rest[members:]
         got_down_b, rest = rest[:steps], rest[steps:]
         cross_up_a, cross_up_b = rest[:steps], rest[steps:]
@@ -967,7 +973,7 @@
         half = stack_rows(pieces)
         other = cores(team, half)
         got_up_a, got_up_b = flow_up.go(cross_up_a), flow_up.go(cross_up_b)
-        out_two = deal(team, out_pieces)
+        out_two = [out_first, out_swapped, deal_second(out_second)]
         branch_parts = [half] + other
         attended_parts = [(attended, k) for k in range(ts)]
         flow_out = Grads(team, branch_parts, attended_parts)
@@ -1003,7 +1009,6 @@
         )
         got_qkv = flow_qkv.go(flow_qkv.cross(far_qkv))
         (near_up,) = beside(team, [flow_up.send_near()])
-        sums = add_ring(team, sums, "l")
         sums, total_down, near_up, *rest = fence(
             sums, total_down, near_up, *out_two, *got, *got_qkv, *cross_out
         )
@@ -1032,7 +1037,9 @@
         grad_tokens = join_cores(team, swapped_home(team, grad_own, swapped))
         home_all = home_pieces(team, jnp.concatenate([total_up, total_qkv, total_out], axis=1))
         output = join_cores(team, dealt_out(team, out_two))
-        sums = add_ring(team, add_ring(team, sums, "h"), "y").reshape(-1)
+        sums = add_ring(
+            team, add_ring(team, add_ring(team, sums, "l"), "h"), "y"
+        ).reshape(-1)
         grad_up, grad_query, grad_key, grad_value, grad_out = home_join(
             team, home_all, [tall] + [wide] * 4
         )

time: 639 us -> 636 us (level)
  waiting for transfers between devices: 308 us -> 332 us
  starting transfers between devices: 114 us -> 98.8 us
  Pallas kernels: 126 us -> 114 us
    ppermute x44, waiting for transfers between devices: 143 us -> 159 us  [ring(): lax.ppermute(value, name, [(i, (i + step) % size) for i in range(size)])]
    ppermute x39, starting transfers between devices: 71.3 us -> 59 us  [shift_(): return lax.ppermute(value, TEAM, perm)]
    ppermute x39, waiting for transfers between devices: 156 us -> 164 us  [shift_(): return lax.ppermute(value, TEAM, perm)]
    unnamed x289 -> x299, local copies, waits for them, and re-layouts: 21 us -> 22.8 us
  transfers between devices with their start and end apart: 89 -> 89, of which waited for: 44 -> 48; matrix products, arithmetic and copies ran while one was open for 7% -> 6% of each run, Pallas kernels for 18% -> 16%
where the time goes in v6:
time: 636 us; the launch traced here: 626 us
  waiting for transfers between devices  332 us (52%)
  Pallas kernels  114 us (18%)
  starting transfers between devices  98.8 us (16%)
  local copies, waits for them, and re-layouts  42.9 us (7%)
  other arithmetic  30.5 us (5%)
  between operations  7.14 us (1%)
    ppermute x39, waiting for transfers between devices, shift_(): return lax.ppermute(value, TEAM, perm)  164 us
    ppermute x44, waiting for transfers between devices, ring(): lax.ppermute(value, name, [(i, (i + step) % size) for i in range(size)])  159 us
    ppermute x39, starting transfers between devices, shift_(): return lax.ppermute(value, TEAM, perm)  59 us
    ppermute x44, starting transfers between devices, ring(): lax.ppermute(value, name, [(i, (i + step) % size) for i in range(size)])  30.1 us
    pallas_call x19, Pallas kernels, outer(): pl.pallas_call(functools.partial(outer_kernel, len(lefts), len(adds)), gr...  29.2 us
    pallas_call x6, Pallas kernels, project(): pl.pallas_call(functools.partial(project_kernel, mode, len(parts), len(pi...  23.9 us
    pallas_call x8, Pallas kernels, spread(): pl.pallas_call(functools.partial(spread_kernel, len(pieces), len(got), sp...  23.9 us
    unnamed x299, local copies, waits for them, and re-layouts  22.8 us
  transfers between devices with their start and end apart: 89, of which 48 were waited for; matrix products, arithmetic and copies ran while one was open for 6% of the time, Pallas kernels for 16%

profile of v6, /device:TPU:0, one launch (start us, length us, event | category | flops | bytes accessed | tf_op | source)
XLA Modules:
  0.0 625.6 jit_solution(8975766208347972841)
XLA Ops:
  26.1 13.4 %collective-permute-start.6 = (bf16[128,2048]{1,0:T(8,128)(2,1)}, bf16[128,2048]{1,0:T(8,128)(2,1)S(1)}, u32[]{:S(2)}, u32[]{:S(2)}) collective-permute-start(bf16[128,2048]{1,0:T(8,128)(2,1)} %a1.2.refs_0_), channel_id=1, source_target_pairs={{0,8},{2,10},{8,0},{10,2},{1,9},{3,11},{9,1},{11,3},{4,12},{6,14},... | collective-permute-start | bytes 1572872 | tf_op jit(solution)/shard_map/a1/team10/ppermute | solution.py:64
  43.5 17.3 %collective-permute-done.6.refs_2_ = bf16[128,2048]{1,0:T(8,128)(2,1)S(1)} collective-permute-done((bf16[128,2048]{1,0:T(8,128)(2,1)}, bf16[128,2048]{1,0:T(8,128)(2,1)S(1)}, u32[]{:S(2)}, u32[]{:S(2)}) %collective-permute-start.6) | collective-permute-done | bytes 524320 | tf_op jit(solution)/shard_map/a1/team10/ppermute | solution.py:64
  61.3 14.8 %collective-permute-done.8.refs_3_.refs_1_ = bf16[512,768]{1,0:T(8,128)(2,1)} collective-permute-done((bf16[512,768]{1,0:T(8,128)(2,1)S(1)}, bf16[512,768]{1,0:T(8,128)(2,1)}, u32[]{:S(2)}, u32[]{:S(2)}) %collective-permute-start.8) | collective-permute-done | bytes 786464 | tf_op jit(solution)/shard_map/a1/ring_h/ppermute | solution.py:69
  84.2 4.8 collective-permute-done.10.refs_1_
  90.3 10.0 %collective-permute-done.12.refs_3_ = bf16[128,1024]{1,0:T(8,128)(2,1)S(1)} collective-permute-done((bf16[128,1024]{1,0:T(8,128)(2,1)S(1)}, bf16[128,1024]{1,0:T(8,128)(2,1)S(1)}, u32[]{:S(2)}, u32[]{:S(2)}) %collective-permute-start.12) | collective-permute-done | bytes 262176 | tf_op jit(solution)/shard_map/a2/team11/ppermute | solution.py:64
  110.6 6.0 c1.5.query_ref.key_ref.value_ref
  116.6 6.3 %c1.6 = (bf16[1024,256]{1,0:T(8,128)(2,1)S(1)}, f32[2,1,1024]{2,1,0:T(1,128)S(1)}) custom-call(s32[8]{0:T(128)S(1)} %multiply_subtract_fusion.limits_ref, bf16[1024,768]{1,0:T(8,128)(2,1)S(1)} %c1.5.query_ref.key_ref.value_ref, bf16[1024,768]{1,0:T(8,128)(2,1)S(1)} %c1.5.query_ref.key_ref.value_ref, bf16[1024,768]{1,0:T(8,128)(2,1)S(1)} %c1.5.query_ref.key_ref.value_ref), custom_call_target="tpu_custom_call" | custom-call | flops 1000000 | bytes 100000 | tf_op jit(solution)/shard_map/c1/pallas_call | solution.py:700
  123.7 5.8 collective-permute-done.19.refs_3_
  141.8 8.8 %collective-permute-done.23 = bf16[128,2048]{1,0:T(8,128)(2,1)S(1)} collective-permute-done((bf16[128,2048]{1,0:T(8,128)(2,1)S(1)}, bf16[128,2048]{1,0:T(8,128)(2,1)S(1)}, u32[]{:S(2)}, u32[]{:S(2)}) %collective-permute-start.23) | collective-permute-done | bytes 524320 | tf_op jit(solution)/shard_map/s3/team01/ppermute | solution.py:64
  155.8 5.7 collective-permute-done.22
  161.5 11.7 %collective-permute-done.26 = bf16[512,1024]{1,0:T(8,128)(2,1)} collective-permute-done((bf16[512,1024]{1,0:T(8,128)(2,1)}, bf16[512,1024]{1,0:T(8,128)(2,1)}, u32[]{:S(2)}, u32[]{:S(2)}) %collective-permute-start.26) | collective-permute-done | bytes 1048608 | tf_op jit(solution)/shard_map/s3/ring_y/ppermute | solution.py:69
  173.3 4.6 collective-permute-done.24
  186.8 20.5 %collective-permute-done.29.refs_2_ = bf16[128,2048]{1,0:T(8,128)(2,1)S(1)} collective-permute-done((bf16[128,2048]{1,0:T(8,128)(2,1)S(1)}, bf16[128,2048]{1,0:T(8,128)(2,1)S(1)}, u32[]{:S(2)}, u32[]{:S(2)}) %collective-permute-start.29) | collective-permute-done | bytes 524320 | tf_op jit(solution)/shard_map/s4/team10/ppermute | solution.py:64
  208.4 9.2 %collective-permute-done.27 = bf16[128,2048]{1,0:T(8,128)(2,1)S(1)} collective-permute-done((bf16[128,2048]{1,0:T(8,128)(2,1)}, bf16[128,2048]{1,0:T(8,128)(2,1)S(1)}, u32[]{:S(2)}, u32[]{:S(2)}) %collective-permute-start.27) | collective-permute-done | bytes 524320 | tf_op jit(solution)/shard_map/s4/flip/ppermute | solution.py:411
  222.4 4.6 c2.4
  228.4 4.4 c2.5
  232.9 13.4 %collective-permute-done.34.refs_3_.refs_4_ = bf16[256,1024]{1,0:T(8,128)(2,1)S(1)} collective-permute-done((bf16[256,1024]{1,0:T(8,128)(2,1)S(1)}, bf16[256,1024]{1,0:T(8,128)(2,1)S(1)}, u32[]{:S(2)}, u32[]{:S(2)}) %collective-permute-start.34) | collective-permute-done | bytes 524320 | tf_op jit(solution)/shard_map/c2/ring_h/ppermute | solution.py:69
  249.1 22.2 %collective-permute-done.36 = bf16[512,1024]{1,0:T(8,128)(2,1)S(1)} collective-permute-done((bf16[512,1024]{1,0:T(8,128)(2,1)S(1)}, bf16[512,1024]{1,0:T(8,128)(2,1)S(1)}, u32[]{:S(2)}, u32[]{:S(2)}) %collective-permute-start.36) | collective-permute-done | bytes 1048608 | tf_op jit(solution)/shard_map/s5/ring_y/ppermute | solution.py:69
  290.3 7.0 %collective-permute-done.39 = bf16[128,2048]{1,0:T(8,128)(2,1)} collective-permute-done((bf16[128,2048]{1,0:T(8,128)(2,1)}, bf16[128,2048]{1,0:T(8,128)(2,1)}, u32[]{:S(2)}, u32[]{:S(2)}) %collective-permute-start.39) | collective-permute-done | bytes 524320 | tf_op jit(solution)/shard_map/s6/team01/ppermute | solution.py:64
  299.2 10.5 %collective-permute-done.41 = bf16[128,2048]{1,0:T(8,128)(2,1)} collective-permute-done((bf16[128,2048]{1,0:T(8,128)(2,1)}, bf16[128,2048]{1,0:T(8,128)(2,1)}, u32[]{:S(2)}, u32[]{:S(2)}) %collective-permute-start.41) | collective-permute-done | bytes 524320 | tf_op jit(solution)/shard_map/s6/team11/ppermute | solution.py:64
  320.9 13.1 %collective-permute-done.43.refs_2_ = bf16[128,2048]{1,0:T(8,128)(2,1)S(1)} collective-permute-done((bf16[128,2048]{1,0:T(8,128)(2,1)S(1)}, bf16[128,2048]{1,0:T(8,128)(2,1)S(1)}, u32[]{:S(2)}, u32[]{:S(2)}) %collective-permute-start.43) | collective-permute-done | bytes 524320 | tf_op jit(solution)/shard_map/s7/team10/ppermute | solution.py:64
  336.6 6.7 %collective-permute-done.45 = bf16[128,2048]{1,0:T(8,128)(2,1)S(1)} collective-permute-done((bf16[128,2048]{1,0:T(8,128)(2,1)}, bf16[128,2048]{1,0:T(8,128)(2,1)S(1)}, u32[]{:S(2)}, u32[]{:S(2)}) %collective-permute-start.45) | collective-permute-done | bytes 524320 | tf_op jit(solution)/shard_map/s7/ring_h/ppermute | solution.py:69
  384.7 4.9 collective-permute-done.52
  394.4 14.0 %collective-permute-done.50.refs_4_ = bf16[512,1024]{1,0:T(8,128)(2,1)S(1)} collective-permute-done((bf16[512,1024]{1,0:T(8,128)(2,1)S(1)}, bf16[512,1024]{1,0:T(8,128)(2,1)S(1)}, u32[]{:S(2)}, u32[]{:S(2)}) %collective-permute-start.50) | collective-permute-done | bytes 1048608 | tf_op jit(solution)/shard_map/s8/ring_y/ppermute | solution.py:69
  425.1 16.3 %collective-permute-done.59.refs_2_ = bf16[128,2048]{1,0:T(8,128)(2,1)} collective-permute-done((bf16[128,2048]{1,0:T(8,128)(2,1)}, bf16[128,2048]{1,0:T(8,128)(2,1)}, u32[]{:S(2)}, u32[]{:S(2)}) %collective-permute-start.59) | collective-permute-done | bytes 524320 | tf_op jit(solution)/shard_map/s9/team10/ppermute | solution.py:64
  461.3 9.3 %c4.10.refs_2_.refs_3_.rows_ref = bf16[1024,768]{1,0:T(8,128)(2,1)S(1)} custom-call(s32[8]{0:T(128)S(1)} %multiply_subtract_fusion.limits_ref, bf16[1024,768]{1,0:T(8,128)(2,1)S(1)} %copy-done.10, bf16[1024,768]{1,0:T(8,128)(2,1)S(1)} %copy-done.10, bf16[1024,768]{1,0:T(8,128)(2,1)S(1)} %copy-done.10, bf16[1024,256]{1,0:T(8,128)(2,1)S(1)} %c4.9.grad_ref, ...), custom_call_target="tpu_custom_call" | custom-call | flops 1000000 | bytes 100000 | tf_op jit(solution)/shard_map/c4/pallas_call | solution.py:725
  470.6 4.6 c4.14
  502.4 6.3 %collective-permute-done.69 = bf16[256,1024]{1,0:T(8,128)(2,1)} collective-permute-done((bf16[256,1024]{1,0:T(8,128)(2,1)}, bf16[256,1024]{1,0:T(8,128)(2,1)}, u32[]{:S(2)}, u32[]{:S(2)}) %collective-permute-start.69) | collective-permute-done | bytes 524320 | tf_op jit(solution)/shard_map/c4/ring_h/ppermute | solution.py:69
  517.4 6.1 collective-permute-done.72
  539.1 12.4 %collective-permute-done.74.refs_5_ = bf16[512,768]{1,0:T(8,128)(2,1)S(1)} collective-permute-done((bf16[512,768]{1,0:T(8,128)(2,1)S(1)}, bf16[512,768]{1,0:T(8,128)(2,1)S(1)}, u32[]{:S(2)}, u32[]{:S(2)}) %collective-permute-start.74) | collective-permute-done | bytes 786464 | tf_op jit(solution)/shard_map/s10/ring_h/ppermute | solution.py:69
  574.3 10.4 %collective-permute-done.79.refs_2_ = bf16[128,1024]{1,0:T(8,128)(2,1)} collective-permute-done((bf16[128,1024]{1,0:T(8,128)(2,1)}, bf16[128,1024]{1,0:T(8,128)(2,1)}, u32[]{:S(2)}, u32[]{:S(2)}) %collective-permute-start.79) | collective-permute-done | bytes 262176 | tf_op jit(solution)/shard_map/s11/team10/ppermute | solution.py:64
  595.1 20.9 %collective-permute-done.87 = f32[144,128]{1,0:T(8,128)S(1)} collective-permute-done((f32[144,128]{1,0:T(8,128)S(1)}, f32[144,128]{1,0:T(8,128)S(1)}, u32[]{:S(2)}, u32[]{:S(2)}) %collective-permute-start.87) | collective-permute-done | bytes 73760 | tf_op jit(solution)/shard_map/s12/ring_h/ppermute | solution.py:69
  (592 shorter events, 292.4 us)
Async XLA Ops:
  26.1 34.7 %collective-permute-start.6 = (bf16[128,2048]{1,0:T(8,128)(2,1)}, bf16[128,2048]{1,0:T(8,128)(2,1)S(1)}, u32[]{:S(2)}, u32[]{:S(2)}) collective-permute-start(bf16[128,2048]{1,0:T(8,128)(2,1)} %a1.2.refs_0_), channel_id=1, source_target_pairs={{0,8},{2,10},{8,0},{10,2},{1,9},{3,11},{9,1},{11,3},{4,12},{6,14},... | collective-permute-start | bytes 1572872 | tf_op jit(solution)/shard_map/a1/team10/ppermute | solution.py:64
  40.2 35.9 %collective-permute-start.4 = (bf16[512,1024]{1,0:T(8,128)(2,1)S(1)}, bf16[512,1024]{1,0:T(8,128)(2,1)S(1)}, u32[]{:S(2)}, u32[]{:S(2)}) collective-permute-start(bf16[512,1024]{1,0:T(8,128)(2,1)S(1)} %a1.3.refs_2_.refs_0_), channel_id=1, source_target_pairs={{0,4},{4,0},{1,5},{5,1},{2,6},{6,2},{3,7},{7,3},{8,12},{12,8},{9,1... | collective-permute-start | bytes 3145736 | tf_op jit(solution)/shard_map/a1/ring_y/ppermute | solution.py:69
  40.3 35.8 %collective-permute-start.8 = (bf16[512,768]{1,0:T(8,128)(2,1)S(1)}, bf16[512,768]{1,0:T(8,128)(2,1)}, u32[]{:S(2)}, u32[]{:S(2)}) collective-permute-start(bf16[512,768]{1,0:T(8,128)(2,1)S(1)} %slice.124), channel_id=1, source_target_pairs={{0,16},{16,0},{1,17},{17,1},{2,18},{18,2},{3,19},{19,3},{4,20},{20... | collective-permute-start | bytes 2359304 | tf_op jit(solution)/shard_map/a1/ring_h/ppermute | solution.py:69
  77.3 26.0 %collective-permute-start.9 = (bf16[512,2048]{1,0:T(8,128)(2,1)S(1)}, bf16[512,2048]{1,0:T(8,128)(2,1)}, u32[]{:S(2)}, u32[]{:S(2)}) collective-permute-start(bf16[512,2048]{1,0:T(8,128)(2,1)S(1)} %a2.1.refs_0_), channel_id=1, source_target_pairs={{0,1},{1,0},{2,3},{3,2},{4,5},{5,4},{6,7},{7,6},{8,9},{9,8},{10,11... | collective-permute-start | bytes 6291464 | tf_op jit(solution)/shard_map/a2/ring_tp/ppermute | solution.py:69
  77.3 25.9 %collective-permute-start.13 = (bf16[512,768]{1,0:T(8,128)(2,1)}, bf16[512,768]{1,0:T(8,128)(2,1)}, u32[]{:S(2)}, u32[]{:S(2)}) collective-permute-start(bf16[512,768]{1,0:T(8,128)(2,1)} %collective-permute-done.8.refs_3_.refs_1_), channel_id=1, source_target_pairs={{0,4},{4,0},{1,5},{5,1},{2,6},{6,2},{3,7},{7,3},{8,12},{12,8},{9,1... | collective-permute-start | bytes 2359304 | tf_op jit(solution)/shard_map/a2/ring_y/ppermute | solution.py:69
  139.0 34.3 %collective-permute-start.26 = (bf16[512,1024]{1,0:T(8,128)(2,1)}, bf16[512,1024]{1,0:T(8,128)(2,1)}, u32[]{:S(2)}, u32[]{:S(2)}) collective-permute-start(bf16[512,1024]{1,0:T(8,128)(2,1)} %pad_maximum_fusion.1), channel_id=1, source_target_pairs={{0,4},{4,0},{1,5},{5,1},{2,6},{6,2},{3,7},{7,3},{8,12},{12,8},{9,1... | collective-permute-start | bytes 3145736 | tf_op jit(solution)/shard_map/s3/ring_y/ppermute | solution.py:69
  151.6 26.3 %collective-permute-start.24 = (bf16[128,2048]{1,0:T(8,128)(2,1)}, bf16[128,2048]{1,0:T(8,128)(2,1)}, u32[]{:S(2)}, u32[]{:S(2)}) collective-permute-start(bf16[128,2048]{1,0:T(8,128)(2,1)} %add_convert_fusion.3), channel_id=1, source_target_pairs={{0,8},{2,10},{8,0},{10,2},{1,9},{3,11},{9,1},{11,3},{4,12},{6,14},... | collective-permute-start | bytes 1572872 | tf_op jit(solution)/shard_map/s3/team10/ppermute | solution.py:64
  179.0 38.6 %collective-permute-start.32 = (bf16[512,1024]{1,0:T(8,128)(2,1)S(1)}, bf16[512,1024]{1,0:T(8,128)(2,1)S(1)}, u32[]{:S(2)}, u32[]{:S(2)}) collective-permute-start(bf16[512,1024]{1,0:T(8,128)(2,1)S(1)} %pad_maximum_fusion.2), channel_id=1, source_target_pairs={{0,4},{4,0},{1,5},{5,1},{2,6},{6,2},{3,7},{7,3},{8,12},{12,8},{9,1... | collective-permute-start | bytes 3145736 | tf_op jit(solution)/shard_map/s4/ring_y/ppermute | solution.py:69
  181.2 26.1 %collective-permute-start.29 = (bf16[128,2048]{1,0:T(8,128)(2,1)S(1)}, bf16[128,2048]{1,0:T(8,128)(2,1)S(1)}, u32[]{:S(2)}, u32[]{:S(2)}) collective-permute-start(bf16[128,2048]{1,0:T(8,128)(2,1)S(1)} %fusion.3.refs_0_), channel_id=1, source_target_pairs={{0,8},{2,10},{8,0},{10,2},{1,9},{3,11},{9,1},{11,3},{4,12},{6,14},... | collective-permute-start | bytes 1572872 | tf_op jit(solution)/shard_map/s4/team10/ppermute | solution.py:64
  183.1 34.4 %collective-permute-start.27 = (bf16[128,2048]{1,0:T(8,128)(2,1)}, bf16[128,2048]{1,0:T(8,128)(2,1)S(1)}, u32[]{:S(2)}, u32[]{:S(2)}) collective-permute-start(bf16[128,2048]{1,0:T(8,128)(2,1)} %constant_dynamic-slice_fusion), channel_id=1, source_target_pairs={{0,4},{4,12},{8,0},{12,8},{1,5},{5,13},{9,1},{13,9},{2,6},{6,14},{... | collective-permute-start | bytes 1572872 | tf_op jit(solution)/shard_map/s4/flip/ppermute | solution.py:411
  184.3 33.2 %collective-permute-start.31 = (bf16[256,1024]{1,0:T(8,128)(2,1)S(1)}, bf16[256,1024]{1,0:T(8,128)(2,1)S(1)}, u32[]{:S(2)}, u32[]{:S(2)}) collective-permute-start(bf16[256,1024]{1,0:T(8,128)(2,1)S(1)} %get-tuple-element.287.refs_0_.refs_1_), channel_id=1, source_target_pairs={{0,16},{16,0},{1,17},{17,1},{2,18},{18,2},{3,19},{19,3},{4,20},{20... | collective-permute-start | bytes 1572872 | tf_op jit(solution)/shard_map/s4/ring_h/ppermute | solution.py:69
  219.7 26.6 %collective-permute-start.35 = (bf16[512,1024]{1,0:T(8,128)(2,1)S(1)}, bf16[512,1024]{1,0:T(8,128)(2,1)S(1)}, u32[]{:S(2)}, u32[]{:S(2)}) collective-permute-start(bf16[512,1024]{1,0:T(8,128)(2,1)S(1)} %pad_maximum_fusion.3), channel_id=1, source_target_pairs={{0,4},{4,0},{1,5},{5,1},{2,6},{6,2},{3,7},{7,3},{8,12},{12,8},{9,1... | collective-permute-start | bytes 3145736 | tf_op jit(solution)/shard_map/c2/ring_y/ppermute | solution.py:69
  219.8 26.5 %collective-permute-start.34 = (bf16[256,1024]{1,0:T(8,128)(2,1)S(1)}, bf16[256,1024]{1,0:T(8,128)(2,1)S(1)}, u32[]{:S(2)}, u32[]{:S(2)}) collective-permute-start(bf16[256,1024]{1,0:T(8,128)(2,1)S(1)} %get-tuple-element.293.refs_1_.refs_2_), channel_id=1, source_target_pairs={{0,16},{16,0},{1,17},{17,1},{2,18},{18,2},{3,19},{19,3},{4,20},{20... | collective-permute-start | bytes 1572872 | tf_op jit(solution)/shard_map/c2/ring_h/ppermute | solution.py:69
  284.1 25.6 %collective-permute-start.41 = (bf16[128,2048]{1,0:T(8,128)(2,1)}, bf16[128,2048]{1,0:T(8,128)(2,1)}, u32[]{:S(2)}, u32[]{:S(2)}) collective-permute-start(bf16[128,2048]{1,0:T(8,128)(2,1)} %get-tuple-element.312), channel_id=1, source_target_pairs={{0,10},{2,8},{8,2},{10,0},{1,11},{3,9},{9,3},{11,1},{4,14},{6,12},... | collective-permute-start | bytes 1572872 | tf_op jit(solution)/shard_map/s6/team11/ppermute | solution.py:64
  315.3 27.9 %collective-permute-start.42 = (bf16[128,2048]{1,0:T(8,128)(2,1)S(1)}, bf16[128,2048]{1,0:T(8,128)(2,1)}, u32[]{:S(2)}, u32[]{:S(2)}) collective-permute-start(bf16[128,2048]{1,0:T(8,128)(2,1)S(1)} %get-tuple-element.318.refs_0_), channel_id=1, source_target_pairs={{0,2},{2,0},{8,10},{10,8},{1,3},{3,1},{9,11},{11,9},{4,6},{6,4},{1... | collective-permute-start | bytes 1572872 | tf_op jit(solution)/shard_map/s7/team01/ppermute | solution.py:64
  382.4 26.1 %collective-permute-start.50 = (bf16[512,1024]{1,0:T(8,128)(2,1)S(1)}, bf16[512,1024]{1,0:T(8,128)(2,1)S(1)}, u32[]{:S(2)}, u32[]{:S(2)}) collective-permute-start(bf16[512,1024]{1,0:T(8,128)(2,1)S(1)} %s8_.3), channel_id=1, source_target_pairs={{0,4},{4,0},{1,5},{5,1},{2,6},{6,2},{3,7},{7,3},{8,12},{12,8},{9,1... | collective-permute-start | bytes 3145736 | tf_op jit(solution)/shard_map/s8/ring_y/ppermute | solution.py:69
  392.3 56.2 %collective-permute-start.56 = (bf16[512,1024]{1,0:T(8,128)(2,1)}, bf16[512,1024]{1,0:T(8,128)(2,1)}, u32[]{:S(2)}, u32[]{:S(2)}) collective-permute-start(bf16[512,1024]{1,0:T(8,128)(2,1)} %s9.5), channel_id=1, source_target_pairs={{0,4},{4,0},{1,5},{5,1},{2,6},{6,2},{3,7},{7,3},{8,12},{12,8},{9,1... | collective-permute-start | bytes 3145736 | tf_op jit(solution)/shard_map/s9/ring_y/ppermute | solution.py:69
  419.6 28.9 %collective-permute-start.57 = (bf16[128,2048]{1,0:T(8,128)(2,1)S(1)}, bf16[128,2048]{1,0:T(8,128)(2,1)S(1)}, u32[]{:S(2)}, u32[]{:S(2)}) collective-permute-start(bf16[128,2048]{1,0:T(8,128)(2,1)S(1)} %get-tuple-element.384), channel_id=1, source_target_pairs={{4,8},{8,4},{5,9},{9,5},{6,10},{10,6},{7,11},{11,7},{20,24},{24,20... | collective-permute-start | bytes 1572872 | tf_op jit(solution)/shard_map/s9/ppermute | solution.py:109
  420.5 28.0 %collective-permute-start.58 = (bf16[128,2048]{1,0:T(8,128)(2,1)}, bf16[128,2048]{1,0:T(8,128)(2,1)S(1)}, u32[]{:S(2)}, u32[]{:S(2)}) collective-permute-start(bf16[128,2048]{1,0:T(8,128)(2,1)} %get-tuple-element.344.refs_0_), channel_id=1, source_target_pairs={{0,2},{2,0},{8,10},{10,8},{1,3},{3,1},{9,11},{11,9},{4,6},{6,4},{1... | collective-permute-start | bytes 1572872 | tf_op jit(solution)/shard_map/s9/team01/ppermute | solution.py:64
  422.4 26.2 %collective-permute-start.61 = (bf16[256,1024]{1,0:T(8,128)(2,1)}, bf16[256,1024]{1,0:T(8,128)(2,1)S(1)}, u32[]{:S(2)}, u32[]{:S(2)}) collective-permute-start(bf16[256,1024]{1,0:T(8,128)(2,1)} %copy-done.101), channel_id=1, source_target_pairs={{0,16},{16,0},{1,17},{17,1},{2,18},{18,2},{3,19},{19,3},{4,20},{20... | collective-permute-start | bytes 1572872 | tf_op jit(solution)/shard_map/s9/ring_h/ppermute | solution.py:69
  452.6 26.5 %collective-permute-start.66 = (bf16[256,1024]{1,0:T(8,128)(2,1)S(1)}, bf16[256,1024]{1,0:T(8,128)(2,1)S(1)}, u32[]{:S(2)}, u32[]{:S(2)}) collective-permute-start(bf16[256,1024]{1,0:T(8,128)(2,1)S(1)} %s9.6), channel_id=1, source_target_pairs={{0,16},{16,0},{1,17},{17,1},{2,18},{18,2},{3,19},{19,3},{4,20},{20... | collective-permute-start | bytes 1572872 | tf_op jit(solution)/shard_map/c4/ring_h/ppermute | solution.py:69
  452.7 26.4 %collective-permute-start.67 = (bf16[128,2048]{1,0:T(8,128)(2,1)S(1)}, bf16[128,2048]{1,0:T(8,128)(2,1)S(1)}, u32[]{:S(2)}, u32[]{:S(2)}) collective-permute-start(bf16[128,2048]{1,0:T(8,128)(2,1)S(1)} %get-tuple-element.353), channel_id=1, source_target_pairs={{0,8},{4,0},{8,12},{12,4},{1,9},{5,1},{9,13},{13,5},{2,10},{6,2},{... | collective-permute-start | bytes 1572872 | tf_op jit(solution)/shard_map/c4/ppermute | solution.py:431
  482.4 26.3 %collective-permute-start.69 = (bf16[256,1024]{1,0:T(8,128)(2,1)}, bf16[256,1024]{1,0:T(8,128)(2,1)}, u32[]{:S(2)}, u32[]{:S(2)}) collective-permute-start(bf16[256,1024]{1,0:T(8,128)(2,1)} %copy-done.104), channel_id=1, source_target_pairs={{0,16},{16,0},{1,17},{17,1},{2,18},{18,2},{3,19},{19,3},{4,20},{20... | collective-permute-start | bytes 1572872 | tf_op jit(solution)/shard_map/c4/ring_h/ppermute | solution.py:69
  512.1 26.1 %collective-permute-start.70 = (bf16[512,1024]{1,0:T(8,128)(2,1)S(1)}, bf16[512,1024]{1,0:T(8,128)(2,1)S(1)}, u32[]{:S(2)}, u32[]{:S(2)}) collective-permute-start(bf16[512,1024]{1,0:T(8,128)(2,1)S(1)} %s10.4), channel_id=1, source_target_pairs={{0,4},{4,0},{1,5},{5,1},{2,6},{6,2},{3,7},{7,3},{8,12},{12,8},{9,1... | collective-permute-start | bytes 3145736 | tf_op jit(solution)/shard_map/s10/ring_y/ppermute | solution.py:69
  514.6 36.9 %collective-permute-start.74 = (bf16[512,768]{1,0:T(8,128)(2,1)S(1)}, bf16[512,768]{1,0:T(8,128)(2,1)S(1)}, u32[]{:S(2)}, u32[]{:S(2)}) collective-permute-start(bf16[512,768]{1,0:T(8,128)(2,1)S(1)} %s10.5), channel_id=1, source_target_pairs={{0,16},{16,0},{1,17},{17,1},{2,18},{18,2},{3,19},{19,3},{4,20},{20... | collective-permute-start | bytes 2359304 | tf_op jit(solution)/shard_map/s10/ring_h/ppermute | solution.py:69
  523.6 29.0 %collective-permute-start.73 = (bf16[128,2048]{1,0:T(8,128)(2,1)S(1)}, bf16[128,2048]{1,0:T(8,128)(2,1)S(1)}, u32[]{:S(2)}, u32[]{:S(2)}) collective-permute-start(bf16[128,2048]{1,0:T(8,128)(2,1)S(1)} %add_convert_fusion.1), channel_id=1, source_target_pairs={{0,8},{2,10},{8,0},{10,2},{1,9},{3,11},{9,1},{11,3},{4,12},{6,14},... | collective-permute-start | bytes 1572872 | tf_op jit(solution)/shard_map/s10/team10/ppermute | solution.py:64
  529.2 34.8 %collective-permute-start.76 = (bf16[512,1024]{1,0:T(8,128)(2,1)}, bf16[512,1024]{1,0:T(8,128)(2,1)}, u32[]{:S(2)}, u32[]{:S(2)}) collective-permute-start(bf16[512,1024]{1,0:T(8,128)(2,1)} %pad_maximum_fusion.7), channel_id=1, source_target_pairs={{0,4},{4,0},{1,5},{5,1},{2,6},{6,2},{3,7},{7,3},{8,12},{12,8},{9,1... | collective-permute-start | bytes 3145736 | tf_op jit(solution)/shard_map/s11/ring_y/ppermute | solution.py:69
  555.6 33.4 %collective-permute-start.75 = (bf16[128,2048]{1,0:T(8,128)(2,1)}, bf16[128,2048]{1,0:T(8,128)(2,1)}, u32[]{:S(2)}, u32[]{:S(2)}) collective-permute-start(bf16[128,2048]{1,0:T(8,128)(2,1)} %s11.7), channel_id=1, source_target_pairs={{4,8},{8,4},{5,9},{9,5},{6,10},{10,6},{7,11},{11,7},{20,24},{24,20... | collective-permute-start | bytes 1572872 | tf_op jit(solution)/shard_map/s11/ppermute | solution.py:109
  589.4 32.9 %collective-permute-start.83 = (bf16[128,2048]{1,0:T(8,128)(2,1)S(1)}, bf16[128,2048]{1,0:T(8,128)(2,1)S(1)}, u32[]{:S(2)}, u32[]{:S(2)}) collective-permute-start(bf16[128,2048]{1,0:T(8,128)(2,1)S(1)} %get-tuple-element.433), channel_id=1, source_target_pairs={{0,2},{2,0},{8,10},{10,8},{1,3},{3,1},{9,11},{11,9},{4,6},{6,4},{1... | collective-permute-start | bytes 1572872 | tf_op jit(solution)/shard_map/s12/team01/ppermute | solution.py:64
  591.2 31.2 %collective-permute-start.84 = (bf16[128,2048]{1,0:T(8,128)(2,1)S(1)}, bf16[128,2048]{1,0:T(8,128)(2,1)S(1)}, u32[]{:S(2)}, u32[]{:S(2)}) collective-permute-start(bf16[128,2048]{1,0:T(8,128)(2,1)S(1)} %get-tuple-element.432), channel_id=1, source_target_pairs={{0,8},{2,10},{8,0},{10,2},{1,9},{3,11},{9,1},{11,3},{4,12},{6,14},... | collective-permute-start | bytes 1572872 | tf_op jit(solution)/shard_map/s12/team10/ppermute | solution.py:64
  593.2 29.2 %collective-permute-start.85 = (bf16[128,2048]{1,0:T(8,128)(2,1)S(1)}, bf16[128,2048]{1,0:T(8,128)(2,1)S(1)}, u32[]{:S(2)}, u32[]{:S(2)}) collective-permute-start(bf16[128,2048]{1,0:T(8,128)(2,1)S(1)} %get-tuple-element.431), channel_id=1, source_target_pairs={{0,10},{2,8},{8,2},{10,0},{1,11},{3,9},{9,3},{11,1},{4,14},{6,12},... | collective-permute-start | bytes 1572872 | tf_op jit(solution)/shard_map/s12/team11/ppermute | solution.py:64
  595.0 27.2 %collective-permute-start.82 = (bf16[128,2048]{1,0:T(8,128)(2,1)S(1)}, bf16[128,2048]{1,0:T(8,128)(2,1)S(1)}, u32[]{:S(2)}, u32[]{:S(2)}) collective-permute-start(bf16[128,2048]{1,0:T(8,128)(2,1)S(1)} %get-tuple-element.416), channel_id=1, source_target_pairs={{0,1},{1,0},{2,3},{3,2},{4,5},{5,4},{6,7},{7,6},{8,9},{9,8},{10,11... | collective-permute-start | bytes 1572872 | tf_op jit(solution)/shard_map/s12/ring_tp/ppermute | solution.py:69
  (205 other events, 3083.3 us)

commit v7 on v6

--- a/solution.py
+++ b/solution.py
@@ -533,7 +533,7 @@
 
 
 LIGHT = pl.CostEstimate(flops=1000000, bytes_accessed=100000, transcendentals=0)
-KERNEL = pltpu.CompilerParams(vmem_limit_bytes=24 * 1024 * 1024)
+KERNEL = pltpu.CompilerParams(vmem_limit_bytes=16 * 1024 * 1024)
 
 
 def gelu_slope(value):
@@ -1007,17 +1007,18 @@
             near_down,
             [jnp.concatenate(both, axis=0) for both in zip(got_down_a, got_down_b)],
         )
-        got_qkv = flow_qkv.go(flow_qkv.cross(far_qkv))
+        got_qkv_a = flow_qkv.go(flow_qkv.cross_half(0, far_qkv))
+        cross_qkv = flow_qkv.cross_half(1, far_qkv)
         (near_up,) = beside(team, [flow_up.send_near()])
         sums, total_down, near_up, *rest = fence(
-            sums, total_down, near_up, *out_two, *got, *got_qkv, *cross_out
+            sums, total_down, near_up, *out_two, *got, *got_qkv_a, *cross_qkv, *cross_out
         )
         out_two, rest = rest[:3], rest[3:]
         got, rest = rest[:team_count], rest[team_count:]
-        got_qkv, cross_out = rest[:steps], rest[steps:]
+        got_qkv_a, cross_qkv, cross_out = rest[:steps], rest[steps : 2 * steps], rest[2 * steps :]
     with jax.named_scope("s11"):
+        got_qkv_b = flow_qkv.go(cross_qkv)
         got_out = flow_out.go(cross_out)
-        home_down = home_pieces(team, total_down)
         grad_own = (team_total(total, got) + grad_inner).astype(LOWER)
         grad_own = from_team_order(team, grad_own)
         swapped = swap_home(grad_own)
@@ -1026,23 +1027,23 @@
         total_up = flow_up.total(
             near_up, [jnp.concatenate(both, axis=0) for both in zip(got_up_a, got_up_b)]
         )
+        home_both = home_pieces(team, jnp.concatenate([total_down, total_up], axis=1))
         total_out = flow_out.total(near_att, got_out, 3)
+        got_qkv = [jnp.concatenate(both, axis=0) for both in zip(got_qkv_a, got_qkv_b)]
         total_qkv = flow_qkv.total(near_att, got_qkv, 0)
-        sums, swapped, total_up, total_out, total_qkv, *rest = fence(
-            sums, swapped, total_up, total_out, total_qkv, *home_down, *out_two
-        )
-        home_down, out_two = rest[:members], rest[members:]
-        (grad_down,) = home_join(team, home_down, [tall])
+        sums, swapped, total_out, total_qkv, *rest = fence(
+            sums, swapped, total_out, total_qkv, *home_both, *out_two
+        )
+        home_both, out_two = rest[:members], rest[members:]
+        grad_down, grad_up = home_join(team, home_both, [tall, tall])
     with jax.named_scope("s12"):
         grad_tokens = join_cores(team, swapped_home(team, grad_own, swapped))
-        home_all = home_pieces(team, jnp.concatenate([total_up, total_qkv, total_out], axis=1))
+        home_att = home_pieces(team, jnp.concatenate([total_qkv, total_out], axis=1))
         output = join_cores(team, dealt_out(team, out_two))
         sums = add_ring(
-            team, add_ring(team, add_ring(team, sums, "l"), "h"), "y"
+            team, add_ring(team, add_ring(team, sums, "h"), "y"), "l"
         ).reshape(-1)
-        grad_up, grad_query, grad_key, grad_value, grad_out = home_join(
-            team, home_all, [tall] + [wide] * 4
-        )
+        grad_query, grad_key, grad_value, grad_out = home_join(team, home_att, [wide] * 4)
     smalls = []
     first = 0
     for size in [width] * 6 + [b_query.shape[0], b_value.shape[0], b_up.shape[0]]:

time: 636 us -> 631 us (level)
  waiting for transfers between devices: 332 us -> 303 us
  starting transfers between devices: 98.8 us -> 113 us
  Pallas kernels: 114 us -> 121 us
    ppermute x44 -> x45, waiting for transfers between devices: 159 us -> 142 us  [ring(): lax.ppermute(value, name, [(i, (i + step) % size) for i in range(size)])]
    ppermute x39, waiting for transfers between devices: 164 us -> 152 us  [shift_(): return lax.ppermute(value, TEAM, perm)]
    ppermute x44 -> x45, starting transfers between devices: 30.1 us -> 40.2 us  [ring(): lax.ppermute(value, name, [(i, (i + step) % size) for i in range(size)])]
    pallas_call x19 -> x20, Pallas kernels: 29.2 us -> 33.9 us  [outer(): pl.pallas_call(functools.partial(outer_kernel, len(lefts), len(adds)), gr...]
    unnamed x299 -> x301, local copies, waits for them, and re-layouts: 22.8 us -> 24 us
  transfers between devices with their start and end apart: 89 -> 90, of which waited for: 48 -> 46; matrix products, arithmetic and copies ran while one was open for 6% -> 7% of each run, Pallas kernels for 16% -> 18%
where the time goes in v7:
time: 631 us; the launch traced here: 621 us
  waiting for transfers between devices  303 us (48%)
  Pallas kernels  121 us (19%)
  starting transfers between devices  113 us (18%)
  local copies, waits for them, and re-layouts  43.3 us (7%)
  other arithmetic  33.8 us (5%)
  between operations  6.99 us (1%)
    ppermute x39, waiting for transfers between devices, shift_(): return lax.ppermute(value, TEAM, perm)  152 us
    ppermute x45, waiting for transfers between devices, ring(): lax.ppermute(value, name, [(i, (i + step) % size) for i in range(size)])  142 us
    ppermute x39, starting transfers between devices, shift_(): return lax.ppermute(value, TEAM, perm)  62.9 us
    ppermute x45, starting transfers between devices, ring(): lax.ppermute(value, name, [(i, (i + step) % size) for i in range(size)])  40.2 us
    pallas_call x20, Pallas kernels, outer(): pl.pallas_call(functools.partial(outer_kernel, len(lefts), len(adds)), gr...  33.9 us
    pallas_call x8, Pallas kernels, spread(): pl.pallas_call(functools.partial(spread_kernel, len(pieces), len(got), sp...  24.9 us
    pallas_call x6, Pallas kernels, project(): pl.pallas_call(functools.partial(project_kernel, mode, len(parts), len(pi...  24.4 us
    unnamed x301, local copies, waits for them, and re-layouts  24 us
  transfers between devices with their start and end apart: 90, of which 46 were waited for; matrix products, arithmetic and copies ran while one was open for 7% of the time, Pallas kernels for 18%

profile of v7, /device:TPU:0, one launch (start us, length us, event | category | flops | bytes accessed | tf_op | source)
XLA Modules:
  0.0 620.6 jit_solution(6159181390715128856)
XLA Ops:
  26.3 13.2 %collective-permute-start.6 = (bf16[128,2048]{1,0:T(8,128)(2,1)}, bf16[128,2048]{1,0:T(8,128)(2,1)S(1)}, u32[]{:S(2)}, u32[]{:S(2)}) collective-permute-start(bf16[128,2048]{1,0:T(8,128)(2,1)} %a1.2.refs_0_), channel_id=1, source_target_pairs={{0,8},{2,10},{8,0},{10,2},{1,9},{3,11},{9,1},{11,3},{4,12},{6,14},... | collective-permute-start | bytes 1572872 | tf_op jit(solution)/shard_map/a1/team10/ppermute | solution.py:64
  43.6 17.3 %collective-permute-done.6.refs_2_ = bf16[128,2048]{1,0:T(8,128)(2,1)S(1)} collective-permute-done((bf16[128,2048]{1,0:T(8,128)(2,1)}, bf16[128,2048]{1,0:T(8,128)(2,1)S(1)}, u32[]{:S(2)}, u32[]{:S(2)}) %collective-permute-start.6) | collective-permute-done | bytes 524320 | tf_op jit(solution)/shard_map/a1/team10/ppermute | solution.py:64
  61.4 14.8 %collective-permute-done.8.refs_3_.refs_1_ = bf16[512,768]{1,0:T(8,128)(2,1)} collective-permute-done((bf16[512,768]{1,0:T(8,128)(2,1)S(1)}, bf16[512,768]{1,0:T(8,128)(2,1)}, u32[]{:S(2)}, u32[]{:S(2)}) %collective-permute-start.8) | collective-permute-done | bytes 786464 | tf_op jit(solution)/shard_map/a1/ring_h/ppermute | solution.py:69
  84.2 4.8 collective-permute-done.10.refs_1_
  90.4 10.0 %collective-permute-done.12.refs_3_ = bf16[128,1024]{1,0:T(8,128)(2,1)S(1)} collective-permute-done((bf16[128,1024]{1,0:T(8,128)(2,1)S(1)}, bf16[128,1024]{1,0:T(8,128)(2,1)S(1)}, u32[]{:S(2)}, u32[]{:S(2)}) %collective-permute-start.12) | collective-permute-done | bytes 262176 | tf_op jit(solution)/shard_map/a2/team11/ppermute | solution.py:64
  110.6 6.1 c1.5.query_ref.key_ref.value_ref
  116.7 6.3 %c1.6 = (bf16[1024,256]{1,0:T(8,128)(2,1)S(1)}, f32[2,1,1024]{2,1,0:T(1,128)S(1)}) custom-call(s32[8]{0:T(128)S(1)} %multiply_subtract_fusion.limits_ref, bf16[1024,768]{1,0:T(8,128)(2,1)S(1)} %c1.5.query_ref.key_ref.value_ref, bf16[1024,768]{1,0:T(8,128)(2,1)S(1)} %c1.5.query_ref.key_ref.value_ref, bf16[1024,768]{1,0:T(8,128)(2,1)S(1)} %c1.5.query_ref.key_ref.value_ref), custom_call_target="tpu_custom_call" | custom-call | flops 1000000 | bytes 100000 | tf_op jit(solution)/shard_map/c1/pallas_call | solution.py:700
  123.8 5.7 collective-permute-done.19.refs_3_
  141.9 8.8 %collective-permute-done.23 = bf16[128,2048]{1,0:T(8,128)(2,1)S(1)} collective-permute-done((bf16[128,2048]{1,0:T(8,128)(2,1)S(1)}, bf16[128,2048]{1,0:T(8,128)(2,1)S(1)}, u32[]{:S(2)}, u32[]{:S(2)}) %collective-permute-start.23) | collective-permute-done | bytes 524320 | tf_op jit(solution)/shard_map/s3/team01/ppermute | solution.py:64
  156.1 5.5 collective-permute-done.22
  161.6 11.7 %collective-permute-done.26 = bf16[512,1024]{1,0:T(8,128)(2,1)} collective-permute-done((bf16[512,1024]{1,0:T(8,128)(2,1)}, bf16[512,1024]{1,0:T(8,128)(2,1)}, u32[]{:S(2)}, u32[]{:S(2)}) %collective-permute-start.26) | collective-permute-done | bytes 1048608 | tf_op jit(solution)/shard_map/s3/ring_y/ppermute | solution.py:69
  173.3 4.6 collective-permute-done.24
  186.9 20.5 %collective-permute-done.29.refs_2_ = bf16[128,2048]{1,0:T(8,128)(2,1)S(1)} collective-permute-done((bf16[128,2048]{1,0:T(8,128)(2,1)S(1)}, bf16[128,2048]{1,0:T(8,128)(2,1)S(1)}, u32[]{:S(2)}, u32[]{:S(2)}) %collective-permute-start.29) | collective-permute-done | bytes 524320 | tf_op jit(solution)/shard_map/s4/team10/ppermute | solution.py:64
  208.5 9.2 %collective-permute-done.27 = bf16[128,2048]{1,0:T(8,128)(2,1)S(1)} collective-permute-done((bf16[128,2048]{1,0:T(8,128)(2,1)}, bf16[128,2048]{1,0:T(8,128)(2,1)S(1)}, u32[]{:S(2)}, u32[]{:S(2)}) %collective-permute-start.27) | collective-permute-done | bytes 524320 | tf_op jit(solution)/shard_map/s4/flip/ppermute | solution.py:411
  222.6 4.6 c2.4
  228.6 4.4 c2.5
  233.1 13.4 %collective-permute-done.34.refs_3_.refs_4_ = bf16[256,1024]{1,0:T(8,128)(2,1)S(1)} collective-permute-done((bf16[256,1024]{1,0:T(8,128)(2,1)S(1)}, bf16[256,1024]{1,0:T(8,128)(2,1)S(1)}, u32[]{:S(2)}, u32[]{:S(2)}) %collective-permute-start.34) | collective-permute-done | bytes 524320 | tf_op jit(solution)/shard_map/c2/ring_h/ppermute | solution.py:69
  249.3 22.2 %collective-permute-done.36 = bf16[512,1024]{1,0:T(8,128)(2,1)S(1)} collective-permute-done((bf16[512,1024]{1,0:T(8,128)(2,1)S(1)}, bf16[512,1024]{1,0:T(8,128)(2,1)S(1)}, u32[]{:S(2)}, u32[]{:S(2)}) %collective-permute-start.36) | collective-permute-done | bytes 1048608 | tf_op jit(solution)/shard_map/s5/ring_y/ppermute | solution.py:69
  290.5 7.0 %collective-permute-done.39 = bf16[128,2048]{1,0:T(8,128)(2,1)} collective-permute-done((bf16[128,2048]{1,0:T(8,128)(2,1)}, bf16[128,2048]{1,0:T(8,128)(2,1)}, u32[]{:S(2)}, u32[]{:S(2)}) %collective-permute-start.39) | collective-permute-done | bytes 524320 | tf_op jit(solution)/shard_map/s6/team01/ppermute | solution.py:64
  299.4 10.5 %collective-permute-done.41 = bf16[128,2048]{1,0:T(8,128)(2,1)} collective-permute-done((bf16[128,2048]{1,0:T(8,128)(2,1)}, bf16[128,2048]{1,0:T(8,128)(2,1)}, u32[]{:S(2)}, u32[]{:S(2)}) %collective-permute-start.41) | collective-permute-done | bytes 524320 | tf_op jit(solution)/shard_map/s6/team11/ppermute | solution.py:64
  321.0 13.1 %collective-permute-done.43.refs_2_ = bf16[128,2048]{1,0:T(8,128)(2,1)S(1)} collective-permute-done((bf16[128,2048]{1,0:T(8,128)(2,1)S(1)}, bf16[128,2048]{1,0:T(8,128)(2,1)S(1)}, u32[]{:S(2)}, u32[]{:S(2)}) %collective-permute-start.43) | collective-permute-done | bytes 524320 | tf_op jit(solution)/shard_map/s7/team10/ppermute | solution.py:64
  336.8 6.6 %collective-permute-done.45 = bf16[128,2048]{1,0:T(8,128)(2,1)S(1)} collective-permute-done((bf16[128,2048]{1,0:T(8,128)(2,1)}, bf16[128,2048]{1,0:T(8,128)(2,1)S(1)}, u32[]{:S(2)}, u32[]{:S(2)}) %collective-permute-start.45) | collective-permute-done | bytes 524320 | tf_op jit(solution)/shard_map/s7/ring_h/ppermute | solution.py:69
  384.9 5.0 collective-permute-done.52
  394.6 14.0 %collective-permute-done.50.refs_4_ = bf16[512,1024]{1,0:T(8,128)(2,1)S(1)} collective-permute-done((bf16[512,1024]{1,0:T(8,128)(2,1)S(1)}, bf16[512,1024]{1,0:T(8,128)(2,1)S(1)}, u32[]{:S(2)}, u32[]{:S(2)}) %collective-permute-start.50) | collective-permute-done | bytes 1048608 | tf_op jit(solution)/shard_map/s8/ring_y/ppermute | solution.py:69
  425.2 16.5 %collective-permute-done.59.refs_2_ = bf16[128,2048]{1,0:T(8,128)(2,1)} collective-permute-done((bf16[128,2048]{1,0:T(8,128)(2,1)}, bf16[128,2048]{1,0:T(8,128)(2,1)}, u32[]{:S(2)}, u32[]{:S(2)}) %collective-permute-start.59) | collective-permute-done | bytes 524320 | tf_op jit(solution)/shard_map/s9/team10/ppermute | solution.py:64
  461.9 9.4 %c4.10.refs_2_.refs_3_.rows_ref = bf16[1024,768]{1,0:T(8,128)(2,1)S(1)} custom-call(s32[8]{0:T(128)S(1)} %multiply_subtract_fusion.limits_ref, bf16[1024,768]{1,0:T(8,128)(2,1)S(1)} %copy-done.15, bf16[1024,768]{1,0:T(8,128)(2,1)S(1)} %copy-done.15, bf16[1024,768]{1,0:T(8,128)(2,1)S(1)} %copy-done.15, bf16[1024,256]{1,0:T(8,128)(2,1)S(1)} %c4.9.grad_ref, ...), custom_call_target="tpu_custom_call" | custom-call | flops 1000000 | bytes 100000 | tf_op jit(solution)/shard_map/c4/pallas_call | solution.py:725
  471.3 4.6 c4.14
  499.1 5.0 c4.15
  504.1 4.9 collective-permute-done.69
  514.6 9.2 %collective-permute-done.72 = bf16[128,2048]{1,0:T(8,128)(2,1)S(1)} collective-permute-done((bf16[128,2048]{1,0:T(8,128)(2,1)S(1)}, bf16[128,2048]{1,0:T(8,128)(2,1)S(1)}, u32[]{:S(2)}, u32[]{:S(2)}) %collective-permute-start.72) | collective-permute-done | bytes 524320 | tf_op jit(solution)/shard_map/s10/team01/ppermute | solution.py:64
  562.2 17.7 %collective-permute-done.77.refs_5_ = bf16[512,256]{1,0:T(8,128)(2,1)} collective-permute-done((bf16[512,256]{1,0:T(8,128)(2,1)S(1)}, bf16[512,256]{1,0:T(8,128)(2,1)}, u32[]{:S(2)}, u32[]{:S(2)}) %collective-permute-start.77) | collective-permute-done | bytes 262176 | tf_op jit(solution)/shard_map/s11/ring_h/ppermute | solution.py:69
  596.1 7.8 %collective-permute-start.85 = (bf16[128,1024]{1,0:T(8,128)(2,1)S(1)}, bf16[128,1024]{1,0:T(8,128)(2,1)S(1)}, u32[]{:S(2)}, u32[]{:S(2)}) collective-permute-start(bf16[128,1024]{1,0:T(8,128)(2,1)S(1)} %get-tuple-element.441), channel_id=1, source_target_pairs={{0,8},{2,10},{8,0},{10,2},{1,9},{3,11},{9,1},{11,3},{4,12},{6,14},... | collective-permute-start | bytes 786440 | tf_op jit(solution)/shard_map/s12/team10/ppermute | solution.py:64
  (599 shorter events, 299.1 us)
Async XLA Ops:
  26.3 34.5 %collective-permute-start.6 = (bf16[128,2048]{1,0:T(8,128)(2,1)}, bf16[128,2048]{1,0:T(8,128)(2,1)S(1)}, u32[]{:S(2)}, u32[]{:S(2)}) collective-permute-start(bf16[128,2048]{1,0:T(8,128)(2,1)} %a1.2.refs_0_), channel_id=1, source_target_pairs={{0,8},{2,10},{8,0},{10,2},{1,9},{3,11},{9,1},{11,3},{4,12},{6,14},... | collective-permute-start | bytes 1572872 | tf_op jit(solution)/shard_map/a1/team10/ppermute | solution.py:64
  40.2 35.9 %collective-permute-start.4 = (bf16[512,1024]{1,0:T(8,128)(2,1)S(1)}, bf16[512,1024]{1,0:T(8,128)(2,1)S(1)}, u32[]{:S(2)}, u32[]{:S(2)}) collective-permute-start(bf16[512,1024]{1,0:T(8,128)(2,1)S(1)} %a1.3.refs_2_.refs_0_), channel_id=1, source_target_pairs={{0,4},{4,0},{1,5},{5,1},{2,6},{6,2},{3,7},{7,3},{8,12},{12,8},{9,1... | collective-permute-start | bytes 3145736 | tf_op jit(solution)/shard_map/a1/ring_y/ppermute | solution.py:69
  40.4 35.8 %collective-permute-start.8 = (bf16[512,768]{1,0:T(8,128)(2,1)S(1)}, bf16[512,768]{1,0:T(8,128)(2,1)}, u32[]{:S(2)}, u32[]{:S(2)}) collective-permute-start(bf16[512,768]{1,0:T(8,128)(2,1)S(1)} %slice.124), channel_id=1, source_target_pairs={{0,16},{16,0},{1,17},{17,1},{2,18},{18,2},{3,19},{19,3},{4,20},{20... | collective-permute-start | bytes 2359304 | tf_op jit(solution)/shard_map/a1/ring_h/ppermute | solution.py:69
  77.3 26.0 %collective-permute-start.9 = (bf16[512,2048]{1,0:T(8,128)(2,1)S(1)}, bf16[512,2048]{1,0:T(8,128)(2,1)}, u32[]{:S(2)}, u32[]{:S(2)}) collective-permute-start(bf16[512,2048]{1,0:T(8,128)(2,1)S(1)} %a2.1.refs_0_), channel_id=1, source_target_pairs={{0,1},{1,0},{2,3},{3,2},{4,5},{5,4},{6,7},{7,6},{8,9},{9,8},{10,11... | collective-permute-start | bytes 6291464 | tf_op jit(solution)/shard_map/a2/ring_tp/ppermute | solution.py:69
  77.4 25.9 %collective-permute-start.13 = (bf16[512,768]{1,0:T(8,128)(2,1)}, bf16[512,768]{1,0:T(8,128)(2,1)}, u32[]{:S(2)}, u32[]{:S(2)}) collective-permute-start(bf16[512,768]{1,0:T(8,128)(2,1)} %collective-permute-done.8.refs_3_.refs_1_), channel_id=1, source_target_pairs={{0,4},{4,0},{1,5},{5,1},{2,6},{6,2},{3,7},{7,3},{8,12},{12,8},{9,1... | collective-permute-start | bytes 2359304 | tf_op jit(solution)/shard_map/a2/ring_y/ppermute | solution.py:69
  139.1 34.3 %collective-permute-start.26 = (bf16[512,1024]{1,0:T(8,128)(2,1)}, bf16[512,1024]{1,0:T(8,128)(2,1)}, u32[]{:S(2)}, u32[]{:S(2)}) collective-permute-start(bf16[512,1024]{1,0:T(8,128)(2,1)} %pad_maximum_fusion.1), channel_id=1, source_target_pairs={{0,4},{4,0},{1,5},{5,1},{2,6},{6,2},{3,7},{7,3},{8,12},{12,8},{9,1... | collective-permute-start | bytes 3145736 | tf_op jit(solution)/shard_map/s3/ring_y/ppermute | solution.py:69
  151.7 26.3 %collective-permute-start.24 = (bf16[128,2048]{1,0:T(8,128)(2,1)}, bf16[128,2048]{1,0:T(8,128)(2,1)}, u32[]{:S(2)}, u32[]{:S(2)}) collective-permute-start(bf16[128,2048]{1,0:T(8,128)(2,1)} %add_convert_fusion.3), channel_id=1, source_target_pairs={{0,8},{2,10},{8,0},{10,2},{1,9},{3,11},{9,1},{11,3},{4,12},{6,14},... | collective-permute-start | bytes 1572872 | tf_op jit(solution)/shard_map/s3/team10/ppermute | solution.py:64
  179.1 38.6 %collective-permute-start.32 = (bf16[512,1024]{1,0:T(8,128)(2,1)S(1)}, bf16[512,1024]{1,0:T(8,128)(2,1)S(1)}, u32[]{:S(2)}, u32[]{:S(2)}) collective-permute-start(bf16[512,1024]{1,0:T(8,128)(2,1)S(1)} %pad_maximum_fusion.2), channel_id=1, source_target_pairs={{0,4},{4,0},{1,5},{5,1},{2,6},{6,2},{3,7},{7,3},{8,12},{12,8},{9,1... | collective-permute-start | bytes 3145736 | tf_op jit(solution)/shard_map/s4/ring_y/ppermute | solution.py:69
  181.4 26.1 %collective-permute-start.29 = (bf16[128,2048]{1,0:T(8,128)(2,1)S(1)}, bf16[128,2048]{1,0:T(8,128)(2,1)S(1)}, u32[]{:S(2)}, u32[]{:S(2)}) collective-permute-start(bf16[128,2048]{1,0:T(8,128)(2,1)S(1)} %fusion.3.refs_0_), channel_id=1, source_target_pairs={{0,8},{2,10},{8,0},{10,2},{1,9},{3,11},{9,1},{11,3},{4,12},{6,14},... | collective-permute-start | bytes 1572872 | tf_op jit(solution)/shard_map/s4/team10/ppermute | solution.py:64
  183.0 25.5 %collective-permute-start.28 = (bf16[128,2048]{1,0:T(8,128)(2,1)S(1)}, bf16[128,2048]{1,0:T(8,128)(2,1)S(1)}, u32[]{:S(2)}, u32[]{:S(2)}) collective-permute-start(bf16[128,2048]{1,0:T(8,128)(2,1)S(1)} %fusion.3.refs_0_), channel_id=1, source_target_pairs={{0,2},{2,0},{8,10},{10,8},{1,3},{3,1},{9,11},{11,9},{4,6},{6,4},{1... | collective-permute-start | bytes 1572872 | tf_op jit(solution)/shard_map/s4/team01/ppermute | solution.py:64
  183.3 34.4 %collective-permute-start.27 = (bf16[128,2048]{1,0:T(8,128)(2,1)}, bf16[128,2048]{1,0:T(8,128)(2,1)S(1)}, u32[]{:S(2)}, u32[]{:S(2)}) collective-permute-start(bf16[128,2048]{1,0:T(8,128)(2,1)} %constant_dynamic-slice_fusion), channel_id=1, source_target_pairs={{0,4},{4,12},{8,0},{12,8},{1,5},{5,13},{9,1},{13,9},{2,6},{6,14},{... | collective-permute-start | bytes 1572872 | tf_op jit(solution)/shard_map/s4/flip/ppermute | solution.py:411
  184.5 33.2 %collective-permute-start.31 = (bf16[256,1024]{1,0:T(8,128)(2,1)S(1)}, bf16[256,1024]{1,0:T(8,128)(2,1)S(1)}, u32[]{:S(2)}, u32[]{:S(2)}) collective-permute-start(bf16[256,1024]{1,0:T(8,128)(2,1)S(1)} %get-tuple-element.288.refs_0_.refs_1_), channel_id=1, source_target_pairs={{0,16},{16,0},{1,17},{17,1},{2,18},{18,2},{3,19},{19,3},{4,20},{20... | collective-permute-start | bytes 1572872 | tf_op jit(solution)/shard_map/s4/ring_h/ppermute | solution.py:69
  219.9 26.6 %collective-permute-start.35 = (bf16[512,1024]{1,0:T(8,128)(2,1)S(1)}, bf16[512,1024]{1,0:T(8,128)(2,1)S(1)}, u32[]{:S(2)}, u32[]{:S(2)}) collective-permute-start(bf16[512,1024]{1,0:T(8,128)(2,1)S(1)} %pad_maximum_fusion.3), channel_id=1, source_target_pairs={{0,4},{4,0},{1,5},{5,1},{2,6},{6,2},{3,7},{7,3},{8,12},{12,8},{9,1... | collective-permute-start | bytes 3145736 | tf_op jit(solution)/shard_map/c2/ring_y/ppermute | solution.py:69
  219.9 26.5 %collective-permute-start.34 = (bf16[256,1024]{1,0:T(8,128)(2,1)S(1)}, bf16[256,1024]{1,0:T(8,128)(2,1)S(1)}, u32[]{:S(2)}, u32[]{:S(2)}) collective-permute-start(bf16[256,1024]{1,0:T(8,128)(2,1)S(1)} %get-tuple-element.294.refs_1_.refs_2_), channel_id=1, source_target_pairs={{0,16},{16,0},{1,17},{17,1},{2,18},{18,2},{3,19},{19,3},{4,20},{20... | collective-permute-start | bytes 1572872 | tf_op jit(solution)/shard_map/c2/ring_h/ppermute | solution.py:69
  284.3 25.6 %collective-permute-start.41 = (bf16[128,2048]{1,0:T(8,128)(2,1)}, bf16[128,2048]{1,0:T(8,128)(2,1)}, u32[]{:S(2)}, u32[]{:S(2)}) collective-permute-start(bf16[128,2048]{1,0:T(8,128)(2,1)} %get-tuple-element.313), channel_id=1, source_target_pairs={{0,10},{2,8},{8,2},{10,0},{1,11},{3,9},{9,3},{11,1},{4,14},{6,12},... | collective-permute-start | bytes 1572872 | tf_op jit(solution)/shard_map/s6/team11/ppermute | solution.py:64
  315.5 27.9 %collective-permute-start.42 = (bf16[128,2048]{1,0:T(8,128)(2,1)S(1)}, bf16[128,2048]{1,0:T(8,128)(2,1)}, u32[]{:S(2)}, u32[]{:S(2)}) collective-permute-start(bf16[128,2048]{1,0:T(8,128)(2,1)S(1)} %get-tuple-element.319.refs_0_), channel_id=1, source_target_pairs={{0,2},{2,0},{8,10},{10,8},{1,3},{3,1},{9,11},{11,9},{4,6},{6,4},{1... | collective-permute-start | bytes 1572872 | tf_op jit(solution)/shard_map/s7/team01/ppermute | solution.py:64
  382.6 26.1 %collective-permute-start.50 = (bf16[512,1024]{1,0:T(8,128)(2,1)S(1)}, bf16[512,1024]{1,0:T(8,128)(2,1)S(1)}, u32[]{:S(2)}, u32[]{:S(2)}) collective-permute-start(bf16[512,1024]{1,0:T(8,128)(2,1)S(1)} %s8_.3), channel_id=1, source_target_pairs={{0,4},{4,0},{1,5},{5,1},{2,6},{6,2},{3,7},{7,3},{8,12},{12,8},{9,1... | collective-permute-start | bytes 3145736 | tf_op jit(solution)/shard_map/s8/ring_y/ppermute | solution.py:69
  392.6 56.3 %collective-permute-start.56 = (bf16[512,1024]{1,0:T(8,128)(2,1)}, bf16[512,1024]{1,0:T(8,128)(2,1)}, u32[]{:S(2)}, u32[]{:S(2)}) collective-permute-start(bf16[512,1024]{1,0:T(8,128)(2,1)} %s9.5), channel_id=1, source_target_pairs={{0,4},{4,0},{1,5},{5,1},{2,6},{6,2},{3,7},{7,3},{8,12},{12,8},{9,1... | collective-permute-start | bytes 3145736 | tf_op jit(solution)/shard_map/s9/ring_y/ppermute | solution.py:69
  416.3 25.5 %collective-permute-start.59 = (bf16[128,2048]{1,0:T(8,128)(2,1)}, bf16[128,2048]{1,0:T(8,128)(2,1)}, u32[]{:S(2)}, u32[]{:S(2)}) collective-permute-start(bf16[128,2048]{1,0:T(8,128)(2,1)} %get-tuple-element.345.refs_0_), channel_id=1, source_target_pairs={{0,8},{2,10},{8,0},{10,2},{1,9},{3,11},{9,1},{11,3},{4,12},{6,14},... | collective-permute-start | bytes 1572872 | tf_op jit(solution)/shard_map/s9/team10/ppermute | solution.py:64
  419.9 28.9 %collective-permute-start.57 = (bf16[128,2048]{1,0:T(8,128)(2,1)S(1)}, bf16[128,2048]{1,0:T(8,128)(2,1)S(1)}, u32[]{:S(2)}, u32[]{:S(2)}) collective-permute-start(bf16[128,2048]{1,0:T(8,128)(2,1)S(1)} %get-tuple-element.386), channel_id=1, source_target_pairs={{4,8},{8,4},{5,9},{9,5},{6,10},{10,6},{7,11},{11,7},{20,24},{24,20... | collective-permute-start | bytes 1572872 | tf_op jit(solution)/shard_map/s9/ppermute | solution.py:109
  420.6 28.3 %collective-permute-start.58 = (bf16[128,2048]{1,0:T(8,128)(2,1)}, bf16[128,2048]{1,0:T(8,128)(2,1)S(1)}, u32[]{:S(2)}, u32[]{:S(2)}) collective-permute-start(bf16[128,2048]{1,0:T(8,128)(2,1)} %get-tuple-element.345.refs_0_), channel_id=1, source_target_pairs={{0,2},{2,0},{8,10},{10,8},{1,3},{3,1},{9,11},{11,9},{4,6},{6,4},{1... | collective-permute-start | bytes 1572872 | tf_op jit(solution)/shard_map/s9/team01/ppermute | solution.py:64
  422.4 26.5 %collective-permute-start.61 = (bf16[256,1024]{1,0:T(8,128)(2,1)}, bf16[256,1024]{1,0:T(8,128)(2,1)S(1)}, u32[]{:S(2)}, u32[]{:S(2)}) collective-permute-start(bf16[256,1024]{1,0:T(8,128)(2,1)} %copy-done.100), channel_id=1, source_target_pairs={{0,16},{16,0},{1,17},{17,1},{2,18},{18,2},{3,19},{19,3},{4,20},{20... | collective-permute-start | bytes 1572872 | tf_op jit(solution)/shard_map/s9/ring_h/ppermute | solution.py:69
  452.9 26.5 %collective-permute-start.66 = (bf16[256,1024]{1,0:T(8,128)(2,1)S(1)}, bf16[256,1024]{1,0:T(8,128)(2,1)S(1)}, u32[]{:S(2)}, u32[]{:S(2)}) collective-permute-start(bf16[256,1024]{1,0:T(8,128)(2,1)S(1)} %s9.6), channel_id=1, source_target_pairs={{0,16},{16,0},{1,17},{17,1},{2,18},{18,2},{3,19},{19,3},{4,20},{20... | collective-permute-start | bytes 1572872 | tf_op jit(solution)/shard_map/c4/ring_h/ppermute | solution.py:69
  452.9 26.4 %collective-permute-start.67 = (bf16[128,2048]{1,0:T(8,128)(2,1)S(1)}, bf16[128,2048]{1,0:T(8,128)(2,1)S(1)}, u32[]{:S(2)}, u32[]{:S(2)}) collective-permute-start(bf16[128,2048]{1,0:T(8,128)(2,1)S(1)} %get-tuple-element.354), channel_id=1, source_target_pairs={{0,8},{4,0},{8,12},{12,4},{1,9},{5,1},{9,13},{13,5},{2,10},{6,2},{... | collective-permute-start | bytes 1572872 | tf_op jit(solution)/shard_map/c4/ppermute | solution.py:431
  482.7 26.3 %collective-permute-start.69 = (bf16[256,1024]{1,0:T(8,128)(2,1)}, bf16[256,1024]{1,0:T(8,128)(2,1)}, u32[]{:S(2)}, u32[]{:S(2)}) collective-permute-start(bf16[256,1024]{1,0:T(8,128)(2,1)} %copy-done.103), channel_id=1, source_target_pairs={{0,16},{16,0},{1,17},{17,1},{2,18},{18,2},{3,19},{19,3},{4,20},{20... | collective-permute-start | bytes 1572872 | tf_op jit(solution)/shard_map/c4/ring_h/ppermute | solution.py:69
  513.2 30.5 %collective-permute-start.70 = (bf16[512,1024]{1,0:T(8,128)(2,1)}, bf16[512,1024]{1,0:T(8,128)(2,1)}, u32[]{:S(2)}, u32[]{:S(2)}) collective-permute-start(bf16[512,1024]{1,0:T(8,128)(2,1)} %s10.5), channel_id=1, source_target_pairs={{0,4},{4,0},{1,5},{5,1},{2,6},{6,2},{3,7},{7,3},{8,12},{12,8},{9,1... | collective-permute-start | bytes 3145736 | tf_op jit(solution)/shard_map/s10/ring_y/ppermute | solution.py:69
  513.5 33.6 %collective-permute-start.71 = (bf16[128,2048]{1,0:T(8,128)(2,1)}, bf16[128,2048]{1,0:T(8,128)(2,1)}, u32[]{:S(2)}, u32[]{:S(2)}) collective-permute-start(bf16[128,2048]{1,0:T(8,128)(2,1)} %get-tuple-element.367), channel_id=1, source_target_pairs={{0,2},{2,0},{8,10},{10,8},{1,3},{3,1},{9,11},{11,9},{4,6},{6,4},{1... | collective-permute-start | bytes 1572872 | tf_op jit(solution)/shard_map/s10/team01/ppermute | solution.py:64
  535.2 25.6 %collective-permute-start.76 = (bf16[512,1024]{1,0:T(8,128)(2,1)}, bf16[512,1024]{1,0:T(8,128)(2,1)}, u32[]{:S(2)}, u32[]{:S(2)}) collective-permute-start(bf16[512,1024]{1,0:T(8,128)(2,1)} %pad_maximum_fusion.6), channel_id=1, source_target_pairs={{0,4},{4,0},{1,5},{5,1},{2,6},{6,2},{3,7},{7,3},{8,12},{12,8},{9,1... | collective-permute-start | bytes 3145736 | tf_op jit(solution)/shard_map/s11/ring_y/ppermute | solution.py:69
  551.5 38.5 %collective-permute-start.79 = (bf16[128,2048]{1,0:T(8,128)(2,1)}, bf16[128,2048]{1,0:T(8,128)(2,1)}, u32[]{:S(2)}, u32[]{:S(2)}) collective-permute-start(bf16[128,2048]{1,0:T(8,128)(2,1)} %get-tuple-element.435), channel_id=1, source_target_pairs={{0,2},{2,0},{8,10},{10,8},{1,3},{3,1},{9,11},{11,9},{4,6},{6,4},{1... | collective-permute-start | bytes 1572872 | tf_op jit(solution)/shard_map/s11/team01/ppermute | solution.py:64
  553.2 36.9 %collective-permute-start.80 = (bf16[128,2048]{1,0:T(8,128)(2,1)}, bf16[128,2048]{1,0:T(8,128)(2,1)}, u32[]{:S(2)}, u32[]{:S(2)}) collective-permute-start(bf16[128,2048]{1,0:T(8,128)(2,1)} %get-tuple-element.434), channel_id=1, source_target_pairs={{0,8},{2,10},{8,0},{10,2},{1,9},{3,11},{9,1},{11,3},{4,12},{6,14},... | collective-permute-start | bytes 1572872 | tf_op jit(solution)/shard_map/s11/team10/ppermute | solution.py:64
  553.2 33.4 %collective-permute-start.78 = (bf16[256,768]{1,0:T(8,128)(2,1)}, bf16[256,768]{1,0:T(8,128)(2,1)}, u32[]{:S(2)}, u32[]{:S(2)}) collective-permute-start(bf16[256,768]{1,0:T(8,128)(2,1)} %s10.7), channel_id=1, source_target_pairs={{0,16},{16,0},{1,17},{17,1},{2,18},{18,2},{3,19},{19,3},{4,20},{20... | collective-permute-start | bytes 1179656 | tf_op jit(solution)/shard_map/s11/ring_h/ppermute | solution.py:69
  560.8 29.3 %collective-permute-start.81 = (bf16[128,2048]{1,0:T(8,128)(2,1)}, bf16[128,2048]{1,0:T(8,128)(2,1)}, u32[]{:S(2)}, u32[]{:S(2)}) collective-permute-start(bf16[128,2048]{1,0:T(8,128)(2,1)} %get-tuple-element.433), channel_id=1, source_target_pairs={{0,10},{2,8},{8,2},{10,0},{1,11},{3,9},{9,3},{11,1},{4,14},{6,12},... | collective-permute-start | bytes 1572872 | tf_op jit(solution)/shard_map/s11/team11/ppermute | solution.py:64
  (207 other events, 3053.0 us)

commit v8 on v7

--- a/solution.py
+++ b/solution.py
@@ -796,6 +796,7 @@
     with jax.named_scope("a0"):
         mine = lax.dynamic_slice_in_dim(tokens, half_at, row_count, 0)
         own = swap_home(mine)
+        w_query, w_key, w_value, w_out = fence(w_query, w_key, w_value, w_out, mine)[:4]
         share = share_columns(team, [w_query, w_key, w_value, w_out])
         own, w_up, w_down, bias_qkv, bias_up, limits, query_live, *rest = fence(
             own, w_up, w_down, bias_qkv, bias_up, limits, query_live, *share, *plan

time: 631 us -> 630 us (level)
  starting transfers between devices: 113 us -> 106 us
    ppermute x39, starting transfers between devices: 62.9 us -> 49 us  [shift_(): return lax.ppermute(value, TEAM, perm)]
    ppermute x39, waiting for transfers between devices: 152 us -> 162 us  [shift_(): return lax.ppermute(value, TEAM, perm)]
    ppermute x45, starting transfers between devices: 40.2 us -> 47.5 us  [ring(): lax.ppermute(value, name, [(i, (i + step) % size) for i in range(size)])]
    unnamed x301 -> x305, local copies, waits for them, and re-layouts: 24 us -> 23.8 us
  transfers between devices with their start and end apart: 90 -> 90, of which waited for: 46 -> 49; matrix products, arithmetic and copies ran while one was open for 7% -> 7% of each run, Pallas kernels for 18% -> 18%
where the time goes in v8:
time: 630 us; the launch traced here: 619 us
  waiting for transfers between devices  309 us (49%)
  Pallas kernels  121 us (19%)
  starting transfers between devices  106 us (17%)
  local copies, waits for them, and re-layouts  42.9 us (7%)
  other arithmetic  33.8 us (5%)
  between operations  6.92 us (1%)
    ppermute x39, waiting for transfers between devices, shift_(): return lax.ppermute(value, TEAM, perm)  162 us
    ppermute x45, waiting for transfers between devices, ring(): lax.ppermute(value, name, [(i, (i + step) % size) for i in range(size)])  140 us
    ppermute x39, starting transfers between devices, shift_(): return lax.ppermute(value, TEAM, perm)  49 us
    ppermute x45, starting transfers between devices, ring(): lax.ppermute(value, name, [(i, (i + step) % size) for i in range(size)])  47.5 us
    pallas_call x20, Pallas kernels, outer(): pl.pallas_call(functools.partial(outer_kernel, len(lefts), len(adds)), gr...  33.6 us
    pallas_call x8, Pallas kernels, spread(): pl.pallas_call(functools.partial(spread_kernel, len(pieces), len(got), sp...  24.9 us
    pallas_call x6, Pallas kernels, project(): pl.pallas_call(functools.partial(project_kernel, mode, len(parts), len(pi...  24.4 us
    unnamed x305, local copies, waits for them, and re-layouts  23.8 us
  transfers between devices with their start and end apart: 90, of which 49 were waited for; matrix products, arithmetic and copies ran while one was open for 7% of the time, Pallas kernels for 18%

profile of v8, /device:TPU:0, one launch (start us, length us, event | category | flops | bytes accessed | tf_op | source)
XLA Modules:
  0.0 619.3 jit_solution(8492316291727990365)
XLA Ops:
  6.9 5.9 collective-permute-start.3
  42.2 16.1 %collective-permute-done.6.refs_2_ = bf16[128,2048]{1,0:T(8,128)(2,1)S(1)} collective-permute-done((bf16[128,2048]{1,0:T(8,128)(2,1)}, bf16[128,2048]{1,0:T(8,128)(2,1)S(1)}, u32[]{:S(2)}, u32[]{:S(2)}) %collective-permute-start.6) | collective-permute-done | bytes 524320 | tf_op jit(solution)/shard_map/a1/team10/ppermute | solution.py:64
  59.8 14.1 %collective-permute-done.8.refs_3_.refs_1_ = bf16[512,768]{1,0:T(8,128)(2,1)} collective-permute-done((bf16[512,768]{1,0:T(8,128)(2,1)S(1)}, bf16[512,768]{1,0:T(8,128)(2,1)}, u32[]{:S(2)}, u32[]{:S(2)}) %collective-permute-start.8) | collective-permute-done | bytes 786464 | tf_op jit(solution)/shard_map/a1/ring_h/ppermute | solution.py:69
  80.8 4.8 collective-permute-done.10.refs_1_
  88.0 9.1 %collective-permute-done.12.refs_3_ = bf16[128,1024]{1,0:T(8,128)(2,1)S(1)} collective-permute-done((bf16[128,1024]{1,0:T(8,128)(2,1)S(1)}, bf16[128,1024]{1,0:T(8,128)(2,1)S(1)}, u32[]{:S(2)}, u32[]{:S(2)}) %collective-permute-start.12) | collective-permute-done | bytes 262176 | tf_op jit(solution)/shard_map/a2/team11/ppermute | solution.py:64
  108.4 6.1 c1.5.query_ref.key_ref.value_ref
  114.5 6.3 %c1.6 = (bf16[1024,256]{1,0:T(8,128)(2,1)S(1)}, f32[2,1,1024]{2,1,0:T(1,128)S(1)}) custom-call(s32[8]{0:T(128)S(1)} %multiply_subtract_fusion.limits_ref, bf16[1024,768]{1,0:T(8,128)(2,1)S(1)} %c1.5.query_ref.key_ref.value_ref, bf16[1024,768]{1,0:T(8,128)(2,1)S(1)} %c1.5.query_ref.key_ref.value_ref, bf16[1024,768]{1,0:T(8,128)(2,1)S(1)} %c1.5.query_ref.key_ref.value_ref), custom_call_target="tpu_custom_call" | custom-call | flops 1000000 | bytes 100000 | tf_op jit(solution)/shard_map/c1/pallas_call | solution.py:700
  121.6 5.3 collective-permute-done.19.refs_3_
  141.0 6.6 %collective-permute-done.23 = bf16[128,2048]{1,0:T(8,128)(2,1)S(1)} collective-permute-done((bf16[128,2048]{1,0:T(8,128)(2,1)S(1)}, bf16[128,2048]{1,0:T(8,128)(2,1)S(1)}, u32[]{:S(2)}, u32[]{:S(2)}) %collective-permute-start.23) | collective-permute-done | bytes 524320 | tf_op jit(solution)/shard_map/s3/team01/ppermute | solution.py:64
  152.7 5.4 collective-permute-done.22
  158.1 8.0 %collective-permute-done.25.refs_4_.refs_3_ = bf16[256,1024]{1,0:T(8,128)(2,1)S(1)} collective-permute-done((bf16[256,1024]{1,0:T(8,128)(2,1)}, bf16[256,1024]{1,0:T(8,128)(2,1)S(1)}, u32[]{:S(2)}, u32[]{:S(2)}) %collective-permute-start.25) | collective-permute-done | bytes 524320 | tf_op jit(solution)/shard_map/s3/ring_h/ppermute | solution.py:69
  166.1 5.8 collective-permute-done.26
  184.7 20.9 %collective-permute-done.29.refs_2_ = bf16[128,2048]{1,0:T(8,128)(2,1)S(1)} collective-permute-done((bf16[128,2048]{1,0:T(8,128)(2,1)S(1)}, bf16[128,2048]{1,0:T(8,128)(2,1)S(1)}, u32[]{:S(2)}, u32[]{:S(2)}) %collective-permute-start.29) | collective-permute-done | bytes 524320 | tf_op jit(solution)/shard_map/s4/team10/ppermute | solution.py:64
  206.9 7.8 %collective-permute-done.27 = bf16[128,2048]{1,0:T(8,128)(2,1)S(1)} collective-permute-done((bf16[128,2048]{1,0:T(8,128)(2,1)}, bf16[128,2048]{1,0:T(8,128)(2,1)S(1)}, u32[]{:S(2)}, u32[]{:S(2)}) %collective-permute-start.27) | collective-permute-done | bytes 524320 | tf_op jit(solution)/shard_map/s4/flip/ppermute | solution.py:411
  221.6 4.6 c2.4
  232.1 11.6 %collective-permute-done.34.refs_3_.refs_4_ = bf16[256,1024]{1,0:T(8,128)(2,1)S(1)} collective-permute-done((bf16[256,1024]{1,0:T(8,128)(2,1)S(1)}, bf16[256,1024]{1,0:T(8,128)(2,1)S(1)}, u32[]{:S(2)}, u32[]{:S(2)}) %collective-permute-start.34) | collective-permute-done | bytes 524320 | tf_op jit(solution)/shard_map/c2/ring_h/ppermute | solution.py:69
  247.9 20.7 %collective-permute-done.36 = bf16[512,1024]{1,0:T(8,128)(2,1)S(1)} collective-permute-done((bf16[512,1024]{1,0:T(8,128)(2,1)S(1)}, bf16[512,1024]{1,0:T(8,128)(2,1)S(1)}, u32[]{:S(2)}, u32[]{:S(2)}) %collective-permute-start.36) | collective-permute-done | bytes 1048608 | tf_op jit(solution)/shard_map/s5/ring_y/ppermute | solution.py:69
  287.5 7.0 %collective-permute-done.39 = bf16[128,2048]{1,0:T(8,128)(2,1)} collective-permute-done((bf16[128,2048]{1,0:T(8,128)(2,1)}, bf16[128,2048]{1,0:T(8,128)(2,1)}, u32[]{:S(2)}, u32[]{:S(2)}) %collective-permute-start.39) | collective-permute-done | bytes 524320 | tf_op jit(solution)/shard_map/s6/team01/ppermute | solution.py:64
  296.9 10.0 %collective-permute-done.41 = bf16[128,2048]{1,0:T(8,128)(2,1)} collective-permute-done((bf16[128,2048]{1,0:T(8,128)(2,1)}, bf16[128,2048]{1,0:T(8,128)(2,1)}, u32[]{:S(2)}, u32[]{:S(2)}) %collective-permute-start.41) | collective-permute-done | bytes 524320 | tf_op jit(solution)/shard_map/s6/team11/ppermute | solution.py:64
  318.6 14.0 %collective-permute-done.43.refs_2_ = bf16[128,2048]{1,0:T(8,128)(2,1)S(1)} collective-permute-done((bf16[128,2048]{1,0:T(8,128)(2,1)S(1)}, bf16[128,2048]{1,0:T(8,128)(2,1)S(1)}, u32[]{:S(2)}, u32[]{:S(2)}) %collective-permute-start.43) | collective-permute-done | bytes 524320 | tf_op jit(solution)/shard_map/s7/team10/ppermute | solution.py:64
  333.9 7.0 %collective-permute-done.45 = bf16[128,2048]{1,0:T(8,128)(2,1)S(1)} collective-permute-done((bf16[128,2048]{1,0:T(8,128)(2,1)}, bf16[128,2048]{1,0:T(8,128)(2,1)S(1)}, u32[]{:S(2)}, u32[]{:S(2)}) %collective-permute-start.45) | collective-permute-done | bytes 524320 | tf_op jit(solution)/shard_map/s7/ring_h/ppermute | solution.py:69
  375.7 5.2 collective-permute-done.49.refs_4_
  382.7 5.5 collective-permute-done.52
  393.2 13.8 %collective-permute-done.50.refs_4_ = bf16[512,1024]{1,0:T(8,128)(2,1)S(1)} collective-permute-done((bf16[512,1024]{1,0:T(8,128)(2,1)S(1)}, bf16[512,1024]{1,0:T(8,128)(2,1)S(1)}, u32[]{:S(2)}, u32[]{:S(2)}) %collective-permute-start.50) | collective-permute-done | bytes 1048608 | tf_op jit(solution)/shard_map/s8/ring_y/ppermute | solution.py:69
  407.1 4.8 collective-permute-done.53
  421.6 18.9 %collective-permute-done.59.refs_2_ = bf16[128,2048]{1,0:T(8,128)(2,1)} collective-permute-done((bf16[128,2048]{1,0:T(8,128)(2,1)}, bf16[128,2048]{1,0:T(8,128)(2,1)}, u32[]{:S(2)}, u32[]{:S(2)}) %collective-permute-start.59) | collective-permute-done | bytes 524320 | tf_op jit(solution)/shard_map/s9/team10/ppermute | solution.py:64
  460.2 9.4 %c4.10.refs_2_.refs_3_.rows_ref = bf16[1024,768]{1,0:T(8,128)(2,1)S(1)} custom-call(s32[8]{0:T(128)S(1)} %multiply_subtract_fusion.limits_ref, bf16[1024,768]{1,0:T(8,128)(2,1)S(1)} %copy-done.15, bf16[1024,768]{1,0:T(8,128)(2,1)S(1)} %copy-done.15, bf16[1024,768]{1,0:T(8,128)(2,1)S(1)} %copy-done.15, bf16[1024,256]{1,0:T(8,128)(2,1)S(1)} %c4.9.grad_ref, ...), custom_call_target="tpu_custom_call" | custom-call | flops 1000000 | bytes 100000 | tf_op jit(solution)/shard_map/c4/pallas_call | solution.py:725
  469.6 4.6 c4.14
  497.7 5.0 c4.15
  513.4 8.4 %collective-permute-done.72 = bf16[128,2048]{1,0:T(8,128)(2,1)S(1)} collective-permute-done((bf16[128,2048]{1,0:T(8,128)(2,1)S(1)}, bf16[128,2048]{1,0:T(8,128)(2,1)S(1)}, u32[]{:S(2)}, u32[]{:S(2)}) %collective-permute-start.72) | collective-permute-done | bytes 524320 | tf_op jit(solution)/shard_map/s10/team01/ppermute | solution.py:64
  560.1 16.4 %collective-permute-done.77.refs_5_ = bf16[512,256]{1,0:T(8,128)(2,1)} collective-permute-done((bf16[512,256]{1,0:T(8,128)(2,1)S(1)}, bf16[512,256]{1,0:T(8,128)(2,1)}, u32[]{:S(2)}, u32[]{:S(2)}) %collective-permute-start.77) | collective-permute-done | bytes 262176 | tf_op jit(solution)/shard_map/s11/ring_h/ppermute | solution.py:69
  592.8 9.8 %collective-permute-start.85 = (bf16[128,1024]{1,0:T(8,128)(2,1)S(1)}, bf16[128,1024]{1,0:T(8,128)(2,1)S(1)}, u32[]{:S(2)}, u32[]{:S(2)}) collective-permute-start(bf16[128,1024]{1,0:T(8,128)(2,1)S(1)} %get-tuple-element.449), channel_id=1, source_target_pairs={{0,8},{2,10},{8,0},{10,2},{1,9},{3,11},{9,1},{11,3},{4,12},{6,14},... | collective-permute-start | bytes 786440 | tf_op jit(solution)/shard_map/s12/team10/ppermute | solution.py:64
  (603 shorter events, 313.5 us)
Async XLA Ops:
  2.7 29.5 %collective-permute-start = (bf16[128,2048]{1,0:T(8,128)(2,1)}, bf16[128,2048]{1,0:T(8,128)(2,1)}, u32[]{:S(2)}, u32[]{:S(2)}) collective-permute-start(bf16[128,2048]{1,0:T(8,128)(2,1)} %constant_dynamic-slice_fusion.25), channel_id=1, source_target_pairs={{4,8},{8,4},{5,9},{9,5},{6,10},{10,6},{7,11},{11,7},{20,24},{24,20... | collective-permute-start | bytes 1572872 | tf_op jit(solution)/shard_map/a0/ppermute | solution.py:109
  36.6 37.4 %collective-permute-start.4 = (bf16[512,1024]{1,0:T(8,128)(2,1)S(1)}, bf16[512,1024]{1,0:T(8,128)(2,1)S(1)}, u32[]{:S(2)}, u32[]{:S(2)}) collective-permute-start(bf16[512,1024]{1,0:T(8,128)(2,1)S(1)} %a1.3.refs_2_.refs_0_), channel_id=1, source_target_pairs={{0,4},{4,0},{1,5},{5,1},{2,6},{6,2},{3,7},{7,3},{8,12},{12,8},{9,1... | collective-permute-start | bytes 3145736 | tf_op jit(solution)/shard_map/a1/ring_y/ppermute | solution.py:69
  38.1 35.8 %collective-permute-start.8 = (bf16[512,768]{1,0:T(8,128)(2,1)S(1)}, bf16[512,768]{1,0:T(8,128)(2,1)}, u32[]{:S(2)}, u32[]{:S(2)}) collective-permute-start(bf16[512,768]{1,0:T(8,128)(2,1)S(1)} %slice.124), channel_id=1, source_target_pairs={{0,16},{16,0},{1,17},{17,1},{2,18},{18,2},{3,19},{19,3},{4,20},{20... | collective-permute-start | bytes 2359304 | tf_op jit(solution)/shard_map/a1/ring_h/ppermute | solution.py:69
  101.5 25.4 %collective-permute-start.16 = (bf16[256,1024]{1,0:T(8,128)(2,1)S(1)}, bf16[256,1024]{1,0:T(8,128)(2,1)S(1)}, u32[]{:S(2)}, u32[]{:S(2)}) collective-permute-start(bf16[256,1024]{1,0:T(8,128)(2,1)S(1)} %get-tuple-element.276.refs_1_.refs_0_), channel_id=1, source_target_pairs={{0,16},{16,0},{1,17},{17,1},{2,18},{18,2},{3,19},{19,3},{4,20},{20... | collective-permute-start | bytes 1572872 | tf_op jit(solution)/shard_map/c1/ring_h/ppermute | solution.py:69
  134.7 37.1 %collective-permute-start.26 = (bf16[512,1024]{1,0:T(8,128)(2,1)}, bf16[512,1024]{1,0:T(8,128)(2,1)}, u32[]{:S(2)}, u32[]{:S(2)}) collective-permute-start(bf16[512,1024]{1,0:T(8,128)(2,1)} %pad_maximum_fusion.1), channel_id=1, source_target_pairs={{0,4},{4,0},{1,5},{5,1},{2,6},{6,2},{3,7},{7,3},{8,12},{12,8},{9,1... | collective-permute-start | bytes 3145736 | tf_op jit(solution)/shard_map/s3/ring_y/ppermute | solution.py:69
  141.0 25.1 %collective-permute-start.25 = (bf16[256,1024]{1,0:T(8,128)(2,1)}, bf16[256,1024]{1,0:T(8,128)(2,1)S(1)}, u32[]{:S(2)}, u32[]{:S(2)}) collective-permute-start(bf16[256,1024]{1,0:T(8,128)(2,1)} %get-tuple-element.284.refs_2_.refs_1_), channel_id=1, source_target_pairs={{0,16},{16,0},{1,17},{17,1},{2,18},{18,2},{3,19},{19,3},{4,20},{20... | collective-permute-start | bytes 1572872 | tf_op jit(solution)/shard_map/s3/ring_h/ppermute | solution.py:69
  148.5 27.2 %collective-permute-start.24 = (bf16[128,2048]{1,0:T(8,128)(2,1)}, bf16[128,2048]{1,0:T(8,128)(2,1)}, u32[]{:S(2)}, u32[]{:S(2)}) collective-permute-start(bf16[128,2048]{1,0:T(8,128)(2,1)} %add_convert_fusion.3), channel_id=1, source_target_pairs={{0,8},{2,10},{8,0},{10,2},{1,9},{3,11},{9,1},{11,3},{4,12},{6,14},... | collective-permute-start | bytes 1572872 | tf_op jit(solution)/shard_map/s3/team10/ppermute | solution.py:64
  176.8 37.9 %collective-permute-start.32 = (bf16[512,1024]{1,0:T(8,128)(2,1)S(1)}, bf16[512,1024]{1,0:T(8,128)(2,1)S(1)}, u32[]{:S(2)}, u32[]{:S(2)}) collective-permute-start(bf16[512,1024]{1,0:T(8,128)(2,1)S(1)} %pad_maximum_fusion.2), channel_id=1, source_target_pairs={{0,4},{4,0},{1,5},{5,1},{2,6},{6,2},{3,7},{7,3},{8,12},{12,8},{9,1... | collective-permute-start | bytes 3145736 | tf_op jit(solution)/shard_map/s4/ring_y/ppermute | solution.py:69
  179.5 26.2 %collective-permute-start.29 = (bf16[128,2048]{1,0:T(8,128)(2,1)S(1)}, bf16[128,2048]{1,0:T(8,128)(2,1)S(1)}, u32[]{:S(2)}, u32[]{:S(2)}) collective-permute-start(bf16[128,2048]{1,0:T(8,128)(2,1)S(1)} %fusion.3.refs_0_), channel_id=1, source_target_pairs={{0,8},{2,10},{8,0},{10,2},{1,9},{3,11},{9,1},{11,3},{4,12},{6,14},... | collective-permute-start | bytes 1572872 | tf_op jit(solution)/shard_map/s4/team10/ppermute | solution.py:64
  180.7 26.3 %collective-permute-start.28 = (bf16[128,2048]{1,0:T(8,128)(2,1)S(1)}, bf16[128,2048]{1,0:T(8,128)(2,1)S(1)}, u32[]{:S(2)}, u32[]{:S(2)}) collective-permute-start(bf16[128,2048]{1,0:T(8,128)(2,1)S(1)} %fusion.3.refs_0_), channel_id=1, source_target_pairs={{0,2},{2,0},{8,10},{10,8},{1,3},{3,1},{9,11},{11,9},{4,6},{6,4},{1... | collective-permute-start | bytes 1572872 | tf_op jit(solution)/shard_map/s4/team01/ppermute | solution.py:64
  181.8 33.0 %collective-permute-start.27 = (bf16[128,2048]{1,0:T(8,128)(2,1)}, bf16[128,2048]{1,0:T(8,128)(2,1)S(1)}, u32[]{:S(2)}, u32[]{:S(2)}) collective-permute-start(bf16[128,2048]{1,0:T(8,128)(2,1)} %constant_dynamic-slice_fusion), channel_id=1, source_target_pairs={{0,4},{4,12},{8,0},{12,8},{1,5},{5,13},{9,1},{13,9},{2,6},{6,14},{... | collective-permute-start | bytes 1572872 | tf_op jit(solution)/shard_map/s4/flip/ppermute | solution.py:411
  182.9 31.9 %collective-permute-start.31 = (bf16[256,1024]{1,0:T(8,128)(2,1)S(1)}, bf16[256,1024]{1,0:T(8,128)(2,1)S(1)}, u32[]{:S(2)}, u32[]{:S(2)}) collective-permute-start(bf16[256,1024]{1,0:T(8,128)(2,1)S(1)} %get-tuple-element.296.refs_0_.refs_1_), channel_id=1, source_target_pairs={{0,16},{16,0},{1,17},{17,1},{2,18},{18,2},{3,19},{19,3},{4,20},{20... | collective-permute-start | bytes 1572872 | tf_op jit(solution)/shard_map/s4/ring_h/ppermute | solution.py:69
  215.9 27.9 %collective-permute-start.35 = (bf16[512,1024]{1,0:T(8,128)(2,1)S(1)}, bf16[512,1024]{1,0:T(8,128)(2,1)S(1)}, u32[]{:S(2)}, u32[]{:S(2)}) collective-permute-start(bf16[512,1024]{1,0:T(8,128)(2,1)S(1)} %pad_maximum_fusion.3), channel_id=1, source_target_pairs={{0,4},{4,0},{1,5},{5,1},{2,6},{6,2},{3,7},{7,3},{8,12},{12,8},{9,1... | collective-permute-start | bytes 3145736 | tf_op jit(solution)/shard_map/c2/ring_y/ppermute | solution.py:69
  215.9 27.8 %collective-permute-start.34 = (bf16[256,1024]{1,0:T(8,128)(2,1)S(1)}, bf16[256,1024]{1,0:T(8,128)(2,1)S(1)}, u32[]{:S(2)}, u32[]{:S(2)}) collective-permute-start(bf16[256,1024]{1,0:T(8,128)(2,1)S(1)} %get-tuple-element.302.refs_1_.refs_2_), channel_id=1, source_target_pairs={{0,16},{16,0},{1,17},{17,1},{2,18},{18,2},{3,19},{19,3},{4,20},{20... | collective-permute-start | bytes 1572872 | tf_op jit(solution)/shard_map/c2/ring_h/ppermute | solution.py:69
  246.2 25.3 %collective-permute-start.37 = (bf16[128,2048]{1,0:T(8,128)(2,1)S(1)}, bf16[128,2048]{1,0:T(8,128)(2,1)S(1)}, u32[]{:S(2)}, u32[]{:S(2)}) collective-permute-start(bf16[128,2048]{1,0:T(8,128)(2,1)S(1)} %get-tuple-element.445), channel_id=1, source_target_pairs={{0,16},{16,0},{1,17},{17,1},{2,18},{18,2},{3,19},{19,3},{4,20},{20... | collective-permute-start | bytes 1572872 | tf_op jit(solution)/shard_map/s5/ring_h/ppermute | solution.py:69
  281.8 25.1 %collective-permute-start.41 = (bf16[128,2048]{1,0:T(8,128)(2,1)}, bf16[128,2048]{1,0:T(8,128)(2,1)}, u32[]{:S(2)}, u32[]{:S(2)}) collective-permute-start(bf16[128,2048]{1,0:T(8,128)(2,1)} %get-tuple-element.321), channel_id=1, source_target_pairs={{0,10},{2,8},{8,2},{10,0},{1,11},{3,9},{9,3},{11,1},{4,14},{6,12},... | collective-permute-start | bytes 1572872 | tf_op jit(solution)/shard_map/s6/team11/ppermute | solution.py:64
  313.0 28.0 %collective-permute-start.42 = (bf16[128,2048]{1,0:T(8,128)(2,1)S(1)}, bf16[128,2048]{1,0:T(8,128)(2,1)}, u32[]{:S(2)}, u32[]{:S(2)}) collective-permute-start(bf16[128,2048]{1,0:T(8,128)(2,1)S(1)} %get-tuple-element.327.refs_0_), channel_id=1, source_target_pairs={{0,2},{2,0},{8,10},{10,8},{1,3},{3,1},{9,11},{11,9},{4,6},{6,4},{1... | collective-permute-start | bytes 1572872 | tf_op jit(solution)/shard_map/s7/team01/ppermute | solution.py:64
  380.9 26.1 %collective-permute-start.50 = (bf16[512,1024]{1,0:T(8,128)(2,1)S(1)}, bf16[512,1024]{1,0:T(8,128)(2,1)S(1)}, u32[]{:S(2)}, u32[]{:S(2)}) collective-permute-start(bf16[512,1024]{1,0:T(8,128)(2,1)S(1)} %s8_.3), channel_id=1, source_target_pairs={{0,4},{4,0},{1,5},{5,1},{2,6},{6,2},{3,7},{7,3},{8,12},{12,8},{9,1... | collective-permute-start | bytes 3145736 | tf_op jit(solution)/shard_map/s8/ring_y/ppermute | solution.py:69
  390.9 54.7 %collective-permute-start.56 = (bf16[512,1024]{1,0:T(8,128)(2,1)}, bf16[512,1024]{1,0:T(8,128)(2,1)}, u32[]{:S(2)}, u32[]{:S(2)}) collective-permute-start(bf16[512,1024]{1,0:T(8,128)(2,1)} %s9.5), channel_id=1, source_target_pairs={{0,4},{4,0},{1,5},{5,1},{2,6},{6,2},{3,7},{7,3},{8,12},{12,8},{9,1... | collective-permute-start | bytes 3145736 | tf_op jit(solution)/shard_map/s9/ring_y/ppermute | solution.py:69
  414.6 25.9 %collective-permute-start.59 = (bf16[128,2048]{1,0:T(8,128)(2,1)}, bf16[128,2048]{1,0:T(8,128)(2,1)}, u32[]{:S(2)}, u32[]{:S(2)}) collective-permute-start(bf16[128,2048]{1,0:T(8,128)(2,1)} %get-tuple-element.353.refs_0_), channel_id=1, source_target_pairs={{0,8},{2,10},{8,0},{10,2},{1,9},{3,11},{9,1},{11,3},{4,12},{6,14},... | collective-permute-start | bytes 1572872 | tf_op jit(solution)/shard_map/s9/team10/ppermute | solution.py:64
  418.3 27.3 %collective-permute-start.57 = (bf16[128,2048]{1,0:T(8,128)(2,1)S(1)}, bf16[128,2048]{1,0:T(8,128)(2,1)S(1)}, u32[]{:S(2)}, u32[]{:S(2)}) collective-permute-start(bf16[128,2048]{1,0:T(8,128)(2,1)S(1)} %get-tuple-element.394), channel_id=1, source_target_pairs={{4,8},{8,4},{5,9},{9,5},{6,10},{10,6},{7,11},{11,7},{20,24},{24,20... | collective-permute-start | bytes 1572872 | tf_op jit(solution)/shard_map/s9/ppermute | solution.py:109
  419.0 26.6 %collective-permute-start.58 = (bf16[128,2048]{1,0:T(8,128)(2,1)}, bf16[128,2048]{1,0:T(8,128)(2,1)S(1)}, u32[]{:S(2)}, u32[]{:S(2)}) collective-permute-start(bf16[128,2048]{1,0:T(8,128)(2,1)} %get-tuple-element.353.refs_0_), channel_id=1, source_target_pairs={{0,2},{2,0},{8,10},{10,8},{1,3},{3,1},{9,11},{11,9},{4,6},{6,4},{1... | collective-permute-start | bytes 1572872 | tf_op jit(solution)/shard_map/s9/team01/ppermute | solution.py:64
  419.6 26.0 %collective-permute-start.61 = (bf16[256,1024]{1,0:T(8,128)(2,1)}, bf16[256,1024]{1,0:T(8,128)(2,1)S(1)}, u32[]{:S(2)}, u32[]{:S(2)}) collective-permute-start(bf16[256,1024]{1,0:T(8,128)(2,1)} %copy-done.100), channel_id=1, source_target_pairs={{0,16},{16,0},{1,17},{17,1},{2,18},{18,2},{3,19},{19,3},{4,20},{20... | collective-permute-start | bytes 1572872 | tf_op jit(solution)/shard_map/s9/ring_h/ppermute | solution.py:69
  451.5 26.4 %collective-permute-start.66 = (bf16[256,1024]{1,0:T(8,128)(2,1)S(1)}, bf16[256,1024]{1,0:T(8,128)(2,1)S(1)}, u32[]{:S(2)}, u32[]{:S(2)}) collective-permute-start(bf16[256,1024]{1,0:T(8,128)(2,1)S(1)} %s9.6), channel_id=1, source_target_pairs={{0,16},{16,0},{1,17},{17,1},{2,18},{18,2},{3,19},{19,3},{4,20},{20... | collective-permute-start | bytes 1572872 | tf_op jit(solution)/shard_map/c4/ring_h/ppermute | solution.py:69
  451.5 26.3 %collective-permute-start.67 = (bf16[128,2048]{1,0:T(8,128)(2,1)S(1)}, bf16[128,2048]{1,0:T(8,128)(2,1)S(1)}, u32[]{:S(2)}, u32[]{:S(2)}) collective-permute-start(bf16[128,2048]{1,0:T(8,128)(2,1)S(1)} %get-tuple-element.362), channel_id=1, source_target_pairs={{0,8},{4,0},{8,12},{12,4},{1,9},{5,1},{9,13},{13,5},{2,10},{6,2},{... | collective-permute-start | bytes 1572872 | tf_op jit(solution)/shard_map/c4/ppermute | solution.py:431
  481.3 25.7 %collective-permute-start.69 = (bf16[256,1024]{1,0:T(8,128)(2,1)}, bf16[256,1024]{1,0:T(8,128)(2,1)}, u32[]{:S(2)}, u32[]{:S(2)}) collective-permute-start(bf16[256,1024]{1,0:T(8,128)(2,1)} %copy-done.103), channel_id=1, source_target_pairs={{0,16},{16,0},{1,17},{17,1},{2,18},{18,2},{3,19},{19,3},{4,20},{20... | collective-permute-start | bytes 1572872 | tf_op jit(solution)/shard_map/c4/ring_h/ppermute | solution.py:69
  509.8 32.3 %collective-permute-start.70 = (bf16[512,1024]{1,0:T(8,128)(2,1)}, bf16[512,1024]{1,0:T(8,128)(2,1)}, u32[]{:S(2)}, u32[]{:S(2)}) collective-permute-start(bf16[512,1024]{1,0:T(8,128)(2,1)} %s10.5), channel_id=1, source_target_pairs={{0,4},{4,0},{1,5},{5,1},{2,6},{6,2},{3,7},{7,3},{8,12},{12,8},{9,1... | collective-permute-start | bytes 3145736 | tf_op jit(solution)/shard_map/s10/ring_y/ppermute | solution.py:69
  511.6 33.5 %collective-permute-start.71 = (bf16[128,2048]{1,0:T(8,128)(2,1)}, bf16[128,2048]{1,0:T(8,128)(2,1)}, u32[]{:S(2)}, u32[]{:S(2)}) collective-permute-start(bf16[128,2048]{1,0:T(8,128)(2,1)} %get-tuple-element.375), channel_id=1, source_target_pairs={{0,2},{2,0},{8,10},{10,8},{1,3},{3,1},{9,11},{11,9},{4,6},{6,4},{1... | collective-permute-start | bytes 1572872 | tf_op jit(solution)/shard_map/s10/team01/ppermute | solution.py:64
  549.5 37.2 %collective-permute-start.79 = (bf16[128,2048]{1,0:T(8,128)(2,1)}, bf16[128,2048]{1,0:T(8,128)(2,1)}, u32[]{:S(2)}, u32[]{:S(2)}) collective-permute-start(bf16[128,2048]{1,0:T(8,128)(2,1)} %get-tuple-element.443), channel_id=1, source_target_pairs={{0,2},{2,0},{8,10},{10,8},{1,3},{3,1},{9,11},{11,9},{4,6},{6,4},{1... | collective-permute-start | bytes 1572872 | tf_op jit(solution)/shard_map/s11/team01/ppermute | solution.py:64
  549.8 36.9 %collective-permute-start.80 = (bf16[128,2048]{1,0:T(8,128)(2,1)}, bf16[128,2048]{1,0:T(8,128)(2,1)}, u32[]{:S(2)}, u32[]{:S(2)}) collective-permute-start(bf16[128,2048]{1,0:T(8,128)(2,1)} %get-tuple-element.442), channel_id=1, source_target_pairs={{0,8},{2,10},{8,0},{10,2},{1,9},{3,11},{9,1},{11,3},{4,12},{6,14},... | collective-permute-start | bytes 1572872 | tf_op jit(solution)/shard_map/s11/team10/ppermute | solution.py:64
  549.8 33.4 %collective-permute-start.78 = (bf16[256,768]{1,0:T(8,128)(2,1)}, bf16[256,768]{1,0:T(8,128)(2,1)}, u32[]{:S(2)}, u32[]{:S(2)}) collective-permute-start(bf16[256,768]{1,0:T(8,128)(2,1)} %s10.7), channel_id=1, source_target_pairs={{0,16},{16,0},{1,17},{17,1},{2,18},{18,2},{3,19},{19,3},{4,20},{20... | collective-permute-start | bytes 1179656 | tf_op jit(solution)/shard_map/s11/ring_h/ppermute | solution.py:69
  557.6 30.6 %collective-permute-start.81 = (bf16[128,2048]{1,0:T(8,128)(2,1)}, bf16[128,2048]{1,0:T(8,128)(2,1)}, u32[]{:S(2)}, u32[]{:S(2)}) collective-permute-start(bf16[128,2048]{1,0:T(8,128)(2,1)} %get-tuple-element.441), channel_id=1, source_target_pairs={{0,10},{2,8},{8,2},{10,0},{1,11},{3,9},{9,3},{11,1},{4,14},{6,12},... | collective-permute-start | bytes 1572872 | tf_op jit(solution)/shard_map/s11/team11/ppermute | solution.py:64
  (209 other events, 3076.8 us)

commit v9 on v8

--- a/solution.py
+++ b/solution.py
@@ -533,7 +533,7 @@
 
 
 LIGHT = pl.CostEstimate(flops=1000000, bytes_accessed=100000, transcendentals=0)
-KERNEL = pltpu.CompilerParams(vmem_limit_bytes=16 * 1024 * 1024)
+KERNEL = pltpu.CompilerParams(vmem_limit_bytes=12 * 1024 * 1024)
 
 
 def gelu_slope(value):

time: 630 us -> 627 us (level)
  waiting for transfers between devices: 309 us -> 297 us
    ppermute x39, starting transfers between devices: 49 us -> 57.5 us  [shift_(): return lax.ppermute(value, TEAM, perm)]
    ppermute x39, waiting for transfers between devices: 162 us -> 155 us  [shift_(): return lax.ppermute(value, TEAM, perm)]
  transfers between devices with their start and end apart: 90 -> 90, of which waited for: 49 -> 44; matrix products, arithmetic and copies ran while one was open for 7% -> 7% of each run, Pallas kernels for 18% -> 18%
where the time goes in v9:
time: 627 us; the launch traced here: 617 us
  waiting for transfers between devices  297 us (47%)
  Pallas kernels  121 us (19%)
  starting transfers between devices  110 us (18%)
  local copies, waits for them, and re-layouts  48.9 us (8%)
  other arithmetic  33.7 us (5%)
  between operations  6.84 us (1%)
    ppermute x39, waiting for transfers between devices, shift_(): return lax.ppermute(value, TEAM, perm)  155 us
    ppermute x45, waiting for transfers between devices, ring(): lax.ppermute(value, name, [(i, (i + step) % size) for i in range(size)])  135 us
    ppermute x39, starting transfers between devices, shift_(): return lax.ppermute(value, TEAM, perm)  57.5 us
    ppermute x45, starting transfers between devices, ring(): lax.ppermute(value, name, [(i, (i + step) % size) for i in range(size)])  43.8 us
    pallas_call x20, Pallas kernels, outer(): pl.pallas_call(functools.partial(outer_kernel, len(lefts), len(adds)), gr...  33.8 us
    unnamed x305, local copies, waits for them, and re-layouts  29.9 us
    pallas_call x8, Pallas kernels, spread(): pl.pallas_call(functools.partial(spread_kernel, len(pieces), len(got), sp...  24.9 us
    pallas_call x6, Pallas kernels, project(): pl.pallas_call(functools.partial(project_kernel, mode, len(parts), len(pi...  24.4 us
  transfers between devices with their start and end apart: 90, of which 44 were waited for; matrix products, arithmetic and copies ran while one was open for 7% of the time, Pallas kernels for 18%

profile of v9, /device:TPU:0, one launch (start us, length us, event | category | flops | bytes accessed | tf_op | source)
XLA Modules:
  0.0 616.6 jit_solution(11223524000306686291)
XLA Ops:
  6.9 5.9 collective-permute-start.3
  42.2 16.1 %collective-permute-done.6.refs_2_ = bf16[128,2048]{1,0:T(8,128)(2,1)S(1)} collective-permute-done((bf16[128,2048]{1,0:T(8,128)(2,1)}, bf16[128,2048]{1,0:T(8,128)(2,1)S(1)}, u32[]{:S(2)}, u32[]{:S(2)}) %collective-permute-start.6) | collective-permute-done | bytes 524320 | tf_op jit(solution)/shard_map/a1/team10/ppermute | solution.py:64
  59.8 14.1 %collective-permute-done.8.refs_3_.refs_1_ = bf16[512,768]{1,0:T(8,128)(2,1)} collective-permute-done((bf16[512,768]{1,0:T(8,128)(2,1)S(1)}, bf16[512,768]{1,0:T(8,128)(2,1)}, u32[]{:S(2)}, u32[]{:S(2)}) %collective-permute-start.8) | collective-permute-done | bytes 786464 | tf_op jit(solution)/shard_map/a1/ring_h/ppermute | solution.py:69
  80.5 4.8 collective-permute-done.10.refs_1_
  85.4 7.7 %collective-permute-done.11.refs_2_ = bf16[128,1024]{1,0:T(8,128)(2,1)S(1)} collective-permute-done((bf16[128,1024]{1,0:T(8,128)(2,1)S(1)}, bf16[128,1024]{1,0:T(8,128)(2,1)S(1)}, u32[]{:S(2)}, u32[]{:S(2)}) %collective-permute-start.11) | collective-permute-done | bytes 262176 | tf_op jit(solution)/shard_map/a2/team10/ppermute | solution.py:64
  106.7 6.1 c1.5.query_ref.key_ref.value_ref
  112.8 6.3 %c1.6 = (bf16[1024,256]{1,0:T(8,128)(2,1)S(1)}, f32[2,1,1024]{2,1,0:T(1,128)S(1)}) custom-call(s32[8]{0:T(128)S(1)} %multiply_subtract_fusion.limits_ref, bf16[1024,768]{1,0:T(8,128)(2,1)S(1)} %c1.5.query_ref.key_ref.value_ref, bf16[1024,768]{1,0:T(8,128)(2,1)S(1)} %c1.5.query_ref.key_ref.value_ref, bf16[1024,768]{1,0:T(8,128)(2,1)S(1)} %c1.5.query_ref.key_ref.value_ref), custom_call_target="tpu_custom_call" | custom-call | flops 1000000 | bytes 100000 | tf_op jit(solution)/shard_map/c1/pallas_call | solution.py:700
  138.6 7.8 %collective-permute-done.23 = bf16[128,2048]{1,0:T(8,128)(2,1)S(1)} collective-permute-done((bf16[128,2048]{1,0:T(8,128)(2,1)S(1)}, bf16[128,2048]{1,0:T(8,128)(2,1)S(1)}, u32[]{:S(2)}, u32[]{:S(2)}) %collective-permute-start.23) | collective-permute-done | bytes 524320 | tf_op jit(solution)/shard_map/s3/team01/ppermute | solution.py:64
  151.5 5.4 collective-permute-done.22
  156.9 6.9 %collective-permute-done.25.refs_4_.refs_3_ = bf16[256,1024]{1,0:T(8,128)(2,1)S(1)} collective-permute-done((bf16[256,1024]{1,0:T(8,128)(2,1)}, bf16[256,1024]{1,0:T(8,128)(2,1)S(1)}, u32[]{:S(2)}, u32[]{:S(2)}) %collective-permute-start.25) | collective-permute-done | bytes 524320 | tf_op jit(solution)/shard_map/s3/ring_h/ppermute | solution.py:69
  163.9 5.5 collective-permute-done.26
  183.4 19.8 %collective-permute-done.29.refs_2_ = bf16[128,2048]{1,0:T(8,128)(2,1)S(1)} collective-permute-done((bf16[128,2048]{1,0:T(8,128)(2,1)S(1)}, bf16[128,2048]{1,0:T(8,128)(2,1)S(1)}, u32[]{:S(2)}, u32[]{:S(2)}) %collective-permute-start.29) | collective-permute-done | bytes 524320 | tf_op jit(solution)/shard_map/s4/team10/ppermute | solution.py:64
  204.5 7.3 %collective-permute-done.27 = bf16[128,2048]{1,0:T(8,128)(2,1)S(1)} collective-permute-done((bf16[128,2048]{1,0:T(8,128)(2,1)}, bf16[128,2048]{1,0:T(8,128)(2,1)S(1)}, u32[]{:S(2)}, u32[]{:S(2)}) %collective-permute-start.27) | collective-permute-done | bytes 524320 | tf_op jit(solution)/shard_map/s4/flip/ppermute | solution.py:411
  218.4 4.6 c2.4
  224.4 4.5 c2.5
  230.2 10.3 %collective-permute-done.34.refs_3_.refs_4_ = bf16[256,1024]{1,0:T(8,128)(2,1)S(1)} collective-permute-done((bf16[256,1024]{1,0:T(8,128)(2,1)S(1)}, bf16[256,1024]{1,0:T(8,128)(2,1)S(1)}, u32[]{:S(2)}, u32[]{:S(2)}) %collective-permute-start.34) | collective-permute-done | bytes 524320 | tf_op jit(solution)/shard_map/c2/ring_h/ppermute | solution.py:69
  244.7 20.7 %collective-permute-done.36 = bf16[512,1024]{1,0:T(8,128)(2,1)S(1)} collective-permute-done((bf16[512,1024]{1,0:T(8,128)(2,1)S(1)}, bf16[512,1024]{1,0:T(8,128)(2,1)S(1)}, u32[]{:S(2)}, u32[]{:S(2)}) %collective-permute-start.36) | collective-permute-done | bytes 1048608 | tf_op jit(solution)/shard_map/s5/ring_y/ppermute | solution.py:69
  268.9 4.2 collective-permute-done.38.refs_8_
  284.9 7.0 %collective-permute-done.39 = bf16[128,2048]{1,0:T(8,128)(2,1)} collective-permute-done((bf16[128,2048]{1,0:T(8,128)(2,1)}, bf16[128,2048]{1,0:T(8,128)(2,1)}, u32[]{:S(2)}, u32[]{:S(2)}) %collective-permute-start.39) | collective-permute-done | bytes 524320 | tf_op jit(solution)/shard_map/s6/team01/ppermute | solution.py:64
  294.5 9.8 %collective-permute-done.41 = bf16[128,2048]{1,0:T(8,128)(2,1)} collective-permute-done((bf16[128,2048]{1,0:T(8,128)(2,1)}, bf16[128,2048]{1,0:T(8,128)(2,1)}, u32[]{:S(2)}, u32[]{:S(2)}) %collective-permute-start.41) | collective-permute-done | bytes 524320 | tf_op jit(solution)/shard_map/s6/team11/ppermute | solution.py:64
  316.8 12.1 %collective-permute-done.43.refs_2_ = bf16[128,2048]{1,0:T(8,128)(2,1)S(1)} collective-permute-done((bf16[128,2048]{1,0:T(8,128)(2,1)S(1)}, bf16[128,2048]{1,0:T(8,128)(2,1)S(1)}, u32[]{:S(2)}, u32[]{:S(2)}) %collective-permute-start.43) | collective-permute-done | bytes 524320 | tf_op jit(solution)/shard_map/s7/team10/ppermute | solution.py:64
  332.9 5.9 collective-permute-done.45
  381.1 4.9 collective-permute-done.52
  390.9 13.9 %collective-permute-done.50.refs_4_ = bf16[512,1024]{1,0:T(8,128)(2,1)S(1)} collective-permute-done((bf16[512,1024]{1,0:T(8,128)(2,1)S(1)}, bf16[512,1024]{1,0:T(8,128)(2,1)S(1)}, u32[]{:S(2)}, u32[]{:S(2)}) %collective-permute-start.50) | collective-permute-done | bytes 1048608 | tf_op jit(solution)/shard_map/s8/ring_y/ppermute | solution.py:69
  419.9 18.4 %collective-permute-done.59.refs_2_ = bf16[128,2048]{1,0:T(8,128)(2,1)} collective-permute-done((bf16[128,2048]{1,0:T(8,128)(2,1)}, bf16[128,2048]{1,0:T(8,128)(2,1)}, u32[]{:S(2)}, u32[]{:S(2)}) %collective-permute-start.59) | collective-permute-done | bytes 524320 | tf_op jit(solution)/shard_map/s9/team10/ppermute | solution.py:64
  457.9 9.4 %c4.10.refs_2_.refs_3_.rows_ref = bf16[1024,768]{1,0:T(8,128)(2,1)S(1)} custom-call(s32[8]{0:T(128)S(1)} %multiply_subtract_fusion.limits_ref, bf16[1024,768]{1,0:T(8,128)(2,1)S(1)} %copy-done.15, bf16[1024,768]{1,0:T(8,128)(2,1)S(1)} %copy-done.15, bf16[1024,768]{1,0:T(8,128)(2,1)S(1)} %copy-done.15, bf16[1024,256]{1,0:T(8,128)(2,1)S(1)} %c4.9.grad_ref, ...), custom_call_target="tpu_custom_call" | custom-call | flops 1000000 | bytes 100000 | tf_op jit(solution)/shard_map/c4/pallas_call | solution.py:725
  467.3 4.6 c4.14
  494.5 5.0 c4.15
  499.5 5.1 collective-permute-done.69
  509.6 9.8 %collective-permute-done.72 = bf16[128,2048]{1,0:T(8,128)(2,1)S(1)} collective-permute-done((bf16[128,2048]{1,0:T(8,128)(2,1)S(1)}, bf16[128,2048]{1,0:T(8,128)(2,1)S(1)}, u32[]{:S(2)}, u32[]{:S(2)}) %collective-permute-start.72) | collective-permute-done | bytes 524320 | tf_op jit(solution)/shard_map/s10/team01/ppermute | solution.py:64
  558.6 17.7 %collective-permute-done.77.refs_5_ = bf16[512,256]{1,0:T(8,128)(2,1)} collective-permute-done((bf16[512,256]{1,0:T(8,128)(2,1)S(1)}, bf16[512,256]{1,0:T(8,128)(2,1)}, u32[]{:S(2)}, u32[]{:S(2)}) %collective-permute-start.77) | collective-permute-done | bytes 262176 | tf_op jit(solution)/shard_map/s11/ring_h/ppermute | solution.py:69
  591.9 7.2 %collective-permute-start.85 = (bf16[128,1024]{1,0:T(8,128)(2,1)S(1)}, bf16[128,1024]{1,0:T(8,128)(2,1)S(1)}, u32[]{:S(2)}, u32[]{:S(2)}) collective-permute-start(bf16[128,1024]{1,0:T(8,128)(2,1)S(1)} %get-tuple-element.449), channel_id=1, source_target_pairs={{0,8},{2,10},{8,0},{10,2},{1,9},{3,11},{9,1},{11,3},{4,12},{6,14},... | collective-permute-start | bytes 786440 | tf_op jit(solution)/shard_map/s12/team10/ppermute | solution.py:64
  (603 shorter events, 321.2 us)
Async XLA Ops:
  2.7 29.5 %collective-permute-start = (bf16[128,2048]{1,0:T(8,128)(2,1)}, bf16[128,2048]{1,0:T(8,128)(2,1)}, u32[]{:S(2)}, u32[]{:S(2)}) collective-permute-start(bf16[128,2048]{1,0:T(8,128)(2,1)} %constant_dynamic-slice_fusion.25), channel_id=1, source_target_pairs={{4,8},{8,4},{5,9},{9,5},{6,10},{10,6},{7,11},{11,7},{20,24},{24,20... | collective-permute-start | bytes 1572872 | tf_op jit(solution)/shard_map/a0/ppermute | solution.py:109
  36.6 37.4 %collective-permute-start.4 = (bf16[512,1024]{1,0:T(8,128)(2,1)S(1)}, bf16[512,1024]{1,0:T(8,128)(2,1)S(1)}, u32[]{:S(2)}, u32[]{:S(2)}) collective-permute-start(bf16[512,1024]{1,0:T(8,128)(2,1)S(1)} %a1.3.refs_2_.refs_0_), channel_id=1, source_target_pairs={{0,4},{4,0},{1,5},{5,1},{2,6},{6,2},{3,7},{7,3},{8,12},{12,8},{9,1... | collective-permute-start | bytes 3145736 | tf_op jit(solution)/shard_map/a1/ring_y/ppermute | solution.py:69
  38.1 35.8 %collective-permute-start.8 = (bf16[512,768]{1,0:T(8,128)(2,1)S(1)}, bf16[512,768]{1,0:T(8,128)(2,1)}, u32[]{:S(2)}, u32[]{:S(2)}) collective-permute-start(bf16[512,768]{1,0:T(8,128)(2,1)S(1)} %slice.124), channel_id=1, source_target_pairs={{0,16},{16,0},{1,17},{17,1},{2,18},{18,2},{3,19},{19,3},{4,20},{20... | collective-permute-start | bytes 2359304 | tf_op jit(solution)/shard_map/a1/ring_h/ppermute | solution.py:69
  98.4 27.4 %collective-permute-start.16 = (bf16[256,1024]{1,0:T(8,128)(2,1)S(1)}, bf16[256,1024]{1,0:T(8,128)(2,1)S(1)}, u32[]{:S(2)}, u32[]{:S(2)}) collective-permute-start(bf16[256,1024]{1,0:T(8,128)(2,1)S(1)} %get-tuple-element.276.refs_1_.refs_0_), channel_id=1, source_target_pairs={{0,16},{16,0},{1,17},{17,1},{2,18},{18,2},{3,19},{19,3},{4,20},{20... | collective-permute-start | bytes 1572872 | tf_op jit(solution)/shard_map/c1/ring_h/ppermute | solution.py:69
  133.8 35.6 %collective-permute-start.26 = (bf16[512,1024]{1,0:T(8,128)(2,1)}, bf16[512,1024]{1,0:T(8,128)(2,1)}, u32[]{:S(2)}, u32[]{:S(2)}) collective-permute-start(bf16[512,1024]{1,0:T(8,128)(2,1)} %pad_maximum_fusion.1), channel_id=1, source_target_pairs={{0,4},{4,0},{1,5},{5,1},{2,6},{6,2},{3,7},{7,3},{8,12},{12,8},{9,1... | collective-permute-start | bytes 3145736 | tf_op jit(solution)/shard_map/s3/ring_y/ppermute | solution.py:69
  138.6 25.3 %collective-permute-start.25 = (bf16[256,1024]{1,0:T(8,128)(2,1)}, bf16[256,1024]{1,0:T(8,128)(2,1)S(1)}, u32[]{:S(2)}, u32[]{:S(2)}) collective-permute-start(bf16[256,1024]{1,0:T(8,128)(2,1)} %get-tuple-element.284.refs_2_.refs_1_), channel_id=1, source_target_pairs={{0,16},{16,0},{1,17},{17,1},{2,18},{18,2},{3,19},{19,3},{4,20},{20... | collective-permute-start | bytes 1572872 | tf_op jit(solution)/shard_map/s3/ring_h/ppermute | solution.py:69
  147.3 26.0 %collective-permute-start.24 = (bf16[128,2048]{1,0:T(8,128)(2,1)}, bf16[128,2048]{1,0:T(8,128)(2,1)}, u32[]{:S(2)}, u32[]{:S(2)}) collective-permute-start(bf16[128,2048]{1,0:T(8,128)(2,1)} %add_convert_fusion.3), channel_id=1, source_target_pairs={{0,8},{2,10},{8,0},{10,2},{1,9},{3,11},{9,1},{11,3},{4,12},{6,14},... | collective-permute-start | bytes 1572872 | tf_op jit(solution)/shard_map/s3/team10/ppermute | solution.py:64
  174.5 37.3 %collective-permute-start.32 = (bf16[512,1024]{1,0:T(8,128)(2,1)S(1)}, bf16[512,1024]{1,0:T(8,128)(2,1)S(1)}, u32[]{:S(2)}, u32[]{:S(2)}) collective-permute-start(bf16[512,1024]{1,0:T(8,128)(2,1)S(1)} %pad_maximum_fusion.2), channel_id=1, source_target_pairs={{0,4},{4,0},{1,5},{5,1},{2,6},{6,2},{3,7},{7,3},{8,12},{12,8},{9,1... | collective-permute-start | bytes 3145736 | tf_op jit(solution)/shard_map/s4/ring_y/ppermute | solution.py:69
  177.0 26.2 %collective-permute-start.29 = (bf16[128,2048]{1,0:T(8,128)(2,1)S(1)}, bf16[128,2048]{1,0:T(8,128)(2,1)S(1)}, u32[]{:S(2)}, u32[]{:S(2)}) collective-permute-start(bf16[128,2048]{1,0:T(8,128)(2,1)S(1)} %fusion.3.refs_0_), channel_id=1, source_target_pairs={{0,8},{2,10},{8,0},{10,2},{1,9},{3,11},{9,1},{11,3},{4,12},{6,14},... | collective-permute-start | bytes 1572872 | tf_op jit(solution)/shard_map/s4/team10/ppermute | solution.py:64
  178.3 26.3 %collective-permute-start.28 = (bf16[128,2048]{1,0:T(8,128)(2,1)S(1)}, bf16[128,2048]{1,0:T(8,128)(2,1)S(1)}, u32[]{:S(2)}, u32[]{:S(2)}) collective-permute-start(bf16[128,2048]{1,0:T(8,128)(2,1)S(1)} %fusion.3.refs_0_), channel_id=1, source_target_pairs={{0,2},{2,0},{8,10},{10,8},{1,3},{3,1},{9,11},{11,9},{4,6},{6,4},{1... | collective-permute-start | bytes 1572872 | tf_op jit(solution)/shard_map/s4/team01/ppermute | solution.py:64
  179.3 32.5 %collective-permute-start.27 = (bf16[128,2048]{1,0:T(8,128)(2,1)}, bf16[128,2048]{1,0:T(8,128)(2,1)S(1)}, u32[]{:S(2)}, u32[]{:S(2)}) collective-permute-start(bf16[128,2048]{1,0:T(8,128)(2,1)} %constant_dynamic-slice_fusion), channel_id=1, source_target_pairs={{0,4},{4,12},{8,0},{12,8},{1,5},{5,13},{9,1},{13,9},{2,6},{6,14},{... | collective-permute-start | bytes 1572872 | tf_op jit(solution)/shard_map/s4/flip/ppermute | solution.py:411
  180.5 31.3 %collective-permute-start.31 = (bf16[256,1024]{1,0:T(8,128)(2,1)S(1)}, bf16[256,1024]{1,0:T(8,128)(2,1)S(1)}, u32[]{:S(2)}, u32[]{:S(2)}) collective-permute-start(bf16[256,1024]{1,0:T(8,128)(2,1)S(1)} %get-tuple-element.296.refs_0_.refs_1_), channel_id=1, source_target_pairs={{0,16},{16,0},{1,17},{17,1},{2,18},{18,2},{3,19},{19,3},{4,20},{20... | collective-permute-start | bytes 1572872 | tf_op jit(solution)/shard_map/s4/ring_h/ppermute | solution.py:69
  213.5 27.0 %collective-permute-start.35 = (bf16[512,1024]{1,0:T(8,128)(2,1)S(1)}, bf16[512,1024]{1,0:T(8,128)(2,1)S(1)}, u32[]{:S(2)}, u32[]{:S(2)}) collective-permute-start(bf16[512,1024]{1,0:T(8,128)(2,1)S(1)} %pad_maximum_fusion.3), channel_id=1, source_target_pairs={{0,4},{4,0},{1,5},{5,1},{2,6},{6,2},{3,7},{7,3},{8,12},{12,8},{9,1... | collective-permute-start | bytes 3145736 | tf_op jit(solution)/shard_map/c2/ring_y/ppermute | solution.py:69
  214.1 26.4 %collective-permute-start.34 = (bf16[256,1024]{1,0:T(8,128)(2,1)S(1)}, bf16[256,1024]{1,0:T(8,128)(2,1)S(1)}, u32[]{:S(2)}, u32[]{:S(2)}) collective-permute-start(bf16[256,1024]{1,0:T(8,128)(2,1)S(1)} %get-tuple-element.302.refs_1_.refs_2_), channel_id=1, source_target_pairs={{0,16},{16,0},{1,17},{17,1},{2,18},{18,2},{3,19},{19,3},{4,20},{20... | collective-permute-start | bytes 1572872 | tf_op jit(solution)/shard_map/c2/ring_h/ppermute | solution.py:69
  309.9 28.9 %collective-permute-start.42 = (bf16[128,2048]{1,0:T(8,128)(2,1)S(1)}, bf16[128,2048]{1,0:T(8,128)(2,1)}, u32[]{:S(2)}, u32[]{:S(2)}) collective-permute-start(bf16[128,2048]{1,0:T(8,128)(2,1)S(1)} %get-tuple-element.327.refs_0_), channel_id=1, source_target_pairs={{0,2},{2,0},{8,10},{10,8},{1,3},{3,1},{9,11},{11,9},{4,6},{6,4},{1... | collective-permute-start | bytes 1572872 | tf_op jit(solution)/shard_map/s7/team01/ppermute | solution.py:64
  378.7 26.1 %collective-permute-start.50 = (bf16[512,1024]{1,0:T(8,128)(2,1)S(1)}, bf16[512,1024]{1,0:T(8,128)(2,1)S(1)}, u32[]{:S(2)}, u32[]{:S(2)}) collective-permute-start(bf16[512,1024]{1,0:T(8,128)(2,1)S(1)} %s8_.3), channel_id=1, source_target_pairs={{0,4},{4,0},{1,5},{5,1},{2,6},{6,2},{3,7},{7,3},{8,12},{12,8},{9,1... | collective-permute-start | bytes 3145736 | tf_op jit(solution)/shard_map/s8/ring_y/ppermute | solution.py:69
  379.4 26.4 %collective-permute-start.51 = (bf16[128,2048]{1,0:T(8,128)(2,1)S(1)}, bf16[128,2048]{1,0:T(8,128)(2,1)S(1)}, u32[]{:S(2)}, u32[]{:S(2)}) collective-permute-start(bf16[128,2048]{1,0:T(8,128)(2,1)S(1)} %get-tuple-element.339), channel_id=1, source_target_pairs={{0,2},{2,0},{8,10},{10,8},{1,3},{3,1},{9,11},{11,9},{4,6},{6,4},{1... | collective-permute-start | bytes 1572872 | tf_op jit(solution)/shard_map/s8/team01/ppermute | solution.py:64
  388.7 56.4 %collective-permute-start.56 = (bf16[512,1024]{1,0:T(8,128)(2,1)}, bf16[512,1024]{1,0:T(8,128)(2,1)}, u32[]{:S(2)}, u32[]{:S(2)}) collective-permute-start(bf16[512,1024]{1,0:T(8,128)(2,1)} %s9.5), channel_id=1, source_target_pairs={{0,4},{4,0},{1,5},{5,1},{2,6},{6,2},{3,7},{7,3},{8,12},{12,8},{9,1... | collective-permute-start | bytes 3145736 | tf_op jit(solution)/shard_map/s9/ring_y/ppermute | solution.py:69
  412.3 26.0 %collective-permute-start.59 = (bf16[128,2048]{1,0:T(8,128)(2,1)}, bf16[128,2048]{1,0:T(8,128)(2,1)}, u32[]{:S(2)}, u32[]{:S(2)}) collective-permute-start(bf16[128,2048]{1,0:T(8,128)(2,1)} %get-tuple-element.353.refs_0_), channel_id=1, source_target_pairs={{0,8},{2,10},{8,0},{10,2},{1,9},{3,11},{9,1},{11,3},{4,12},{6,14},... | collective-permute-start | bytes 1572872 | tf_op jit(solution)/shard_map/s9/team10/ppermute | solution.py:64
  415.9 29.1 %collective-permute-start.57 = (bf16[128,2048]{1,0:T(8,128)(2,1)S(1)}, bf16[128,2048]{1,0:T(8,128)(2,1)S(1)}, u32[]{:S(2)}, u32[]{:S(2)}) collective-permute-start(bf16[128,2048]{1,0:T(8,128)(2,1)S(1)} %get-tuple-element.394), channel_id=1, source_target_pairs={{4,8},{8,4},{5,9},{9,5},{6,10},{10,6},{7,11},{11,7},{20,24},{24,20... | collective-permute-start | bytes 1572872 | tf_op jit(solution)/shard_map/s9/ppermute | solution.py:109
  416.6 28.4 %collective-permute-start.58 = (bf16[128,2048]{1,0:T(8,128)(2,1)}, bf16[128,2048]{1,0:T(8,128)(2,1)S(1)}, u32[]{:S(2)}, u32[]{:S(2)}) collective-permute-start(bf16[128,2048]{1,0:T(8,128)(2,1)} %get-tuple-element.353.refs_0_), channel_id=1, source_target_pairs={{0,2},{2,0},{8,10},{10,8},{1,3},{3,1},{9,11},{11,9},{4,6},{6,4},{1... | collective-permute-start | bytes 1572872 | tf_op jit(solution)/shard_map/s9/team01/ppermute | solution.py:64
  418.5 26.6 %collective-permute-start.61 = (bf16[256,1024]{1,0:T(8,128)(2,1)}, bf16[256,1024]{1,0:T(8,128)(2,1)S(1)}, u32[]{:S(2)}, u32[]{:S(2)}) collective-permute-start(bf16[256,1024]{1,0:T(8,128)(2,1)} %copy-done.100), channel_id=1, source_target_pairs={{0,16},{16,0},{1,17},{17,1},{2,18},{18,2},{3,19},{19,3},{4,20},{20... | collective-permute-start | bytes 1572872 | tf_op jit(solution)/shard_map/s9/ring_h/ppermute | solution.py:69
  449.2 25.5 %collective-permute-start.66 = (bf16[256,1024]{1,0:T(8,128)(2,1)S(1)}, bf16[256,1024]{1,0:T(8,128)(2,1)S(1)}, u32[]{:S(2)}, u32[]{:S(2)}) collective-permute-start(bf16[256,1024]{1,0:T(8,128)(2,1)S(1)} %s9.6), channel_id=1, source_target_pairs={{0,16},{16,0},{1,17},{17,1},{2,18},{18,2},{3,19},{19,3},{4,20},{20... | collective-permute-start | bytes 1572872 | tf_op jit(solution)/shard_map/c4/ring_h/ppermute | solution.py:69
  449.3 25.4 %collective-permute-start.67 = (bf16[128,2048]{1,0:T(8,128)(2,1)S(1)}, bf16[128,2048]{1,0:T(8,128)(2,1)S(1)}, u32[]{:S(2)}, u32[]{:S(2)}) collective-permute-start(bf16[128,2048]{1,0:T(8,128)(2,1)S(1)} %get-tuple-element.362), channel_id=1, source_target_pairs={{0,8},{4,0},{8,12},{12,4},{1,9},{5,1},{9,13},{13,5},{2,10},{6,2},{... | collective-permute-start | bytes 1572872 | tf_op jit(solution)/shard_map/c4/ppermute | solution.py:431
  478.1 26.5 %collective-permute-start.69 = (bf16[256,1024]{1,0:T(8,128)(2,1)}, bf16[256,1024]{1,0:T(8,128)(2,1)}, u32[]{:S(2)}, u32[]{:S(2)}) collective-permute-start(bf16[256,1024]{1,0:T(8,128)(2,1)} %copy-done.103), channel_id=1, source_target_pairs={{0,16},{16,0},{1,17},{17,1},{2,18},{18,2},{3,19},{19,3},{4,20},{20... | collective-permute-start | bytes 1572872 | tf_op jit(solution)/shard_map/c4/ring_h/ppermute | solution.py:69
  509.0 29.9 %collective-permute-start.70 = (bf16[512,1024]{1,0:T(8,128)(2,1)}, bf16[512,1024]{1,0:T(8,128)(2,1)}, u32[]{:S(2)}, u32[]{:S(2)}) collective-permute-start(bf16[512,1024]{1,0:T(8,128)(2,1)} %s10.5), channel_id=1, source_target_pairs={{0,4},{4,0},{1,5},{5,1},{2,6},{6,2},{3,7},{7,3},{8,12},{12,8},{9,1... | collective-permute-start | bytes 3145736 | tf_op jit(solution)/shard_map/s10/ring_y/ppermute | solution.py:69
  509.4 33.6 %collective-permute-start.71 = (bf16[128,2048]{1,0:T(8,128)(2,1)}, bf16[128,2048]{1,0:T(8,128)(2,1)}, u32[]{:S(2)}, u32[]{:S(2)}) collective-permute-start(bf16[128,2048]{1,0:T(8,128)(2,1)} %get-tuple-element.375), channel_id=1, source_target_pairs={{0,2},{2,0},{8,10},{10,8},{1,3},{3,1},{9,11},{11,9},{4,6},{6,4},{1... | collective-permute-start | bytes 1572872 | tf_op jit(solution)/shard_map/s10/team01/ppermute | solution.py:64
  530.8 26.0 %collective-permute-start.76 = (bf16[512,1024]{1,0:T(8,128)(2,1)}, bf16[512,1024]{1,0:T(8,128)(2,1)}, u32[]{:S(2)}, u32[]{:S(2)}) collective-permute-start(bf16[512,1024]{1,0:T(8,128)(2,1)} %pad_maximum_fusion.6), channel_id=1, source_target_pairs={{0,4},{4,0},{1,5},{5,1},{2,6},{6,2},{3,7},{7,3},{8,12},{12,8},{9,1... | collective-permute-start | bytes 3145736 | tf_op jit(solution)/shard_map/s11/ring_y/ppermute | solution.py:69
  548.0 38.5 %collective-permute-start.79 = (bf16[128,2048]{1,0:T(8,128)(2,1)}, bf16[128,2048]{1,0:T(8,128)(2,1)}, u32[]{:S(2)}, u32[]{:S(2)}) collective-permute-start(bf16[128,2048]{1,0:T(8,128)(2,1)} %get-tuple-element.443), channel_id=1, source_target_pairs={{0,2},{2,0},{8,10},{10,8},{1,3},{3,1},{9,11},{11,9},{4,6},{6,4},{1... | collective-permute-start | bytes 1572872 | tf_op jit(solution)/shard_map/s11/team01/ppermute | solution.py:64
  549.6 36.9 %collective-permute-start.80 = (bf16[128,2048]{1,0:T(8,128)(2,1)}, bf16[128,2048]{1,0:T(8,128)(2,1)}, u32[]{:S(2)}, u32[]{:S(2)}) collective-permute-start(bf16[128,2048]{1,0:T(8,128)(2,1)} %get-tuple-element.442), channel_id=1, source_target_pairs={{0,8},{2,10},{8,0},{10,2},{1,9},{3,11},{9,1},{11,3},{4,12},{6,14},... | collective-permute-start | bytes 1572872 | tf_op jit(solution)/shard_map/s11/team10/ppermute | solution.py:64
  549.6 33.4 %collective-permute-start.78 = (bf16[256,768]{1,0:T(8,128)(2,1)}, bf16[256,768]{1,0:T(8,128)(2,1)}, u32[]{:S(2)}, u32[]{:S(2)}) collective-permute-start(bf16[256,768]{1,0:T(8,128)(2,1)} %s10.7), channel_id=1, source_target_pairs={{0,16},{16,0},{1,17},{17,1},{2,18},{18,2},{3,19},{19,3},{4,20},{20... | collective-permute-start | bytes 1179656 | tf_op jit(solution)/shard_map/s11/ring_h/ppermute | solution.py:69
  556.7 29.7 %collective-permute-start.81 = (bf16[128,2048]{1,0:T(8,128)(2,1)}, bf16[128,2048]{1,0:T(8,128)(2,1)}, u32[]{:S(2)}, u32[]{:S(2)}) collective-permute-start(bf16[128,2048]{1,0:T(8,128)(2,1)} %get-tuple-element.441), channel_id=1, source_target_pairs={{0,10},{2,8},{8,2},{10,0},{1,11},{3,9},{9,3},{11,1},{4,14},{6,12},... | collective-permute-start | bytes 1572872 | tf_op jit(solution)/shard_map/s11/team11/ppermute | solution.py:64
  (209 other events, 3014.5 us)
